TPU v7x, 32 devices: a whole 2x2x4 slice. The times are simulated.
32 devices in a mesh: comp: 4 (over y, x), lat: 4 (over z), lon: 2 (over core).
Axes of the slice: x: 2, y: 2, z: 4, core: 2. Of those that a mesh axis runs over, the one named last changes fastest.
Arguments:
- state: float32 [2048, 256, 128], P(('comp', 'lat'), 'lon'), may hold values from -6 to 6
- land_mask: int32 [2048, 256], P(('comp', 'lat'), 'lon'), may hold values 0 or 1
- intersection_list: int32 [2048, 2, 2, 3], P(('comp', 'lat'), 'lon'), may hold values from 0 to 127, as said below
- mix_atm: float32 [128, 128], replicated, may hold values from -0.5 to 0.5
- mix_ocn: float32 [128, 128], replicated, may hold values from -0.5 to 0.5
- flux_map: float32 [128, 8], replicated, may hold values from -0.5 to 0.5
- ocean_map: float32 [8, 128], replicated, may hold values from -2 to 2
- regrid_weights: bfloat16 [32, 128, 128], replicated, may hold values from -0.25 to 0.25
Outputs:
- state_out: float32 [2048, 256, 128], P(('comp', 'lat'), 'lon')
- surface_out: float32 [2048, 256], P(('comp', 'lat'), 'lon')
Inputs may be any that keep to these rules, and one draw needn't show every extreme that they name: `intersection_list`: entry 0 is an ocean tile lat * 2 + lon, entry 1 a row of that tile below 128, entry 2 a weight block below 32. With t the tile lat * 2 + lon of the list's own rows and r = min(4, 2), the entries of one tile name exactly the 2 r tiles (t + a * 2 + b - (r - 1) // 2) mod (4 * 2) for a in 0, 1 and b in 0 to r - 1, each by exactly 64 entries.
All inputs are finite; a program needn't handle non-finite values. No bound on the sum of `land_mask` on one device may be relied on, other than what follows from the above.
Results may differ from a plain program's by a relative error of at most 0.0012.
Values may be sent and summed in bfloat16 or wider, within the bound.
No kernel may reach another device: no remote copies, remote signals or barrier semaphores. Data moves between devices by JAX's collectives and lax.ppermute only.
A program may use at most 192 MiB of HBM per device.

v0:
```python
import functools

import jax
import jax.numpy as jnp
from jax import lax
from jax.experimental import pallas as pl
from jax.experimental.pallas import tpu as pltpu
from jax.sharding import PartitionSpec as P

SMOOTHING = 0.2
PHYSICS = 0.5
MIB = 1024 * 1024
F32 = jnp.float32
BF16 = jnp.bfloat16
EDGE = 8
CHUNK = 8
AXES = ("comp", "lat", "lon")


def split_two(x):
    high = x.astype(BF16)
    low = (x - high.astype(F32)).astype(BF16)
    return high, low


def side_by_side(x):
    return jnp.concatenate(split_two(x), axis=1)


def dot_nt(a, b):
    return lax.dot_general(a, b, (((1,), (1,)), ((), ())), preferred_element_type=F32)


def dot_nn(a, b):
    return jnp.dot(a, b, preferred_element_type=F32)


def edges_kernel(
    state, first_rows, last_rows, first_cols, last_cols, top_corners, low_corners, left, right, sems
):
    rows, cols, _ = state.shape
    copies = [
        pltpu.make_async_copy(state.at[:, pl.ds(0, EDGE)], left, sems.at[0]),
        pltpu.make_async_copy(state.at[:, pl.ds(cols - EDGE, EDGE)], right, sems.at[1]),
        pltpu.make_async_copy(state.at[pl.ds(0, 2)], first_rows, sems.at[2]),
        pltpu.make_async_copy(state.at[pl.ds(rows - 2, 2)], last_rows, sems.at[3]),
    ]
    for copy in copies:
        copy.start()
    for copy in copies:
        copy.wait()
    for i in range(2):
        first_cols[i] = left[:, i, :]
        last_cols[i] = right[:, EDGE - 2 + i, :]
    top_corners[...] = jnp.zeros(top_corners.shape, F32)
    low_corners[...] = jnp.zeros(low_corners.shape, F32)
    top_corners[0:1] = left[0, 0:1]
    top_corners[1:2] = right[0, EDGE - 1 :]
    low_corners[0:1] = left[rows - 1, 0:1]
    low_corners[1:2] = right[rows - 1, EDGE - 1 :]


def take_edges(state):
    rows, cols, levels = state.shape
    slab = jax.ShapeDtypeStruct((2, cols, levels), F32)
    side = jax.ShapeDtypeStruct((2, rows, levels), F32)
    corner = jax.ShapeDtypeStruct((EDGE, levels), F32)
    vmem = pl.BlockSpec(memory_space=pltpu.VMEM)
    return pl.pallas_call(
        edges_kernel,
        out_shape=(slab, slab, side, side, corner, corner),
        in_specs=[pl.BlockSpec(memory_space=pl.ANY)],
        out_specs=(vmem,) * 6,
        scratch_shapes=[
            pltpu.VMEM((rows, EDGE, levels), F32),
            pltpu.VMEM((rows, EDGE, levels), F32),
            pltpu.SemaphoreType.DMA((4,)),
        ],
        compiler_params=pltpu.CompilerParams(vmem_limit_bytes=16 * MIB),
        name="edges",
    )(state)


def advance_kernel(neighbours, capacity, *refs):
    (flags, sources, state, up_rows, low_rows, left_cols, right_cols, own_first, own_last) = refs[:9]
    (up_left, up_right, low_left, low_right, mask, mix_atm, mix_ocn, flux_map) = refs[9:17]
    out = refs[17]
    packed = refs[18 : 18 + neighbours]
    (values, moved, halo, halo_moved, smooth, pairs, mixed, weights, flux_weights, fluxes, staged) = refs[
        18 + neighbours : 29 + neighbours
    ]
    in_sems, out_sems = refs[29 + neighbours :]
    rows, cols, levels = state.shape
    chunks = rows // CHUNK
    inner = pl.ds(EDGE, cols)
    flux_count = flux_map.shape[0]

    def fetch(q):
        return pltpu.make_async_copy(
            state.at[pl.ds(q * CHUNK, CHUNK)],
            values.at[pl.ds(q * CHUNK + 2, CHUNK), inner],
            in_sems.at[q],
        )

    def put(q, slot):
        return pltpu.make_async_copy(
            staged.at[slot], out.at[pl.ds(q * CHUNK, CHUNK)], out_sems.at[slot]
        )

    def begin(q, _):
        fetch(q).start()
        return 0

    lax.fori_loop(0, chunks, begin, 0)
    ocean = flags[0] == 1
    mix = jnp.where(ocean, mix_ocn[...], mix_atm[...])
    mix_high, mix_low = split_two(mix)
    weights[:levels, :levels] = mix_high
    weights[levels:, :levels] = mix_high
    weights[:levels, levels:] = mix_low
    weights[levels:, levels:] = mix_low
    map_high, map_low = split_two(flux_map[...])
    flux_weights[...] = jnp.concatenate(
        [
            jnp.concatenate([map_high.astype(F32), map_high.astype(F32)], axis=1),
            jnp.concatenate([map_low.astype(F32), map_low.astype(F32)], axis=1),
        ],
        axis=0,
    ).astype(BF16)
    values[0:2, EDGE : EDGE + cols, :] = up_rows[...]
    values[rows + 2 : rows + 4, EDGE : EDGE + cols, :] = low_rows[...]
    values[1, EDGE - 1 : EDGE, :] = up_left[1:2]
    values[1, EDGE + cols : EDGE + cols + 1, :] = up_right[0:1]
    values[rows + 2, EDGE - 1 : EDGE, :] = low_left[1:2]
    values[rows + 2, EDGE + cols : EDGE + cols + 1, :] = low_right[0:1]

    def side_cells(r, _):
        values[r + 2, EDGE - 1 : EDGE, :] = left_cols[1, pl.ds(r, 1), :]
        values[r + 2, EDGE + cols : EDGE + cols + 1, :] = right_cols[0, pl.ds(r, 1), :]
        return 0

    lax.fori_loop(0, rows, side_cells, 0, unroll=8)

    def stage(row, total):
        line = SMOOTHING * total
        smooth[row] = line
        pairs[row * cols : (row + 1) * cols, :] = side_by_side(line)

    def mix_rows(count):
        mixed[: count * cols, :] = dot_nn(pairs[: count * cols, :], weights[...])

    def finish(row):
        part = mixed[row * cols : (row + 1) * cols, :]
        return smooth[row] + PHYSICS * jnp.tanh(part[:, :levels] + part[:, levels:])

    def gather_row(ref, i):
        here = ref[i, EDGE : EDGE + cols, :] + (
            ref[i - 1, EDGE : EDGE + cols, :] + ref[i + 1, EDGE : EDGE + cols, :]
        )
        return here + (
            ref[i, EDGE - 1 : EDGE - 1 + cols, :] + ref[i, EDGE + 1 : EDGE + 1 + cols, :]
        )

    @pl.when(jnp.logical_not(ocean))
    def atmosphere():
        halo[0, EDGE : EDGE + rows, :] = left_cols[1]
        halo[0, EDGE - 1 : EDGE, :] = up_left[1:2]
        halo[0, EDGE + rows : EDGE + rows + 1, :] = low_left[1:2]
        halo[1, EDGE : EDGE + rows, :] = right_cols[0]
        halo[1, EDGE - 1 : EDGE, :] = up_right[0:1]
        halo[1, EDGE + rows : EDGE + rows + 1, :] = low_right[0:1]
        beyond = (left_cols.at[0], right_cols.at[1])
        within = (own_first.at[0], own_last.at[1])
        for s in range(2):
            total = (
                halo[s, EDGE : EDGE + rows, :]
                + halo[s, EDGE - 1 : EDGE - 1 + rows, :]
                + halo[s, EDGE + 1 : EDGE + 1 + rows, :]
            )
            stage(s, total + (beyond[s][...] + within[s][...]))
        mix_rows(2)
        for s in range(2):
            halo_moved[s] = finish(s)

        def moved_sides(r, _):
            moved[r + 1, EDGE - 1 : EDGE, :] = halo_moved[0, pl.ds(r, 1), :]
            moved[r + 1, EDGE + cols : EDGE + cols + 1, :] = halo_moved[1, pl.ds(r, 1), :]
            return 0

        lax.fori_loop(0, rows, moved_sides, 0, unroll=8)
        fetch(0).wait()
        for row in range(2):
            stage(row, gather_row(values, row + 1))
        mix_rows(2)
        moved[0, EDGE : EDGE + cols, :] = finish(0)
        moved[1, EDGE : EDGE + cols, :] = finish(1)

        @pl.when(flags[1] == 0)
        def _():
            moved[0, EDGE : EDGE + cols, :] = jnp.zeros((cols, levels), F32)


        def one_chunk(q, _):
            base = q * CHUNK

            @pl.when(q + 1 < chunks)
            def _():
                fetch(q + 1).wait()

            for row in range(CHUNK):
                stage(row, gather_row(values, base + row + 3))
            mix_rows(CHUNK)
            for row in range(CHUNK):
                moved[base + row + 2, EDGE : EDGE + cols, :] = finish(row)

            @pl.when((q + 1 == chunks) & (flags[2] == 0))
            def _():
                moved[rows + 1, EDGE : EDGE + cols, :] = jnp.zeros((cols, levels), F32)

            for row in range(CHUNK):
                stage(row, gather_row(moved, base + row + 1))
            mix_rows(CHUNK)
            slot = q % 2

            @pl.when(q >= 2)
            def _():
                put(q - 2, slot).wait()

            for row in range(CHUNK):
                line = finish(row)
                staged[slot, row] = line
                both = line + moved[base + row + 1, EDGE : EDGE + cols, :]
                pairs[row * cols : (row + 1) * cols, :] = side_by_side(both)
            put(q, slot).start()
            flux = dot_nt(flux_weights[...], pairs[...])
            flux = flux[:flux_count] + flux[flux_count:]
            for row in range(CHUNK):
                block = PHYSICS * flux[:, row * cols : (row + 1) * cols]
                sea = jnp.broadcast_to(mask[pl.ds(base + row, 1), :], block.shape)
                block = jnp.where(sea > 0.5, block, 0.0)
                fluxes[base + row] = block.astype(BF16).astype(F32)
            return 0

        lax.fori_loop(0, chunks, one_chunk, 0)
        put(chunks - 2, (chunks - 2) % 2).wait()
        put(chunks - 1, (chunks - 1) % 2).wait()
        for n in range(neighbours):

            def pack(i, _, n=n):
                first = fluxes[sources[n * capacity + 2 * i]]
                second = fluxes[sources[n * capacity + 2 * i + 1]]
                packed[n][i] = jnp.concatenate([first, second], axis=0).astype(BF16)
                return 0

            lax.fori_loop(0, capacity // 2, pack, 0, unroll=8)

    @pl.when(ocean)
    def sea_side():
        fetch(0).wait()
        lanes = lax.broadcasted_iota(jnp.int32, (CHUNK, CHUNK * levels), 1) // levels
        lines = lax.broadcasted_iota(jnp.int32, (CHUNK, CHUNK * levels), 0)
        spreader = jnp.where(lanes == lines, 1.0, 0.0).astype(F32)

        def one_chunk(q, _):
            base = q * CHUNK

            @pl.when(q + 1 < chunks)
            def _():
                fetch(q + 1).wait()

            for row in range(CHUNK):
                stage(row, gather_row(values, base + row + 2))
            mix_rows(CHUNK)
            slot = q % 2

            @pl.when(q >= 2)
            def _():
                put(q - 2, slot).wait()

            sea = dot_nn(mask[pl.ds(pl.multiple_of(base, CHUNK), CHUNK), :].T, spreader)
            for row in range(CHUNK):
                chosen = sea[:, row * levels : (row + 1) * levels] > 0.5
                before = values[base + row + 2, EDGE : EDGE + cols, :]
                staged[slot, row] = jnp.where(chosen, finish(row), before)
            put(q, slot).start()
            return 0

        lax.fori_loop(0, chunks, one_chunk, 0)
        put(chunks - 2, (chunks - 2) % 2).wait()
        put(chunks - 1, (chunks - 1) % 2).wait()


def advance(flags, sources, state, halos, mask, mix_atm, mix_ocn, flux_map_t, neighbours, capacity):
    rows, cols, levels = state.shape
    fluxes = flux_map_t.shape[0]
    vmem = pl.BlockSpec(memory_space=pltpu.VMEM)
    smem = pl.BlockSpec(memory_space=pltpu.SMEM)
    hbm = pl.BlockSpec(memory_space=pl.ANY)
    entry = jax.ShapeDtypeStruct((capacity // 2, 2 * fluxes, cols), BF16)
    cells = rows * cols
    return pl.pallas_call(
        functools.partial(advance_kernel, neighbours, capacity),
        out_shape=(jax.ShapeDtypeStruct(state.shape, F32),) + (entry,) * neighbours,
        in_specs=[smem, smem, hbm] + [vmem] * (len(halos) + 4),
        out_specs=(hbm,) + (vmem,) * neighbours,
        scratch_shapes=[
            pltpu.VMEM((rows + 4, cols + 2 * EDGE, levels), F32),
            pltpu.VMEM((rows + 2, cols + 2 * EDGE, levels), F32),
            pltpu.VMEM((2, rows + 2 * EDGE, levels), F32),
            pltpu.VMEM((2, rows, levels), F32),
            pltpu.VMEM((CHUNK, cols, levels), F32),
            pltpu.VMEM((CHUNK * cols, 2 * levels), BF16),
            pltpu.VMEM((CHUNK * cols, 2 * levels), F32),
            pltpu.VMEM((2 * levels, 2 * levels), BF16),
            pltpu.VMEM((2 * fluxes, 2 * levels), BF16),
            pltpu.VMEM((rows, fluxes, cols), F32),
            pltpu.VMEM((2, CHUNK, cols, levels), F32),
            pltpu.SemaphoreType.DMA((rows // CHUNK,)),
            pltpu.SemaphoreType.DMA((2,)),
        ],
        compiler_params=pltpu.CompilerParams(vmem_limit_bytes=48 * MIB),
        cost_estimate=pl.CostEstimate(
            flops=8 * cells * levels * levels, bytes_accessed=8 * cells * levels, transcendentals=0
        ),
        name="advance",
    )(flags, sources, state, *halos, mask, mix_atm, mix_ocn, flux_map_t)


def regrid_kernel(groups, capacity, *refs):
    flags, labels = refs[:2]
    entries = refs[2 : 2 + groups]
    target_column, weights, surface, mask, ocean_first = refs[2 + groups : 7 + groups]
    forcing, new_surface = refs[7 + groups : 9 + groups]
    picked = refs[9 + groups : 9 + 2 * groups]
    (bins,) = refs[9 + 2 * groups :]
    rows, flux_count, cols = forcing.shape
    weight_count = weights.shape[0]

    @pl.when(flags[0] == 1)
    def ocean():
        def clear(i, _):
            bins[pl.ds(i * 32, 32)] = jnp.zeros((32, flux_count, cols), F32)
            return 0

        lax.fori_loop(0, weight_count * rows // 32, clear, 0)
        for j in range(groups):

            def add(i, _, j=j):
                pair = entries[j][i].astype(F32)
                bins[labels[j * capacity + 2 * i]] += pair[:flux_count]
                bins[labels[j * capacity + 2 * i + 1]] += pair[flux_count:]
                return 0

            lax.fori_loop(0, capacity // 2, add, 0, unroll=8)

        def products(w):
            block = bins[pl.ds(w * rows, rows)].reshape(rows * flux_count, cols)
            once = weights[w]
            return dot_nn(side_by_side(block), jnp.concatenate([once, once], axis=0))

        forcing[...] = products(0).reshape(forcing.shape)

        def accumulate(w, _):
            forcing[...] += products(w).reshape(forcing.shape)
            return 0

        lax.fori_loop(1, weight_count, accumulate, 0)
        change = jnp.sum(forcing[...] * ocean_first[...][None], axis=1)
        now = surface[...] + jnp.where(mask[...] > 0.5, change, 0.0)
        new_surface[...] = now
        now_pair = jnp.concatenate(split_two(now), axis=0)
        spots = lax.broadcasted_iota(jnp.int32, (capacity, rows), 1)
        for j in range(groups):
            chosen = target_column[j * capacity : (j + 1) * capacity, :] == spots
            chosen = jnp.where(chosen, 1.0, 0.0).astype(BF16)
            picked[j][...] = dot_nn(jnp.concatenate([chosen, chosen], axis=1), now_pair)


def regrid(flags, labels, entries, target_column, weights, surface, mask, ocean_first, capacity):
    groups = len(entries)
    rows, cols = mask.shape
    flux_count = ocean_first.shape[0]
    weight_count = weights.shape[0]
    vmem = pl.BlockSpec(memory_space=pltpu.VMEM)
    smem = pl.BlockSpec(memory_space=pltpu.SMEM)
    return pl.pallas_call(
        functools.partial(regrid_kernel, groups, capacity),
        out_shape=(
            jax.ShapeDtypeStruct((rows, flux_count, cols), F32),
            jax.ShapeDtypeStruct((rows, cols), F32),
        )
        + (jax.ShapeDtypeStruct((capacity, cols), F32),) * groups,
        in_specs=[smem, smem] + [vmem] * (groups + 5),
        out_specs=(vmem,) * (2 + groups),
        scratch_shapes=[pltpu.VMEM((weight_count * rows, flux_count, cols), F32)],
        compiler_params=pltpu.CompilerParams(vmem_limit_bytes=40 * MIB),
        cost_estimate=pl.CostEstimate(
            flops=4 * weight_count * rows * flux_count * cols * cols,
            bytes_accessed=8 * MIB,
            transcendentals=0,
        ),
        name="regrid",
    )(flags, labels, *entries, target_column, weights, surface, mask, ocean_first)


LINES = 16


def update_kernel(flags, state, forcing, mask, ocean_map, out, held, table, wide, in_sems, out_sems):
    rows, cols, levels = state.shape
    flux_count = forcing.shape[1]
    chunks = rows // LINES
    depth = LINES * flux_count

    def fetch(q):
        return pltpu.make_async_copy(
            state.at[pl.ds(q * LINES, LINES)], held.at[pl.ds(q * LINES, LINES)], in_sems.at[q]
        )

    def put(q):
        return pltpu.make_async_copy(
            held.at[pl.ds(q * LINES, LINES)], out.at[pl.ds(q * LINES, LINES)], out_sems.at[q]
        )

    @pl.when(flags[0] == 1)
    def ocean():
        for q in range(chunks):
            fetch(q).start()
        table[...] = jnp.zeros(table.shape, F32)
        for line in range(LINES):
            table[
                line * flux_count : (line + 1) * flux_count, line * levels : (line + 1) * levels
            ] = ocean_map[...]
        high, low = split_two(table[...])
        wide[:depth] = high
        wide[depth : 2 * depth] = high
        wide[2 * depth :] = low

        def one(q, _):
            start = pl.multiple_of(q * LINES, LINES)
            sea = mask[pl.ds(start, LINES), :]
            part = jnp.where(sea[:, None, :] > 0.5, forcing[pl.ds(start, LINES)], 0.0)
            turned = part.reshape(depth, cols).T
            first, second = split_two(turned)
            change = dot_nn(jnp.concatenate([first, second, first], axis=1), wide[...])
            fetch(q).wait()
            for line in range(LINES):
                held[start + line] += change[:, line * levels : (line + 1) * levels]
            put(q).start()
            return 0

        lax.fori_loop(0, chunks, one, 0)
        for q in range(chunks):
            put(q).wait()


def update(flags, state, forcing, mask, ocean_map):
    rows, cols, levels = state.shape
    depth = LINES * forcing.shape[1]
    vmem = pl.BlockSpec(memory_space=pltpu.VMEM)
    smem = pl.BlockSpec(memory_space=pltpu.SMEM)
    hbm = pl.BlockSpec(memory_space=pl.ANY)
    return pl.pallas_call(
        update_kernel,
        out_shape=jax.ShapeDtypeStruct(state.shape, F32),
        in_specs=[smem, hbm, vmem, vmem, vmem],
        out_specs=hbm,
        input_output_aliases={1: 0},
        scratch_shapes=[
            pltpu.VMEM(state.shape, F32),
            pltpu.VMEM((depth, LINES * levels), F32),
            pltpu.VMEM((3 * depth, LINES * levels), BF16),
            pltpu.SemaphoreType.DMA((rows // LINES,)),
            pltpu.SemaphoreType.DMA((rows // LINES,)),
        ],
        compiler_params=pltpu.CompilerParams(vmem_limit_bytes=24 * MIB),
        cost_estimate=pl.CostEstimate(
            flops=6 * rows * cols * depth * levels,
            bytes_accessed=8 * rows * cols * levels,
            transcendentals=0,
        ),
        name="update",
    )(flags, state, forcing, mask, ocean_map)


def returned_kernel(groups, flags, *refs):
    picked = refs[:groups]
    weight_column, row_line, weights, mask, surface, new_surface, out, total = refs[groups:]
    rows, cols = mask.shape
    weight_count = weights.shape[0]

    @pl.when(flags[0] == 1)
    def ocean():
        out[...] = new_surface[...]

    @pl.when(flags[0] == 0)
    def atmosphere():
        values = jnp.concatenate([p[...] for p in picked], axis=0)
        pair = side_by_side(values)
        which = jnp.broadcast_to(weight_column[...], values.shape)
        total[...] = jnp.zeros(values.shape, F32)

        def one(i, _):
            both = jnp.concatenate([weights[2 * i], weights[2 * i + 1]], axis=0)
            images = dot_nt(pair, jnp.concatenate([both, both], axis=1))
            total[...] += jnp.where(which == 2 * i, images[:, :cols], 0.0) + jnp.where(
                which == 2 * i + 1, images[:, cols:], 0.0
            )
            return 0

        lax.fori_loop(0, weight_count // 2, one, 0, unroll=2)
        spots = lax.broadcasted_iota(jnp.int32, (rows, values.shape[0]), 0)
        chosen = jnp.where(jnp.broadcast_to(row_line[...], spots.shape) == spots, 1.0, 0.0).astype(BF16)
        high, low = split_two(total[...])
        back = dot_nn(chosen, high) + dot_nn(chosen, low)
        out[...] = jnp.where(mask[...] > 0.5, back, surface[...])


def returned(flags, picked, weight_column, row_line, weights, mask, surface, new_surface):
    rows, cols = mask.shape
    entry_total = weight_column.shape[0]
    vmem = pl.BlockSpec(memory_space=pltpu.VMEM)
    smem = pl.BlockSpec(memory_space=pltpu.SMEM)
    return pl.pallas_call(
        functools.partial(returned_kernel, len(picked)),
        out_shape=jax.ShapeDtypeStruct((rows, cols), F32),
        in_specs=[smem] + [vmem] * (len(picked) + 6),
        out_specs=vmem,
        scratch_shapes=[pltpu.VMEM((entry_total, cols), F32)],
        compiler_params=pltpu.CompilerParams(vmem_limit_bytes=16 * MIB),
        name="returned",
    )(flags, *picked, weight_column, row_line, weights, mask, surface, new_surface)


def local(
    state, land_mask, intersection_list, mix_atm, mix_ocn, flux_map, ocean_map, regrid_weights
):
    rows, cols, levels = state.shape
    intersections = intersection_list.shape[2]
    comp_count = lax.axis_size("comp")
    lat_count = lax.axis_size("lat")
    lon_count = lax.axis_size("lon")
    tile_count = lat_count * lon_count
    reach = min(4, lon_count)
    neighbours = 2 * reach
    entry_total = intersections * rows
    capacity = entry_total // neighbours
    comp_index = lax.axis_index("comp")
    lat_index = lax.axis_index("lat")
    tile_index = lat_index * lon_count + lax.axis_index("lon")
    bands = comp_count * lat_count
    ocean_band = (comp_count - 1) * lat_count
    ocean_comp = comp_count - 1
    band = comp_index * lat_count + lat_index
    is_ocean = comp_index == ocean_comp
    upper_valid = (band > 0) & (band != ocean_band)
    lower_valid = (band < bands - 1) & (band != ocean_band - 1)
    flags = jnp.stack([is_ocean, upper_valid, lower_valid]).astype(jnp.int32)
    mask = (land_mask == 1).astype(F32)

    def band_shift(value, by, lon_by):
        pairs = []
        for b in range(bands):
            target = b + by
            if 0 <= target < bands and (b >= ocean_band) == (target >= ocean_band):
                for lon in range(lon_count):
                    pairs.append(
                        (b * lon_count + lon, target * lon_count + (lon + lon_by) % lon_count)
                    )
        return lax.ppermute(value, AXES, pairs)

    first_rows, last_rows, first_cols, last_cols, top_corners, low_corners = take_edges(state)
    up_rows = band_shift(last_rows, 1, 0)
    low_rows = band_shift(first_rows, -1, 0)
    left_cols = band_shift(last_cols, 0, 1)
    right_cols = band_shift(first_cols, 0, -1)
    up_left = band_shift(low_corners, 1, 1)
    low_left = band_shift(top_corners, -1, 1)
    if lon_count == 2:
        up_right, low_right = up_left, low_left
    else:
        up_right = band_shift(low_corners, 1, -1)
        low_right = band_shift(top_corners, -1, -1)

    entry_list = intersection_list.reshape(entry_total, 3)
    owners = entry_list[:, 0]
    labels = entry_list[:, 2] * rows + entry_list[:, 1]
    offsets = [
        (n // reach * lon_count + n % reach - (reach - 1) // 2) % tile_count
        for n in range(neighbours)
    ]
    distance = (owners - tile_index + tile_count) % tile_count
    hits = distance[:, None] == jnp.array(offsets, jnp.int32)[None, :]
    neighbour_ids = jnp.sum(
        jnp.where(hits, jnp.arange(neighbours, dtype=jnp.int32)[None, :], 0), axis=1
    )
    positions = jnp.arange(entry_total, dtype=jnp.int32)
    earlier = (neighbour_ids[None, :] == neighbour_ids[:, None]) & (
        positions[None, :] < positions[:, None]
    )
    slots = neighbour_ids * capacity + jnp.sum(earlier.astype(jnp.int32), axis=1)
    placing = positions[:, None] == slots[None, :]
    sources = jnp.sum(jnp.where(placing, (positions // intersections)[None, :], 0), axis=1)
    packed_labels = jnp.sum(jnp.where(placing, labels[None, :], 0), axis=1)

    def to_ocean(value, comp, offset):
        pairs = [
            (comp * tile_count + t, ocean_comp * tile_count + (t + offset) % tile_count)
            for t in range(tile_count)
        ]
        return lax.ppermute(value, AXES, pairs)

    def from_ocean(value, comp, offset):
        pairs = [
            (ocean_comp * tile_count + (t + offset) % tile_count, comp * tile_count + t)
            for t in range(tile_count)
        ]
        return lax.ppermute(value, AXES, pairs)

    order = [(c, n) for n in range(neighbours) for c in range(comp_count - 1)]
    arrived_labels = jnp.concatenate(
        [
            to_ocean(packed_labels[n * capacity : (n + 1) * capacity], c, offsets[n])
            for c, n in order
        ]
    )
    target_column = (arrived_labels % rows)[:, None]

    halos = (up_rows, low_rows, left_cols, right_cols, first_cols, last_cols)
    halos = halos + (up_left, up_right, low_left, low_right)
    moved = advance(
        flags, sources, state, halos, mask, mix_atm, mix_ocn, flux_map.T, neighbours, capacity
    )
    moved, packed = moved[0], moved[1:]
    entries = [to_ocean(packed[n], c, offsets[n]) for c, n in order]
    surface = moved[:, :, 0]
    ocean_first = jnp.broadcast_to(ocean_map[:, :1], (ocean_map.shape[0], cols))
    regridded = regrid(
        flags, arrived_labels, entries, target_column, regrid_weights, surface, mask,
        ocean_first, capacity,
    )
    forcing, new_surface, picked = regridded[0], regridded[1], regridded[2:]
    arrived = [None] * neighbours
    for (c, n), value in zip(order, picked):
        one = from_ocean(value, c, offsets[n])
        arrived[n] = one if arrived[n] is None else jnp.where(comp_index == c, one, arrived[n])
    final_state = update(flags, moved, forcing, mask, ocean_map)
    weight_column = (packed_labels // rows)[:, None]
    surface_out = returned(
        flags, arrived, weight_column, sources[None, :], regrid_weights, mask, surface, new_surface
    )
    return (final_state, surface_out)


def solution(mesh):
    placed = (
        P(("comp", "lat"), "lon", None),
        P(("comp", "lat"), "lon"),
        P(("comp", "lat"), "lon", None, None),
        P(),
        P(),
        P(),
        P(),
        P(),
    )
    return jax.shard_map(
        local,
        mesh=mesh,
        in_specs=placed,
        out_specs=(P(("comp", "lat"), "lon", None), P(("comp", "lat"), "lon")),
        check_vma=False,
    )
```

profile of v0, /device:TPU:16, one launch (start us, length us, event | category | flops | bytes accessed | tf_op | source)
XLA Modules:
  0.0 152.9 jit_solution(2119528814603930259)
XLA Ops:
  0.7 0.9 copy.55
  2.3 5.4 %collective-permute-start.12 = (s32[64]{0:T(128)S(1)}, s32[64]{0:T(128)S(1)}, u32[]{:S(2)}, u32[]{:S(2)}) collective-permute-start(s32[64]{0:T(128)S(1)} %get-tuple-element.57), channel_id=1, source_target_pairs={{0,26},{1,27},{2,28},{3,29},{4,30},{5,31},{6,24},{7,25}} | collective-permute-start | bytes 776 | tf_op jit(solution)/shard_map/ppermute | solution.py:611
  7.6 0.7 collective-permute-start.13
  8.3 0.7 collective-permute-start.14
  9.0 0.7 collective-permute-start.11
  9.6 2.6 %collective-permute-start.15 = (s32[64]{0:T(128)S(1)}, s32[64]{0:T(128)S(1)}, u32[]{:S(2)}, u32[]{:S(2)}) collective-permute-start(s32[64]{0:T(128)S(1)} %get-tuple-element.56), channel_id=1, source_target_pairs={{0,27},{1,28},{2,29},{3,30},{4,31},{5,24},{6,25},{7,26}} | collective-permute-start | bytes 776 | tf_op jit(solution)/shard_map/ppermute | solution.py:611
  12.5 0.8 compare_convert_fusion.refs_13_.refs_17_.mask.refs_7_
  13.4 3.4 %copy-done = f32[128,128,128]{2,1,0:T(8,128)S(1)} copy-done((f32[128,128,128]{2,1,0:T(8,128)S(1)}, f32[128,128,128]{2,1,0:T(8,128)}, u32[]{:S(2)}) %copy-start) | copy-done | bytes 8388632
  16.7 0.7 edges.1
  17.4 0.7 collective-permute-start.16
  18.8 2.1 %collective-permute-start.6 = (s32[64]{0:T(128)S(1)}, s32[64]{0:T(128)S(1)}, u32[]{:S(2)}, u32[]{:S(2)}) collective-permute-start(s32[64]{0:T(128)S(1)} %get-tuple-element.59), channel_id=1, source_target_pairs={{0,24},{1,25},{2,26},{3,27},{4,28},{5,29},{6,30},{7,31}} | collective-permute-start | bytes 776 | tf_op jit(solution)/shard_map/ppermute | solution.py:611
  22.3 2.0 %collective-permute-start.9 = (s32[64]{0:T(128)S(1)}, s32[64]{0:T(128)S(1)}, u32[]{:S(2)}, u32[]{:S(2)}) collective-permute-start(s32[64]{0:T(128)S(1)} %get-tuple-element.58), channel_id=1, source_target_pairs={{0,25},{1,26},{2,27},{3,28},{4,29},{5,30},{6,31},{7,24}} | collective-permute-start | bytes 776 | tf_op jit(solution)/shard_map/ppermute | solution.py:611
  25.0 1.8 %collective-permute-start.2 = (f32[2,128,128]{2,1,0:T(8,128)S(1)}, f32[2,128,128]{2,1,0:T(8,128)S(1)}, u32[]{:S(2)}, u32[]{:S(2)}) collective-permute-start(f32[2,128,128]{2,1,0:T(8,128)S(1)} %get-tuple-element.29.refs_8_), channel_id=1, source_target_pairs={{0,1},{1,0},{2,3},{3,2},{4,5},{5,4},{6,7},{7,6},{8,9},{9,8},{10,11... | collective-permute-start | bytes 393224 | tf_op jit(solution)/shard_map/ppermute | solution.py:570
  26.9 2.1 %collective-permute-start = (f32[2,128,128]{2,1,0:T(8,128)S(1)}, f32[2,128,128]{2,1,0:T(8,128)S(1)}, u32[]{:S(2)}, u32[]{:S(2)}) collective-permute-start(f32[2,128,128]{2,1,0:T(8,128)S(1)} %get-tuple-element.27), channel_id=1, source_target_pairs={{0,2},{1,3},{2,4},{3,5},{4,6},{5,7},{6,8},{7,9},{8,10},{9,11},{10,... | collective-permute-start | bytes 393224 | tf_op jit(solution)/shard_map/ppermute | solution.py:570
  29.0 3.7 %collective-permute-start.1 = (f32[2,128,128]{2,1,0:T(8,128)S(1)}, f32[2,128,128]{2,1,0:T(8,128)S(1)}, u32[]{:S(2)}, u32[]{:S(2)}) collective-permute-start(f32[2,128,128]{2,1,0:T(8,128)S(1)} %get-tuple-element.28), channel_id=1, source_target_pairs={{2,0},{3,1},{4,2},{5,3},{6,4},{7,5},{8,6},{9,7},{10,8},{11,9},{12,... | collective-permute-start | bytes 393224 | tf_op jit(solution)/shard_map/ppermute | solution.py:570
  32.8 2.1 %collective-permute-start.4 = (f32[8,128]{1,0:T(8,128)S(1)}, f32[8,128]{1,0:T(8,128)S(1)}, u32[]{:S(2)}, u32[]{:S(2)}) collective-permute-start(f32[8,128]{1,0:T(8,128)S(1)} %get-tuple-element.31), channel_id=1, source_target_pairs={{0,3},{1,2},{2,5},{3,4},{4,7},{5,6},{6,9},{7,8},{8,11},{9,10},{10,... | collective-permute-start | bytes 12296 | tf_op jit(solution)/shard_map/ppermute | solution.py:570
  35.0 2.7 %collective-permute-done.4.refs_9_.refs_10_ = f32[8,128]{1,0:T(8,128)S(1)} collective-permute-done((f32[8,128]{1,0:T(8,128)S(1)}, f32[8,128]{1,0:T(8,128)S(1)}, u32[]{:S(2)}, u32[]{:S(2)}) %collective-permute-start.4) | collective-permute-done | bytes 4128 | tf_op jit(solution)/shard_map/ppermute | solution.py:570
  37.7 2.1 %collective-permute-start.5 = (f32[8,128]{1,0:T(8,128)S(1)}, f32[8,128]{1,0:T(8,128)S(1)}, u32[]{:S(2)}, u32[]{:S(2)}) collective-permute-start(f32[8,128]{1,0:T(8,128)S(1)} %get-tuple-element.32), channel_id=1, source_target_pairs={{2,1},{3,0},{4,3},{5,2},{6,5},{7,4},{8,7},{9,6},{10,9},{11,8},{12,... | collective-permute-start | bytes 12296 | tf_op jit(solution)/shard_map/ppermute | solution.py:570
  40.2 3.2 %collective-permute-done.5.refs_11_.refs_12_ = f32[8,128]{1,0:T(8,128)S(1)} collective-permute-done((f32[8,128]{1,0:T(8,128)S(1)}, f32[8,128]{1,0:T(8,128)S(1)}, u32[]{:S(2)}, u32[]{:S(2)}) %collective-permute-start.5) | collective-permute-done | bytes 4128 | tf_op jit(solution)/shard_map/ppermute | solution.py:570
  43.5 21.7 %advance.1 = (f32[128,128,128]{2,1,0:T(8,128)}, bf16[32,16,128]{2,1,0:T(8,128)(2,1)S(1)}, bf16[32,16,128]{2,1,0:T(8,128)(2,1)S(1)}, bf16[32,16,128]{2,1,0:T(8,128)(2,1)S(1)}, bf16[32,16,128]{2,1,0:T(8,128)(2,1)S(1)}) custom-call(s32[3]{0:T(128)S(1)} %add_convert_fusion.refs_0_.flags, s32[256]{0:T(256)S(1)} %get-tuple-element.55.refs_1_, ...), custom_call_target="tpu_custom_call" | custom-call | flops 2147483648 | bytes 16777216 | tf_op jit(solution)/shard_map/advance/pallas_call | solution.py:301
  65.2 1.3 collective-permute-start.18
  66.5 0.7 collective-permute-start.19
  68.2 1.3 collective-permute-start.21
  69.5 0.7 collective-permute-start.22
  70.2 1.4 collective-permute-done.18.refs_2_
  72.3 14.1 %collective-permute-start.24 = (bf16[32,16,128]{2,1,0:T(8,128)(2,1)S(1)}, bf16[32,16,128]{2,1,0:T(8,128)(2,1)S(1)}, u32[]{:S(2)}, u32[]{:S(2)}) collective-permute-start(bf16[32,16,128]{2,1,0:T(8,128)(2,1)S(1)} %get-tuple-element.36), channel_id=1, source_target_pairs={{0,26},{1,27},{2,28},{3,29},{4,30},{5,31},{6,24},{7,25}} | collective-permute-start | bytes 393224 | tf_op jit(solution)/shard_map/ppermute | solution.py:611
  86.5 9.4 %copy.61 = f32[128,128,128]{1,0,2:T(8,128)} copy(f32[128,128,128]{2,1,0:T(8,128)} %get-tuple-element.33.state) | data formatting | bytes 16777216 | tf_op jit(solution)/shard_map/advance/pallas_call | solution.py:301
  96.6 0.7 collective-permute-start.26
  97.3 2.2 %collective-permute-start.27 = (bf16[32,16,128]{2,1,0:T(8,128)(2,1)S(1)}, bf16[32,16,128]{2,1,0:T(8,128)(2,1)S(1)}, u32[]{:S(2)}, u32[]{:S(2)}) collective-permute-start(bf16[32,16,128]{2,1,0:T(8,128)(2,1)S(1)} %get-tuple-element.37), channel_id=1, source_target_pairs={{0,27},{1,28},{2,29},{3,30},{4,31},{5,24},{6,25},{7,26}} | collective-permute-start | bytes 393224 | tf_op jit(solution)/shard_map/ppermute | solution.py:611
  99.5 0.7 collective-permute-start.28
  100.2 0.7 collective-permute-start.29
  100.9 0.8 slice_bitcast_fusion.refs_16_.refs_8_
  101.7 2.0 %collective-permute-done.27.refs_11_ = bf16[32,16,128]{2,1,0:T(8,128)(2,1)S(1)} collective-permute-done((bf16[32,16,128]{2,1,0:T(8,128)(2,1)S(1)}, bf16[32,16,128]{2,1,0:T(8,128)(2,1)S(1)}, u32[]{:S(2)}, u32[]{:S(2)}) %collective-permute-start.27) | collective-permute-done | bytes 131104 | tf_op jit(solution)/shard_map/ppermute | solution.py:611
  104.4 0.7 collective-permute-start.39
  105.1 0.7 collective-permute-start.40
  105.7 1.3 collective-permute-start.41
  107.0 0.7 collective-permute-start.36
  107.7 0.7 collective-permute-start.37
  108.4 0.7 update.1
  109.1 1.3 collective-permute-start.38
  110.4 0.7 collective-permute-start.33
  111.1 19.1 %collective-permute-done.41 = f32[64,128]{1,0:T(8,128)S(1)} collective-permute-done((f32[64,128]{1,0:T(8,128)S(1)}, f32[64,128]{1,0:T(8,128)S(1)}, u32[]{:S(2)}, u32[]{:S(2)}) %collective-permute-start.41) | collective-permute-done | bytes 32800 | tf_op jit(solution)/shard_map/ppermute | solution.py:618
  130.8 1.3 collective-permute-start.35
  132.1 0.7 collective-permute-start.30
  132.8 9.1 %collective-permute-done.38 = f32[64,128]{1,0:T(8,128)S(1)} collective-permute-done((f32[64,128]{1,0:T(8,128)S(1)}, f32[64,128]{1,0:T(8,128)S(1)}, u32[]{:S(2)}, u32[]{:S(2)}) %collective-permute-start.38) | collective-permute-done | bytes 32800 | tf_op jit(solution)/shard_map/ppermute | solution.py:618
  142.6 1.3 collective-permute-start.32
  143.9 5.3 %collective-permute-done.32 = f32[64,128]{1,0:T(8,128)S(1)} collective-permute-done((f32[64,128]{1,0:T(8,128)S(1)}, f32[64,128]{1,0:T(8,128)S(1)}, u32[]{:S(2)}, u32[]{:S(2)}) %collective-permute-start.32) | collective-permute-done | bytes 32800 | tf_op jit(solution)/shard_map/ppermute | solution.py:618
  149.3 3.6 %returned.1 = f32[128,128]{1,0:T(8,128)} custom-call(s32[3]{0:T(128)S(1)} %add_convert_fusion.refs_0_.flags, f32[64,128]{1,0:T(8,128)S(1)} %select_select_fusion.3.refs_0_, f32[64,128]{1,0:T(8,128)S(1)} %select_select_fusion.2.refs_1_, f32[64,128]{1,0:T(8,128)S(1)} %select_select_fusion.1.refs_2_, f32[64,128]{1,0:T(8,128)S(1)} %select_select_fusion.refs_3_, ...), custom_call_target="tpu_custom_call" | custom-call | tf_op jit(solution)/shard_map/returned/pallas_call | solution.py:524
  (78 shorter events, 8.7 us)
Async XLA Ops:
  0.6 34.2 %copy-start.4 = (f32[8,128]{1,0:T(8,128)S(1)}, f32[8,128]{1,0:T(8,128)}, u32[]{:S(2)}) copy-start(f32[8,128]{1,0:T(8,128)} %ocean_map.1) | copy-start | bytes 12292
  0.6 42.8 %copy-start.5 = (f32[128,8]{0,1:T(8,128)S(1)}, f32[128,8]{0,1:T(8,128)}, u32[]{:S(2)}) copy-start(f32[128,8]{0,1:T(8,128)} %param.14) | copy-start | bytes 12292
  0.7 42.8 %copy-start.2 = (f32[128,128]{1,0:T(8,128)S(1)}, f32[128,128]{1,0:T(8,128)}, u32[]{:S(2)}) copy-start(f32[128,128]{1,0:T(8,128)} %refs_14_.1) | copy-start | bytes 196612
  0.7 42.8 %copy-start.3 = (f32[128,128]{1,0:T(8,128)S(1)}, f32[128,128]{1,0:T(8,128)}, u32[]{:S(2)}) copy-start(f32[128,128]{1,0:T(8,128)} %refs_15_.2) | copy-start | bytes 196612
  2.3 15.8 %collective-permute-start.12 = (s32[64]{0:T(128)S(1)}, s32[64]{0:T(128)S(1)}, u32[]{:S(2)}, u32[]{:S(2)}) collective-permute-start(s32[64]{0:T(128)S(1)} %get-tuple-element.57), channel_id=1, source_target_pairs={{0,26},{1,27},{2,28},{3,29},{4,30},{5,31},{6,24},{7,25}} | collective-permute-start | bytes 776 | tf_op jit(solution)/shard_map/ppermute | solution.py:611
  7.6 11.1 %collective-permute-start.13 = (s32[64]{0:T(128)S(1)}, s32[64]{0:T(128)S(1)}, u32[]{:S(2)}, u32[]{:S(2)}) collective-permute-start(s32[64]{0:T(128)S(1)} %get-tuple-element.57), channel_id=1, source_target_pairs={{8,26},{9,27},{10,28},{11,29},{12,30},{13,31},{14,24},{15,25}} | collective-permute-start | bytes 776 | tf_op jit(solution)/shard_map/ppermute | solution.py:611
  8.3 12.6 %collective-permute-start.14 = (s32[64]{0:T(128)S(1)}, s32[64]{0:T(128)S(1)}, u32[]{:S(2)}, u32[]{:S(2)}) collective-permute-start(s32[64]{0:T(128)S(1)} %get-tuple-element.57), channel_id=1, source_target_pairs={{16,26},{17,27},{18,28},{19,29},{20,30},{21,31},{22,24},{23,25}} | collective-permute-start | bytes 776 | tf_op jit(solution)/shard_map/ppermute | solution.py:611
  9.0 8.4 %collective-permute-start.11 = (s32[64]{0:T(128)S(1)}, s32[64]{0:T(128)S(1)}, u32[]{:S(2)}, u32[]{:S(2)}) collective-permute-start(s32[64]{0:T(128)S(1)} %get-tuple-element.58), channel_id=1, source_target_pairs={{16,25},{17,26},{18,27},{19,28},{20,29},{21,30},{22,31},{23,24}} | collective-permute-start | bytes 776 | tf_op jit(solution)/shard_map/ppermute | solution.py:611
  9.6 11.9 %collective-permute-start.15 = (s32[64]{0:T(128)S(1)}, s32[64]{0:T(128)S(1)}, u32[]{:S(2)}, u32[]{:S(2)}) collective-permute-start(s32[64]{0:T(128)S(1)} %get-tuple-element.56), channel_id=1, source_target_pairs={{0,27},{1,28},{2,29},{3,30},{4,31},{5,24},{6,25},{7,26}} | collective-permute-start | bytes 776 | tf_op jit(solution)/shard_map/ppermute | solution.py:611
  13.4 3.4 %copy-start = (f32[128,128,128]{2,1,0:T(8,128)S(1)}, f32[128,128,128]{2,1,0:T(8,128)}, u32[]{:S(2)}) copy-start(f32[128,128,128]{2,1,0:T(8,128)} %refs_2_.1) | copy-start | bytes 25165828
  17.4 4.8 %collective-permute-start.16 = (s32[64]{0:T(128)S(1)}, s32[64]{0:T(128)S(1)}, u32[]{:S(2)}, u32[]{:S(2)}) collective-permute-start(s32[64]{0:T(128)S(1)} %get-tuple-element.56), channel_id=1, source_target_pairs={{8,27},{9,28},{10,29},{11,30},{12,31},{13,24},{14,25},{15,26}} | collective-permute-start | bytes 776 | tf_op jit(solution)/shard_map/ppermute | solution.py:611
  18.1 6.2 %collective-permute-start.17 = (s32[64]{0:T(128)S(1)}, s32[64]{0:T(128)S(1)}, u32[]{:S(2)}, u32[]{:S(2)}) collective-permute-start(s32[64]{0:T(128)S(1)} %get-tuple-element.56), channel_id=1, source_target_pairs={{16,27},{17,28},{18,29},{19,30},{20,31},{21,24},{22,25},{23,26}} | collective-permute-start | bytes 776 | tf_op jit(solution)/shard_map/ppermute | solution.py:611
  18.8 6.2 %collective-permute-start.6 = (s32[64]{0:T(128)S(1)}, s32[64]{0:T(128)S(1)}, u32[]{:S(2)}, u32[]{:S(2)}) collective-permute-start(s32[64]{0:T(128)S(1)} %get-tuple-element.59), channel_id=1, source_target_pairs={{0,24},{1,25},{2,26},{3,27},{4,28},{5,29},{6,30},{7,31}} | collective-permute-start | bytes 776 | tf_op jit(solution)/shard_map/ppermute | solution.py:611
  20.9 5.9 %collective-permute-start.7 = (s32[64]{0:T(128)S(1)}, s32[64]{0:T(128)S(1)}, u32[]{:S(2)}, u32[]{:S(2)}) collective-permute-start(s32[64]{0:T(128)S(1)} %get-tuple-element.59), channel_id=1, source_target_pairs={{8,24},{9,25},{10,26},{11,27},{12,28},{13,29},{14,30},{15,31}} | collective-permute-start | bytes 776 | tf_op jit(solution)/shard_map/ppermute | solution.py:611
  21.6 5.3 %collective-permute-start.8 = (s32[64]{0:T(128)S(1)}, s32[64]{0:T(128)S(1)}, u32[]{:S(2)}, u32[]{:S(2)}) collective-permute-start(s32[64]{0:T(128)S(1)} %get-tuple-element.59), channel_id=1, source_target_pairs={{16,24},{17,25},{18,26},{19,27},{20,28},{21,29},{22,30},{23,31}} | collective-permute-start | bytes 776 | tf_op jit(solution)/shard_map/ppermute | solution.py:611
  22.3 6.8 %collective-permute-start.9 = (s32[64]{0:T(128)S(1)}, s32[64]{0:T(128)S(1)}, u32[]{:S(2)}, u32[]{:S(2)}) collective-permute-start(s32[64]{0:T(128)S(1)} %get-tuple-element.58), channel_id=1, source_target_pairs={{0,25},{1,26},{2,27},{3,28},{4,29},{5,30},{6,31},{7,24}} | collective-permute-start | bytes 776 | tf_op jit(solution)/shard_map/ppermute | solution.py:611
  24.3 8.5 %collective-permute-start.10 = (s32[64]{0:T(128)S(1)}, s32[64]{0:T(128)S(1)}, u32[]{:S(2)}, u32[]{:S(2)}) collective-permute-start(s32[64]{0:T(128)S(1)} %get-tuple-element.58), channel_id=1, source_target_pairs={{8,25},{9,26},{10,27},{11,28},{12,29},{13,30},{14,31},{15,24}} | collective-permute-start | bytes 776 | tf_op jit(solution)/shard_map/ppermute | solution.py:611
  25.0 18.5 %collective-permute-start.2 = (f32[2,128,128]{2,1,0:T(8,128)S(1)}, f32[2,128,128]{2,1,0:T(8,128)S(1)}, u32[]{:S(2)}, u32[]{:S(2)}) collective-permute-start(f32[2,128,128]{2,1,0:T(8,128)S(1)} %get-tuple-element.29.refs_8_), channel_id=1, source_target_pairs={{0,1},{1,0},{2,3},{3,2},{4,5},{5,4},{6,7},{7,6},{8,9},{9,8},{10,11... | collective-permute-start | bytes 393224 | tf_op jit(solution)/shard_map/ppermute | solution.py:570
  26.8 16.6 %collective-permute-start.3 = (f32[2,128,128]{2,1,0:T(8,128)S(1)}, f32[2,128,128]{2,1,0:T(8,128)S(1)}, u32[]{:S(2)}, u32[]{:S(2)}) collective-permute-start(f32[2,128,128]{2,1,0:T(8,128)S(1)} %get-tuple-element.30.refs_7_), channel_id=1, source_target_pairs={{0,1},{1,0},{2,3},{3,2},{4,5},{5,4},{6,7},{7,6},{8,9},{9,8},{10,11... | collective-permute-start | bytes 393224 | tf_op jit(solution)/shard_map/ppermute | solution.py:570
  26.9 16.6 %collective-permute-start = (f32[2,128,128]{2,1,0:T(8,128)S(1)}, f32[2,128,128]{2,1,0:T(8,128)S(1)}, u32[]{:S(2)}, u32[]{:S(2)}) collective-permute-start(f32[2,128,128]{2,1,0:T(8,128)S(1)} %get-tuple-element.27), channel_id=1, source_target_pairs={{0,2},{1,3},{2,4},{3,5},{4,6},{5,7},{6,8},{7,9},{8,10},{9,11},{10,... | collective-permute-start | bytes 393224 | tf_op jit(solution)/shard_map/ppermute | solution.py:570
  29.0 14.4 %collective-permute-start.1 = (f32[2,128,128]{2,1,0:T(8,128)S(1)}, f32[2,128,128]{2,1,0:T(8,128)S(1)}, u32[]{:S(2)}, u32[]{:S(2)}) collective-permute-start(f32[2,128,128]{2,1,0:T(8,128)S(1)} %get-tuple-element.28), channel_id=1, source_target_pairs={{2,0},{3,1},{4,2},{5,3},{6,4},{7,5},{8,6},{9,7},{10,8},{11,9},{12,... | collective-permute-start | bytes 393224 | tf_op jit(solution)/shard_map/ppermute | solution.py:570
  32.8 4.9 %collective-permute-start.4 = (f32[8,128]{1,0:T(8,128)S(1)}, f32[8,128]{1,0:T(8,128)S(1)}, u32[]{:S(2)}, u32[]{:S(2)}) collective-permute-start(f32[8,128]{1,0:T(8,128)S(1)} %get-tuple-element.31), channel_id=1, source_target_pairs={{0,3},{1,2},{2,5},{3,4},{4,7},{5,6},{6,9},{7,8},{8,11},{9,10},{10,... | collective-permute-start | bytes 12296 | tf_op jit(solution)/shard_map/ppermute | solution.py:570
  37.7 5.7 %collective-permute-start.5 = (f32[8,128]{1,0:T(8,128)S(1)}, f32[8,128]{1,0:T(8,128)S(1)}, u32[]{:S(2)}, u32[]{:S(2)}) collective-permute-start(f32[8,128]{1,0:T(8,128)S(1)} %get-tuple-element.32), channel_id=1, source_target_pairs={{2,1},{3,0},{4,3},{5,2},{6,5},{7,4},{8,7},{9,6},{10,9},{11,8},{12,... | collective-permute-start | bytes 12296 | tf_op jit(solution)/shard_map/ppermute | solution.py:570
  65.2 6.4 %collective-permute-start.18 = (bf16[32,16,128]{2,1,0:T(8,128)(2,1)S(1)}, bf16[32,16,128]{2,1,0:T(8,128)(2,1)S(1)}, u32[]{:S(2)}, u32[]{:S(2)}) collective-permute-start(bf16[32,16,128]{2,1,0:T(8,128)(2,1)S(1)} %get-tuple-element.34), channel_id=1, source_target_pairs={{0,24},{1,25},{2,26},{3,27},{4,28},{5,29},{6,30},{7,31}} | collective-permute-start | bytes 393224 | tf_op jit(solution)/shard_map/ppermute | solution.py:611
  66.5 5.7 %collective-permute-start.19 = (bf16[32,16,128]{2,1,0:T(8,128)(2,1)S(1)}, bf16[32,16,128]{2,1,0:T(8,128)(2,1)S(1)}, u32[]{:S(2)}, u32[]{:S(2)}) collective-permute-start(bf16[32,16,128]{2,1,0:T(8,128)(2,1)S(1)} %get-tuple-element.34), channel_id=1, source_target_pairs={{8,24},{9,25},{10,26},{11,27},{12,28},{13,29},{14,30},{15,31}} | collective-permute-start | bytes 393224 | tf_op jit(solution)/shard_map/ppermute | solution.py:611
  67.5 28.4 %collective-permute-start.20 = (bf16[32,16,128]{2,1,0:T(8,128)(2,1)S(1)}, bf16[32,16,128]{2,1,0:T(8,128)(2,1)S(1)}, u32[]{:S(2)}, u32[]{:S(2)}) collective-permute-start(bf16[32,16,128]{2,1,0:T(8,128)(2,1)S(1)} %get-tuple-element.34), channel_id=1, source_target_pairs={{16,24},{17,25},{18,26},{19,27},{20,28},{21,29},{22,30},{23,31}} | collective-permute-start | bytes 393224 | tf_op jit(solution)/shard_map/ppermute | solution.py:611
  68.2 28.4 %collective-permute-start.21 = (bf16[32,16,128]{2,1,0:T(8,128)(2,1)S(1)}, bf16[32,16,128]{2,1,0:T(8,128)(2,1)S(1)}, u32[]{:S(2)}, u32[]{:S(2)}) collective-permute-start(bf16[32,16,128]{2,1,0:T(8,128)(2,1)S(1)} %get-tuple-element.35), channel_id=1, source_target_pairs={{0,25},{1,26},{2,27},{3,28},{4,29},{5,30},{6,31},{7,24}} | collective-permute-start | bytes 393224 | tf_op jit(solution)/shard_map/ppermute | solution.py:611
  69.5 27.8 %collective-permute-start.22 = (bf16[32,16,128]{2,1,0:T(8,128)(2,1)S(1)}, bf16[32,16,128]{2,1,0:T(8,128)(2,1)S(1)}, u32[]{:S(2)}, u32[]{:S(2)}) collective-permute-start(bf16[32,16,128]{2,1,0:T(8,128)(2,1)S(1)} %get-tuple-element.35), channel_id=1, source_target_pairs={{8,25},{9,26},{10,27},{11,28},{12,29},{13,30},{14,31},{15,24}} | collective-permute-start | bytes 393224 | tf_op jit(solution)/shard_map/ppermute | solution.py:611
  71.6 27.9 %collective-permute-start.23 = (bf16[32,16,128]{2,1,0:T(8,128)(2,1)S(1)}, bf16[32,16,128]{2,1,0:T(8,128)(2,1)S(1)}, u32[]{:S(2)}, u32[]{:S(2)}) collective-permute-start(bf16[32,16,128]{2,1,0:T(8,128)(2,1)S(1)} %get-tuple-element.35), channel_id=1, source_target_pairs={{16,25},{17,26},{18,27},{19,28},{20,29},{21,30},{22,31},{23,24}} | collective-permute-start | bytes 393224 | tf_op jit(solution)/shard_map/ppermute | solution.py:611
  72.3 28.0 %collective-permute-start.24 = (bf16[32,16,128]{2,1,0:T(8,128)(2,1)S(1)}, bf16[32,16,128]{2,1,0:T(8,128)(2,1)S(1)}, u32[]{:S(2)}, u32[]{:S(2)}) collective-permute-start(bf16[32,16,128]{2,1,0:T(8,128)(2,1)S(1)} %get-tuple-element.36), channel_id=1, source_target_pairs={{0,26},{1,27},{2,28},{3,29},{4,30},{5,31},{6,24},{7,25}} | collective-permute-start | bytes 393224 | tf_op jit(solution)/shard_map/ppermute | solution.py:611
  86.5 17.3 %copy-start.1 = (bf16[32,128,128]{2,1,0:T(8,128)(2,1)S(1)}, bf16[32,128,128]{2,1,0:T(8,128)(2,1)}, u32[]{:S(2)}) copy-start(bf16[32,128,128]{2,1,0:T(8,128)(2,1)} %refs_6_.1) | copy-start | bytes 3145732
  95.9 5.8 %collective-permute-start.25 = (bf16[32,16,128]{2,1,0:T(8,128)(2,1)S(1)}, bf16[32,16,128]{2,1,0:T(8,128)(2,1)S(1)}, u32[]{:S(2)}, u32[]{:S(2)}) collective-permute-start(bf16[32,16,128]{2,1,0:T(8,128)(2,1)S(1)} %get-tuple-element.36), channel_id=1, source_target_pairs={{8,26},{9,27},{10,28},{11,29},{12,30},{13,31},{14,24},{15,25}} | collective-permute-start | bytes 393224 | tf_op jit(solution)/shard_map/ppermute | solution.py:611
  96.6 5.2 %collective-permute-start.26 = (bf16[32,16,128]{2,1,0:T(8,128)(2,1)S(1)}, bf16[32,16,128]{2,1,0:T(8,128)(2,1)S(1)}, u32[]{:S(2)}, u32[]{:S(2)}) collective-permute-start(bf16[32,16,128]{2,1,0:T(8,128)(2,1)S(1)} %get-tuple-element.36), channel_id=1, source_target_pairs={{16,26},{17,27},{18,28},{19,29},{20,30},{21,31},{22,24},{23,25}} | collective-permute-start | bytes 393224 | tf_op jit(solution)/shard_map/ppermute | solution.py:611
  97.3 6.4 %collective-permute-start.27 = (bf16[32,16,128]{2,1,0:T(8,128)(2,1)S(1)}, bf16[32,16,128]{2,1,0:T(8,128)(2,1)S(1)}, u32[]{:S(2)}, u32[]{:S(2)}) collective-permute-start(bf16[32,16,128]{2,1,0:T(8,128)(2,1)S(1)} %get-tuple-element.37), channel_id=1, source_target_pairs={{0,27},{1,28},{2,29},{3,30},{4,31},{5,24},{6,25},{7,26}} | collective-permute-start | bytes 393224 | tf_op jit(solution)/shard_map/ppermute | solution.py:611
  99.5 4.2 %collective-permute-start.28 = (bf16[32,16,128]{2,1,0:T(8,128)(2,1)S(1)}, bf16[32,16,128]{2,1,0:T(8,128)(2,1)S(1)}, u32[]{:S(2)}, u32[]{:S(2)}) collective-permute-start(bf16[32,16,128]{2,1,0:T(8,128)(2,1)S(1)} %get-tuple-element.37), channel_id=1, source_target_pairs={{8,27},{9,28},{10,29},{11,30},{12,31},{13,24},{14,25},{15,26}} | collective-permute-start | bytes 393224 | tf_op jit(solution)/shard_map/ppermute | solution.py:611
  100.2 3.5 %collective-permute-start.29 = (bf16[32,16,128]{2,1,0:T(8,128)(2,1)S(1)}, bf16[32,16,128]{2,1,0:T(8,128)(2,1)S(1)}, u32[]{:S(2)}, u32[]{:S(2)}) collective-permute-start(bf16[32,16,128]{2,1,0:T(8,128)(2,1)S(1)} %get-tuple-element.37), channel_id=1, source_target_pairs={{16,27},{17,28},{18,29},{19,30},{20,31},{21,24},{22,25},{23,26}} | collective-permute-start | bytes 393224 | tf_op jit(solution)/shard_map/ppermute | solution.py:611
  104.4 4.7 %collective-permute-start.39 = (f32[64,128]{1,0:T(8,128)S(1)}, f32[64,128]{1,0:T(8,128)S(1)}, u32[]{:S(2)}, u32[]{:S(2)}) collective-permute-start(f32[64,128]{1,0:T(8,128)S(1)} %get-tuple-element.48), channel_id=1, source_target_pairs={{27,16},{28,17},{29,18},{30,19},{31,20},{24,21},{25,22},{26,23}} | collective-permute-start | bytes 98312 | tf_op jit(solution)/shard_map/ppermute | solution.py:618
  105.1 5.3 %collective-permute-start.40 = (f32[64,128]{1,0:T(8,128)S(1)}, f32[64,128]{1,0:T(8,128)S(1)}, u32[]{:S(2)}, u32[]{:S(2)}) collective-permute-start(f32[64,128]{1,0:T(8,128)S(1)} %get-tuple-element.49), channel_id=1, source_target_pairs={{27,8},{28,9},{29,10},{30,11},{31,12},{24,13},{25,14},{26,15}} | collective-permute-start | bytes 98312 | tf_op jit(solution)/shard_map/ppermute | solution.py:618
  105.7 24.4 %collective-permute-start.41 = (f32[64,128]{1,0:T(8,128)S(1)}, f32[64,128]{1,0:T(8,128)S(1)}, u32[]{:S(2)}, u32[]{:S(2)}) collective-permute-start(f32[64,128]{1,0:T(8,128)S(1)} %get-tuple-element.50), channel_id=1, source_target_pairs={{27,0},{28,1},{29,2},{30,3},{31,4},{24,5},{25,6},{26,7}} | collective-permute-start | bytes 98312 | tf_op jit(solution)/shard_map/ppermute | solution.py:618
  107.0 23.8 %collective-permute-start.36 = (f32[64,128]{1,0:T(8,128)S(1)}, f32[64,128]{1,0:T(8,128)S(1)}, u32[]{:S(2)}, u32[]{:S(2)}) collective-permute-start(f32[64,128]{1,0:T(8,128)S(1)} %get-tuple-element.45), channel_id=1, source_target_pairs={{26,16},{27,17},{28,18},{29,19},{30,20},{31,21},{24,22},{25,23}} | collective-permute-start | bytes 98312 | tf_op jit(solution)/shard_map/ppermute | solution.py:618
  107.7 24.4 %collective-permute-start.37 = (f32[64,128]{1,0:T(8,128)S(1)}, f32[64,128]{1,0:T(8,128)S(1)}, u32[]{:S(2)}, u32[]{:S(2)}) collective-permute-start(f32[64,128]{1,0:T(8,128)S(1)} %get-tuple-element.46), channel_id=1, source_target_pairs={{26,8},{27,9},{28,10},{29,11},{30,12},{31,13},{24,14},{25,15}} | collective-permute-start | bytes 98312 | tf_op jit(solution)/shard_map/ppermute | solution.py:618
  109.1 32.8 %collective-permute-start.38 = (f32[64,128]{1,0:T(8,128)S(1)}, f32[64,128]{1,0:T(8,128)S(1)}, u32[]{:S(2)}, u32[]{:S(2)}) collective-permute-start(f32[64,128]{1,0:T(8,128)S(1)} %get-tuple-element.47), channel_id=1, source_target_pairs={{26,0},{27,1},{28,2},{29,3},{30,4},{31,5},{24,6},{25,7}} | collective-permute-start | bytes 98312 | tf_op jit(solution)/shard_map/ppermute | solution.py:618
  110.4 32.2 %collective-permute-start.33 = (f32[64,128]{1,0:T(8,128)S(1)}, f32[64,128]{1,0:T(8,128)S(1)}, u32[]{:S(2)}, u32[]{:S(2)}) collective-permute-start(f32[64,128]{1,0:T(8,128)S(1)} %get-tuple-element.42), channel_id=1, source_target_pairs={{25,16},{26,17},{27,18},{28,19},{29,20},{30,21},{31,22},{24,23}} | collective-permute-start | bytes 98312 | tf_op jit(solution)/shard_map/ppermute | solution.py:618
  130.1 13.7 %collective-permute-start.34 = (f32[64,128]{1,0:T(8,128)S(1)}, f32[64,128]{1,0:T(8,128)S(1)}, u32[]{:S(2)}, u32[]{:S(2)}) collective-permute-start(f32[64,128]{1,0:T(8,128)S(1)} %get-tuple-element.43), channel_id=1, source_target_pairs={{25,8},{26,9},{27,10},{28,11},{29,12},{30,13},{31,14},{24,15}} | collective-permute-start | bytes 98312 | tf_op jit(solution)/shard_map/ppermute | solution.py:618
  130.8 13.1 %collective-permute-start.35 = (f32[64,128]{1,0:T(8,128)S(1)}, f32[64,128]{1,0:T(8,128)S(1)}, u32[]{:S(2)}, u32[]{:S(2)}) collective-permute-start(f32[64,128]{1,0:T(8,128)S(1)} %get-tuple-element.44), channel_id=1, source_target_pairs={{25,0},{26,1},{27,2},{28,3},{29,4},{30,5},{31,6},{24,7}} | collective-permute-start | bytes 98312 | tf_op jit(solution)/shard_map/ppermute | solution.py:618
  132.1 11.8 %collective-permute-start.30 = (f32[64,128]{1,0:T(8,128)S(1)}, f32[64,128]{1,0:T(8,128)S(1)}, u32[]{:S(2)}, u32[]{:S(2)}) collective-permute-start(f32[64,128]{1,0:T(8,128)S(1)} %get-tuple-element.39), channel_id=1, source_target_pairs={{24,16},{25,17},{26,18},{27,19},{28,20},{29,21},{30,22},{31,23}} | collective-permute-start | bytes 98312 | tf_op jit(solution)/shard_map/ppermute | solution.py:618
  141.9 2.0 %collective-permute-start.31 = (f32[64,128]{1,0:T(8,128)S(1)}, f32[64,128]{1,0:T(8,128)S(1)}, u32[]{:S(2)}, u32[]{:S(2)}) collective-permute-start(f32[64,128]{1,0:T(8,128)S(1)} %get-tuple-element.40), channel_id=1, source_target_pairs={{24,8},{25,9},{26,10},{27,11},{28,12},{29,13},{30,14},{31,15}} | collective-permute-start | bytes 98312 | tf_op jit(solution)/shard_map/ppermute | solution.py:618
  142.6 6.7 %collective-permute-start.32 = (f32[64,128]{1,0:T(8,128)S(1)}, f32[64,128]{1,0:T(8,128)S(1)}, u32[]{:S(2)}, u32[]{:S(2)}) collective-permute-start(f32[64,128]{1,0:T(8,128)S(1)} %get-tuple-element.41), channel_id=1, source_target_pairs={{24,0},{25,1},{26,2},{27,3},{28,4},{29,5},{30,6},{31,7}} | collective-permute-start | bytes 98312 | tf_op jit(solution)/shard_map/ppermute | solution.py:618
where the time goes:
time: 154 us; the launch traced here: 153 us
  starting transfers between devices  64 us (42%)
  waiting for transfers between devices  42.9 us (28%)
  Pallas kernels  27.2 us (18%)
  local copies, waits for them, and re-layouts  15.5 us (10%)
  other arithmetic  1.83 us (1%)
    ppermute x24, starting transfers between devices, to_ocean(): return lax.ppermute(value, AXES, pairs)  41.6 us
    ppermute x12, waiting for transfers between devices, from_ocean(): return lax.ppermute(value, AXES, pairs)  33.5 us
    pallas_call x1, Pallas kernels, advance(): pl.pallas_call(functools.partial(advance_kernel, neighbours, capacity), o...  21.7 us
    ppermute x6, starting transfers between devices, band_shift(): return lax.ppermute(value, AXES, pairs)  12 us
    ppermute x12, starting transfers between devices, from_ocean(): return lax.ppermute(value, AXES, pairs)  10.5 us
    pallas_call x1, local copies, waits for them, and re-layouts, advance(): pl.pallas_call(functools.partial(advance_kernel, neighbours, capacity), o...  9.4 us
    ppermute x6, waiting for transfers between devices, band_shift(): return lax.ppermute(value, AXES, pairs)  5.94 us
    unnamed x13, local copies, waits for them, and re-layouts  4.28 us
  transfers between devices with their start and end apart: 42, of which 7 were waited for; matrix products, arithmetic and copies ran while one was open for 8% of the time, Pallas kernels for 1%

commit v1 on v0

--- a/solution.py
+++ b/solution.py
@@ -35,9 +35,7 @@
     return jnp.dot(a, b, preferred_element_type=F32)
 
 
-def edges_kernel(
-    state, first_rows, last_rows, first_cols, last_cols, top_corners, low_corners, left, right, sems
-):
+def edges_kernel(state, first_rows, last_rows, sides, top_corners, low_corners, left, right, sems):
     rows, cols, _ = state.shape
     copies = [
         pltpu.make_async_copy(state.at[:, pl.ds(0, EDGE)], left, sems.at[0]),
@@ -50,8 +48,8 @@
     for copy in copies:
         copy.wait()
     for i in range(2):
-        first_cols[i] = left[:, i, :]
-        last_cols[i] = right[:, EDGE - 2 + i, :]
+        sides[i] = left[:, i, :]
+        sides[2 + i] = right[:, EDGE - 2 + i, :]
     top_corners[...] = jnp.zeros(top_corners.shape, F32)
     low_corners[...] = jnp.zeros(low_corners.shape, F32)
     top_corners[0:1] = left[0, 0:1]
@@ -63,14 +61,14 @@
 def take_edges(state):
     rows, cols, levels = state.shape
     slab = jax.ShapeDtypeStruct((2, cols, levels), F32)
-    side = jax.ShapeDtypeStruct((2, rows, levels), F32)
+    side = jax.ShapeDtypeStruct((4, rows, levels), F32)
     corner = jax.ShapeDtypeStruct((EDGE, levels), F32)
     vmem = pl.BlockSpec(memory_space=pltpu.VMEM)
     return pl.pallas_call(
         edges_kernel,
-        out_shape=(slab, slab, side, side, corner, corner),
+        out_shape=(slab, slab, side, corner, corner),
         in_specs=[pl.BlockSpec(memory_space=pl.ANY)],
-        out_specs=(vmem,) * 6,
+        out_specs=(vmem,) * 5,
         scratch_shapes=[
             pltpu.VMEM((rows, EDGE, levels), F32),
             pltpu.VMEM((rows, EDGE, levels), F32),
@@ -81,15 +79,17 @@
     )(state)
 
 
-def advance_kernel(neighbours, capacity, *refs):
-    (flags, sources, state, up_rows, low_rows, left_cols, right_cols, own_first, own_last) = refs[:9]
-    (up_left, up_right, low_left, low_right, mask, mix_atm, mix_ocn, flux_map) = refs[9:17]
-    out = refs[17]
-    packed = refs[18 : 18 + neighbours]
+def advance_kernel(comp_count, left_at, right_at, *refs):
+    (flags, source_column, state, up_rows, low_rows, left_in, right_in, own_sides) = refs[:8]
+    (up_left, up_right, low_left, low_right, mask, mix_atm, mix_ocn, flux_map) = refs[8:16]
+    out = refs[16]
+    packed = refs[17 : 17 + comp_count]
     (values, moved, halo, halo_moved, smooth, pairs, mixed, weights, flux_weights, fluxes, staged) = refs[
-        18 + neighbours : 29 + neighbours
+        17 + comp_count : 28 + comp_count
     ]
-    in_sems, out_sems = refs[29 + neighbours :]
+    in_sems, out_sems = refs[28 + comp_count :]
+    left_cols = left_in.at[left_at : left_at + 2]
+    right_cols = right_in.at[right_at : right_at + 2]
     rows, cols, levels = state.shape
     chunks = rows // CHUNK
     inner = pl.ds(EDGE, cols)
@@ -170,7 +170,7 @@
         halo[1, EDGE - 1 : EDGE, :] = up_right[0:1]
         halo[1, EDGE + rows : EDGE + rows + 1, :] = low_right[0:1]
         beyond = (left_cols.at[0], right_cols.at[1])
-        within = (own_first.at[0], own_last.at[1])
+        within = (own_sides.at[0], own_sides.at[3])
         for s in range(2):
             total = (
                 halo[s, EDGE : EDGE + rows, :]
@@ -238,21 +238,20 @@
                 block = PHYSICS * flux[:, row * cols : (row + 1) * cols]
                 sea = jnp.broadcast_to(mask[pl.ds(base + row, 1), :], block.shape)
                 block = jnp.where(sea > 0.5, block, 0.0)
-                fluxes[base + row] = block.astype(BF16).astype(F32)
+                fluxes[pl.ds(pl.multiple_of((base + row) * flux_count, flux_count), flux_count), :] = block
             return 0
 
         lax.fori_loop(0, chunks, one_chunk, 0)
         put(chunks - 2, (chunks - 2) % 2).wait()
         put(chunks - 1, (chunks - 1) % 2).wait()
-        for n in range(neighbours):
-
-            def pack(i, _, n=n):
-                first = fluxes[sources[n * capacity + 2 * i]]
-                second = fluxes[sources[n * capacity + 2 * i + 1]]
-                packed[n][i] = jnp.concatenate([first, second], axis=0).astype(BF16)
-                return 0
-
-            lax.fori_loop(0, capacity // 2, pack, 0, unroll=8)
+        spots = lax.broadcasted_iota(jnp.int32, (source_column.shape[0], rows), 1)
+        placing = jnp.where(source_column[...] == spots, 1.0, 0.0).astype(BF16)
+        share = flux_count // comp_count
+        for shift in range(comp_count):
+            first = lax.rem(flags[3] + shift, comp_count) * share
+            for f in range(share):
+                field = fluxes[pl.ds(first + f, rows, stride=flux_count), :].astype(BF16)
+                packed[shift][:, f * cols : (f + 1) * cols] = dot_nn(placing, field).astype(BF16)
 
     @pl.when(ocean)
     def sea_side():
@@ -290,19 +289,21 @@
         put(chunks - 1, (chunks - 1) % 2).wait()
 
 
-def advance(flags, sources, state, halos, mask, mix_atm, mix_ocn, flux_map_t, neighbours, capacity):
+def advance(
+    flags, source_column, state, halos, mask, mix_atm, mix_ocn, flux_map_t, comp_count, left_at, right_at
+):
     rows, cols, levels = state.shape
     fluxes = flux_map_t.shape[0]
     vmem = pl.BlockSpec(memory_space=pltpu.VMEM)
     smem = pl.BlockSpec(memory_space=pltpu.SMEM)
     hbm = pl.BlockSpec(memory_space=pl.ANY)
-    entry = jax.ShapeDtypeStruct((capacity // 2, 2 * fluxes, cols), BF16)
+    entry = jax.ShapeDtypeStruct((source_column.shape[0], fluxes // comp_count * cols), BF16)
     cells = rows * cols
     return pl.pallas_call(
-        functools.partial(advance_kernel, neighbours, capacity),
-        out_shape=(jax.ShapeDtypeStruct(state.shape, F32),) + (entry,) * neighbours,
-        in_specs=[smem, smem, hbm] + [vmem] * (len(halos) + 4),
-        out_specs=(hbm,) + (vmem,) * neighbours,
+        functools.partial(advance_kernel, comp_count, left_at, right_at),
+        out_shape=(jax.ShapeDtypeStruct(state.shape, F32),) + (entry,) * comp_count,
+        in_specs=[smem, vmem, hbm] + [vmem] * (len(halos) + 4),
+        out_specs=(hbm,) + (vmem,) * comp_count,
         scratch_shapes=[
             pltpu.VMEM((rows + 4, cols + 2 * EDGE, levels), F32),
             pltpu.VMEM((rows + 2, cols + 2 * EDGE, levels), F32),
@@ -313,7 +314,7 @@
             pltpu.VMEM((CHUNK * cols, 2 * levels), F32),
             pltpu.VMEM((2 * levels, 2 * levels), BF16),
             pltpu.VMEM((2 * fluxes, 2 * levels), BF16),
-            pltpu.VMEM((rows, fluxes, cols), F32),
+            pltpu.VMEM((rows * fluxes, cols), F32),
             pltpu.VMEM((2, CHUNK, cols, levels), F32),
             pltpu.SemaphoreType.DMA((rows // CHUNK,)),
             pltpu.SemaphoreType.DMA((2,)),
@@ -323,92 +324,132 @@
             flops=8 * cells * levels * levels, bytes_accessed=8 * cells * levels, transcendentals=0
         ),
         name="advance",
-    )(flags, sources, state, *halos, mask, mix_atm, mix_ocn, flux_map_t)
-
-
-def regrid_kernel(groups, capacity, *refs):
-    flags, labels = refs[:2]
-    entries = refs[2 : 2 + groups]
-    target_column, weights, surface, mask, ocean_first = refs[2 + groups : 7 + groups]
-    forcing, new_surface = refs[7 + groups : 9 + groups]
-    picked = refs[9 + groups : 9 + 2 * groups]
-    (bins,) = refs[9 + 2 * groups :]
-    rows, flux_count, cols = forcing.shape
+    )(flags, source_column, state, *halos, mask, mix_atm, mix_ocn, flux_map_t)
+
+
+BATCH = 8
+
+
+def regrid_body(count, flags, ocean_first, *refs):
+    blocks = refs[:count]
+    target_line, weight_line, weights, surface, mask, forcing, shared, entries, chosen, binned = refs[count:]
+    rows, cols = mask.shape
+    share = forcing.shape[0]
     weight_count = weights.shape[0]
-
-    @pl.when(flags[0] == 1)
-    def ocean():
-        def clear(i, _):
-            bins[pl.ds(i * 32, 32)] = jnp.zeros((32, flux_count, cols), F32)
-            return 0
-
-        lax.fori_loop(0, weight_count * rows // 32, clear, 0)
-        for j in range(groups):
-
-            def add(i, _, j=j):
-                pair = entries[j][i].astype(F32)
-                bins[labels[j * capacity + 2 * i]] += pair[:flux_count]
-                bins[labels[j * capacity + 2 * i + 1]] += pair[flux_count:]
-                return 0
-
-            lax.fori_loop(0, capacity // 2, add, 0, unroll=8)
-
-        def products(w):
-            block = bins[pl.ds(w * rows, rows)].reshape(rows * flux_count, cols)
-            once = weights[w]
-            return dot_nn(side_by_side(block), jnp.concatenate([once, once], axis=0))
-
-        forcing[...] = products(0).reshape(forcing.shape)
-
-        def accumulate(w, _):
-            forcing[...] += products(w).reshape(forcing.shape)
-            return 0
-
-        lax.fori_loop(1, weight_count, accumulate, 0)
-        change = jnp.sum(forcing[...] * ocean_first[...][None], axis=1)
-        now = surface[...] + jnp.where(mask[...] > 0.5, change, 0.0)
-        new_surface[...] = now
-        now_pair = jnp.concatenate(split_two(now), axis=0)
-        spots = lax.broadcasted_iota(jnp.int32, (capacity, rows), 1)
-        for j in range(groups):
-            chosen = target_column[j * capacity : (j + 1) * capacity, :] == spots
-            chosen = jnp.where(chosen, 1.0, 0.0).astype(BF16)
-            picked[j][...] = dot_nn(jnp.concatenate([chosen, chosen], axis=1), now_pair)
-
-
-def regrid(flags, labels, entries, target_column, weights, surface, mask, ocean_first, capacity):
-    groups = len(entries)
+    size = blocks[0].shape[0]
+    total = count * size
+    for n in range(count):
+        entries[n * size : (n + 1) * size, :] = blocks[n][...]
+    spots = lax.broadcasted_iota(jnp.int32, (rows, total), 0)
+    by_target = jnp.where(target_line[...] == spots, 1.0, 0.0).astype(BF16)
+    numbers = lax.broadcasted_iota(jnp.int32, (weight_count, total), 0)
+    by_weight = jnp.where(weight_line[...] == numbers, 1.0, 0.0).astype(BF16)
+    for g in range(weight_count // BATCH):
+        for i in range(BATCH):
+            w = g * BATCH + i
+            chosen[i * rows : (i + 1) * rows, :] = by_target * by_weight[w : w + 1, :]
+        binned[...] = dot_nn(chosen[...], entries[...])
+        wide = weights[g * BATCH : (g + 1) * BATCH].reshape(BATCH * cols, cols)
+        for f in range(share):
+            halves = [
+                split_two(binned[i * rows : (i + 1) * rows, f * cols : (f + 1) * cols])
+                for i in range(BATCH)
+            ]
+            part = dot_nn(jnp.concatenate([h for h, _ in halves], axis=1), wide) + dot_nn(
+                jnp.concatenate([l for _, l in halves], axis=1), wide
+            )
+            forcing[f] = part if g == 0 else forcing[f] + part
+    change = ocean_first[flags[3] * share] * forcing[0]
+    for f in range(1, share):
+        change = change + ocean_first[flags[3] * share + f] * forcing[f]
+    base = jnp.where(flags[0] == 1, surface[...], 0.0)
+    held = jnp.where((mask[...] > 0.5) | (flags[0] == 0), change, 0.0)
+    shared[0] = base + held
+    shared[1] = mask[...]
+
+
+def regrid(flags, ocean_first, blocks, target_line, weight_line, weights, surface, mask):
     rows, cols = mask.shape
-    flux_count = ocean_first.shape[0]
+    count = len(blocks)
+    size, width = blocks[0].shape
+    share = width // cols
     weight_count = weights.shape[0]
     vmem = pl.BlockSpec(memory_space=pltpu.VMEM)
     smem = pl.BlockSpec(memory_space=pltpu.SMEM)
     return pl.pallas_call(
-        functools.partial(regrid_kernel, groups, capacity),
+        functools.partial(regrid_body, count),
         out_shape=(
-            jax.ShapeDtypeStruct((rows, flux_count, cols), F32),
-            jax.ShapeDtypeStruct((rows, cols), F32),
-        )
-        + (jax.ShapeDtypeStruct((capacity, cols), F32),) * groups,
-        in_specs=[smem, smem] + [vmem] * (groups + 5),
-        out_specs=(vmem,) * (2 + groups),
-        scratch_shapes=[pltpu.VMEM((weight_count * rows, flux_count, cols), F32)],
-        compiler_params=pltpu.CompilerParams(vmem_limit_bytes=40 * MIB),
+            jax.ShapeDtypeStruct((share, rows, cols), F32),
+            jax.ShapeDtypeStruct((2, rows, cols), F32),
+        ),
+        in_specs=[smem, smem] + [vmem] * (count + 5),
+        out_specs=(vmem, vmem),
+        scratch_shapes=[
+            pltpu.VMEM((count * size, width), BF16),
+            pltpu.VMEM((BATCH * rows, count * size), BF16),
+            pltpu.VMEM((BATCH * rows, width), F32),
+        ],
+        compiler_params=pltpu.CompilerParams(vmem_limit_bytes=32 * MIB),
         cost_estimate=pl.CostEstimate(
-            flops=4 * weight_count * rows * flux_count * cols * cols,
-            bytes_accessed=8 * MIB,
+            flops=2 * weight_count * rows * width * (count * size + 2 * cols),
+            bytes_accessed=2 * MIB,
             transcendentals=0,
         ),
         name="regrid",
-    )(flags, labels, *entries, target_column, weights, surface, mask, ocean_first)
+    )(flags, ocean_first, *blocks, target_line, weight_line, weights, surface, mask)
+
+
+def pick_kernel(comp_count, *refs):
+    flags = refs[0]
+    parts = refs[1 : 1 + comp_count]
+    target_column, surface = refs[1 + comp_count : 3 + comp_count]
+    picked = refs[3 + comp_count :]
+    rows, cols = surface.shape
+    from_ocean = lax.rem(flags[3] + 1, comp_count)
+    base = jnp.zeros((rows, cols), F32)
+    sea = base
+    change = base
+    for shift in range(comp_count):
+        is_base = from_ocean == shift
+        base = base + jnp.where(is_base, parts[shift][0], 0.0)
+        sea = sea + jnp.where(is_base, parts[shift][1], 0.0)
+        change = change + jnp.where(is_base, 0.0, parts[shift][0])
+    now = base + jnp.where(sea > 0.5, change, 0.0)
+    surface[...] = now
+    pair = jnp.concatenate(split_two(now), axis=0)
+    size = picked[0].shape[0]
+    spots = lax.broadcasted_iota(jnp.int32, (size, rows), 1)
+    for n in range(len(picked)):
+        hits = target_column[n * size : (n + 1) * size, :] == spots
+        hits = jnp.where(hits, 1.0, 0.0).astype(BF16)
+        picked[n][...] = dot_nn(jnp.concatenate([hits, hits], axis=1), pair)
+
+
+def pick(flags, parts, target_column, neighbours):
+    _, rows, cols = parts[0].shape
+    size = target_column.shape[0] // neighbours
+    vmem = pl.BlockSpec(memory_space=pltpu.VMEM)
+    smem = pl.BlockSpec(memory_space=pltpu.SMEM)
+    return pl.pallas_call(
+        functools.partial(pick_kernel, len(parts)),
+        out_shape=(jax.ShapeDtypeStruct((rows, cols), F32),)
+        + (jax.ShapeDtypeStruct((size, cols), F32),) * neighbours,
+        in_specs=[smem] + [vmem] * (len(parts) + 1),
+        out_specs=(vmem,) * (1 + neighbours),
+        compiler_params=pltpu.CompilerParams(vmem_limit_bytes=16 * MIB),
+        name="pick",
+    )(flags, *parts, target_column)
 
 
 LINES = 16
 
 
-def update_kernel(flags, state, forcing, mask, ocean_map, out, held, table, wide, in_sems, out_sems):
+def update_kernel(groups, flags, state, *refs):
+    parts = refs[:groups]
+    mask, ocean_map, out, held, table, wide, in_sems, out_sems = refs[groups:]
     rows, cols, levels = state.shape
-    flux_count = forcing.shape[1]
+    share = parts[0].shape[0]
+    flux_count = groups * share
     chunks = rows // LINES
     depth = LINES * flux_count
 
@@ -428,9 +469,9 @@
             fetch(q).start()
         table[...] = jnp.zeros(table.shape, F32)
         for line in range(LINES):
-            table[
-                line * flux_count : (line + 1) * flux_count, line * levels : (line + 1) * levels
-            ] = ocean_map[...]
+            for f in range(flux_count):
+                spot = f * LINES + line
+                table[spot : spot + 1, line * levels : (line + 1) * levels] = ocean_map[f : f + 1]
         high, low = split_two(table[...])
         wide[:depth] = high
         wide[depth : 2 * depth] = high
@@ -438,10 +479,15 @@
 
         def one(q, _):
             start = pl.multiple_of(q * LINES, LINES)
-            sea = mask[pl.ds(start, LINES), :]
-            part = jnp.where(sea[:, None, :] > 0.5, forcing[pl.ds(start, LINES)], 0.0)
-            turned = part.reshape(depth, cols).T
-            first, second = split_two(turned)
+            sea = mask[pl.ds(start, LINES), :] > 0.5
+            part = jnp.concatenate(
+                [
+                    jnp.where(sea, parts[f // share][f % share, pl.ds(start, LINES), :], 0.0)
+                    for f in range(flux_count)
+                ],
+                axis=0,
+            )
+            first, second = split_two(part.T)
             change = dot_nn(jnp.concatenate([first, second, first], axis=1), wide[...])
             fetch(q).wait()
             for line in range(LINES):
@@ -454,16 +500,16 @@
             put(q).wait()
 
 
-def update(flags, state, forcing, mask, ocean_map):
+def update(flags, state, parts, mask, ocean_map):
     rows, cols, levels = state.shape
-    depth = LINES * forcing.shape[1]
+    depth = LINES * ocean_map.shape[0]
     vmem = pl.BlockSpec(memory_space=pltpu.VMEM)
     smem = pl.BlockSpec(memory_space=pltpu.SMEM)
     hbm = pl.BlockSpec(memory_space=pl.ANY)
     return pl.pallas_call(
-        update_kernel,
+        functools.partial(update_kernel, len(parts)),
         out_shape=jax.ShapeDtypeStruct(state.shape, F32),
-        in_specs=[smem, hbm, vmem, vmem, vmem],
+        in_specs=[smem, hbm] + [vmem] * (len(parts) + 2),
         out_specs=hbm,
         input_output_aliases={1: 0},
         scratch_shapes=[
@@ -480,7 +526,7 @@
             transcendentals=0,
         ),
         name="update",
-    )(flags, state, forcing, mask, ocean_map)
+    )(flags, state, *parts, mask, ocean_map)
 
 
 def returned_kernel(groups, flags, *refs):
@@ -555,7 +601,7 @@
     is_ocean = comp_index == ocean_comp
     upper_valid = (band > 0) & (band != ocean_band)
     lower_valid = (band < bands - 1) & (band != ocean_band - 1)
-    flags = jnp.stack([is_ocean, upper_valid, lower_valid]).astype(jnp.int32)
+    flags = jnp.stack([is_ocean, upper_valid, lower_valid, comp_index]).astype(jnp.int32)
     mask = (land_mask == 1).astype(F32)
 
     def band_shift(value, by, lon_by):
@@ -569,11 +615,16 @@
                     )
         return lax.ppermute(value, AXES, pairs)
 
-    first_rows, last_rows, first_cols, last_cols, top_corners, low_corners = take_edges(state)
+    first_rows, last_rows, sides, top_corners, low_corners = take_edges(state)
     up_rows = band_shift(last_rows, 1, 0)
     low_rows = band_shift(first_rows, -1, 0)
-    left_cols = band_shift(last_cols, 0, 1)
-    right_cols = band_shift(first_cols, 0, -1)
+    if lon_count == 2:
+        left_cols = right_cols = band_shift(sides, 0, 1)
+        left_at, right_at = 2, 0
+    else:
+        left_cols = band_shift(sides[2:], 0, 1)
+        right_cols = band_shift(sides[:2], 0, -1)
+        left_at, right_at = 0, 0
     up_left = band_shift(low_corners, 1, 1)
     low_left = band_shift(top_corners, -1, 1)
     if lon_count == 2:
@@ -603,48 +654,74 @@
     sources = jnp.sum(jnp.where(placing, (positions // intersections)[None, :], 0), axis=1)
     packed_labels = jnp.sum(jnp.where(placing, labels[None, :], 0), axis=1)
 
-    def to_ocean(value, comp, offset):
+    def over_comp(value, shift, last):
         pairs = [
-            (comp * tile_count + t, ocean_comp * tile_count + (t + offset) % tile_count)
+            (c * tile_count + t, (c + shift) % comp_count * tile_count + t)
+            for c in range(comp_count if last else comp_count - 1)
             for t in range(tile_count)
         ]
         return lax.ppermute(value, AXES, pairs)
 
-    def from_ocean(value, comp, offset):
+    def over_tiles(value, offset):
+        if offset % tile_count == 0:
+            return value
         pairs = [
-            (ocean_comp * tile_count + (t + offset) % tile_count, comp * tile_count + t)
+            (c * tile_count + t, c * tile_count + (t + offset) % tile_count)
+            for c in range(comp_count)
             for t in range(tile_count)
         ]
         return lax.ppermute(value, AXES, pairs)
 
-    order = [(c, n) for n in range(neighbours) for c in range(comp_count - 1)]
-    arrived_labels = jnp.concatenate(
-        [
-            to_ocean(packed_labels[n * capacity : (n + 1) * capacity], c, offsets[n])
-            for c, n in order
+    def to_ocean(value, comp):
+        pairs = [
+            (comp * tile_count + t, ocean_comp * tile_count + t) for t in range(tile_count)
         ]
-    )
-    target_column = (arrived_labels % rows)[:, None]
-
-    halos = (up_rows, low_rows, left_cols, right_cols, first_cols, last_cols)
+        return lax.ppermute(value, AXES, pairs)
+
+    every = lax.all_gather(packed_labels, AXES).reshape(
+        comp_count, tile_count, neighbours, capacity
+    )
+    ordered = (comp_index - jnp.arange(comp_count, dtype=jnp.int32) + comp_count) % comp_count
+    from_tiles = [
+        lax.dynamic_index_in_dim(
+            every[:, :, n], (tile_index - offsets[n] + tile_count) % tile_count, 1, False
+        )
+        for n in range(neighbours)
+    ]
+    by_comp = jnp.stack(from_tiles)
+    mine = by_comp[:, :, None, :]
+    wanted = ordered[None, :, None, None] == jnp.arange(comp_count, dtype=jnp.int32)[None, None, :, None]
+    arrived_labels = jnp.sum(jnp.where(wanted, mine.transpose(0, 2, 1, 3), 0), axis=2).reshape(1, -1)
+    own_labels = jnp.sum(
+        jnp.where((jnp.arange(comp_count, dtype=jnp.int32) == comp_index)[None, :, None], by_comp, 0),
+        axis=1,
+    )
+    target_column = (own_labels % rows).reshape(-1, 1)
+
+    halos = (up_rows, low_rows, left_cols, right_cols, sides)
     halos = halos + (up_left, up_right, low_left, low_right)
     moved = advance(
-        flags, sources, state, halos, mask, mix_atm, mix_ocn, flux_map.T, neighbours, capacity
+        flags, sources[:, None], state, halos, mask, mix_atm, mix_ocn, flux_map.T, comp_count,
+        left_at, right_at,
     )
     moved, packed = moved[0], moved[1:]
-    entries = [to_ocean(packed[n], c, offsets[n]) for c, n in order]
+    own = jnp.where(is_ocean, jnp.zeros((), BF16), packed[0])
+    slabs = [own] + [over_comp(packed[s], s, False) for s in range(1, comp_count)]
+    blocks = []
+    for n in range(neighbours):
+        block = jnp.concatenate([slab[n * capacity : (n + 1) * capacity] for slab in slabs])
+        blocks.append(over_tiles(block, offsets[n]))
     surface = moved[:, :, 0]
-    ocean_first = jnp.broadcast_to(ocean_map[:, :1], (ocean_map.shape[0], cols))
-    regridded = regrid(
-        flags, arrived_labels, entries, target_column, regrid_weights, surface, mask,
-        ocean_first, capacity,
-    )
-    forcing, new_surface, picked = regridded[0], regridded[1], regridded[2:]
-    arrived = [None] * neighbours
-    for (c, n), value in zip(order, picked):
-        one = from_ocean(value, c, offsets[n])
-        arrived[n] = one if arrived[n] is None else jnp.where(comp_index == c, one, arrived[n])
-    final_state = update(flags, moved, forcing, mask, ocean_map)
+    forcing, shared = regrid(
+        flags, ocean_map[:, 0], blocks, arrived_labels % rows, arrived_labels // rows,
+        regrid_weights, surface, mask,
+    )
+    parts = [shared] + [over_comp(shared, s, True) for s in range(1, comp_count)]
+    picks = pick(flags, parts, target_column, neighbours)
+    new_surface, picked = picks[0], picks[1:]
+    arrived = [over_tiles(picked[n], -offsets[n]) for n in range(neighbours)]
+    fields = [to_ocean(forcing, c) for c in range(comp_count - 1)] + [forcing]
+    final_state = update(flags, moved, fields, mask, ocean_map)
     weight_column = (packed_labels // rows)[:, None]
     surface_out = returned(
         flags, arrived, weight_column, sources[None, :], regrid_weights, mask, surface, new_surface

time: 154 us -> 143 us (0.929)
  the two profiles are of different devices: /device:TPU:16 before, /device:TPU:7 now
where the time goes in v1:
time: 143 us
  blocking collectives  38.3 us (27%)
  starting transfers between devices  37 us (26%)
  Pallas kernels  30.5 us (21%)
  waiting for transfers between devices  19.9 us (14%)
  local copies, waits for them, and re-layouts  14.7 us (10%)
    all_gather x1, blocking collectives, local(): lax.all_gather(packed_labels, AXES)  38.3 us
    pallas_call x1, Pallas kernels, advance(): pl.pallas_call(functools.partial(advance_kernel, comp_count, left_at, rig...  13.8 us
    ppermute x6, waiting for transfers between devices, over_comp(): return lax.ppermute(value, AXES, pairs)  13.2 us
    ppermute x6, starting transfers between devices, over_comp(): return lax.ppermute(value, AXES, pairs)  11.8 us
    ppermute x5, starting transfers between devices, band_shift(): return lax.ppermute(value, AXES, pairs)  11 us
    ppermute x6, starting transfers between devices, over_tiles(): return lax.ppermute(value, AXES, pairs)  10.4 us
    pallas_call x1, local copies, waits for them, and re-layouts, advance(): pl.pallas_call(functools.partial(advance_kernel, comp_count, left_at, rig...  9.45 us
    pallas_call x1, Pallas kernels, update(): pl.pallas_call(functools.partial(update_kernel, len(parts)), out_shape=ja...  7.41 us
  transfers between devices with their start and end apart: 20, of which 6 were waited for; matrix products, arithmetic and copies ran while one was open for 9% of the time, Pallas kernels for 6%

profile of v1, /device:TPU:7, one launch (start us, length us, event | category | flops | bytes accessed | tf_op | source)
XLA Modules:
  0.0 142.8 jit_solution(14575234966885988632)
XLA Ops:
  0.6 3.4 %copy-done = f32[128,128,128]{2,1,0:T(8,128)S(1)} copy-done((f32[128,128,128]{2,1,0:T(8,128)S(1)}, f32[128,128,128]{2,1,0:T(8,128)}, u32[]{:S(2)}) %copy-start) | copy-done | bytes 8388632
  4.0 0.7 edges.1
  4.7 0.7 collective-permute-start.2
  5.5 3.2 %collective-permute-start = (f32[2,128,128]{2,1,0:T(8,128)S(1)}, f32[2,128,128]{2,1,0:T(8,128)S(1)}, u32[]{:S(2)}, u32[]{:S(2)}) collective-permute-start(f32[2,128,128]{2,1,0:T(8,128)S(1)} %get-tuple-element.19), channel_id=1, source_target_pairs={{0,2},{1,3},{2,4},{3,5},{4,6},{5,7},{6,8},{7,9},{8,10},{9,11},{10,... | collective-permute-start | bytes 393224 | tf_op jit(solution)/shard_map/ppermute | solution.py:616
  8.7 1.3 collective-permute-start.1
  10.0 4.5 %collective-permute-start.3 = (f32[8,128]{1,0:T(8,128)S(1)}, f32[8,128]{1,0:T(8,128)S(1)}, u32[]{:S(2)}, u32[]{:S(2)}) collective-permute-start(f32[8,128]{1,0:T(8,128)S(1)} %get-tuple-element.22), channel_id=1, source_target_pairs={{0,3},{1,2},{2,5},{3,4},{4,7},{5,6},{6,9},{7,8},{8,11},{9,10},{10,... | collective-permute-start | bytes 12296 | tf_op jit(solution)/shard_map/ppermute | solution.py:616
  14.4 1.3 collective-permute-start.4
  15.8 0.2 copy.34
  16.0 0.3 fusion.5
  16.3 0.2 convert_reduce_fusion
  16.5 0.2 select_reduce_fusion
  16.7 38.3 %all-gather.1 = s32[32,1,256]{2,1,0:T(1,128)S(1)} all-gather(s32[1,1,256]{2,1,0:T(1,128)S(1)} %bitcast.20), channel_id=2, replica_groups=mesh['comp'=4,'lat'=4,'lon'=2] {'comp','lat','lon'}, dimensions={0}, use_global_device_ids=true | all-gather | bytes 33792 | tf_op jit(solution)/shard_map/all_gather | solution.py:681
  54.9 0.1 reduce.3
  55.0 0.1 reshape.350
  55.2 0.1 select_reduce_fusion.3
  55.3 0.1 select_reduce_fusion.2
  55.4 0.1 reshape.351
  55.6 0.1 slice_reduce_fusion.ocean_first
  55.7 0.1 pad_add_fusion.1.refs_0_.flags
  55.8 0.1 copy.35.refs_1_
  55.9 0.1 reduce_sum.66
  56.1 0.1 copy.40
  56.3 13.8 %advance.1 = (f32[128,128,128]{2,1,0:T(8,128)}, bf16[256,256]{1,0:T(8,128)(2,1)S(1)}, bf16[256,256]{1,0:T(8,128)(2,1)S(1)}, bf16[256,256]{1,0:T(8,128)(2,1)S(1)}, bf16[256,256]{1,0:T(8,128)(2,1)S(1)}) custom-call(s32[4]{0:T(128)S(1)} %pad_add_fusion.1.refs_0_.flags, s32[256,1]{1,0:T(8,128)S(1)} %copy.35.refs_1_, f32[128,128,128]{2,1,0:T(8,128)} %refs_2_.1, ...), custom_call_target="tpu_custom_call" | custom-call | flops 2147483648 | bytes 16777216 | tf_op jit(solution)/shard_map/advance/pallas_call | solution.py:302
  70.1 1.3 collective-permute-start.5
  71.4 1.3 collective-permute-start.6
  72.7 1.3 collective-permute-start.7
  74.0 9.5 %copy.36 = f32[128,128,128]{1,0,2:T(8,128)} copy(f32[128,128,128]{2,1,0:T(8,128)} %get-tuple-element.24.state) | data formatting | bytes 16777216 | tf_op jit(solution)/shard_map/advance/pallas_call | solution.py:302
  83.5 6.7 %collective-permute-done.5 = bf16[256,256]{1,0:T(8,128)(2,1)S(1)} collective-permute-done((bf16[256,256]{1,0:T(8,128)(2,1)S(1)}, bf16[256,256]{1,0:T(8,128)(2,1)S(1)}, u32[]{:S(2)}, u32[]{:S(2)}) %collective-permute-start.5) | collective-permute-done | bytes 131104 | tf_op jit(solution)/shard_map/ppermute | solution.py:663
  90.2 2.1 %collective-permute-done.6 = bf16[256,256]{1,0:T(8,128)(2,1)S(1)} collective-permute-done((bf16[256,256]{1,0:T(8,128)(2,1)S(1)}, bf16[256,256]{1,0:T(8,128)(2,1)S(1)}, u32[]{:S(2)}, u32[]{:S(2)}) %collective-permute-start.6) | collective-permute-done | bytes 131104 | tf_op jit(solution)/shard_map/ppermute | solution.py:663
  92.3 2.6 %collective-permute-done.7 = bf16[256,256]{1,0:T(8,128)(2,1)S(1)} collective-permute-done((bf16[256,256]{1,0:T(8,128)(2,1)S(1)}, bf16[256,256]{1,0:T(8,128)(2,1)S(1)}, u32[]{:S(2)}, u32[]{:S(2)}) %collective-permute-start.7) | collective-permute-done | bytes 131104 | tf_op jit(solution)/shard_map/ppermute | solution.py:663
  95.0 2.0 %collective-permute-start.9 = (bf16[256,256]{1,0:T(8,128)(2,1)S(1)}, bf16[256,256]{1,0:T(8,128)(2,1)S(1)}, u32[]{:S(2)}, u32[]{:S(2)}) collective-permute-start(bf16[256,256]{1,0:T(8,128)(2,1)S(1)} %pad_maximum_fusion.2), channel_id=1, source_target_pairs={{0,2},{1,3},{2,4},{3,5},{4,6},{5,7},{6,0},{7,1},{8,10},{9,11},{10,... | collective-permute-start | bytes 393224 | tf_op jit(solution)/shard_map/ppermute | solution.py:673
  97.0 1.0 collective-permute-start.8
  98.0 0.8 slice_bitcast_fusion.refs_7_.refs_8_
  98.8 2.8 %collective-permute-done.10.refs_3_ = bf16[256,256]{1,0:T(8,128)(2,1)S(1)} collective-permute-done((bf16[256,256]{1,0:T(8,128)(2,1)S(1)}, bf16[256,256]{1,0:T(8,128)(2,1)S(1)}, u32[]{:S(2)}, u32[]{:S(2)}) %collective-permute-start.10) | collective-permute-done | bytes 131104 | tf_op jit(solution)/shard_map/ppermute | solution.py:673
  101.6 3.8 %collective-permute-done.9.refs_2_ = bf16[256,256]{1,0:T(8,128)(2,1)S(1)} collective-permute-done((bf16[256,256]{1,0:T(8,128)(2,1)S(1)}, bf16[256,256]{1,0:T(8,128)(2,1)S(1)}, u32[]{:S(2)}, u32[]{:S(2)}) %collective-permute-start.9) | collective-permute-done | bytes 131104 | tf_op jit(solution)/shard_map/ppermute | solution.py:673
  105.5 6.7 %regrid.1 = (f32[2,128,128]{2,1,0:T(8,128)S(1)}, f32[2,128,128]{2,1,0:T(8,128)S(1)}) custom-call(s32[4]{0:T(128)S(1)} %pad_add_fusion.1.refs_0_.flags, f32[8]{0:T(128)S(1)} %slice_reduce_fusion.ocean_first, bf16[256,256]{1,0:T(8,128)(2,1)S(1)} %pad_maximum_fusion.refs_0_, bf16[256,256]{1,0:T(8,128)(2,1)S(1)} %collective-permute-done.8.refs_1_, ...), custom_call_target="tpu_custom_call" | custom-call | flops 2684354560 | bytes 2097152 | tf_op jit(solution)/shard_map/regrid/pallas_call | solution.py:379
  112.2 6.1 %collective-permute-start.14 = (f32[2,128,128]{2,1,0:T(8,128)S(1)}, f32[2,128,128]{2,1,0:T(8,128)S(1)}, u32[]{:S(2)}, u32[]{:S(2)}) collective-permute-start(f32[2,128,128]{2,1,0:T(8,128)S(1)} %get-tuple-element.30.refs_1_), channel_id=1, source_target_pairs={{0,8},{1,9},{2,10},{3,11},{4,12},{5,13},{6,14},{7,15},{8,16},{9,17... | collective-permute-start | bytes 393224 | tf_op jit(solution)/shard_map/ppermute | solution.py:663
  118.4 1.8 %collective-permute-start.15 = (f32[2,128,128]{2,1,0:T(8,128)S(1)}, f32[2,128,128]{2,1,0:T(8,128)S(1)}, u32[]{:S(2)}, u32[]{:S(2)}) collective-permute-start(f32[2,128,128]{2,1,0:T(8,128)S(1)} %get-tuple-element.30.refs_1_), channel_id=1, source_target_pairs={{0,16},{1,17},{2,18},{3,19},{4,20},{5,21},{6,22},{7,23},{8,24},{9,... | collective-permute-start | bytes 393224 | tf_op jit(solution)/shard_map/ppermute | solution.py:663
  120.2 1.3 collective-permute-start.11
  121.5 1.3 collective-permute-start.12
  122.8 1.3 collective-permute-start.13
  124.1 0.1 add_select_fusion.refs_4_
  124.2 1.9 %collective-permute-done.16.refs_4_ = f32[2,128,128]{2,1,0:T(8,128)S(1)} collective-permute-done((f32[2,128,128]{2,1,0:T(8,128)S(1)}, f32[2,128,128]{2,1,0:T(8,128)S(1)}, u32[]{:S(2)}, u32[]{:S(2)}) %collective-permute-start.16) | collective-permute-done | bytes 131104 | tf_op jit(solution)/shard_map/ppermute | solution.py:663
  126.0 0.8 pick.1
  126.8 6.0 %collective-permute-start.17 = (f32[64,128]{1,0:T(8,128)S(1)}, f32[64,128]{1,0:T(8,128)S(1)}, u32[]{:S(2)}, u32[]{:S(2)}) collective-permute-start(f32[64,128]{1,0:T(8,128)S(1)} %get-tuple-element.32), channel_id=1, source_target_pairs={{0,7},{1,0},{2,1},{3,2},{4,3},{5,4},{6,5},{7,6},{8,15},{9,8},{10,9... | collective-permute-start | bytes 98312 | tf_op jit(solution)/shard_map/ppermute | solution.py:673
  132.8 1.4 collective-permute-start.19
  134.1 7.4 %update.1 = f32[128,128,128]{2,1,0:T(8,128)} custom-call(s32[4]{0:T(128)S(1)} %pad_add_fusion.1.refs_0_.flags, f32[128,128,128]{2,1,0:T(8,128)} %get-tuple-element.24.state, f32[2,128,128]{2,1,0:T(8,128)S(1)} %collective-permute-done.11.refs_0_, f32[2,128,128]{2,1,0:T(8,128)S(1)} %collective-permute-done.12.refs_1_, ...), custom_call_target="tpu_custom_call", output_to_operand_aliasing={{}: (1, {})} | custom-call | flops 1610612736 | bytes 16777216 | tf_op jit(solution)/shard_map/update/pallas_call | solution.py:509
  141.6 1.2 returned.1
  (55 shorter events, 0.5 us)
Async XLA Ops:
  0.6 3.4 %copy-start = (f32[128,128,128]{2,1,0:T(8,128)S(1)}, f32[128,128,128]{2,1,0:T(8,128)}, u32[]{:S(2)}) copy-start(f32[128,128,128]{2,1,0:T(8,128)} %refs_2_.1) | copy-start | bytes 25165828
  4.0 11.8 %copy-start.7 = (s32[128,1,2,3]{0,2,3,1:T(2,128)S(1)}, s32[128,1,2,3]{0,2,3,1:T(2,128)}, u32[]{:S(2)}) copy-start(s32[128,1,2,3]{0,2,3,1:T(2,128)} %param.11) | copy-start | bytes 9220
  4.0 12.5 %copy-start.6 = (s32[128,128]{1,0:T(8,128)S(1)}, s32[128,128]{1,0:T(8,128)}, u32[]{:S(2)}) copy-start(s32[128,128]{1,0:T(8,128)} %param.10) | copy-start | bytes 196612
  4.0 51.6 %copy-start.4 = (f32[8,128]{1,0:T(8,128)S(1)}, f32[8,128]{1,0:T(8,128)}, u32[]{:S(2)}) copy-start(f32[8,128]{1,0:T(8,128)} %refs_5_.1) | copy-start | bytes 12292
  4.0 52.3 %copy-start.2 = (f32[128,128]{1,0:T(8,128)S(1)}, f32[128,128]{1,0:T(8,128)}, u32[]{:S(2)}) copy-start(f32[128,128]{1,0:T(8,128)} %refs_13_.1) | copy-start | bytes 196612
  4.0 52.3 %copy-start.3 = (f32[128,128]{1,0:T(8,128)S(1)}, f32[128,128]{1,0:T(8,128)}, u32[]{:S(2)}) copy-start(f32[128,128]{1,0:T(8,128)} %refs_14_.1) | copy-start | bytes 196612
  4.0 52.3 %copy-start.5 = (f32[128,8]{0,1:T(8,128)S(1)}, f32[128,8]{0,1:T(8,128)}, u32[]{:S(2)}) copy-start(f32[128,8]{0,1:T(8,128)} %param.14) | copy-start | bytes 12292
  4.7 51.5 %collective-permute-start.2 = (f32[4,128,128]{2,1,0:T(8,128)S(1)}, f32[4,128,128]{2,1,0:T(8,128)S(1)}, u32[]{:S(2)}, u32[]{:S(2)}) collective-permute-start(f32[4,128,128]{2,1,0:T(8,128)S(1)} %get-tuple-element.21.refs_7_), channel_id=1, source_target_pairs={{0,1},{1,0},{2,3},{3,2},{4,5},{5,4},{6,7},{7,6},{8,9},{9,8},{10,11... | collective-permute-start | bytes 786440 | tf_op jit(solution)/shard_map/ppermute | solution.py:616
  5.5 50.8 %collective-permute-start = (f32[2,128,128]{2,1,0:T(8,128)S(1)}, f32[2,128,128]{2,1,0:T(8,128)S(1)}, u32[]{:S(2)}, u32[]{:S(2)}) collective-permute-start(f32[2,128,128]{2,1,0:T(8,128)S(1)} %get-tuple-element.19), channel_id=1, source_target_pairs={{0,2},{1,3},{2,4},{3,5},{4,6},{5,7},{6,8},{7,9},{8,10},{9,11},{10,... | collective-permute-start | bytes 393224 | tf_op jit(solution)/shard_map/ppermute | solution.py:616
  8.7 47.6 %collective-permute-start.1 = (f32[2,128,128]{2,1,0:T(8,128)S(1)}, f32[2,128,128]{2,1,0:T(8,128)S(1)}, u32[]{:S(2)}, u32[]{:S(2)}) collective-permute-start(f32[2,128,128]{2,1,0:T(8,128)S(1)} %get-tuple-element.20), channel_id=1, source_target_pairs={{2,0},{3,1},{4,2},{5,3},{6,4},{7,5},{8,6},{9,7},{10,8},{11,9},{12,... | collective-permute-start | bytes 393224 | tf_op jit(solution)/shard_map/ppermute | solution.py:616
  10.0 46.3 %collective-permute-start.3 = (f32[8,128]{1,0:T(8,128)S(1)}, f32[8,128]{1,0:T(8,128)S(1)}, u32[]{:S(2)}, u32[]{:S(2)}) collective-permute-start(f32[8,128]{1,0:T(8,128)S(1)} %get-tuple-element.22), channel_id=1, source_target_pairs={{0,3},{1,2},{2,5},{3,4},{4,7},{5,6},{6,9},{7,8},{8,11},{9,10},{10,... | collective-permute-start | bytes 12296 | tf_op jit(solution)/shard_map/ppermute | solution.py:616
  14.4 41.8 %collective-permute-start.4 = (f32[8,128]{1,0:T(8,128)S(1)}, f32[8,128]{1,0:T(8,128)S(1)}, u32[]{:S(2)}, u32[]{:S(2)}) collective-permute-start(f32[8,128]{1,0:T(8,128)S(1)} %get-tuple-element.23), channel_id=1, source_target_pairs={{2,1},{3,0},{4,3},{5,2},{6,5},{7,4},{8,7},{9,6},{10,9},{11,8},{12,... | collective-permute-start | bytes 12296 | tf_op jit(solution)/shard_map/ppermute | solution.py:616
  70.1 20.0 %collective-permute-start.5 = (bf16[256,256]{1,0:T(8,128)(2,1)S(1)}, bf16[256,256]{1,0:T(8,128)(2,1)S(1)}, u32[]{:S(2)}, u32[]{:S(2)}) collective-permute-start(bf16[256,256]{1,0:T(8,128)(2,1)S(1)} %get-tuple-element.26), channel_id=1, source_target_pairs={{0,8},{1,9},{2,10},{3,11},{4,12},{5,13},{6,14},{7,15},{8,16},{9,17... | collective-permute-start | bytes 393224 | tf_op jit(solution)/shard_map/ppermute | solution.py:663
  71.4 20.9 %collective-permute-start.6 = (bf16[256,256]{1,0:T(8,128)(2,1)S(1)}, bf16[256,256]{1,0:T(8,128)(2,1)S(1)}, u32[]{:S(2)}, u32[]{:S(2)}) collective-permute-start(bf16[256,256]{1,0:T(8,128)(2,1)S(1)} %get-tuple-element.27), channel_id=1, source_target_pairs={{0,16},{1,17},{2,18},{3,19},{4,20},{5,21},{6,22},{7,23},{8,24},{9,... | collective-permute-start | bytes 393224 | tf_op jit(solution)/shard_map/ppermute | solution.py:663
  72.7 22.2 %collective-permute-start.7 = (bf16[256,256]{1,0:T(8,128)(2,1)S(1)}, bf16[256,256]{1,0:T(8,128)(2,1)S(1)}, u32[]{:S(2)}, u32[]{:S(2)}) collective-permute-start(bf16[256,256]{1,0:T(8,128)(2,1)S(1)} %get-tuple-element.28), channel_id=1, source_target_pairs={{0,24},{1,25},{2,26},{3,27},{4,28},{5,29},{6,30},{7,31},{8,0},{9,1... | collective-permute-start | bytes 393224 | tf_op jit(solution)/shard_map/ppermute | solution.py:663
  74.0 31.5 %copy-start.1 = (bf16[32,128,128]{2,1,0:T(8,128)(2,1)S(1)}, bf16[32,128,128]{2,1,0:T(8,128)(2,1)}, u32[]{:S(2)}) copy-start(bf16[32,128,128]{2,1,0:T(8,128)(2,1)} %refs_6_.3) | copy-start | bytes 3145732
  94.9 6.7 %collective-permute-start.10 = (bf16[256,256]{1,0:T(8,128)(2,1)S(1)}, bf16[256,256]{1,0:T(8,128)(2,1)S(1)}, u32[]{:S(2)}, u32[]{:S(2)}) collective-permute-start(bf16[256,256]{1,0:T(8,128)(2,1)S(1)} %pad_maximum_fusion.3), channel_id=1, source_target_pairs={{0,3},{1,4},{2,5},{3,6},{4,7},{5,0},{6,1},{7,2},{8,11},{9,12},{10,... | collective-permute-start | bytes 393224 | tf_op jit(solution)/shard_map/ppermute | solution.py:673
  95.0 10.5 %collective-permute-start.9 = (bf16[256,256]{1,0:T(8,128)(2,1)S(1)}, bf16[256,256]{1,0:T(8,128)(2,1)S(1)}, u32[]{:S(2)}, u32[]{:S(2)}) collective-permute-start(bf16[256,256]{1,0:T(8,128)(2,1)S(1)} %pad_maximum_fusion.2), channel_id=1, source_target_pairs={{0,2},{1,3},{2,4},{3,5},{4,6},{5,7},{6,0},{7,1},{8,10},{9,11},{10,... | collective-permute-start | bytes 393224 | tf_op jit(solution)/shard_map/ppermute | solution.py:673
  97.0 8.5 %collective-permute-start.8 = (bf16[256,256]{1,0:T(8,128)(2,1)S(1)}, bf16[256,256]{1,0:T(8,128)(2,1)S(1)}, u32[]{:S(2)}, u32[]{:S(2)}) collective-permute-start(bf16[256,256]{1,0:T(8,128)(2,1)S(1)} %pad_maximum_fusion.1), channel_id=1, source_target_pairs={{0,1},{1,2},{2,3},{3,4},{4,5},{5,6},{6,7},{7,0},{8,9},{9,10},{10,1... | collective-permute-start | bytes 393224 | tf_op jit(solution)/shard_map/ppermute | solution.py:673
  112.2 10.6 %collective-permute-start.14 = (f32[2,128,128]{2,1,0:T(8,128)S(1)}, f32[2,128,128]{2,1,0:T(8,128)S(1)}, u32[]{:S(2)}, u32[]{:S(2)}) collective-permute-start(f32[2,128,128]{2,1,0:T(8,128)S(1)} %get-tuple-element.30.refs_1_), channel_id=1, source_target_pairs={{0,8},{1,9},{2,10},{3,11},{4,12},{5,13},{6,14},{7,15},{8,16},{9,17... | collective-permute-start | bytes 393224 | tf_op jit(solution)/shard_map/ppermute | solution.py:663
  118.4 5.8 %collective-permute-start.15 = (f32[2,128,128]{2,1,0:T(8,128)S(1)}, f32[2,128,128]{2,1,0:T(8,128)S(1)}, u32[]{:S(2)}, u32[]{:S(2)}) collective-permute-start(f32[2,128,128]{2,1,0:T(8,128)S(1)} %get-tuple-element.30.refs_1_), channel_id=1, source_target_pairs={{0,16},{1,17},{2,18},{3,19},{4,20},{5,21},{6,22},{7,23},{8,24},{9,... | collective-permute-start | bytes 393224 | tf_op jit(solution)/shard_map/ppermute | solution.py:663
  120.2 5.9 %collective-permute-start.16 = (f32[2,128,128]{2,1,0:T(8,128)S(1)}, f32[2,128,128]{2,1,0:T(8,128)S(1)}, u32[]{:S(2)}, u32[]{:S(2)}) collective-permute-start(f32[2,128,128]{2,1,0:T(8,128)S(1)} %get-tuple-element.30.refs_1_), channel_id=1, source_target_pairs={{0,24},{1,25},{2,26},{3,27},{4,28},{5,29},{6,30},{7,31},{8,0},{9,1... | collective-permute-start | bytes 393224 | tf_op jit(solution)/shard_map/ppermute | solution.py:663
  120.2 12.6 %collective-permute-start.11 = (f32[2,128,128]{2,1,0:T(8,128)S(1)}, f32[2,128,128]{2,1,0:T(8,128)S(1)}, u32[]{:S(2)}, u32[]{:S(2)}) collective-permute-start(f32[2,128,128]{2,1,0:T(8,128)S(1)} %get-tuple-element.29.refs_3_), channel_id=1, source_target_pairs={{0,24},{1,25},{2,26},{3,27},{4,28},{5,29},{6,30},{7,31}} | collective-permute-start | bytes 393224 | tf_op jit(solution)/shard_map/ppermute | solution.py:679
  121.5 12.7 %collective-permute-start.12 = (f32[2,128,128]{2,1,0:T(8,128)S(1)}, f32[2,128,128]{2,1,0:T(8,128)S(1)}, u32[]{:S(2)}, u32[]{:S(2)}) collective-permute-start(f32[2,128,128]{2,1,0:T(8,128)S(1)} %get-tuple-element.29.refs_3_), channel_id=1, source_target_pairs={{8,24},{9,25},{10,26},{11,27},{12,28},{13,29},{14,30},{15,31}} | collective-permute-start | bytes 393224 | tf_op jit(solution)/shard_map/ppermute | solution.py:679
  122.8 11.4 %collective-permute-start.13 = (f32[2,128,128]{2,1,0:T(8,128)S(1)}, f32[2,128,128]{2,1,0:T(8,128)S(1)}, u32[]{:S(2)}, u32[]{:S(2)}) collective-permute-start(f32[2,128,128]{2,1,0:T(8,128)S(1)} %get-tuple-element.29.refs_3_), channel_id=1, source_target_pairs={{16,24},{17,25},{18,26},{19,27},{20,28},{21,29},{22,30},{23,31}} | collective-permute-start | bytes 393224 | tf_op jit(solution)/shard_map/ppermute | solution.py:679
  126.8 14.8 %collective-permute-start.17 = (f32[64,128]{1,0:T(8,128)S(1)}, f32[64,128]{1,0:T(8,128)S(1)}, u32[]{:S(2)}, u32[]{:S(2)}) collective-permute-start(f32[64,128]{1,0:T(8,128)S(1)} %get-tuple-element.32), channel_id=1, source_target_pairs={{0,7},{1,0},{2,1},{3,2},{4,3},{5,4},{6,5},{7,6},{8,15},{9,8},{10,9... | collective-permute-start | bytes 98312 | tf_op jit(solution)/shard_map/ppermute | solution.py:673
  132.7 8.8 %collective-permute-start.18 = (f32[64,128]{1,0:T(8,128)S(1)}, f32[64,128]{1,0:T(8,128)S(1)}, u32[]{:S(2)}, u32[]{:S(2)}) collective-permute-start(f32[64,128]{1,0:T(8,128)S(1)} %get-tuple-element.33), channel_id=1, source_target_pairs={{0,6},{1,7},{2,0},{3,1},{4,2},{5,3},{6,4},{7,5},{8,14},{9,15},{10,... | collective-permute-start | bytes 98312 | tf_op jit(solution)/shard_map/ppermute | solution.py:673
  132.8 8.8 %collective-permute-start.19 = (f32[64,128]{1,0:T(8,128)S(1)}, f32[64,128]{1,0:T(8,128)S(1)}, u32[]{:S(2)}, u32[]{:S(2)}) collective-permute-start(f32[64,128]{1,0:T(8,128)S(1)} %get-tuple-element.34), channel_id=1, source_target_pairs={{0,5},{1,6},{2,7},{3,0},{4,1},{5,2},{6,3},{7,4},{8,13},{9,14},{10,... | collective-permute-start | bytes 98312 | tf_op jit(solution)/shard_map/ppermute | solution.py:673

commit v2 on v1

--- a/solution.py
+++ b/solution.py
@@ -74,20 +74,20 @@
             pltpu.VMEM((rows, EDGE, levels), F32),
             pltpu.SemaphoreType.DMA((4,)),
         ],
-        compiler_params=pltpu.CompilerParams(vmem_limit_bytes=16 * MIB),
+        compiler_params=pltpu.CompilerParams(vmem_limit_bytes=56 * MIB),
         name="edges",
     )(state)
 
 
 def advance_kernel(comp_count, left_at, right_at, *refs):
-    (flags, source_column, state, up_rows, low_rows, left_in, right_in, own_sides) = refs[:8]
-    (up_left, up_right, low_left, low_right, mask, mix_atm, mix_ocn, flux_map) = refs[8:16]
-    out = refs[16]
-    packed = refs[17 : 17 + comp_count]
+    (flags, source_column, labels, state, up_rows, low_rows, left_in, right_in, own_sides) = refs[:9]
+    (up_left, up_right, low_left, low_right, mask, mix_atm, mix_ocn, flux_map) = refs[9:17]
+    out, surface = refs[17:19]
+    packed = refs[19 : 19 + comp_count]
     (values, moved, halo, halo_moved, smooth, pairs, mixed, weights, flux_weights, fluxes, staged) = refs[
-        17 + comp_count : 28 + comp_count
+        19 + comp_count : 30 + comp_count
     ]
-    in_sems, out_sems = refs[28 + comp_count :]
+    top, in_sems, out_sems = refs[30 + comp_count :]
     left_cols = left_in.at[left_at : left_at + 2]
     right_cols = right_in.at[right_at : right_at + 2]
     rows, cols, levels = state.shape
@@ -146,6 +146,14 @@
         smooth[row] = line
         pairs[row * cols : (row + 1) * cols, :] = side_by_side(line)
 
+    def note_top(q, lines):
+        lanes = lax.broadcasted_iota(jnp.int32, (cols, levels), 1)
+        kept = lines[0]
+        for row in range(1, CHUNK):
+            kept = jnp.where(lanes == row, pltpu.roll(lines[row], row, 1), kept)
+        turned = pltpu.roll(kept, q * CHUNK, 1)
+        top[...] = jnp.where(lanes // CHUNK == q, turned, top[...])
+
     def mix_rows(count):
         mixed[: count * cols, :] = dot_nn(pairs[: count * cols, :], weights[...])
 
@@ -232,6 +240,7 @@
                 both = line + moved[base + row + 1, EDGE : EDGE + cols, :]
                 pairs[row * cols : (row + 1) * cols, :] = side_by_side(both)
             put(q, slot).start()
+            note_top(q, [staged[slot, row] for row in range(CHUNK)])
             flux = dot_nt(flux_weights[...], pairs[...])
             flux = flux[:flux_count] + flux[flux_count:]
             for row in range(CHUNK):
@@ -251,7 +260,11 @@
             first = lax.rem(flags[3] + shift, comp_count) * share
             for f in range(share):
                 field = fluxes[pl.ds(first + f, rows, stride=flux_count), :].astype(BF16)
-                packed[shift][:, f * cols : (f + 1) * cols] = dot_nn(placing, field).astype(BF16)
+                packed[shift][: placing.shape[0], f * cols : (f + 1) * cols] = dot_nn(
+                    placing, field
+                ).astype(BF16)
+            packed[shift][placing.shape[0] :, :] = labels[...]
+        surface[...] = top[...].T
 
     @pl.when(ocean)
     def sea_side():
@@ -282,28 +295,38 @@
                 before = values[base + row + 2, EDGE : EDGE + cols, :]
                 staged[slot, row] = jnp.where(chosen, finish(row), before)
             put(q, slot).start()
+            note_top(q, [staged[slot, row] for row in range(CHUNK)])
             return 0
 
         lax.fori_loop(0, chunks, one_chunk, 0)
         put(chunks - 2, (chunks - 2) % 2).wait()
         put(chunks - 1, (chunks - 1) % 2).wait()
+        surface[...] = top[...].T
+        for shift in range(comp_count):
+            packed[shift][...] = jnp.zeros(packed[shift].shape, BF16)
 
 
 def advance(
-    flags, source_column, state, halos, mask, mix_atm, mix_ocn, flux_map_t, comp_count, left_at, right_at
+    flags, source_column, labels, state, halos, mask, mix_atm, mix_ocn, flux_map_t, comp_count, left_at, right_at
 ):
     rows, cols, levels = state.shape
     fluxes = flux_map_t.shape[0]
     vmem = pl.BlockSpec(memory_space=pltpu.VMEM)
     smem = pl.BlockSpec(memory_space=pltpu.SMEM)
     hbm = pl.BlockSpec(memory_space=pl.ANY)
-    entry = jax.ShapeDtypeStruct((source_column.shape[0], fluxes // comp_count * cols), BF16)
+    entry = jax.ShapeDtypeStruct(
+        (source_column.shape[0] + labels.shape[0], fluxes // comp_count * cols), BF16
+    )
     cells = rows * cols
     return pl.pallas_call(
         functools.partial(advance_kernel, comp_count, left_at, right_at),
-        out_shape=(jax.ShapeDtypeStruct(state.shape, F32),) + (entry,) * comp_count,
-        in_specs=[smem, vmem, hbm] + [vmem] * (len(halos) + 4),
-        out_specs=(hbm,) + (vmem,) * comp_count,
+        out_shape=(
+            jax.ShapeDtypeStruct(state.shape, F32),
+            jax.ShapeDtypeStruct((rows, cols), F32),
+        )
+        + (entry,) * comp_count,
+        in_specs=[smem, vmem, vmem, hbm] + [vmem] * (len(halos) + 4),
+        out_specs=(hbm,) + (vmem,) * (1 + comp_count),
         scratch_shapes=[
             pltpu.VMEM((rows + 4, cols + 2 * EDGE, levels), F32),
             pltpu.VMEM((rows + 2, cols + 2 * EDGE, levels), F32),
@@ -316,6 +339,7 @@
             pltpu.VMEM((2 * fluxes, 2 * levels), BF16),
             pltpu.VMEM((rows * fluxes, cols), F32),
             pltpu.VMEM((2, CHUNK, cols, levels), F32),
+            pltpu.VMEM((cols, levels), F32),
             pltpu.SemaphoreType.DMA((rows // CHUNK,)),
             pltpu.SemaphoreType.DMA((2,)),
         ],
@@ -324,26 +348,73 @@
             flops=8 * cells * levels * levels, bytes_accessed=8 * cells * levels, transcendentals=0
         ),
         name="advance",
-    )(flags, source_column, state, *halos, mask, mix_atm, mix_ocn, flux_map_t)
+    )(flags, source_column, labels, state, *halos, mask, mix_atm, mix_ocn, flux_map_t)
 
 
 BATCH = 8
-
-
-def regrid_body(count, flags, ocean_first, *refs):
+LABEL_ROWS = 16
+
+
+def regroup_kernel(count, *refs):
+    slabs, blocks = refs[:-count], refs[-count:]
+    comp_count = len(slabs)
+    capacity = blocks[0].shape[0] // comp_count - LABEL_ROWS // comp_count
+    size = count * capacity
+    heads = [slab[size : size + LABEL_ROWS, :].astype(F32) for slab in slabs]
+    lines = [head[i : i + 1] for i in range(2) for head in heads]
+    spare = jnp.zeros((LABEL_ROWS - len(lines), heads[0].shape[1]), F32)
+    labels = jnp.concatenate(lines + [spare], axis=0).astype(BF16)
+    for n in range(count):
+        for s in range(comp_count):
+            blocks[n][s * capacity : (s + 1) * capacity, :] = slabs[s][
+                n * capacity : (n + 1) * capacity, :
+            ]
+        blocks[n][comp_count * capacity :, :] = labels
+
+
+def regroup(slabs, count):
+    rows, width = slabs[0].shape
+    size = (rows - LABEL_ROWS) // count * len(slabs) + LABEL_ROWS
+    vmem = pl.BlockSpec(memory_space=pltpu.VMEM)
+    return pl.pallas_call(
+        functools.partial(regroup_kernel, count),
+        out_shape=(jax.ShapeDtypeStruct((size, width), BF16),) * count,
+        in_specs=[vmem] * len(slabs),
+        out_specs=(vmem,) * count,
+        compiler_params=pltpu.CompilerParams(vmem_limit_bytes=16 * MIB),
+        name="regroup",
+    )(*slabs)
+
+
+def regrid_body(count, comp_count, flags, ocean_first, *refs):
     blocks = refs[:count]
-    target_line, weight_line, weights, surface, mask, forcing, shared, entries, chosen, binned = refs[count:]
+    weights, surface, mask, forcing, shared, hits, entries, chosen, binned = refs[count:]
     rows, cols = mask.shape
     share = forcing.shape[0]
     weight_count = weights.shape[0]
-    size = blocks[0].shape[0]
-    total = count * size
+    capacity = (blocks[0].shape[0] - LABEL_ROWS) // comp_count
+    size = count * capacity
+    total = comp_count * size
+    width = blocks[0].shape[1]
+    for s in range(comp_count):
+        for n in range(count):
+            start = s * size + n * capacity
+            entries[start : start + capacity, :] = blocks[n][s * capacity : (s + 1) * capacity, :]
+    lanes = lax.broadcasted_iota(jnp.int32, (LABEL_ROWS, width), 1) // capacity
+    labels = jnp.zeros((LABEL_ROWS, width), F32)
     for n in range(count):
-        entries[n * size : (n + 1) * size, :] = blocks[n][...]
+        labels = jnp.where(lanes == n, blocks[n][comp_count * capacity :, :].astype(F32), labels)
+    labels = labels.astype(jnp.int32)
+    weight_line = jnp.concatenate([labels[s : s + 1, :size] for s in range(comp_count)], axis=1)
+    target_line = jnp.concatenate(
+        [labels[comp_count + s : comp_count + s + 1, :size] for s in range(comp_count)], axis=1
+    )
     spots = lax.broadcasted_iota(jnp.int32, (rows, total), 0)
-    by_target = jnp.where(target_line[...] == spots, 1.0, 0.0).astype(BF16)
+    by_target = jnp.where(target_line == spots, 1.0, 0.0)
+    hits[...] = by_target[:, :size].T.astype(BF16)
+    by_target = by_target.astype(BF16)
     numbers = lax.broadcasted_iota(jnp.int32, (weight_count, total), 0)
-    by_weight = jnp.where(weight_line[...] == numbers, 1.0, 0.0).astype(BF16)
+    by_weight = jnp.where(weight_line == numbers, 1.0, 0.0).astype(BF16)
     for g in range(weight_count // BATCH):
         for i in range(BATCH):
             w = g * BATCH + i
@@ -368,41 +439,44 @@
     shared[1] = mask[...]
 
 
-def regrid(flags, ocean_first, blocks, target_line, weight_line, weights, surface, mask):
+def regrid(flags, ocean_first, blocks, comp_count, weights, surface, mask):
     rows, cols = mask.shape
     count = len(blocks)
-    size, width = blocks[0].shape
+    height, width = blocks[0].shape
+    size = (height - LABEL_ROWS) // comp_count * count
+    total = size * comp_count
     share = width // cols
     weight_count = weights.shape[0]
     vmem = pl.BlockSpec(memory_space=pltpu.VMEM)
     smem = pl.BlockSpec(memory_space=pltpu.SMEM)
     return pl.pallas_call(
-        functools.partial(regrid_body, count),
+        functools.partial(regrid_body, count, comp_count),
         out_shape=(
             jax.ShapeDtypeStruct((share, rows, cols), F32),
             jax.ShapeDtypeStruct((2, rows, cols), F32),
+            jax.ShapeDtypeStruct((size, rows), BF16),
         ),
-        in_specs=[smem, smem] + [vmem] * (count + 5),
-        out_specs=(vmem, vmem),
+        in_specs=[smem, smem] + [vmem] * (count + 3),
+        out_specs=(vmem, vmem, vmem),
         scratch_shapes=[
-            pltpu.VMEM((count * size, width), BF16),
-            pltpu.VMEM((BATCH * rows, count * size), BF16),
+            pltpu.VMEM((total, width), BF16),
+            pltpu.VMEM((BATCH * rows, total), BF16),
             pltpu.VMEM((BATCH * rows, width), F32),
         ],
         compiler_params=pltpu.CompilerParams(vmem_limit_bytes=32 * MIB),
         cost_estimate=pl.CostEstimate(
-            flops=2 * weight_count * rows * width * (count * size + 2 * cols),
+            flops=2 * weight_count * rows * width * (total + 2 * cols),
             bytes_accessed=2 * MIB,
             transcendentals=0,
         ),
         name="regrid",
-    )(flags, ocean_first, *blocks, target_line, weight_line, weights, surface, mask)
+    )(flags, ocean_first, *blocks, weights, surface, mask)
 
 
 def pick_kernel(comp_count, *refs):
     flags = refs[0]
     parts = refs[1 : 1 + comp_count]
-    target_column, surface = refs[1 + comp_count : 3 + comp_count]
+    hits, surface = refs[1 + comp_count : 3 + comp_count]
     picked = refs[3 + comp_count :]
     rows, cols = surface.shape
     from_ocean = lax.rem(flags[3] + 1, comp_count)
@@ -418,16 +492,14 @@
     surface[...] = now
     pair = jnp.concatenate(split_two(now), axis=0)
     size = picked[0].shape[0]
-    spots = lax.broadcasted_iota(jnp.int32, (size, rows), 1)
     for n in range(len(picked)):
-        hits = target_column[n * size : (n + 1) * size, :] == spots
-        hits = jnp.where(hits, 1.0, 0.0).astype(BF16)
-        picked[n][...] = dot_nn(jnp.concatenate([hits, hits], axis=1), pair)
-
-
-def pick(flags, parts, target_column, neighbours):
+        some = hits[n * size : (n + 1) * size, :]
+        picked[n][...] = dot_nn(jnp.concatenate([some, some], axis=1), pair)
+
+
+def pick(flags, parts, hits, neighbours):
     _, rows, cols = parts[0].shape
-    size = target_column.shape[0] // neighbours
+    size = hits.shape[0] // neighbours
     vmem = pl.BlockSpec(memory_space=pltpu.VMEM)
     smem = pl.BlockSpec(memory_space=pltpu.SMEM)
     return pl.pallas_call(
@@ -438,7 +510,7 @@
         out_specs=(vmem,) * (1 + neighbours),
         compiler_params=pltpu.CompilerParams(vmem_limit_bytes=16 * MIB),
         name="pick",
-    )(flags, *parts, target_column)
+    )(flags, *parts, hits)
 
 
 LINES = 16
@@ -678,46 +750,24 @@
         ]
         return lax.ppermute(value, AXES, pairs)
 
-    every = lax.all_gather(packed_labels, AXES).reshape(
-        comp_count, tile_count, neighbours, capacity
-    )
-    ordered = (comp_index - jnp.arange(comp_count, dtype=jnp.int32) + comp_count) % comp_count
-    from_tiles = [
-        lax.dynamic_index_in_dim(
-            every[:, :, n], (tile_index - offsets[n] + tile_count) % tile_count, 1, False
-        )
-        for n in range(neighbours)
-    ]
-    by_comp = jnp.stack(from_tiles)
-    mine = by_comp[:, :, None, :]
-    wanted = ordered[None, :, None, None] == jnp.arange(comp_count, dtype=jnp.int32)[None, None, :, None]
-    arrived_labels = jnp.sum(jnp.where(wanted, mine.transpose(0, 2, 1, 3), 0), axis=2).reshape(1, -1)
-    own_labels = jnp.sum(
-        jnp.where((jnp.arange(comp_count, dtype=jnp.int32) == comp_index)[None, :, None], by_comp, 0),
-        axis=1,
-    )
-    target_column = (own_labels % rows).reshape(-1, 1)
+    label_lines = jnp.stack([packed_labels // rows, packed_labels % rows]).astype(BF16)
+    label_lines = jnp.pad(label_lines, ((0, LABEL_ROWS - 2), (0, 0)))
 
     halos = (up_rows, low_rows, left_cols, right_cols, sides)
     halos = halos + (up_left, up_right, low_left, low_right)
     moved = advance(
-        flags, sources[:, None], state, halos, mask, mix_atm, mix_ocn, flux_map.T, comp_count,
-        left_at, right_at,
-    )
-    moved, packed = moved[0], moved[1:]
-    own = jnp.where(is_ocean, jnp.zeros((), BF16), packed[0])
-    slabs = [own] + [over_comp(packed[s], s, False) for s in range(1, comp_count)]
-    blocks = []
-    for n in range(neighbours):
-        block = jnp.concatenate([slab[n * capacity : (n + 1) * capacity] for slab in slabs])
-        blocks.append(over_tiles(block, offsets[n]))
-    surface = moved[:, :, 0]
-    forcing, shared = regrid(
-        flags, ocean_map[:, 0], blocks, arrived_labels % rows, arrived_labels // rows,
-        regrid_weights, surface, mask,
+        flags, sources[:, None], label_lines, state, halos, mask, mix_atm, mix_ocn, flux_map.T,
+        comp_count, left_at, right_at,
+    )
+    moved, surface, packed = moved[0], moved[1], moved[2:]
+    slabs = [packed[0]] + [over_comp(packed[s], s, False) for s in range(1, comp_count)]
+    blocks = regroup(slabs, neighbours)
+    blocks = [over_tiles(blocks[n], offsets[n]) for n in range(neighbours)]
+    forcing, shared, hits = regrid(
+        flags, ocean_map[:, 0], blocks, comp_count, regrid_weights, surface, mask
     )
     parts = [shared] + [over_comp(shared, s, True) for s in range(1, comp_count)]
-    picks = pick(flags, parts, target_column, neighbours)
+    picks = pick(flags, parts, hits, neighbours)
     new_surface, picked = picks[0], picks[1:]
     arrived = [over_tiles(picked[n], -offsets[n]) for n in range(neighbours)]
     fields = [to_ocean(forcing, c) for c in range(comp_count - 1)] + [forcing]

time: 143 us -> 102 us (0.71)
  the two profiles are of different devices: /device:TPU:7 before, /device:TPU:15 now
where the time goes in v2:
time: 102 us
  starting transfers between devices  37.8 us (37%)
  Pallas kernels  33.8 us (33%)
  waiting for transfers between devices  27.2 us (27%)
  local copies, waits for them, and re-layouts  1.51 us (1%)
  between operations  1.02 us (1%)
    ppermute x6, waiting for transfers between devices, over_comp(): return lax.ppermute(value, AXES, pairs)  19.1 us
    ppermute x6, starting transfers between devices, over_tiles(): return lax.ppermute(value, AXES, pairs)  16 us
    pallas_call x1, Pallas kernels, advance(): pl.pallas_call(functools.partial(advance_kernel, comp_count, left_at, rig...  15.8 us
    ppermute x5, starting transfers between devices, band_shift(): return lax.ppermute(value, AXES, pairs)  11.6 us
    pallas_call x1, Pallas kernels, update(): pl.pallas_call(functools.partial(update_kernel, len(parts)), out_shape=ja...  7.14 us
    pallas_call x1, Pallas kernels, regrid(): pl.pallas_call(functools.partial(regrid_body, count, comp_count), out_sha...  6.66 us
    ppermute x6, starting transfers between devices, over_comp(): return lax.ppermute(value, AXES, pairs)  6.28 us
    ppermute x6, waiting for transfers between devices, over_tiles(): return lax.ppermute(value, AXES, pairs)  6.02 us
  transfers between devices with their start and end apart: 20, of which 9 were waited for; matrix products, arithmetic and copies ran while one was open for 1% of the time, Pallas kernels for 8%

profile of v2, /device:TPU:15, one launch (start us, length us, event | category | flops | bytes accessed | tf_op | source)
XLA Modules:
  0.0 102.1 jit_solution(760022671250373141)
XLA Ops:
  0.7 2.3 %edges.1 = (f32[2,128,128]{2,1,0:T(8,128)}, f32[2,128,128]{2,1,0:T(8,128)}, f32[4,128,128]{2,1,0:T(8,128)}, f32[8,128]{1,0:T(8,128)}, f32[8,128]{1,0:T(8,128)}) custom-call(f32[128,128,128]{2,1,0:T(8,128)} %refs_3_.1), custom_call_target="tpu_custom_call" | custom-call | tf_op jit(solution)/shard_map/edges/pallas_call | solution.py:67
  3.0 0.7 collective-permute-start.2
  3.7 3.2 %collective-permute-start = (f32[2,128,128]{2,1,0:T(8,128)}, f32[2,128,128]{2,1,0:T(8,128)S(1)}, u32[]{:S(2)}, u32[]{:S(2)}) collective-permute-start(f32[2,128,128]{2,1,0:T(8,128)} %get-tuple-element.25), channel_id=1, source_target_pairs={{0,2},{1,3},{2,4},{3,5},{4,6},{5,7},{6,8},{7,9},{8,10},{9,11},{10,... | collective-permute-start | bytes 393224 | tf_op jit(solution)/shard_map/ppermute | solution.py:688
  6.9 2.1 %collective-permute-start.1 = (f32[2,128,128]{2,1,0:T(8,128)}, f32[2,128,128]{2,1,0:T(8,128)S(1)}, u32[]{:S(2)}, u32[]{:S(2)}) collective-permute-start(f32[2,128,128]{2,1,0:T(8,128)} %get-tuple-element.26), channel_id=1, source_target_pairs={{2,0},{3,1},{4,2},{5,3},{6,4},{7,5},{8,6},{9,7},{10,8},{11,9},{12,... | collective-permute-start | bytes 393224 | tf_op jit(solution)/shard_map/ppermute | solution.py:688
  9.0 3.7 %collective-permute-start.3 = (f32[8,128]{1,0:T(8,128)}, f32[8,128]{1,0:T(8,128)S(1)}, u32[]{:S(2)}, u32[]{:S(2)}) collective-permute-start(f32[8,128]{1,0:T(8,128)} %get-tuple-element.28), channel_id=1, source_target_pairs={{0,3},{1,2},{2,5},{3,4},{4,7},{5,6},{6,9},{7,8},{8,11},{9,10},{10,... | collective-permute-start | bytes 12296 | tf_op jit(solution)/shard_map/ppermute | solution.py:688
  12.7 1.9 %collective-permute-start.4 = (f32[8,128]{1,0:T(8,128)}, f32[8,128]{1,0:T(8,128)S(1)}, u32[]{:S(2)}, u32[]{:S(2)}) collective-permute-start(f32[8,128]{1,0:T(8,128)} %get-tuple-element.29), channel_id=1, source_target_pairs={{2,1},{3,0},{4,3},{5,2},{6,5},{7,4},{8,7},{9,6},{10,9},{11,8},{12,... | collective-permute-start | bytes 12296 | tf_op jit(solution)/shard_map/ppermute | solution.py:688
  14.6 0.2 copy.19
  14.8 0.3 fusion.4
  15.1 0.2 convert_reduce_fusion
  15.3 0.2 select_reduce_fusion
  15.5 0.1 pad_add_fusion.refs_0_.flags
  15.6 0.1 copy.20.refs_1_
  15.8 2.1 %collective-permute-done.4.refs_11_.refs_12_ = f32[8,128]{1,0:T(8,128)S(1)} collective-permute-done((f32[8,128]{1,0:T(8,128)}, f32[8,128]{1,0:T(8,128)S(1)}, u32[]{:S(2)}, u32[]{:S(2)}) %collective-permute-start.4) | collective-permute-done | bytes 4128 | tf_op jit(solution)/shard_map/ppermute | solution.py:688
  17.8 0.0 collective-permute-done.1.refs_5_
  17.8 0.0 collective-permute-done.2.refs_6_.refs_7_
  17.9 0.0 copy-start.1
  17.9 0.9 copy-done.1
  18.8 15.8 %advance.1 = (f32[128,128,128]{2,1,0:T(8,128)}, f32[128,128]{1,0:T(8,128)S(1)}, bf16[272,256]{1,0:T(8,128)(2,1)S(1)}, bf16[272,256]{1,0:T(8,128)(2,1)S(1)}, bf16...) custom-call(s32[4]{0:T(128)S(1)} %pad_add_fusion.refs_0_.flags, s32[256,1]{1,0:T(8,128)S(1)} %copy.20.refs_1_, ...), custom_call_target="tpu_custom_call" | custom-call | flops 2147483648 | bytes 16777216 | tf_op jit(solution)/shard_map/advance/pallas_call | solution.py:321
  34.6 1.3 %collective-permute-start.5 = (bf16[272,256]{1,0:T(8,128)(2,1)S(1)}, bf16[272,256]{1,0:T(8,128)(2,1)S(1)}, u32[]{:S(2)}, u32[]{:S(2)}) collective-permute-start(bf16[272,256]{1,0:T(8,128)(2,1)S(1)} %get-tuple-element.32), channel_id=1, source_target_pairs={{0,8},{1,9},{2,10},{3,11},{4,12},{5,13},{6,14},{7,15},{8,16},{9,17... | collective-permute-start | bytes 417800 | tf_op jit(solution)/shard_map/ppermute | solution.py:735
  35.9 1.3 %collective-permute-start.6 = (bf16[272,256]{1,0:T(8,128)(2,1)S(1)}, bf16[272,256]{1,0:T(8,128)(2,1)S(1)}, u32[]{:S(2)}, u32[]{:S(2)}) collective-permute-start(bf16[272,256]{1,0:T(8,128)(2,1)S(1)} %get-tuple-element.33), channel_id=1, source_target_pairs={{0,16},{1,17},{2,18},{3,19},{4,20},{5,21},{6,22},{7,23},{8,24},{9,... | collective-permute-start | bytes 417800 | tf_op jit(solution)/shard_map/ppermute | solution.py:735
  37.2 1.3 %collective-permute-start.7 = (bf16[272,256]{1,0:T(8,128)(2,1)S(1)}, bf16[272,256]{1,0:T(8,128)(2,1)S(1)}, u32[]{:S(2)}, u32[]{:S(2)}) collective-permute-start(bf16[272,256]{1,0:T(8,128)(2,1)S(1)} %get-tuple-element.34), channel_id=1, source_target_pairs={{0,24},{1,25},{2,26},{3,27},{4,28},{5,29},{6,30},{7,31},{8,0},{9,1... | collective-permute-start | bytes 417800 | tf_op jit(solution)/shard_map/ppermute | solution.py:735
  38.5 8.2 %collective-permute-done.5.refs_1_ = bf16[272,256]{1,0:T(8,128)(2,1)S(1)} collective-permute-done((bf16[272,256]{1,0:T(8,128)(2,1)S(1)}, bf16[272,256]{1,0:T(8,128)(2,1)S(1)}, u32[]{:S(2)}, u32[]{:S(2)}) %collective-permute-start.5) | collective-permute-done | bytes 139296 | tf_op jit(solution)/shard_map/ppermute | solution.py:735
  46.7 2.2 %collective-permute-done.6.refs_2_ = bf16[272,256]{1,0:T(8,128)(2,1)S(1)} collective-permute-done((bf16[272,256]{1,0:T(8,128)(2,1)S(1)}, bf16[272,256]{1,0:T(8,128)(2,1)S(1)}, u32[]{:S(2)}, u32[]{:S(2)}) %collective-permute-start.6) | collective-permute-done | bytes 139296 | tf_op jit(solution)/shard_map/ppermute | solution.py:735
  48.9 2.6 %collective-permute-done.7.refs_3_ = bf16[272,256]{1,0:T(8,128)(2,1)S(1)} collective-permute-done((bf16[272,256]{1,0:T(8,128)(2,1)S(1)}, bf16[272,256]{1,0:T(8,128)(2,1)S(1)}, u32[]{:S(2)}, u32[]{:S(2)}) %collective-permute-start.7) | collective-permute-done | bytes 139296 | tf_op jit(solution)/shard_map/ppermute | solution.py:735
  51.5 9.6 %collective-permute-start.10 = (bf16[272,256]{1,0:T(8,128)(2,1)S(1)}, bf16[272,256]{1,0:T(8,128)(2,1)S(1)}, u32[]{:S(2)}, u32[]{:S(2)}) collective-permute-start(bf16[272,256]{1,0:T(8,128)(2,1)S(1)} %get-tuple-element.38), channel_id=1, source_target_pairs={{0,3},{1,4},{2,5},{3,6},{4,7},{5,0},{6,1},{7,2},{8,11},{9,12},{10,... | collective-permute-start | bytes 417800 | tf_op jit(solution)/shard_map/ppermute | solution.py:745
  61.1 0.0 collective-permute-start.8
  61.1 0.3 collective-permute-start.9
  61.4 0.1 slice_reduce_fusion.ocean_first
  61.6 2.4 %collective-permute-done.10.refs_3_ = bf16[272,256]{1,0:T(8,128)(2,1)S(1)} collective-permute-done((bf16[272,256]{1,0:T(8,128)(2,1)S(1)}, bf16[272,256]{1,0:T(8,128)(2,1)S(1)}, u32[]{:S(2)}, u32[]{:S(2)}) %collective-permute-start.10) | collective-permute-done | bytes 139296 | tf_op jit(solution)/shard_map/ppermute | solution.py:745
  63.9 2.1 %collective-permute-done.8.refs_1_ = bf16[272,256]{1,0:T(8,128)(2,1)S(1)} collective-permute-done((bf16[272,256]{1,0:T(8,128)(2,1)S(1)}, bf16[272,256]{1,0:T(8,128)(2,1)S(1)}, u32[]{:S(2)}, u32[]{:S(2)}) %collective-permute-start.8) | collective-permute-done | bytes 139296 | tf_op jit(solution)/shard_map/ppermute | solution.py:745
  66.1 1.5 %collective-permute-done.9.refs_2_ = bf16[272,256]{1,0:T(8,128)(2,1)S(1)} collective-permute-done((bf16[272,256]{1,0:T(8,128)(2,1)S(1)}, bf16[272,256]{1,0:T(8,128)(2,1)S(1)}, u32[]{:S(2)}, u32[]{:S(2)}) %collective-permute-start.9) | collective-permute-done | bytes 139296 | tf_op jit(solution)/shard_map/ppermute | solution.py:745
  67.6 6.7 %regrid.1 = (f32[2,128,128]{2,1,0:T(8,128)S(1)}, f32[2,128,128]{2,1,0:T(8,128)S(1)}, bf16[256,128]{1,0:T(8,128)(2,1)S(1)}) custom-call(s32[4]{0:T(128)S(1)} %pad_add_fusion.refs_0_.flags, f32[8]{0:T(128)S(1)} %slice_reduce_fusion.ocean_first, bf16[272,256]{1,0:T(8,128)(2,1)S(1)} %get-tuple-element.35.refs_0_, ...), custom_call_target="tpu_custom_call" | custom-call | flops 2684354560 | bytes 2097152 | tf_op jit(solution)/shard_map/regrid/pallas_call | solution.py:452
  74.2 1.5 %collective-permute-start.14 = (f32[2,128,128]{2,1,0:T(8,128)S(1)}, f32[2,128,128]{2,1,0:T(8,128)S(1)}, u32[]{:S(2)}, u32[]{:S(2)}) collective-permute-start(f32[2,128,128]{2,1,0:T(8,128)S(1)} %get-tuple-element.41.refs_1_), channel_id=1, source_target_pairs={{0,8},{1,9},{2,10},{3,11},{4,12},{5,13},{6,14},{7,15},{8,16},{9,17... | collective-permute-start | bytes 393224 | tf_op jit(solution)/shard_map/ppermute | solution.py:735
  75.7 0.1 copy.21
  75.9 0.1 collective-permute-start.15
  76.0 0.8 collective-permute-start.16
  76.8 1.3 %collective-permute-start.11 = (f32[2,128,128]{2,1,0:T(8,128)S(1)}, f32[2,128,128]{2,1,0:T(8,128)S(1)}, u32[]{:S(2)}, u32[]{:S(2)}) collective-permute-start(f32[2,128,128]{2,1,0:T(8,128)S(1)} %get-tuple-element.40.refs_3_), channel_id=1, source_target_pairs={{0,24},{1,25},{2,26},{3,27},{4,28},{5,29},{6,30},{7,31}} | collective-permute-start | bytes 393224 | tf_op jit(solution)/shard_map/ppermute | solution.py:751
  78.1 1.3 %collective-permute-start.12 = (f32[2,128,128]{2,1,0:T(8,128)S(1)}, f32[2,128,128]{2,1,0:T(8,128)S(1)}, u32[]{:S(2)}, u32[]{:S(2)}) collective-permute-start(f32[2,128,128]{2,1,0:T(8,128)S(1)} %get-tuple-element.40.refs_3_), channel_id=1, source_target_pairs={{8,24},{9,25},{10,26},{11,27},{12,28},{13,29},{14,30},{15,31}} | collective-permute-start | bytes 393224 | tf_op jit(solution)/shard_map/ppermute | solution.py:751
  79.4 0.4 collective-permute-done.14.refs_2_
  79.7 1.3 %collective-permute-start.13 = (f32[2,128,128]{2,1,0:T(8,128)S(1)}, f32[2,128,128]{2,1,0:T(8,128)S(1)}, u32[]{:S(2)}, u32[]{:S(2)}) collective-permute-start(f32[2,128,128]{2,1,0:T(8,128)S(1)} %get-tuple-element.40.refs_3_), channel_id=1, source_target_pairs={{16,24},{17,25},{18,26},{19,27},{20,28},{21,29},{22,30},{23,31}} | collective-permute-start | bytes 393224 | tf_op jit(solution)/shard_map/ppermute | solution.py:751
  81.0 0.1 add_select_fusion.refs_4_
  81.1 5.7 %collective-permute-done.15.refs_3_ = f32[2,128,128]{2,1,0:T(8,128)S(1)} collective-permute-done((f32[2,128,128]{2,1,0:T(8,128)S(1)}, f32[2,128,128]{2,1,0:T(8,128)S(1)}, u32[]{:S(2)}, u32[]{:S(2)}) %collective-permute-start.15) | collective-permute-done | bytes 131104 | tf_op jit(solution)/shard_map/ppermute | solution.py:735
  86.8 0.8 pick.1
  87.6 1.0 collective-permute-start.17
  88.6 2.3 %collective-permute-start.18 = (f32[64,128]{1,0:T(8,128)S(1)}, f32[64,128]{1,0:T(8,128)S(1)}, u32[]{:S(2)}, u32[]{:S(2)}) collective-permute-start(f32[64,128]{1,0:T(8,128)S(1)} %get-tuple-element.45), channel_id=1, source_target_pairs={{0,6},{1,7},{2,0},{3,1},{4,2},{5,3},{6,4},{7,5},{8,14},{9,15},{10,... | collective-permute-start | bytes 98312 | tf_op jit(solution)/shard_map/ppermute | solution.py:745
  90.9 2.9 %collective-permute-start.19 = (f32[64,128]{1,0:T(8,128)S(1)}, f32[64,128]{1,0:T(8,128)S(1)}, u32[]{:S(2)}, u32[]{:S(2)}) collective-permute-start(f32[64,128]{1,0:T(8,128)S(1)} %get-tuple-element.46), channel_id=1, source_target_pairs={{0,5},{1,6},{2,7},{3,0},{4,1},{5,2},{6,3},{7,4},{8,13},{9,14},{10,... | collective-permute-start | bytes 98312 | tf_op jit(solution)/shard_map/ppermute | solution.py:745
  93.7 7.1 %update.1 = f32[128,128,128]{2,1,0:T(8,128)} custom-call(s32[4]{0:T(128)S(1)} %pad_add_fusion.refs_0_.flags, f32[128,128,128]{2,1,0:T(8,128)} %get-tuple-element.30.state, f32[2,128,128]{2,1,0:T(8,128)S(1)} %collective-permute-done.11.refs_0_, f32[2,128,128]{2,1,0:T(8,128)S(1)} %collective-permute-done.12.refs_1_, ...), custom_call_target="tpu_custom_call", output_to_operand_aliasing={{}: (1, {})} | custom-call | flops 1610612736 | bytes 16777216 | tf_op jit(solution)/shard_map/update/pallas_call | solution.py:581
  100.9 1.2 %returned.1 = f32[128,128]{1,0:T(8,128)} custom-call(s32[4]{0:T(128)S(1)} %pad_add_fusion.refs_0_.flags, f32[64,128]{1,0:T(8,128)S(1)} %get-tuple-element.43.refs_0_, f32[64,128]{1,0:T(8,128)S(1)} %collective-permute-done.17.refs_1_, f32[64,128]{1,0:T(8,128)S(1)} %collective-permute-done.18.refs_2_, f32[64,128]{1,0:T(8,128)S(1)} %collective-permute-done.19.refs_3_, ...), custom_call_target="tpu_custom_call" | custom-call | tf_op jit(solution)/shard_map/returned/pallas_call | solution.py:642
  (30 shorter events, 0.2 us)
Async XLA Ops:
  0.6 14.0 %copy-start.7 = (s32[128,1,2,3]{0,2,3,1:T(2,128)S(1)}, s32[128,1,2,3]{0,2,3,1:T(2,128)}, u32[]{:S(2)}) copy-start(s32[128,1,2,3]{0,2,3,1:T(2,128)} %param.11) | copy-start | bytes 9220
  0.6 14.8 %copy-start.6 = (s32[128,128]{1,0:T(8,128)S(1)}, s32[128,128]{1,0:T(8,128)}, u32[]{:S(2)}) copy-start(s32[128,128]{1,0:T(8,128)} %param.10) | copy-start | bytes 196612
  0.7 17.2 %copy-start.5 = (f32[128,8]{0,1:T(8,128)S(1)}, f32[128,8]{0,1:T(8,128)}, u32[]{:S(2)}) copy-start(f32[128,8]{0,1:T(8,128)} %param.14) | copy-start | bytes 12292
  0.7 17.2 %copy-start.2 = (f32[128,128]{1,0:T(8,128)S(1)}, f32[128,128]{1,0:T(8,128)}, u32[]{:S(2)}) copy-start(f32[128,128]{1,0:T(8,128)} %refs_14_.1) | copy-start | bytes 196612
  0.7 17.2 %copy-start.3 = (f32[128,128]{1,0:T(8,128)S(1)}, f32[128,128]{1,0:T(8,128)}, u32[]{:S(2)}) copy-start(f32[128,128]{1,0:T(8,128)} %refs_15_.1) | copy-start | bytes 196612
  0.7 60.8 %copy-start.4 = (f32[8,128]{1,0:T(8,128)S(1)}, f32[8,128]{1,0:T(8,128)}, u32[]{:S(2)}) copy-start(f32[8,128]{1,0:T(8,128)} %refs_5_.1) | copy-start | bytes 12292
  0.7 66.9 %copy-start = (bf16[32,128,128]{2,1,0:T(8,128)(2,1)S(1)}, bf16[32,128,128]{2,1,0:T(8,128)(2,1)}, u32[]{:S(2)}) copy-start(bf16[32,128,128]{2,1,0:T(8,128)(2,1)} %refs_6_.1) | copy-start | bytes 3145732
  3.0 14.9 %collective-permute-start.2 = (f32[4,128,128]{2,1,0:T(8,128)}, f32[4,128,128]{2,1,0:T(8,128)S(1)}, u32[]{:S(2)}, u32[]{:S(2)}) collective-permute-start(f32[4,128,128]{2,1,0:T(8,128)} %get-tuple-element.27.refs_8_), channel_id=1, source_target_pairs={{0,1},{1,0},{2,3},{3,2},{4,5},{5,4},{6,7},{7,6},{8,9},{9,8},{10,11... | collective-permute-start | bytes 786440 | tf_op jit(solution)/shard_map/ppermute | solution.py:688
  3.7 14.1 %collective-permute-start = (f32[2,128,128]{2,1,0:T(8,128)}, f32[2,128,128]{2,1,0:T(8,128)S(1)}, u32[]{:S(2)}, u32[]{:S(2)}) collective-permute-start(f32[2,128,128]{2,1,0:T(8,128)} %get-tuple-element.25), channel_id=1, source_target_pairs={{0,2},{1,3},{2,4},{3,5},{4,6},{5,7},{6,8},{7,9},{8,10},{9,11},{10,... | collective-permute-start | bytes 393224 | tf_op jit(solution)/shard_map/ppermute | solution.py:688
  6.9 10.9 %collective-permute-start.1 = (f32[2,128,128]{2,1,0:T(8,128)}, f32[2,128,128]{2,1,0:T(8,128)S(1)}, u32[]{:S(2)}, u32[]{:S(2)}) collective-permute-start(f32[2,128,128]{2,1,0:T(8,128)} %get-tuple-element.26), channel_id=1, source_target_pairs={{2,0},{3,1},{4,2},{5,3},{6,4},{7,5},{8,6},{9,7},{10,8},{11,9},{12,... | collective-permute-start | bytes 393224 | tf_op jit(solution)/shard_map/ppermute | solution.py:688
  9.0 6.7 %collective-permute-start.3 = (f32[8,128]{1,0:T(8,128)}, f32[8,128]{1,0:T(8,128)S(1)}, u32[]{:S(2)}, u32[]{:S(2)}) collective-permute-start(f32[8,128]{1,0:T(8,128)} %get-tuple-element.28), channel_id=1, source_target_pairs={{0,3},{1,2},{2,5},{3,4},{4,7},{5,6},{6,9},{7,8},{8,11},{9,10},{10,... | collective-permute-start | bytes 12296 | tf_op jit(solution)/shard_map/ppermute | solution.py:688
  12.7 5.1 %collective-permute-start.4 = (f32[8,128]{1,0:T(8,128)}, f32[8,128]{1,0:T(8,128)S(1)}, u32[]{:S(2)}, u32[]{:S(2)}) collective-permute-start(f32[8,128]{1,0:T(8,128)} %get-tuple-element.29), channel_id=1, source_target_pairs={{2,1},{3,0},{4,3},{5,2},{6,5},{7,4},{8,7},{9,6},{10,9},{11,8},{12,... | collective-permute-start | bytes 12296 | tf_op jit(solution)/shard_map/ppermute | solution.py:688
  17.9 1.0 copy-start.1
  34.6 12.1 %collective-permute-start.5 = (bf16[272,256]{1,0:T(8,128)(2,1)S(1)}, bf16[272,256]{1,0:T(8,128)(2,1)S(1)}, u32[]{:S(2)}, u32[]{:S(2)}) collective-permute-start(bf16[272,256]{1,0:T(8,128)(2,1)S(1)} %get-tuple-element.32), channel_id=1, source_target_pairs={{0,8},{1,9},{2,10},{3,11},{4,12},{5,13},{6,14},{7,15},{8,16},{9,17... | collective-permute-start | bytes 417800 | tf_op jit(solution)/shard_map/ppermute | solution.py:735
  35.9 13.0 %collective-permute-start.6 = (bf16[272,256]{1,0:T(8,128)(2,1)S(1)}, bf16[272,256]{1,0:T(8,128)(2,1)S(1)}, u32[]{:S(2)}, u32[]{:S(2)}) collective-permute-start(bf16[272,256]{1,0:T(8,128)(2,1)S(1)} %get-tuple-element.33), channel_id=1, source_target_pairs={{0,16},{1,17},{2,18},{3,19},{4,20},{5,21},{6,22},{7,23},{8,24},{9,... | collective-permute-start | bytes 417800 | tf_op jit(solution)/shard_map/ppermute | solution.py:735
  37.2 14.3 %collective-permute-start.7 = (bf16[272,256]{1,0:T(8,128)(2,1)S(1)}, bf16[272,256]{1,0:T(8,128)(2,1)S(1)}, u32[]{:S(2)}, u32[]{:S(2)}) collective-permute-start(bf16[272,256]{1,0:T(8,128)(2,1)S(1)} %get-tuple-element.34), channel_id=1, source_target_pairs={{0,24},{1,25},{2,26},{3,27},{4,28},{5,29},{6,30},{7,31},{8,0},{9,1... | collective-permute-start | bytes 417800 | tf_op jit(solution)/shard_map/ppermute | solution.py:735
  51.5 12.4 %collective-permute-start.10 = (bf16[272,256]{1,0:T(8,128)(2,1)S(1)}, bf16[272,256]{1,0:T(8,128)(2,1)S(1)}, u32[]{:S(2)}, u32[]{:S(2)}) collective-permute-start(bf16[272,256]{1,0:T(8,128)(2,1)S(1)} %get-tuple-element.38), channel_id=1, source_target_pairs={{0,3},{1,4},{2,5},{3,6},{4,7},{5,0},{6,1},{7,2},{8,11},{9,12},{10,... | collective-permute-start | bytes 417800 | tf_op jit(solution)/shard_map/ppermute | solution.py:745
  61.1 5.0 %collective-permute-start.8 = (bf16[272,256]{1,0:T(8,128)(2,1)S(1)}, bf16[272,256]{1,0:T(8,128)(2,1)S(1)}, u32[]{:S(2)}, u32[]{:S(2)}) collective-permute-start(bf16[272,256]{1,0:T(8,128)(2,1)S(1)} %get-tuple-element.36), channel_id=1, source_target_pairs={{0,1},{1,2},{2,3},{3,4},{4,5},{5,6},{6,7},{7,0},{8,9},{9,10},{10,1... | collective-permute-start | bytes 417800 | tf_op jit(solution)/shard_map/ppermute | solution.py:745
  61.1 6.5 %collective-permute-start.9 = (bf16[272,256]{1,0:T(8,128)(2,1)S(1)}, bf16[272,256]{1,0:T(8,128)(2,1)S(1)}, u32[]{:S(2)}, u32[]{:S(2)}) collective-permute-start(bf16[272,256]{1,0:T(8,128)(2,1)S(1)} %get-tuple-element.37), channel_id=1, source_target_pairs={{0,2},{1,3},{2,4},{3,5},{4,6},{5,7},{6,0},{7,1},{8,10},{9,11},{10,... | collective-permute-start | bytes 417800 | tf_op jit(solution)/shard_map/ppermute | solution.py:745
  74.2 5.5 %collective-permute-start.14 = (f32[2,128,128]{2,1,0:T(8,128)S(1)}, f32[2,128,128]{2,1,0:T(8,128)S(1)}, u32[]{:S(2)}, u32[]{:S(2)}) collective-permute-start(f32[2,128,128]{2,1,0:T(8,128)S(1)} %get-tuple-element.41.refs_1_), channel_id=1, source_target_pairs={{0,8},{1,9},{2,10},{3,11},{4,12},{5,13},{6,14},{7,15},{8,16},{9,17... | collective-permute-start | bytes 393224 | tf_op jit(solution)/shard_map/ppermute | solution.py:735
  75.9 10.9 %collective-permute-start.15 = (f32[2,128,128]{2,1,0:T(8,128)S(1)}, f32[2,128,128]{2,1,0:T(8,128)S(1)}, u32[]{:S(2)}, u32[]{:S(2)}) collective-permute-start(f32[2,128,128]{2,1,0:T(8,128)S(1)} %get-tuple-element.41.refs_1_), channel_id=1, source_target_pairs={{0,16},{1,17},{2,18},{3,19},{4,20},{5,21},{6,22},{7,23},{8,24},{9,... | collective-permute-start | bytes 393224 | tf_op jit(solution)/shard_map/ppermute | solution.py:735
  76.0 10.9 %collective-permute-start.16 = (f32[2,128,128]{2,1,0:T(8,128)S(1)}, f32[2,128,128]{2,1,0:T(8,128)S(1)}, u32[]{:S(2)}, u32[]{:S(2)}) collective-permute-start(f32[2,128,128]{2,1,0:T(8,128)S(1)} %get-tuple-element.41.refs_1_), channel_id=1, source_target_pairs={{0,24},{1,25},{2,26},{3,27},{4,28},{5,29},{6,30},{7,31},{8,0},{9,1... | collective-permute-start | bytes 393224 | tf_op jit(solution)/shard_map/ppermute | solution.py:735
  76.8 14.1 %collective-permute-start.11 = (f32[2,128,128]{2,1,0:T(8,128)S(1)}, f32[2,128,128]{2,1,0:T(8,128)S(1)}, u32[]{:S(2)}, u32[]{:S(2)}) collective-permute-start(f32[2,128,128]{2,1,0:T(8,128)S(1)} %get-tuple-element.40.refs_3_), channel_id=1, source_target_pairs={{0,24},{1,25},{2,26},{3,27},{4,28},{5,29},{6,30},{7,31}} | collective-permute-start | bytes 393224 | tf_op jit(solution)/shard_map/ppermute | solution.py:751
  78.1 15.7 %collective-permute-start.12 = (f32[2,128,128]{2,1,0:T(8,128)S(1)}, f32[2,128,128]{2,1,0:T(8,128)S(1)}, u32[]{:S(2)}, u32[]{:S(2)}) collective-permute-start(f32[2,128,128]{2,1,0:T(8,128)S(1)} %get-tuple-element.40.refs_3_), channel_id=1, source_target_pairs={{8,24},{9,25},{10,26},{11,27},{12,28},{13,29},{14,30},{15,31}} | collective-permute-start | bytes 393224 | tf_op jit(solution)/shard_map/ppermute | solution.py:751
  79.7 14.0 %collective-permute-start.13 = (f32[2,128,128]{2,1,0:T(8,128)S(1)}, f32[2,128,128]{2,1,0:T(8,128)S(1)}, u32[]{:S(2)}, u32[]{:S(2)}) collective-permute-start(f32[2,128,128]{2,1,0:T(8,128)S(1)} %get-tuple-element.40.refs_3_), channel_id=1, source_target_pairs={{16,24},{17,25},{18,26},{19,27},{20,28},{21,29},{22,30},{23,31}} | collective-permute-start | bytes 393224 | tf_op jit(solution)/shard_map/ppermute | solution.py:751
  87.6 13.3 %collective-permute-start.17 = (f32[64,128]{1,0:T(8,128)S(1)}, f32[64,128]{1,0:T(8,128)S(1)}, u32[]{:S(2)}, u32[]{:S(2)}) collective-permute-start(f32[64,128]{1,0:T(8,128)S(1)} %get-tuple-element.44), channel_id=1, source_target_pairs={{0,7},{1,0},{2,1},{3,2},{4,3},{5,4},{6,5},{7,6},{8,15},{9,8},{10,9... | collective-permute-start | bytes 98312 | tf_op jit(solution)/shard_map/ppermute | solution.py:745
  88.6 12.3 %collective-permute-start.18 = (f32[64,128]{1,0:T(8,128)S(1)}, f32[64,128]{1,0:T(8,128)S(1)}, u32[]{:S(2)}, u32[]{:S(2)}) collective-permute-start(f32[64,128]{1,0:T(8,128)S(1)} %get-tuple-element.45), channel_id=1, source_target_pairs={{0,6},{1,7},{2,0},{3,1},{4,2},{5,3},{6,4},{7,5},{8,14},{9,15},{10,... | collective-permute-start | bytes 98312 | tf_op jit(solution)/shard_map/ppermute | solution.py:745
  90.9 10.1 %collective-permute-start.19 = (f32[64,128]{1,0:T(8,128)S(1)}, f32[64,128]{1,0:T(8,128)S(1)}, u32[]{:S(2)}, u32[]{:S(2)}) collective-permute-start(f32[64,128]{1,0:T(8,128)S(1)} %get-tuple-element.46), channel_id=1, source_target_pairs={{0,5},{1,6},{2,7},{3,0},{4,1},{5,2},{6,3},{7,4},{8,13},{9,14},{10,... | collective-permute-start | bytes 98312 | tf_op jit(solution)/shard_map/ppermute | solution.py:745

commit v3 on v2

--- a/solution.py
+++ b/solution.py
@@ -35,13 +35,13 @@
     return jnp.dot(a, b, preferred_element_type=F32)
 
 
-def edges_kernel(state, first_rows, last_rows, sides, top_corners, low_corners, left, right, sems):
+def edges_kernel(state, first_rows, last_rows, sides, left, right, sems):
     rows, cols, _ = state.shape
     copies = [
-        pltpu.make_async_copy(state.at[:, pl.ds(0, EDGE)], left, sems.at[0]),
-        pltpu.make_async_copy(state.at[:, pl.ds(cols - EDGE, EDGE)], right, sems.at[1]),
-        pltpu.make_async_copy(state.at[pl.ds(0, 2)], first_rows, sems.at[2]),
-        pltpu.make_async_copy(state.at[pl.ds(rows - 2, 2)], last_rows, sems.at[3]),
+        pltpu.make_async_copy(state.at[pl.ds(0, 2)], first_rows, sems.at[0]),
+        pltpu.make_async_copy(state.at[pl.ds(rows - 2, 2)], last_rows, sems.at[1]),
+        pltpu.make_async_copy(state.at[:, pl.ds(0, EDGE)], left, sems.at[2]),
+        pltpu.make_async_copy(state.at[:, pl.ds(cols - EDGE, EDGE)], right, sems.at[3]),
     ]
     for copy in copies:
         copy.start()
@@ -50,25 +50,18 @@
     for i in range(2):
         sides[i] = left[:, i, :]
         sides[2 + i] = right[:, EDGE - 2 + i, :]
-    top_corners[...] = jnp.zeros(top_corners.shape, F32)
-    low_corners[...] = jnp.zeros(low_corners.shape, F32)
-    top_corners[0:1] = left[0, 0:1]
-    top_corners[1:2] = right[0, EDGE - 1 :]
-    low_corners[0:1] = left[rows - 1, 0:1]
-    low_corners[1:2] = right[rows - 1, EDGE - 1 :]
 
 
 def take_edges(state):
     rows, cols, levels = state.shape
     slab = jax.ShapeDtypeStruct((2, cols, levels), F32)
     side = jax.ShapeDtypeStruct((4, rows, levels), F32)
-    corner = jax.ShapeDtypeStruct((EDGE, levels), F32)
     vmem = pl.BlockSpec(memory_space=pltpu.VMEM)
     return pl.pallas_call(
         edges_kernel,
-        out_shape=(slab, slab, side, corner, corner),
+        out_shape=(slab, slab, side),
         in_specs=[pl.BlockSpec(memory_space=pl.ANY)],
-        out_specs=(vmem,) * 5,
+        out_specs=(vmem,) * 3,
         scratch_shapes=[
             pltpu.VMEM((rows, EDGE, levels), F32),
             pltpu.VMEM((rows, EDGE, levels), F32),
@@ -79,17 +72,42 @@
     )(state)
 
 
+def frame_kernel(sides, up_rows, low_rows, framed):
+    _, rows, levels = sides.shape
+    cols = up_rows.shape[1]
+    framed[...] = jnp.zeros(framed.shape, F32)
+    for i, col in enumerate((0, 1, cols - 2, cols - 1)):
+        framed[i, EDGE : EDGE + rows, :] = sides[i]
+        framed[i, EDGE - 1 : EDGE, :] = up_rows[1, col : col + 1, :]
+        framed[i, EDGE + rows : EDGE + rows + 1, :] = low_rows[0, col : col + 1, :]
+
+
+def frame_sides(sides, up_rows, low_rows):
+    count, rows, levels = sides.shape
+    vmem = pl.BlockSpec(memory_space=pltpu.VMEM)
+    return pl.pallas_call(
+        frame_kernel,
+        out_shape=jax.ShapeDtypeStruct((count, rows + 2 * EDGE, levels), F32),
+        in_specs=[vmem] * 3,
+        out_specs=vmem,
+        compiler_params=pltpu.CompilerParams(vmem_limit_bytes=56 * MIB),
+        name="frame",
+    )(sides, up_rows, low_rows)
+
+
 def advance_kernel(comp_count, left_at, right_at, *refs):
     (flags, source_column, labels, state, up_rows, low_rows, left_in, right_in, own_sides) = refs[:9]
-    (up_left, up_right, low_left, low_right, mask, mix_atm, mix_ocn, flux_map) = refs[9:17]
-    out, surface = refs[17:19]
-    packed = refs[19 : 19 + comp_count]
-    (values, moved, halo, halo_moved, smooth, pairs, mixed, weights, flux_weights, fluxes, staged) = refs[
-        19 + comp_count : 30 + comp_count
+    (mask, mix_atm, mix_ocn, flux_map) = refs[9:13]
+    out, surface, sea_copy = refs[13:16]
+    packed = refs[16 : 16 + comp_count]
+    (values, moved, halo_moved, smooth, pairs, mixed, later_smooth, later_pairs, later_mixed) = refs[
+        16 + comp_count : 25 + comp_count
     ]
-    top, in_sems, out_sems = refs[30 + comp_count :]
+    (weights, flux_weights, fluxes, staged, top, in_sems, out_sems) = refs[25 + comp_count :]
     left_cols = left_in.at[left_at : left_at + 2]
     right_cols = right_in.at[right_at : right_at + 2]
+    first = (smooth, pairs, mixed)
+    second = (later_smooth, later_pairs, later_mixed)
     rows, cols, levels = state.shape
     chunks = rows // CHUNK
     inner = pl.ds(EDGE, cols)
@@ -115,10 +133,10 @@
     ocean = flags[0] == 1
     mix = jnp.where(ocean, mix_ocn[...], mix_atm[...])
     mix_high, mix_low = split_two(mix)
-    weights[:levels, :levels] = mix_high
-    weights[levels:, :levels] = mix_high
-    weights[:levels, levels:] = mix_low
-    weights[levels:, levels:] = mix_low
+    weights[:levels, :] = mix_high
+    weights[levels : 2 * levels, :] = mix_high
+    weights[2 * levels :, :] = mix_low
+    sea_copy[...] = mask[...].astype(BF16)
     map_high, map_low = split_two(flux_map[...])
     flux_weights[...] = jnp.concatenate(
         [
@@ -129,22 +147,22 @@
     ).astype(BF16)
     values[0:2, EDGE : EDGE + cols, :] = up_rows[...]
     values[rows + 2 : rows + 4, EDGE : EDGE + cols, :] = low_rows[...]
-    values[1, EDGE - 1 : EDGE, :] = up_left[1:2]
-    values[1, EDGE + cols : EDGE + cols + 1, :] = up_right[0:1]
-    values[rows + 2, EDGE - 1 : EDGE, :] = low_left[1:2]
-    values[rows + 2, EDGE + cols : EDGE + cols + 1, :] = low_right[0:1]
+    for r, i in ((1, EDGE - 1), (rows + 2, EDGE + rows)):
+        values[r, EDGE - 1 : EDGE, :] = left_cols[1, i : i + 1, :]
+        values[r, EDGE + cols : EDGE + cols + 1, :] = right_cols[0, i : i + 1, :]
 
     def side_cells(r, _):
-        values[r + 2, EDGE - 1 : EDGE, :] = left_cols[1, pl.ds(r, 1), :]
-        values[r + 2, EDGE + cols : EDGE + cols + 1, :] = right_cols[0, pl.ds(r, 1), :]
+        values[r + 2, EDGE - 1 : EDGE, :] = left_cols[1, pl.ds(r + EDGE, 1), :]
+        values[r + 2, EDGE + cols : EDGE + cols + 1, :] = right_cols[0, pl.ds(r + EDGE, 1), :]
         return 0
 
     lax.fori_loop(0, rows, side_cells, 0, unroll=8)
 
-    def stage(row, total):
+    def stage(refs, row, total):
         line = SMOOTHING * total
-        smooth[row] = line
-        pairs[row * cols : (row + 1) * cols, :] = side_by_side(line)
+        high, low = split_two(line)
+        refs[0][row] = line
+        refs[1][row * cols : (row + 1) * cols, :] = jnp.concatenate([high, low, high], axis=1)
 
     def note_top(q, lines):
         lanes = lax.broadcasted_iota(jnp.int32, (cols, levels), 1)
@@ -154,12 +172,11 @@
         turned = pltpu.roll(kept, q * CHUNK, 1)
         top[...] = jnp.where(lanes // CHUNK == q, turned, top[...])
 
-    def mix_rows(count):
-        mixed[: count * cols, :] = dot_nn(pairs[: count * cols, :], weights[...])
-
-    def finish(row):
-        part = mixed[row * cols : (row + 1) * cols, :]
-        return smooth[row] + PHYSICS * jnp.tanh(part[:, :levels] + part[:, levels:])
+    def mix_rows(refs, count):
+        refs[2][: count * cols, :] = dot_nn(refs[1][: count * cols, :], weights[...])
+
+    def finish(refs, row):
+        return refs[0][row] + PHYSICS * jnp.tanh(refs[2][row * cols : (row + 1) * cols, :])
 
     def gather_row(ref, i):
         here = ref[i, EDGE : EDGE + cols, :] + (
@@ -171,24 +188,19 @@
 
     @pl.when(jnp.logical_not(ocean))
     def atmosphere():
-        halo[0, EDGE : EDGE + rows, :] = left_cols[1]
-        halo[0, EDGE - 1 : EDGE, :] = up_left[1:2]
-        halo[0, EDGE + rows : EDGE + rows + 1, :] = low_left[1:2]
-        halo[1, EDGE : EDGE + rows, :] = right_cols[0]
-        halo[1, EDGE - 1 : EDGE, :] = up_right[0:1]
-        halo[1, EDGE + rows : EDGE + rows + 1, :] = low_right[0:1]
+        nearest = (left_cols.at[1], right_cols.at[0])
         beyond = (left_cols.at[0], right_cols.at[1])
         within = (own_sides.at[0], own_sides.at[3])
         for s in range(2):
             total = (
-                halo[s, EDGE : EDGE + rows, :]
-                + halo[s, EDGE - 1 : EDGE - 1 + rows, :]
-                + halo[s, EDGE + 1 : EDGE + 1 + rows, :]
+                nearest[s][EDGE : EDGE + rows, :]
+                + nearest[s][EDGE - 1 : EDGE - 1 + rows, :]
+                + nearest[s][EDGE + 1 : EDGE + 1 + rows, :]
             )
-            stage(s, total + (beyond[s][...] + within[s][...]))
-        mix_rows(2)
+            stage(first, s, total + (beyond[s][EDGE : EDGE + rows, :] + within[s][...]))
+        mix_rows(first, 2)
         for s in range(2):
-            halo_moved[s] = finish(s)
+            halo_moved[s] = finish(first, s)
 
         def moved_sides(r, _):
             moved[r + 1, EDGE - 1 : EDGE, :] = halo_moved[0, pl.ds(r, 1), :]
@@ -197,69 +209,88 @@
 
         lax.fori_loop(0, rows, moved_sides, 0, unroll=8)
         fetch(0).wait()
+        fetch(1).wait()
         for row in range(2):
-            stage(row, gather_row(values, row + 1))
-        mix_rows(2)
-        moved[0, EDGE : EDGE + cols, :] = finish(0)
-        moved[1, EDGE : EDGE + cols, :] = finish(1)
+            stage(second, row, gather_row(values, row + 1))
+        mix_rows(second, 2)
+        moved[0, EDGE : EDGE + cols, :] = finish(second, 0)
+        moved[1, EDGE : EDGE + cols, :] = finish(second, 1)
 
         @pl.when(flags[1] == 0)
         def _():
             moved[0, EDGE : EDGE + cols, :] = jnp.zeros((cols, levels), F32)
 
+        def begin_first(q):
+            for row in range(CHUNK):
+                stage(first, row, gather_row(values, q * CHUNK + row + 3))
+            mix_rows(first, CHUNK)
+
+        def end_first(q):
+            for row in range(CHUNK):
+                moved[q * CHUNK + row + 2, EDGE : EDGE + cols, :] = finish(first, row)
+
+        def begin_second(q):
+            for row in range(CHUNK):
+                stage(second, row, gather_row(moved, q * CHUNK + row + 1))
+
+        def end_second(q, slot):
+            for row in range(CHUNK):
+                line = finish(second, row)
+                staged[slot, row] = line
+                both = line + moved[q * CHUNK + row + 1, EDGE : EDGE + cols, :]
+                later_pairs[row * cols : (row + 1) * cols, : 2 * levels] = side_by_side(both)
+            put(q, slot).start()
+            note_top(q, [staged[slot, row] for row in range(CHUNK)])
+            flux = dot_nt(flux_weights[...], later_pairs[:, : 2 * levels])
+            flux = flux[:flux_count] + flux[flux_count:]
+            for row in range(CHUNK):
+                r = q * CHUNK + row
+                block = PHYSICS * flux[:, row * cols : (row + 1) * cols]
+                sea = jnp.broadcast_to(mask[pl.ds(r, 1), :], block.shape)
+                block = jnp.where(sea > 0.5, block, 0.0)
+                fluxes[pl.ds(pl.multiple_of(r * flux_count, flux_count), flux_count), :] = block
+
+        begin_first(0)
+        end_first(0)
 
         def one_chunk(q, _):
-            base = q * CHUNK
-
             @pl.when(q + 1 < chunks)
             def _():
                 fetch(q + 1).wait()
 
-            for row in range(CHUNK):
-                stage(row, gather_row(values, base + row + 3))
-            mix_rows(CHUNK)
-            for row in range(CHUNK):
-                moved[base + row + 2, EDGE : EDGE + cols, :] = finish(row)
-
-            @pl.when((q + 1 == chunks) & (flags[2] == 0))
+            slot = (q - 1) % 2
+
+            @pl.when(q >= 3)
             def _():
-                moved[rows + 1, EDGE : EDGE + cols, :] = jnp.zeros((cols, levels), F32)
-
-            for row in range(CHUNK):
-                stage(row, gather_row(moved, base + row + 1))
-            mix_rows(CHUNK)
-            slot = q % 2
-
-            @pl.when(q >= 2)
-            def _():
-                put(q - 2, slot).wait()
-
-            for row in range(CHUNK):
-                line = finish(row)
-                staged[slot, row] = line
-                both = line + moved[base + row + 1, EDGE : EDGE + cols, :]
-                pairs[row * cols : (row + 1) * cols, :] = side_by_side(both)
-            put(q, slot).start()
-            note_top(q, [staged[slot, row] for row in range(CHUNK)])
-            flux = dot_nt(flux_weights[...], pairs[...])
-            flux = flux[:flux_count] + flux[flux_count:]
-            for row in range(CHUNK):
-                block = PHYSICS * flux[:, row * cols : (row + 1) * cols]
-                sea = jnp.broadcast_to(mask[pl.ds(base + row, 1), :], block.shape)
-                block = jnp.where(sea > 0.5, block, 0.0)
-                fluxes[pl.ds(pl.multiple_of((base + row) * flux_count, flux_count), flux_count), :] = block
+                put(q - 3, slot).wait()
+
+            begin_first(q)
+            begin_second(q - 1)
+            end_first(q)
+            mix_rows(second, CHUNK)
+            end_second(q - 1, slot)
             return 0
 
-        lax.fori_loop(0, chunks, one_chunk, 0)
-        put(chunks - 2, (chunks - 2) % 2).wait()
-        put(chunks - 1, (chunks - 1) % 2).wait()
+        lax.fori_loop(1, chunks, one_chunk, 0)
+
+        @pl.when(flags[2] == 0)
+        def _():
+            moved[rows + 1, EDGE : EDGE + cols, :] = jnp.zeros((cols, levels), F32)
+
+        last = chunks - 1
+        put(last - 2, last % 2).wait()
+        begin_second(last)
+        mix_rows(second, CHUNK)
+        end_second(last, last % 2)
+        put(last - 1, (last - 1) % 2).wait()
+        put(last, last % 2).wait()
         spots = lax.broadcasted_iota(jnp.int32, (source_column.shape[0], rows), 1)
         placing = jnp.where(source_column[...] == spots, 1.0, 0.0).astype(BF16)
         share = flux_count // comp_count
         for shift in range(comp_count):
-            first = lax.rem(flags[3] + shift, comp_count) * share
+            begin_field = lax.rem(flags[3] + shift, comp_count) * share
             for f in range(share):
-                field = fluxes[pl.ds(first + f, rows, stride=flux_count), :].astype(BF16)
+                field = fluxes[pl.ds(begin_field + f, rows, stride=flux_count), :].astype(BF16)
                 packed[shift][: placing.shape[0], f * cols : (f + 1) * cols] = dot_nn(
                     placing, field
                 ).astype(BF16)
@@ -281,8 +312,8 @@
                 fetch(q + 1).wait()
 
             for row in range(CHUNK):
-                stage(row, gather_row(values, base + row + 2))
-            mix_rows(CHUNK)
+                stage(first, row, gather_row(values, base + row + 2))
+            mix_rows(first, CHUNK)
             slot = q % 2
 
             @pl.when(q >= 2)
@@ -293,7 +324,7 @@
             for row in range(CHUNK):
                 chosen = sea[:, row * levels : (row + 1) * levels] > 0.5
                 before = values[base + row + 2, EDGE : EDGE + cols, :]
-                staged[slot, row] = jnp.where(chosen, finish(row), before)
+                staged[slot, row] = jnp.where(chosen, finish(first, row), before)
             put(q, slot).start()
             note_top(q, [staged[slot, row] for row in range(CHUNK)])
             return 0
@@ -323,19 +354,22 @@
         out_shape=(
             jax.ShapeDtypeStruct(state.shape, F32),
             jax.ShapeDtypeStruct((rows, cols), F32),
+            jax.ShapeDtypeStruct((rows, cols), BF16),
         )
         + (entry,) * comp_count,
         in_specs=[smem, vmem, vmem, hbm] + [vmem] * (len(halos) + 4),
-        out_specs=(hbm,) + (vmem,) * (1 + comp_count),
+        out_specs=(hbm,) + (vmem,) * (2 + comp_count),
         scratch_shapes=[
             pltpu.VMEM((rows + 4, cols + 2 * EDGE, levels), F32),
             pltpu.VMEM((rows + 2, cols + 2 * EDGE, levels), F32),
-            pltpu.VMEM((2, rows + 2 * EDGE, levels), F32),
             pltpu.VMEM((2, rows, levels), F32),
             pltpu.VMEM((CHUNK, cols, levels), F32),
-            pltpu.VMEM((CHUNK * cols, 2 * levels), BF16),
-            pltpu.VMEM((CHUNK * cols, 2 * levels), F32),
-            pltpu.VMEM((2 * levels, 2 * levels), BF16),
+            pltpu.VMEM((CHUNK * cols, 3 * levels), BF16),
+            pltpu.VMEM((CHUNK * cols, levels), F32),
+            pltpu.VMEM((CHUNK, cols, levels), F32),
+            pltpu.VMEM((CHUNK * cols, 3 * levels), BF16),
+            pltpu.VMEM((CHUNK * cols, levels), F32),
+            pltpu.VMEM((3 * levels, levels), BF16),
             pltpu.VMEM((2 * fluxes, 2 * levels), BF16),
             pltpu.VMEM((rows * fluxes, cols), F32),
             pltpu.VMEM((2, CHUNK, cols, levels), F32),
@@ -355,63 +389,76 @@
 LABEL_ROWS = 16
 
 
-def regroup_kernel(count, *refs):
+def regroup_kernel(count, flags, *refs):
     slabs, blocks = refs[:-count], refs[-count:]
-    comp_count = len(slabs)
-    capacity = blocks[0].shape[0] // comp_count - LABEL_ROWS // comp_count
+    sources = len(slabs) - 1
+    capacity = (blocks[0].shape[0] - LABEL_ROWS) // sources
     size = count * capacity
-    heads = [slab[size : size + LABEL_ROWS, :].astype(F32) for slab in slabs]
+
+    def chosen(c, start, stop):
+        shift = lax.rem(flags[3] - c + len(slabs), len(slabs))
+        value = slabs[0][start:stop, :].astype(F32)
+        for s in range(1, len(slabs)):
+            value = jnp.where(shift == s, slabs[s][start:stop, :].astype(F32), value)
+        return value
+
+    heads = [chosen(c, size, size + LABEL_ROWS) for c in range(sources)]
     lines = [head[i : i + 1] for i in range(2) for head in heads]
     spare = jnp.zeros((LABEL_ROWS - len(lines), heads[0].shape[1]), F32)
     labels = jnp.concatenate(lines + [spare], axis=0).astype(BF16)
     for n in range(count):
-        for s in range(comp_count):
-            blocks[n][s * capacity : (s + 1) * capacity, :] = slabs[s][
-                n * capacity : (n + 1) * capacity, :
-            ]
-        blocks[n][comp_count * capacity :, :] = labels
-
-
-def regroup(slabs, count):
+        for c in range(sources):
+            blocks[n][c * capacity : (c + 1) * capacity, :] = chosen(
+                c, n * capacity, (n + 1) * capacity
+            ).astype(BF16)
+        blocks[n][sources * capacity :, :] = labels
+
+
+def regroup(flags, slabs, count):
     rows, width = slabs[0].shape
-    size = (rows - LABEL_ROWS) // count * len(slabs) + LABEL_ROWS
+    size = (rows - LABEL_ROWS) // count * (len(slabs) - 1) + LABEL_ROWS
     vmem = pl.BlockSpec(memory_space=pltpu.VMEM)
     return pl.pallas_call(
         functools.partial(regroup_kernel, count),
         out_shape=(jax.ShapeDtypeStruct((size, width), BF16),) * count,
-        in_specs=[vmem] * len(slabs),
+        in_specs=[pl.BlockSpec(memory_space=pltpu.SMEM)] + [vmem] * len(slabs),
         out_specs=(vmem,) * count,
         compiler_params=pltpu.CompilerParams(vmem_limit_bytes=16 * MIB),
         name="regroup",
-    )(*slabs)
+    )(flags, *slabs)
 
 
 def regrid_body(count, comp_count, flags, ocean_first, *refs):
     blocks = refs[:count]
-    weights, surface, mask, forcing, shared, hits, entries, chosen, binned = refs[count:]
+    seas = refs[count : count + comp_count]
+    weights, surface, mask, forcing, shared, hits, entries, chosen, binned = refs[count + comp_count :]
+    sources = comp_count - 1
     rows, cols = mask.shape
     share = forcing.shape[0]
     weight_count = weights.shape[0]
-    capacity = (blocks[0].shape[0] - LABEL_ROWS) // comp_count
+    capacity = (blocks[0].shape[0] - LABEL_ROWS) // sources
     size = count * capacity
-    total = comp_count * size
+    total = sources * size
     width = blocks[0].shape[1]
-    for s in range(comp_count):
+    for c in range(sources):
         for n in range(count):
-            start = s * size + n * capacity
-            entries[start : start + capacity, :] = blocks[n][s * capacity : (s + 1) * capacity, :]
+            start = c * size + n * capacity
+            entries[start : start + capacity, :] = blocks[n][c * capacity : (c + 1) * capacity, :]
     lanes = lax.broadcasted_iota(jnp.int32, (LABEL_ROWS, width), 1) // capacity
     labels = jnp.zeros((LABEL_ROWS, width), F32)
     for n in range(count):
-        labels = jnp.where(lanes == n, blocks[n][comp_count * capacity :, :].astype(F32), labels)
+        labels = jnp.where(lanes == n, blocks[n][sources * capacity :, :].astype(F32), labels)
     labels = labels.astype(jnp.int32)
-    weight_line = jnp.concatenate([labels[s : s + 1, :size] for s in range(comp_count)], axis=1)
+    weight_line = jnp.concatenate([labels[c : c + 1, :size] for c in range(sources)], axis=1)
     target_line = jnp.concatenate(
-        [labels[comp_count + s : comp_count + s + 1, :size] for s in range(comp_count)], axis=1
+        [labels[sources + c : sources + c + 1, :size] for c in range(sources)], axis=1
     )
     spots = lax.broadcasted_iota(jnp.int32, (rows, total), 0)
     by_target = jnp.where(target_line == spots, 1.0, 0.0)
-    hits[...] = by_target[:, :size].T.astype(BF16)
+    own = by_target[:, :size]
+    for c in range(1, sources):
+        own = jnp.where(flags[3] == c, by_target[:, c * size : (c + 1) * size], own)
+    hits[...] = own.T.astype(BF16)
     by_target = by_target.astype(BF16)
     numbers = lax.broadcasted_iota(jnp.int32, (weight_count, total), 0)
     by_weight = jnp.where(weight_line == numbers, 1.0, 0.0).astype(BF16)
@@ -433,18 +480,21 @@
     change = ocean_first[flags[3] * share] * forcing[0]
     for f in range(1, share):
         change = change + ocean_first[flags[3] * share + f] * forcing[f]
+    sea = jnp.where(flags[0] == 1, seas[sources][...].astype(F32), 0.0)
+    for c in range(sources):
+        sea = sea + jnp.where(flags[3] == c, seas[c][...].astype(F32), 0.0)
     base = jnp.where(flags[0] == 1, surface[...], 0.0)
-    held = jnp.where((mask[...] > 0.5) | (flags[0] == 0), change, 0.0)
-    shared[0] = base + held
-    shared[1] = mask[...]
-
-
-def regrid(flags, ocean_first, blocks, comp_count, weights, surface, mask):
+    shared[...] = base + jnp.where(sea > 0.5, change, 0.0)
+
+
+def regrid(flags, ocean_first, blocks, seas, weights, surface, mask):
+    comp_count = len(seas)
+    sources = comp_count - 1
     rows, cols = mask.shape
     count = len(blocks)
     height, width = blocks[0].shape
-    size = (height - LABEL_ROWS) // comp_count * count
-    total = size * comp_count
+    size = (height - LABEL_ROWS) // sources * count
+    total = size * sources
     share = width // cols
     weight_count = weights.shape[0]
     vmem = pl.BlockSpec(memory_space=pltpu.VMEM)
@@ -453,10 +503,10 @@
         functools.partial(regrid_body, count, comp_count),
         out_shape=(
             jax.ShapeDtypeStruct((share, rows, cols), F32),
-            jax.ShapeDtypeStruct((2, rows, cols), F32),
+            jax.ShapeDtypeStruct((rows, cols), F32),
             jax.ShapeDtypeStruct((size, rows), BF16),
         ),
-        in_specs=[smem, smem] + [vmem] * (count + 3),
+        in_specs=[smem, smem] + [vmem] * (count + comp_count + 3),
         out_specs=(vmem, vmem, vmem),
         scratch_shapes=[
             pltpu.VMEM((total, width), BF16),
@@ -470,25 +520,16 @@
             transcendentals=0,
         ),
         name="regrid",
-    )(flags, ocean_first, *blocks, weights, surface, mask)
-
-
-def pick_kernel(comp_count, *refs):
-    flags = refs[0]
-    parts = refs[1 : 1 + comp_count]
-    hits, surface = refs[1 + comp_count : 3 + comp_count]
-    picked = refs[3 + comp_count :]
-    rows, cols = surface.shape
-    from_ocean = lax.rem(flags[3] + 1, comp_count)
-    base = jnp.zeros((rows, cols), F32)
-    sea = base
-    change = base
-    for shift in range(comp_count):
-        is_base = from_ocean == shift
-        base = base + jnp.where(is_base, parts[shift][0], 0.0)
-        sea = sea + jnp.where(is_base, parts[shift][1], 0.0)
-        change = change + jnp.where(is_base, 0.0, parts[shift][0])
-    now = base + jnp.where(sea > 0.5, change, 0.0)
+    )(flags, ocean_first, *blocks, *seas, weights, surface, mask)
+
+
+def pick_kernel(count, *refs):
+    parts = refs[:count]
+    hits, surface = refs[count : count + 2]
+    picked = refs[count + 2 :]
+    now = parts[0][...]
+    for part in parts[1:]:
+        now = now + part[...]
     surface[...] = now
     pair = jnp.concatenate(split_two(now), axis=0)
     size = picked[0].shape[0]
@@ -497,23 +538,22 @@
         picked[n][...] = dot_nn(jnp.concatenate([some, some], axis=1), pair)
 
 
-def pick(flags, parts, hits, neighbours):
-    _, rows, cols = parts[0].shape
+def pick(parts, hits, neighbours):
+    rows, cols = parts[0].shape
     size = hits.shape[0] // neighbours
     vmem = pl.BlockSpec(memory_space=pltpu.VMEM)
-    smem = pl.BlockSpec(memory_space=pltpu.SMEM)
     return pl.pallas_call(
         functools.partial(pick_kernel, len(parts)),
         out_shape=(jax.ShapeDtypeStruct((rows, cols), F32),)
         + (jax.ShapeDtypeStruct((size, cols), F32),) * neighbours,
-        in_specs=[smem] + [vmem] * (len(parts) + 1),
+        in_specs=[vmem] * (len(parts) + 1),
         out_specs=(vmem,) * (1 + neighbours),
         compiler_params=pltpu.CompilerParams(vmem_limit_bytes=16 * MIB),
         name="pick",
-    )(flags, *parts, hits)
-
-
-LINES = 16
+    )(*parts, hits)
+
+
+LINES = 8
 
 
 def update_kernel(groups, flags, state, *refs):
@@ -559,15 +599,16 @@
                 ],
                 axis=0,
             )
-            first, second = split_two(part.T)
-            change = dot_nn(jnp.concatenate([first, second, first], axis=1), wide[...])
+            rough = part.astype(BF16).astype(F32)
+            turned = jnp.concatenate([rough, part - rough, rough], axis=0).T.astype(BF16)
+            change = dot_nn(turned, wide[...])
             fetch(q).wait()
             for line in range(LINES):
                 held[start + line] += change[:, line * levels : (line + 1) * levels]
             put(q).start()
             return 0
 
-        lax.fori_loop(0, chunks, one, 0)
+        lax.fori_loop(0, chunks, one, 0, unroll=2)
         for q in range(chunks):
             put(q).wait()
 
@@ -626,7 +667,7 @@
             )
             return 0
 
-        lax.fori_loop(0, weight_count // 2, one, 0, unroll=2)
+        lax.fori_loop(0, weight_count // 2, one, 0, unroll=8)
         spots = lax.broadcasted_iota(jnp.int32, (rows, values.shape[0]), 0)
         chosen = jnp.where(jnp.broadcast_to(row_line[...], spots.shape) == spots, 1.0, 0.0).astype(BF16)
         high, low = split_two(total[...])
@@ -687,23 +728,17 @@
                     )
         return lax.ppermute(value, AXES, pairs)
 
-    first_rows, last_rows, sides, top_corners, low_corners = take_edges(state)
+    first_rows, last_rows, sides = take_edges(state)
     up_rows = band_shift(last_rows, 1, 0)
     low_rows = band_shift(first_rows, -1, 0)
+    framed = frame_sides(sides, up_rows, low_rows)
     if lon_count == 2:
-        left_cols = right_cols = band_shift(sides, 0, 1)
+        left_cols = right_cols = band_shift(framed, 0, 1)
         left_at, right_at = 2, 0
     else:
-        left_cols = band_shift(sides[2:], 0, 1)
-        right_cols = band_shift(sides[:2], 0, -1)
+        left_cols = band_shift(framed[2:], 0, 1)
+        right_cols = band_shift(framed[:2], 0, -1)
         left_at, right_at = 0, 0
-    up_left = band_shift(low_corners, 1, 1)
-    low_left = band_shift(top_corners, -1, 1)
-    if lon_count == 2:
-        up_right, low_right = up_left, low_left
-    else:
-        up_right = band_shift(low_corners, 1, -1)
-        low_right = band_shift(top_corners, -1, -1)
 
     entry_list = intersection_list.reshape(entry_total, 3)
     owners = entry_list[:, 0]
@@ -734,43 +769,45 @@
         ]
         return lax.ppermute(value, AXES, pairs)
 
-    def over_tiles(value, offset):
+    def over_tiles(value, offset, comps):
         if offset % tile_count == 0:
             return value
         pairs = [
             (c * tile_count + t, c * tile_count + (t + offset) % tile_count)
-            for c in range(comp_count)
+            for c in range(comps)
             for t in range(tile_count)
         ]
         return lax.ppermute(value, AXES, pairs)
 
-    def to_ocean(value, comp):
+    def with_ocean(value, comp, back):
         pairs = [
             (comp * tile_count + t, ocean_comp * tile_count + t) for t in range(tile_count)
         ]
+        if back:
+            pairs = [(there, here) for here, there in pairs]
         return lax.ppermute(value, AXES, pairs)
 
     label_lines = jnp.stack([packed_labels // rows, packed_labels % rows]).astype(BF16)
     label_lines = jnp.pad(label_lines, ((0, LABEL_ROWS - 2), (0, 0)))
 
     halos = (up_rows, low_rows, left_cols, right_cols, sides)
-    halos = halos + (up_left, up_right, low_left, low_right)
     moved = advance(
         flags, sources[:, None], label_lines, state, halos, mask, mix_atm, mix_ocn, flux_map.T,
         comp_count, left_at, right_at,
     )
-    moved, surface, packed = moved[0], moved[1], moved[2:]
+    moved, surface, sea_copy, packed = moved[0], moved[1], moved[2], moved[3:]
     slabs = [packed[0]] + [over_comp(packed[s], s, False) for s in range(1, comp_count)]
-    blocks = regroup(slabs, neighbours)
-    blocks = [over_tiles(blocks[n], offsets[n]) for n in range(neighbours)]
+    seas = [with_ocean(sea_copy, c, True) for c in range(ocean_comp)] + [sea_copy]
+    blocks = regroup(flags, slabs, neighbours)
+    blocks = [over_tiles(blocks[n], offsets[n], comp_count) for n in range(neighbours)]
     forcing, shared, hits = regrid(
-        flags, ocean_map[:, 0], blocks, comp_count, regrid_weights, surface, mask
+        flags, ocean_map[:, 0], blocks, seas, regrid_weights, surface, mask
     )
     parts = [shared] + [over_comp(shared, s, True) for s in range(1, comp_count)]
-    picks = pick(flags, parts, hits, neighbours)
+    picks = pick(parts, hits, neighbours)
     new_surface, picked = picks[0], picks[1:]
-    arrived = [over_tiles(picked[n], -offsets[n]) for n in range(neighbours)]
-    fields = [to_ocean(forcing, c) for c in range(comp_count - 1)] + [forcing]
+    arrived = [over_tiles(picked[n], -offsets[n], ocean_comp) for n in range(neighbours)]
+    fields = [with_ocean(forcing, c, False) for c in range(ocean_comp)] + [forcing]
     final_state = update(flags, moved, fields, mask, ocean_map)
     weight_column = (packed_labels // rows)[:, None]
     surface_out = returned(

time: 102 us -> 101 us (level)
  the two profiles are of different devices: /device:TPU:15 before, /device:TPU:1 now
where the time goes in v3:
time: 101 us; the launch traced here: 100 us
  starting transfers between devices  37.3 us (37%)
  Pallas kernels  33.4 us (33%)
  waiting for transfers between devices  23.7 us (23%)
  local copies, waits for them, and re-layouts  3.96 us (4%)
  between operations  1.02 us (1%)
    pallas_call x1, Pallas kernels, advance(): pl.pallas_call(functools.partial(advance_kernel, comp_count, left_at, rig...  19.6 us
    ppermute x6, starting transfers between devices, over_tiles(): return lax.ppermute(value, AXES, pairs)  17 us
    ppermute x6, starting transfers between devices, over_comp(): return lax.ppermute(value, AXES, pairs)  9.23 us
    ppermute x6, waiting for transfers between devices, over_tiles(): return lax.ppermute(value, AXES, pairs)  8.9 us
    ppermute x3, waiting for transfers between devices, band_shift(): return lax.ppermute(value, AXES, pairs)  8.83 us
    ppermute x6, waiting for transfers between devices, over_comp(): return lax.ppermute(value, AXES, pairs)  5.97 us
    ppermute x3, starting transfers between devices, band_shift(): return lax.ppermute(value, AXES, pairs)  5.82 us
    pallas_call x1, Pallas kernels, regrid(): pl.pallas_call(functools.partial(regrid_body, count, comp_count), out_sha...  5.61 us
  transfers between devices with their start and end apart: 21, of which 11 were waited for; matrix products, arithmetic and copies ran while one was open for 1% of the time, Pallas kernels for 3%

profile of v3, /device:TPU:1, one launch (start us, length us, event | category | flops | bytes accessed | tf_op | source)
XLA Modules:
  0.0 100.2 jit_solution(13322209380895401590)
XLA Ops:
  0.7 2.3 %edges.1 = (f32[2,128,128]{2,1,0:T(8,128)}, f32[2,128,128]{2,1,0:T(8,128)}, f32[4,128,128]{2,1,0:T(8,128)}) custom-call(f32[128,128,128]{2,1,0:T(8,128)} %refs_3_.1), custom_call_target="tpu_custom_call" | custom-call | tf_op jit(solution)/shard_map/edges/pallas_call | solution.py:60
  3.0 4.0 %collective-permute-start = (f32[2,128,128]{2,1,0:T(8,128)}, f32[2,128,128]{2,1,0:T(8,128)S(1)}, u32[]{:S(2)}, u32[]{:S(2)}) collective-permute-start(f32[2,128,128]{2,1,0:T(8,128)} %get-tuple-element.24), channel_id=1, source_target_pairs={{0,2},{1,3},{2,4},{3,5},{4,6},{5,7},{6,8},{7,9},{8,10},{9,11},{10,... | collective-permute-start | bytes 393224 | tf_op jit(solution)/shard_map/ppermute | solution.py:729
  7.1 1.3 %collective-permute-start.1 = (f32[2,128,128]{2,1,0:T(8,128)}, f32[2,128,128]{2,1,0:T(8,128)S(1)}, u32[]{:S(2)}, u32[]{:S(2)}) collective-permute-start(f32[2,128,128]{2,1,0:T(8,128)} %get-tuple-element.25), channel_id=1, source_target_pairs={{2,0},{3,1},{4,2},{5,3},{6,4},{7,5},{8,6},{9,7},{10,8},{11,9},{12,... | collective-permute-start | bytes 393224 | tf_op jit(solution)/shard_map/ppermute | solution.py:729
  8.4 0.2 copy.19
  8.5 0.3 fusion.4
  8.8 0.2 convert_reduce_fusion
  9.0 0.2 select_reduce_fusion
  9.2 0.1 copy.20.refs_1_
  9.5 7.4 %collective-permute-done.1.low_rows.refs_5_ = f32[2,128,128]{2,1,0:T(8,128)S(1)} collective-permute-done((f32[2,128,128]{2,1,0:T(8,128)}, f32[2,128,128]{2,1,0:T(8,128)S(1)}, u32[]{:S(2)}, u32[]{:S(2)}) %collective-permute-start.1) | collective-permute-done | bytes 131104 | tf_op jit(solution)/shard_map/ppermute | solution.py:729
  16.9 0.6 copy-done.4
  17.5 1.8 %frame.1 = f32[4,144,128]{2,1,0:T(8,128)} custom-call(f32[4,128,128]{2,1,0:T(8,128)} %get-tuple-element.26.sides.refs_8_, f32[2,128,128]{2,1,0:T(8,128)} %copy-done.2, f32[2,128,128]{2,1,0:T(8,128)} %copy-done.4), custom_call_target="tpu_custom_call" | custom-call | tf_op jit(solution)/shard_map/frame/pallas_call | solution.py:88
  19.3 0.5 collective-permute-start.2
  19.9 1.3 %collective-permute-done.2.refs_6_.refs_7_ = f32[4,144,128]{2,1,0:T(8,128)S(1)} collective-permute-done((f32[4,144,128]{2,1,0:T(8,128)}, f32[4,144,128]{2,1,0:T(8,128)S(1)}, u32[]{:S(2)}, u32[]{:S(2)}) %collective-permute-start.2) | collective-permute-done | bytes 294944 | tf_op jit(solution)/shard_map/ppermute | solution.py:729
  21.2 0.9 copy-done
  22.2 0.9 copy-done.3
  23.1 0.9 copy-done.5
  24.0 19.6 %advance.1 = (f32[128,128,128]{2,1,0:T(8,128)}, f32[128,128]{1,0:T(8,128)S(1)}, bf16[128,128]{1,0:T(8,128)(2,1)S(1)}, bf16[272,256]{1,0:T(8,128)(2,1)S(1)}, bf16...) custom-call(s32[4]{0:T(128)S(1)} %pad_add_fusion.refs_0_.flags, ...), custom_call_target="tpu_custom_call" | custom-call | flops 2147483648 | bytes 16777216 | tf_op jit(solution)/shard_map/advance/pallas_call | solution.py:352
  43.6 3.1 %collective-permute-start.3 = (bf16[272,256]{1,0:T(8,128)(2,1)S(1)}, bf16[272,256]{1,0:T(8,128)(2,1)S(1)}, u32[]{:S(2)}, u32[]{:S(2)}) collective-permute-start(bf16[272,256]{1,0:T(8,128)(2,1)S(1)} %get-tuple-element.29), channel_id=1, source_target_pairs={{0,8},{1,9},{2,10},{3,11},{4,12},{5,13},{6,14},{7,15},{8,16},{9,17... | collective-permute-start | bytes 417800 | tf_op jit(solution)/shard_map/ppermute | solution.py:770
  46.8 1.9 %collective-permute-start.4 = (bf16[272,256]{1,0:T(8,128)(2,1)S(1)}, bf16[272,256]{1,0:T(8,128)(2,1)S(1)}, u32[]{:S(2)}, u32[]{:S(2)}) collective-permute-start(bf16[272,256]{1,0:T(8,128)(2,1)S(1)} %get-tuple-element.30), channel_id=1, source_target_pairs={{0,16},{1,17},{2,18},{3,19},{4,20},{5,21},{6,22},{7,23},{8,24},{9,... | collective-permute-start | bytes 417800 | tf_op jit(solution)/shard_map/ppermute | solution.py:770
  48.7 1.9 %collective-permute-start.5 = (bf16[272,256]{1,0:T(8,128)(2,1)S(1)}, bf16[272,256]{1,0:T(8,128)(2,1)S(1)}, u32[]{:S(2)}, u32[]{:S(2)}) collective-permute-start(bf16[272,256]{1,0:T(8,128)(2,1)S(1)} %get-tuple-element.31), channel_id=1, source_target_pairs={{0,24},{1,25},{2,26},{3,27},{4,28},{5,29},{6,30},{7,31},{8,0},{9,1... | collective-permute-start | bytes 417800 | tf_op jit(solution)/shard_map/ppermute | solution.py:770
  50.6 0.7 collective-permute-start.11
  51.3 0.7 collective-permute-start.10
  52.0 1.3 %collective-permute-start.9 = (bf16[128,128]{1,0:T(8,128)(2,1)S(1)}, bf16[128,128]{1,0:T(8,128)(2,1)S(1)}, u32[]{:S(2)}, u32[]{:S(2)}) collective-permute-start(bf16[128,128]{1,0:T(8,128)(2,1)S(1)} %get-tuple-element.36.refs_7_), channel_id=1, source_target_pairs={{24,0},{25,1},{26,2},{27,3},{28,4},{29,5},{30,6},{31,7}} | collective-permute-start | bytes 98312 | tf_op jit(solution)/shard_map/ppermute | solution.py:788
  53.3 0.2 collective-permute-done.4.refs_2_
  53.5 1.7 %collective-permute-done.5.refs_3_ = bf16[272,256]{1,0:T(8,128)(2,1)S(1)} collective-permute-done((bf16[272,256]{1,0:T(8,128)(2,1)S(1)}, bf16[272,256]{1,0:T(8,128)(2,1)S(1)}, u32[]{:S(2)}, u32[]{:S(2)}) %collective-permute-start.5) | collective-permute-done | bytes 139296 | tf_op jit(solution)/shard_map/ppermute | solution.py:770
  55.1 0.7 regroup.1
  55.8 1.8 %collective-permute-start.6 = (bf16[208,256]{1,0:T(8,128)(2,1)S(1)}, bf16[208,256]{1,0:T(8,128)(2,1)S(1)}, u32[]{:S(2)}, u32[]{:S(2)}) collective-permute-start(bf16[208,256]{1,0:T(8,128)(2,1)S(1)} %get-tuple-element.33), channel_id=1, source_target_pairs={{0,1},{1,2},{2,3},{3,4},{4,5},{5,6},{6,7},{7,0},{8,9},{9,10},{10,1... | collective-permute-start | bytes 319496 | tf_op jit(solution)/shard_map/ppermute | solution.py:780
  57.6 0.3 collective-permute-start.7
  57.9 4.2 %collective-permute-start.8 = (bf16[208,256]{1,0:T(8,128)(2,1)S(1)}, bf16[208,256]{1,0:T(8,128)(2,1)S(1)}, u32[]{:S(2)}, u32[]{:S(2)}) collective-permute-start(bf16[208,256]{1,0:T(8,128)(2,1)S(1)} %get-tuple-element.35), channel_id=1, source_target_pairs={{0,3},{1,4},{2,5},{3,6},{4,7},{5,0},{6,1},{7,2},{8,11},{9,12},{10,... | collective-permute-start | bytes 319496 | tf_op jit(solution)/shard_map/ppermute | solution.py:780
  62.3 2.8 %collective-permute-done.7.refs_2_ = bf16[208,256]{1,0:T(8,128)(2,1)S(1)} collective-permute-done((bf16[208,256]{1,0:T(8,128)(2,1)S(1)}, bf16[208,256]{1,0:T(8,128)(2,1)S(1)}, u32[]{:S(2)}, u32[]{:S(2)}) %collective-permute-start.7) | collective-permute-done | bytes 106528 | tf_op jit(solution)/shard_map/ppermute | solution.py:780
  65.1 2.2 %collective-permute-done.8.refs_3_ = bf16[208,256]{1,0:T(8,128)(2,1)S(1)} collective-permute-done((bf16[208,256]{1,0:T(8,128)(2,1)S(1)}, bf16[208,256]{1,0:T(8,128)(2,1)S(1)}, u32[]{:S(2)}, u32[]{:S(2)}) %collective-permute-start.8) | collective-permute-done | bytes 106528 | tf_op jit(solution)/shard_map/ppermute | solution.py:780
  67.3 5.6 %regrid.1 = (f32[2,128,128]{2,1,0:T(8,128)S(1)}, f32[128,128]{1,0:T(8,128)S(1)}, bf16[256,128]{1,0:T(8,128)(2,1)S(1)}) custom-call(s32[4]{0:T(128)S(1)} %pad_add_fusion.refs_0_.flags, f32[8]{0:T(128)S(1)} %slice_reduce_fusion.ocean_first, bf16[208,256]{1,0:T(8,128)(2,1)S(1)} %get-tuple-element.32.refs_0_, ...), custom_call_target="tpu_custom_call" | custom-call | flops 2147483648 | bytes 2097152 | tf_op jit(solution)/shard_map/regrid/pallas_call | solution.py:502
  72.9 1.9 %collective-permute-start.17 = (f32[128,128]{1,0:T(8,128)S(1)}, f32[128,128]{1,0:T(8,128)S(1)}, u32[]{:S(2)}, u32[]{:S(2)}) collective-permute-start(f32[128,128]{1,0:T(8,128)S(1)} %get-tuple-element.39.refs_0_), channel_id=1, source_target_pairs={{0,24},{1,25},{2,26},{3,27},{4,28},{5,29},{6,30},{7,31},{8,0},{9,1... | collective-permute-start | bytes 196616 | tf_op jit(solution)/shard_map/ppermute | solution.py:770
  74.9 0.3 collective-permute-start.15
  75.2 1.0 collective-permute-done.17.refs_3_
  76.2 2.1 %collective-permute-done.16.refs_2_ = f32[128,128]{1,0:T(8,128)S(1)} collective-permute-done((f32[128,128]{1,0:T(8,128)S(1)}, f32[128,128]{1,0:T(8,128)S(1)}, u32[]{:S(2)}, u32[]{:S(2)}) %collective-permute-start.16) | collective-permute-done | bytes 65568 | tf_op jit(solution)/shard_map/ppermute | solution.py:770
  78.3 1.1 %collective-permute-done.15.refs_1_ = f32[128,128]{1,0:T(8,128)S(1)} collective-permute-done((f32[128,128]{1,0:T(8,128)S(1)}, f32[128,128]{1,0:T(8,128)S(1)}, u32[]{:S(2)}, u32[]{:S(2)}) %collective-permute-start.15) | collective-permute-done | bytes 65568 | tf_op jit(solution)/shard_map/ppermute | solution.py:770
  79.3 0.2 pick.1
  79.5 5.1 %collective-permute-start.18 = (f32[64,128]{1,0:T(8,128)S(1)}, f32[64,128]{1,0:T(8,128)S(1)}, u32[]{:S(2)}, u32[]{:S(2)}) collective-permute-start(f32[64,128]{1,0:T(8,128)S(1)} %get-tuple-element.42), channel_id=1, source_target_pairs={{0,7},{1,0},{2,1},{3,2},{4,3},{5,4},{6,5},{7,6},{8,15},{9,8},{10,9... | collective-permute-start | bytes 98312 | tf_op jit(solution)/shard_map/ppermute | solution.py:780
  84.6 0.1 copy.21
  84.8 0.7 collective-permute-start.14
  85.4 0.7 collective-permute-start.13
  86.1 1.3 %collective-permute-start.12 = (f32[2,128,128]{2,1,0:T(8,128)S(1)}, f32[2,128,128]{2,1,0:T(8,128)S(1)}, u32[]{:S(2)}, u32[]{:S(2)}) collective-permute-start(f32[2,128,128]{2,1,0:T(8,128)S(1)} %get-tuple-element.38.refs_3_), channel_id=1, source_target_pairs={{0,24},{1,25},{2,26},{3,27},{4,28},{5,29},{6,30},{7,31}} | collective-permute-start | bytes 393224 | tf_op jit(solution)/shard_map/ppermute | solution.py:788
  87.4 2.9 %collective-permute-start.19 = (f32[64,128]{1,0:T(8,128)S(1)}, f32[64,128]{1,0:T(8,128)S(1)}, u32[]{:S(2)}, u32[]{:S(2)}) collective-permute-start(f32[64,128]{1,0:T(8,128)S(1)} %get-tuple-element.43), channel_id=1, source_target_pairs={{0,6},{1,7},{2,0},{3,1},{4,2},{5,3},{6,4},{7,5},{8,14},{9,15},{10,... | collective-permute-start | bytes 98312 | tf_op jit(solution)/shard_map/ppermute | solution.py:780
  90.3 2.7 %collective-permute-start.20 = (f32[64,128]{1,0:T(8,128)S(1)}, f32[64,128]{1,0:T(8,128)S(1)}, u32[]{:S(2)}, u32[]{:S(2)}) collective-permute-start(f32[64,128]{1,0:T(8,128)S(1)} %get-tuple-element.44), channel_id=1, source_target_pairs={{0,5},{1,6},{2,7},{3,0},{4,1},{5,2},{6,3},{7,4},{8,13},{9,14},{10,... | collective-permute-start | bytes 98312 | tf_op jit(solution)/shard_map/ppermute | solution.py:780
  93.1 3.8 %collective-permute-done.20.refs_3_ = f32[64,128]{1,0:T(8,128)S(1)} collective-permute-done((f32[64,128]{1,0:T(8,128)S(1)}, f32[64,128]{1,0:T(8,128)S(1)}, u32[]{:S(2)}, u32[]{:S(2)}) %collective-permute-start.20) | collective-permute-done | bytes 32800 | tf_op jit(solution)/shard_map/ppermute | solution.py:780
  96.9 2.4 %returned.1 = f32[128,128]{1,0:T(8,128)} custom-call(s32[4]{0:T(128)S(1)} %pad_add_fusion.refs_0_.flags, f32[64,128]{1,0:T(8,128)S(1)} %get-tuple-element.41.refs_0_, f32[64,128]{1,0:T(8,128)S(1)} %collective-permute-done.18.refs_1_, f32[64,128]{1,0:T(8,128)S(1)} %collective-permute-done.19.refs_2_, f32[64,128]{1,0:T(8,128)S(1)} %collective-permute-done.20.refs_3_, ...), custom_call_target="tpu_custom_call" | custom-call | tf_op jit(solution)/shard_map/returned/pallas_call | solution.py:683
  99.4 0.8 update.1
  (41 shorter events, 0.5 us)
Async XLA Ops:
  0.6 7.7 %copy-start.11 = (s32[128,1,2,3]{0,2,3,1:T(2,128)S(1)}, s32[128,1,2,3]{0,2,3,1:T(2,128)}, u32[]{:S(2)}) copy-start(s32[128,1,2,3]{0,2,3,1:T(2,128)} %param.11) | copy-start | bytes 9220
  0.6 19.3 %copy-start.10 = (s32[128,128]{1,0:T(8,128)S(1)}, s32[128,128]{1,0:T(8,128)}, u32[]{:S(2)}) copy-start(s32[128,128]{1,0:T(8,128)} %param.10) | copy-start | bytes 196612
  0.7 20.6 %copy-start.9 = (f32[128,8]{0,1:T(8,128)S(1)}, f32[128,8]{0,1:T(8,128)}, u32[]{:S(2)}) copy-start(f32[128,8]{0,1:T(8,128)} %param.14) | copy-start | bytes 12292
  0.7 20.6 %copy-start.7 = (f32[128,128]{1,0:T(8,128)S(1)}, f32[128,128]{1,0:T(8,128)}, u32[]{:S(2)}) copy-start(f32[128,128]{1,0:T(8,128)} %refs_11_.1) | copy-start | bytes 196612
  0.7 20.6 %copy-start.6 = (f32[128,128]{1,0:T(8,128)S(1)}, f32[128,128]{1,0:T(8,128)}, u32[]{:S(2)}) copy-start(f32[128,128]{1,0:T(8,128)} %refs_10_.1) | copy-start | bytes 196612
  0.7 61.4 %copy-start.8 = (f32[8,128]{1,0:T(8,128)S(1)}, f32[8,128]{1,0:T(8,128)}, u32[]{:S(2)}) copy-start(f32[8,128]{1,0:T(8,128)} %refs_5_.1) | copy-start | bytes 12292
  0.7 66.6 %copy-start.1 = (bf16[32,128,128]{2,1,0:T(8,128)(2,1)S(1)}, bf16[32,128,128]{2,1,0:T(8,128)(2,1)}, u32[]{:S(2)}) copy-start(bf16[32,128,128]{2,1,0:T(8,128)(2,1)} %refs_6_.1) | copy-start | bytes 3145732
  3.0 6.5 %collective-permute-start = (f32[2,128,128]{2,1,0:T(8,128)}, f32[2,128,128]{2,1,0:T(8,128)S(1)}, u32[]{:S(2)}, u32[]{:S(2)}) collective-permute-start(f32[2,128,128]{2,1,0:T(8,128)} %get-tuple-element.24), channel_id=1, source_target_pairs={{0,2},{1,3},{2,4},{3,5},{4,6},{5,7},{6,8},{7,9},{8,10},{9,11},{10,... | collective-permute-start | bytes 393224 | tf_op jit(solution)/shard_map/ppermute | solution.py:729
  7.1 9.8 %collective-permute-start.1 = (f32[2,128,128]{2,1,0:T(8,128)}, f32[2,128,128]{2,1,0:T(8,128)S(1)}, u32[]{:S(2)}, u32[]{:S(2)}) collective-permute-start(f32[2,128,128]{2,1,0:T(8,128)} %get-tuple-element.25), channel_id=1, source_target_pairs={{2,0},{3,1},{4,2},{5,3},{6,4},{7,5},{8,6},{9,7},{10,8},{11,9},{12,... | collective-permute-start | bytes 393224 | tf_op jit(solution)/shard_map/ppermute | solution.py:729
  9.5 7.4 %copy-start.2 = (f32[2,128,128]{2,1,0:T(8,128)}, f32[2,128,128]{2,1,0:T(8,128)S(1)}, u32[]{:S(2)}) copy-start(f32[2,128,128]{2,1,0:T(8,128)S(1)} %collective-permute-done.up_rows.refs_4_) | copy-start | bytes 393220
  16.9 0.6 copy-start.4
  19.3 1.9 %collective-permute-start.2 = (f32[4,144,128]{2,1,0:T(8,128)}, f32[4,144,128]{2,1,0:T(8,128)S(1)}, u32[]{:S(2)}, u32[]{:S(2)}) collective-permute-start(f32[4,144,128]{2,1,0:T(8,128)} %frame.1), channel_id=1, source_target_pairs={{0,1},{1,0},{2,3},{3,2},{4,5},{5,4},{6,7},{7,6},{8,9},{9,8},{10,11... | collective-permute-start | bytes 884744 | tf_op jit(solution)/shard_map/ppermute | solution.py:729
  21.2 1.0 copy-start
  22.2 0.9 copy-start.3
  23.1 0.9 copy-start.5
  43.6 8.3 %collective-permute-start.3 = (bf16[272,256]{1,0:T(8,128)(2,1)S(1)}, bf16[272,256]{1,0:T(8,128)(2,1)S(1)}, u32[]{:S(2)}, u32[]{:S(2)}) collective-permute-start(bf16[272,256]{1,0:T(8,128)(2,1)S(1)} %get-tuple-element.29), channel_id=1, source_target_pairs={{0,8},{1,9},{2,10},{3,11},{4,12},{5,13},{6,14},{7,15},{8,16},{9,17... | collective-permute-start | bytes 417800 | tf_op jit(solution)/shard_map/ppermute | solution.py:770
  46.8 6.7 %collective-permute-start.4 = (bf16[272,256]{1,0:T(8,128)(2,1)S(1)}, bf16[272,256]{1,0:T(8,128)(2,1)S(1)}, u32[]{:S(2)}, u32[]{:S(2)}) collective-permute-start(bf16[272,256]{1,0:T(8,128)(2,1)S(1)} %get-tuple-element.30), channel_id=1, source_target_pairs={{0,16},{1,17},{2,18},{3,19},{4,20},{5,21},{6,22},{7,23},{8,24},{9,... | collective-permute-start | bytes 417800 | tf_op jit(solution)/shard_map/ppermute | solution.py:770
  48.7 6.4 %collective-permute-start.5 = (bf16[272,256]{1,0:T(8,128)(2,1)S(1)}, bf16[272,256]{1,0:T(8,128)(2,1)S(1)}, u32[]{:S(2)}, u32[]{:S(2)}) collective-permute-start(bf16[272,256]{1,0:T(8,128)(2,1)S(1)} %get-tuple-element.31), channel_id=1, source_target_pairs={{0,24},{1,25},{2,26},{3,27},{4,28},{5,29},{6,30},{7,31},{8,0},{9,1... | collective-permute-start | bytes 417800 | tf_op jit(solution)/shard_map/ppermute | solution.py:770
  50.6 7.3 %collective-permute-start.11 = (bf16[128,128]{1,0:T(8,128)(2,1)S(1)}, bf16[128,128]{1,0:T(8,128)(2,1)S(1)}, u32[]{:S(2)}, u32[]{:S(2)}) collective-permute-start(bf16[128,128]{1,0:T(8,128)(2,1)S(1)} %get-tuple-element.36.refs_7_), channel_id=1, source_target_pairs={{24,16},{25,17},{26,18},{27,19},{28,20},{29,21},{30,22},{31,23}} | collective-permute-start | bytes 98312 | tf_op jit(solution)/shard_map/ppermute | solution.py:788
  51.3 10.9 %collective-permute-start.10 = (bf16[128,128]{1,0:T(8,128)(2,1)S(1)}, bf16[128,128]{1,0:T(8,128)(2,1)S(1)}, u32[]{:S(2)}, u32[]{:S(2)}) collective-permute-start(bf16[128,128]{1,0:T(8,128)(2,1)S(1)} %get-tuple-element.36.refs_7_), channel_id=1, source_target_pairs={{24,8},{25,9},{26,10},{27,11},{28,12},{29,13},{30,14},{31,15}} | collective-permute-start | bytes 98312 | tf_op jit(solution)/shard_map/ppermute | solution.py:788
  52.0 10.3 %collective-permute-start.9 = (bf16[128,128]{1,0:T(8,128)(2,1)S(1)}, bf16[128,128]{1,0:T(8,128)(2,1)S(1)}, u32[]{:S(2)}, u32[]{:S(2)}) collective-permute-start(bf16[128,128]{1,0:T(8,128)(2,1)S(1)} %get-tuple-element.36.refs_7_), channel_id=1, source_target_pairs={{24,0},{25,1},{26,2},{27,3},{28,4},{29,5},{30,6},{31,7}} | collective-permute-start | bytes 98312 | tf_op jit(solution)/shard_map/ppermute | solution.py:788
  55.8 6.4 %collective-permute-start.6 = (bf16[208,256]{1,0:T(8,128)(2,1)S(1)}, bf16[208,256]{1,0:T(8,128)(2,1)S(1)}, u32[]{:S(2)}, u32[]{:S(2)}) collective-permute-start(bf16[208,256]{1,0:T(8,128)(2,1)S(1)} %get-tuple-element.33), channel_id=1, source_target_pairs={{0,1},{1,2},{2,3},{3,4},{4,5},{5,6},{6,7},{7,0},{8,9},{9,10},{10,1... | collective-permute-start | bytes 319496 | tf_op jit(solution)/shard_map/ppermute | solution.py:780
  57.6 7.5 %collective-permute-start.7 = (bf16[208,256]{1,0:T(8,128)(2,1)S(1)}, bf16[208,256]{1,0:T(8,128)(2,1)S(1)}, u32[]{:S(2)}, u32[]{:S(2)}) collective-permute-start(bf16[208,256]{1,0:T(8,128)(2,1)S(1)} %get-tuple-element.34), channel_id=1, source_target_pairs={{0,2},{1,3},{2,4},{3,5},{4,6},{5,7},{6,0},{7,1},{8,10},{9,11},{10,... | collective-permute-start | bytes 319496 | tf_op jit(solution)/shard_map/ppermute | solution.py:780
  57.9 9.4 %collective-permute-start.8 = (bf16[208,256]{1,0:T(8,128)(2,1)S(1)}, bf16[208,256]{1,0:T(8,128)(2,1)S(1)}, u32[]{:S(2)}, u32[]{:S(2)}) collective-permute-start(bf16[208,256]{1,0:T(8,128)(2,1)S(1)} %get-tuple-element.35), channel_id=1, source_target_pairs={{0,3},{1,4},{2,5},{3,6},{4,7},{5,0},{6,1},{7,2},{8,11},{9,12},{10,... | collective-permute-start | bytes 319496 | tf_op jit(solution)/shard_map/ppermute | solution.py:780
  72.9 3.2 %collective-permute-start.17 = (f32[128,128]{1,0:T(8,128)S(1)}, f32[128,128]{1,0:T(8,128)S(1)}, u32[]{:S(2)}, u32[]{:S(2)}) collective-permute-start(f32[128,128]{1,0:T(8,128)S(1)} %get-tuple-element.39.refs_0_), channel_id=1, source_target_pairs={{0,24},{1,25},{2,26},{3,27},{4,28},{5,29},{6,30},{7,31},{8,0},{9,1... | collective-permute-start | bytes 196616 | tf_op jit(solution)/shard_map/ppermute | solution.py:770
  74.8 3.4 %collective-permute-start.16 = (f32[128,128]{1,0:T(8,128)S(1)}, f32[128,128]{1,0:T(8,128)S(1)}, u32[]{:S(2)}, u32[]{:S(2)}) collective-permute-start(f32[128,128]{1,0:T(8,128)S(1)} %get-tuple-element.39.refs_0_), channel_id=1, source_target_pairs={{0,16},{1,17},{2,18},{3,19},{4,20},{5,21},{6,22},{7,23},{8,24},{9,... | collective-permute-start | bytes 196616 | tf_op jit(solution)/shard_map/ppermute | solution.py:770
  74.9 4.5 %collective-permute-start.15 = (f32[128,128]{1,0:T(8,128)S(1)}, f32[128,128]{1,0:T(8,128)S(1)}, u32[]{:S(2)}, u32[]{:S(2)}) collective-permute-start(f32[128,128]{1,0:T(8,128)S(1)} %get-tuple-element.39.refs_0_), channel_id=1, source_target_pairs={{0,8},{1,9},{2,10},{3,11},{4,12},{5,13},{6,14},{7,15},{8,16},{9,17... | collective-permute-start | bytes 196616 | tf_op jit(solution)/shard_map/ppermute | solution.py:770
  79.5 10.8 %collective-permute-start.18 = (f32[64,128]{1,0:T(8,128)S(1)}, f32[64,128]{1,0:T(8,128)S(1)}, u32[]{:S(2)}, u32[]{:S(2)}) collective-permute-start(f32[64,128]{1,0:T(8,128)S(1)} %get-tuple-element.42), channel_id=1, source_target_pairs={{0,7},{1,0},{2,1},{3,2},{4,3},{5,4},{6,5},{7,6},{8,15},{9,8},{10,9... | collective-permute-start | bytes 98312 | tf_op jit(solution)/shard_map/ppermute | solution.py:780
  84.8 14.6 %collective-permute-start.14 = (f32[2,128,128]{2,1,0:T(8,128)S(1)}, f32[2,128,128]{2,1,0:T(8,128)S(1)}, u32[]{:S(2)}, u32[]{:S(2)}) collective-permute-start(f32[2,128,128]{2,1,0:T(8,128)S(1)} %get-tuple-element.38.refs_3_), channel_id=1, source_target_pairs={{16,24},{17,25},{18,26},{19,27},{20,28},{21,29},{22,30},{23,31}} | collective-permute-start | bytes 393224 | tf_op jit(solution)/shard_map/ppermute | solution.py:788
  85.4 13.9 %collective-permute-start.13 = (f32[2,128,128]{2,1,0:T(8,128)S(1)}, f32[2,128,128]{2,1,0:T(8,128)S(1)}, u32[]{:S(2)}, u32[]{:S(2)}) collective-permute-start(f32[2,128,128]{2,1,0:T(8,128)S(1)} %get-tuple-element.38.refs_3_), channel_id=1, source_target_pairs={{8,24},{9,25},{10,26},{11,27},{12,28},{13,29},{14,30},{15,31}} | collective-permute-start | bytes 393224 | tf_op jit(solution)/shard_map/ppermute | solution.py:788
  86.1 13.3 %collective-permute-start.12 = (f32[2,128,128]{2,1,0:T(8,128)S(1)}, f32[2,128,128]{2,1,0:T(8,128)S(1)}, u32[]{:S(2)}, u32[]{:S(2)}) collective-permute-start(f32[2,128,128]{2,1,0:T(8,128)S(1)} %get-tuple-element.38.refs_3_), channel_id=1, source_target_pairs={{0,24},{1,25},{2,26},{3,27},{4,28},{5,29},{6,30},{7,31}} | collective-permute-start | bytes 393224 | tf_op jit(solution)/shard_map/ppermute | solution.py:788
  87.4 5.7 %collective-permute-start.19 = (f32[64,128]{1,0:T(8,128)S(1)}, f32[64,128]{1,0:T(8,128)S(1)}, u32[]{:S(2)}, u32[]{:S(2)}) collective-permute-start(f32[64,128]{1,0:T(8,128)S(1)} %get-tuple-element.43), channel_id=1, source_target_pairs={{0,6},{1,7},{2,0},{3,1},{4,2},{5,3},{6,4},{7,5},{8,14},{9,15},{10,... | collective-permute-start | bytes 98312 | tf_op jit(solution)/shard_map/ppermute | solution.py:780
  90.3 6.6 %collective-permute-start.20 = (f32[64,128]{1,0:T(8,128)S(1)}, f32[64,128]{1,0:T(8,128)S(1)}, u32[]{:S(2)}, u32[]{:S(2)}) collective-permute-start(f32[64,128]{1,0:T(8,128)S(1)} %get-tuple-element.44), channel_id=1, source_target_pairs={{0,5},{1,6},{2,7},{3,0},{4,1},{5,2},{6,3},{7,4},{8,13},{9,14},{10,... | collective-permute-start | bytes 98312 | tf_op jit(solution)/shard_map/ppermute | solution.py:780

commit v4 on v3

--- a/solution.py
+++ b/solution.py
@@ -35,11 +35,11 @@
     return jnp.dot(a, b, preferred_element_type=F32)
 
 
-def edges_kernel(state, first_rows, last_rows, sides, left, right, sems):
+def edges_kernel(state, first_rows, last_rows, sides, top, bottom, left, right, sems):
     rows, cols, _ = state.shape
     copies = [
-        pltpu.make_async_copy(state.at[pl.ds(0, 2)], first_rows, sems.at[0]),
-        pltpu.make_async_copy(state.at[pl.ds(rows - 2, 2)], last_rows, sems.at[1]),
+        pltpu.make_async_copy(state.at[pl.ds(0, 2)], top, sems.at[0]),
+        pltpu.make_async_copy(state.at[pl.ds(rows - 2, 2)], bottom, sems.at[1]),
         pltpu.make_async_copy(state.at[:, pl.ds(0, EDGE)], left, sems.at[2]),
         pltpu.make_async_copy(state.at[:, pl.ds(cols - EDGE, EDGE)], right, sems.at[3]),
     ]
@@ -47,6 +47,8 @@
         copy.start()
     for copy in copies:
         copy.wait()
+    first_rows[...] = top[...].astype(BF16)
+    last_rows[...] = bottom[...].astype(BF16)
     for i in range(2):
         sides[i] = left[:, i, :]
         sides[2 + i] = right[:, EDGE - 2 + i, :]
@@ -54,20 +56,22 @@
 
 def take_edges(state):
     rows, cols, levels = state.shape
-    slab = jax.ShapeDtypeStruct((2, cols, levels), F32)
+    slab = jax.ShapeDtypeStruct((2, cols, levels), BF16)
     side = jax.ShapeDtypeStruct((4, rows, levels), F32)
     vmem = pl.BlockSpec(memory_space=pltpu.VMEM)
     return pl.pallas_call(
         edges_kernel,
         out_shape=(slab, slab, side),
-        in_specs=[pl.BlockSpec(memory_space=pl.ANY)],
+        in_specs=[pl.BlockSpec(memory_space=pltpu.HBM)],
         out_specs=(vmem,) * 3,
         scratch_shapes=[
+            pltpu.VMEM((2, cols, levels), F32),
+            pltpu.VMEM((2, cols, levels), F32),
             pltpu.VMEM((rows, EDGE, levels), F32),
             pltpu.VMEM((rows, EDGE, levels), F32),
             pltpu.SemaphoreType.DMA((4,)),
         ],
-        compiler_params=pltpu.CompilerParams(vmem_limit_bytes=56 * MIB),
+        compiler_params=pltpu.CompilerParams(vmem_limit_bytes=16 * MIB),
         name="edges",
     )(state)
 
@@ -76,10 +80,12 @@
     _, rows, levels = sides.shape
     cols = up_rows.shape[1]
     framed[...] = jnp.zeros(framed.shape, F32)
+    above = up_rows[1].astype(F32)
+    below = low_rows[0].astype(F32)
     for i, col in enumerate((0, 1, cols - 2, cols - 1)):
         framed[i, EDGE : EDGE + rows, :] = sides[i]
-        framed[i, EDGE - 1 : EDGE, :] = up_rows[1, col : col + 1, :]
-        framed[i, EDGE + rows : EDGE + rows + 1, :] = low_rows[0, col : col + 1, :]
+        framed[i, EDGE - 1 : EDGE, :] = above[col : col + 1, :]
+        framed[i, EDGE + rows : EDGE + rows + 1, :] = below[col : col + 1, :]
 
 
 def frame_sides(sides, up_rows, low_rows):
@@ -90,7 +96,7 @@
         out_shape=jax.ShapeDtypeStruct((count, rows + 2 * EDGE, levels), F32),
         in_specs=[vmem] * 3,
         out_specs=vmem,
-        compiler_params=pltpu.CompilerParams(vmem_limit_bytes=56 * MIB),
+        compiler_params=pltpu.CompilerParams(vmem_limit_bytes=16 * MIB),
         name="frame",
     )(sides, up_rows, low_rows)
 
@@ -133,9 +139,10 @@
     ocean = flags[0] == 1
     mix = jnp.where(ocean, mix_ocn[...], mix_atm[...])
     mix_high, mix_low = split_two(mix)
-    weights[:levels, :] = mix_high
-    weights[levels : 2 * levels, :] = mix_high
-    weights[2 * levels :, :] = mix_low
+    weights[:levels, :levels] = mix_high
+    weights[levels:, :levels] = mix_high
+    weights[:levels, levels:] = mix_low
+    weights[levels:, levels:] = mix_low
     sea_copy[...] = mask[...].astype(BF16)
     map_high, map_low = split_two(flux_map[...])
     flux_weights[...] = jnp.concatenate(
@@ -145,8 +152,8 @@
         ],
         axis=0,
     ).astype(BF16)
-    values[0:2, EDGE : EDGE + cols, :] = up_rows[...]
-    values[rows + 2 : rows + 4, EDGE : EDGE + cols, :] = low_rows[...]
+    values[0:2, EDGE : EDGE + cols, :] = up_rows[...].astype(F32)
+    values[rows + 2 : rows + 4, EDGE : EDGE + cols, :] = low_rows[...].astype(F32)
     for r, i in ((1, EDGE - 1), (rows + 2, EDGE + rows)):
         values[r, EDGE - 1 : EDGE, :] = left_cols[1, i : i + 1, :]
         values[r, EDGE + cols : EDGE + cols + 1, :] = right_cols[0, i : i + 1, :]
@@ -160,9 +167,8 @@
 
     def stage(refs, row, total):
         line = SMOOTHING * total
-        high, low = split_two(line)
         refs[0][row] = line
-        refs[1][row * cols : (row + 1) * cols, :] = jnp.concatenate([high, low, high], axis=1)
+        refs[1][row * cols : (row + 1) * cols, :] = side_by_side(line)
 
     def note_top(q, lines):
         lanes = lax.broadcasted_iota(jnp.int32, (cols, levels), 1)
@@ -176,7 +182,8 @@
         refs[2][: count * cols, :] = dot_nn(refs[1][: count * cols, :], weights[...])
 
     def finish(refs, row):
-        return refs[0][row] + PHYSICS * jnp.tanh(refs[2][row * cols : (row + 1) * cols, :])
+        part = refs[2][row * cols : (row + 1) * cols, :]
+        return refs[0][row] + PHYSICS * jnp.tanh(part[:, :levels] + part[:, levels:])
 
     def gather_row(ref, i):
         here = ref[i, EDGE : EDGE + cols, :] + (
@@ -238,10 +245,10 @@
                 line = finish(second, row)
                 staged[slot, row] = line
                 both = line + moved[q * CHUNK + row + 1, EDGE : EDGE + cols, :]
-                later_pairs[row * cols : (row + 1) * cols, : 2 * levels] = side_by_side(both)
+                later_pairs[row * cols : (row + 1) * cols, :] = side_by_side(both)
             put(q, slot).start()
             note_top(q, [staged[slot, row] for row in range(CHUNK)])
-            flux = dot_nt(flux_weights[...], later_pairs[:, : 2 * levels])
+            flux = dot_nt(flux_weights[...], later_pairs[...])
             flux = flux[:flux_count] + flux[flux_count:]
             for row in range(CHUNK):
                 r = q * CHUNK + row
@@ -344,7 +351,7 @@
     fluxes = flux_map_t.shape[0]
     vmem = pl.BlockSpec(memory_space=pltpu.VMEM)
     smem = pl.BlockSpec(memory_space=pltpu.SMEM)
-    hbm = pl.BlockSpec(memory_space=pl.ANY)
+    hbm = pl.BlockSpec(memory_space=pltpu.HBM)
     entry = jax.ShapeDtypeStruct(
         (source_column.shape[0] + labels.shape[0], fluxes // comp_count * cols), BF16
     )
@@ -364,12 +371,12 @@
             pltpu.VMEM((rows + 2, cols + 2 * EDGE, levels), F32),
             pltpu.VMEM((2, rows, levels), F32),
             pltpu.VMEM((CHUNK, cols, levels), F32),
-            pltpu.VMEM((CHUNK * cols, 3 * levels), BF16),
-            pltpu.VMEM((CHUNK * cols, levels), F32),
+            pltpu.VMEM((CHUNK * cols, 2 * levels), BF16),
+            pltpu.VMEM((CHUNK * cols, 2 * levels), F32),
             pltpu.VMEM((CHUNK, cols, levels), F32),
-            pltpu.VMEM((CHUNK * cols, 3 * levels), BF16),
-            pltpu.VMEM((CHUNK * cols, levels), F32),
-            pltpu.VMEM((3 * levels, levels), BF16),
+            pltpu.VMEM((CHUNK * cols, 2 * levels), BF16),
+            pltpu.VMEM((CHUNK * cols, 2 * levels), F32),
+            pltpu.VMEM((2 * levels, 2 * levels), BF16),
             pltpu.VMEM((2 * fluxes, 2 * levels), BF16),
             pltpu.VMEM((rows * fluxes, cols), F32),
             pltpu.VMEM((2, CHUNK, cols, levels), F32),
@@ -558,12 +565,13 @@
 
 def update_kernel(groups, flags, state, *refs):
     parts = refs[:groups]
-    mask, ocean_map, out, held, table, wide, in_sems, out_sems = refs[groups:]
+    mask, ocean_map, out, token, held, table, wide, in_sems, out_sems = refs[groups:]
     rows, cols, levels = state.shape
     share = parts[0].shape[0]
     flux_count = groups * share
     chunks = rows // LINES
     depth = LINES * flux_count
+    token[...] = jnp.zeros(token.shape, F32)
 
     def fetch(q):
         return pltpu.make_async_copy(
@@ -618,12 +626,15 @@
     depth = LINES * ocean_map.shape[0]
     vmem = pl.BlockSpec(memory_space=pltpu.VMEM)
     smem = pl.BlockSpec(memory_space=pltpu.SMEM)
-    hbm = pl.BlockSpec(memory_space=pl.ANY)
+    hbm = pl.BlockSpec(memory_space=pltpu.HBM)
     return pl.pallas_call(
         functools.partial(update_kernel, len(parts)),
-        out_shape=jax.ShapeDtypeStruct(state.shape, F32),
+        out_shape=(
+            jax.ShapeDtypeStruct(state.shape, F32),
+            jax.ShapeDtypeStruct((EDGE, levels), F32),
+        ),
         in_specs=[smem, hbm] + [vmem] * (len(parts) + 2),
-        out_specs=hbm,
+        out_specs=(hbm, vmem),
         input_output_aliases={1: 0},
         scratch_shapes=[
             pltpu.VMEM(state.shape, F32),
@@ -644,7 +655,7 @@
 
 def returned_kernel(groups, flags, *refs):
     picked = refs[:groups]
-    weight_column, row_line, weights, mask, surface, new_surface, out, total = refs[groups:]
+    weight_column, row_line, weights, mask, surface, new_surface, token, out, total = refs[groups:]
     rows, cols = mask.shape
     weight_count = weights.shape[0]
 
@@ -675,7 +686,7 @@
         out[...] = jnp.where(mask[...] > 0.5, back, surface[...])
 
 
-def returned(flags, picked, weight_column, row_line, weights, mask, surface, new_surface):
+def returned(flags, picked, weight_column, row_line, weights, mask, surface, new_surface, token):
     rows, cols = mask.shape
     entry_total = weight_column.shape[0]
     vmem = pl.BlockSpec(memory_space=pltpu.VMEM)
@@ -683,12 +694,12 @@
     return pl.pallas_call(
         functools.partial(returned_kernel, len(picked)),
         out_shape=jax.ShapeDtypeStruct((rows, cols), F32),
-        in_specs=[smem] + [vmem] * (len(picked) + 6),
+        in_specs=[smem] + [vmem] * (len(picked) + 7),
         out_specs=vmem,
         scratch_shapes=[pltpu.VMEM((entry_total, cols), F32)],
         compiler_params=pltpu.CompilerParams(vmem_limit_bytes=16 * MIB),
         name="returned",
-    )(flags, *picked, weight_column, row_line, weights, mask, surface, new_surface)
+    )(flags, *picked, weight_column, row_line, weights, mask, surface, new_surface, token)
 
 
 def local(
@@ -808,10 +819,11 @@
     new_surface, picked = picks[0], picks[1:]
     arrived = [over_tiles(picked[n], -offsets[n], ocean_comp) for n in range(neighbours)]
     fields = [with_ocean(forcing, c, False) for c in range(ocean_comp)] + [forcing]
-    final_state = update(flags, moved, fields, mask, ocean_map)
+    final_state, token = update(flags, moved, fields, mask, ocean_map)
     weight_column = (packed_labels // rows)[:, None]
     surface_out = returned(
-        flags, arrived, weight_column, sources[None, :], regrid_weights, mask, surface, new_surface
+        flags, arrived, weight_column, sources[None, :], regrid_weights, mask, surface, new_surface,
+        token,
     )
     return (final_state, surface_out)
 

time: 101 us -> 96.4 us (0.954)
  waiting for transfers between devices: 23.7 us -> 17.3 us
  starting transfers between devices: 37.3 us -> 43.4 us
  Pallas kernels: 33.4 us -> 29.4 us
    ppermute x3, waiting for transfers between devices: 8.83 us -> 5.14 us  [band_shift(): return lax.ppermute(value, AXES, pairs)]
    ppermute x6, starting transfers between devices: 9.23 us -> 11.9 us  [over_comp(): return lax.ppermute(value, AXES, pairs)]
    ppermute x6, starting transfers between devices: 5.25 us -> 7.09 us  [with_ocean(): return lax.ppermute(value, AXES, pairs)]
    pallas_call x1, Pallas kernels: 1.78 us -> 0.02 us  [frame_sides(): pl.pallas_call(frame_kernel, out_shape=jax.ShapeDtypeStruct((count, rows...]
    ppermute x6, waiting for transfers between devices: 5.97 us -> 4.33 us  [over_comp(): return lax.ppermute(value, AXES, pairs)]
    pallas_call x1, Pallas kernels: 2.3 us -> 0.69 us  [take_edges(): pl.pallas_call(edges_kernel, out_shape=(slab, slab, side), in_specs=[pl.B...]
    ppermute x6, starting transfers between devices: 17 us -> 18.1 us  [over_tiles(): return lax.ppermute(value, AXES, pairs)]
    ppermute x6, waiting for transfers between devices: 8.9 us -> 7.87 us  [over_tiles(): return lax.ppermute(value, AXES, pairs)]
  transfers between devices with their start and end apart: 21 -> 21, of which waited for: 11 -> 9; matrix products, arithmetic and copies ran while one was open for 1% -> 1% of each run, Pallas kernels for 3% -> 2%
where the time goes in v4:
time: 96.4 us; the launch traced here: 96 us
  starting transfers between devices  43.4 us (45%)
  Pallas kernels  29.4 us (30%)
  waiting for transfers between devices  17.3 us (18%)
  local copies, waits for them, and re-layouts  3.94 us (4%)
  between operations  1.01 us (1%)
    pallas_call x1, Pallas kernels, advance(): pl.pallas_call(functools.partial(advance_kernel, comp_count, left_at, rig...  19 us
    ppermute x6, starting transfers between devices, over_tiles(): return lax.ppermute(value, AXES, pairs)  18.1 us
    ppermute x6, starting transfers between devices, over_comp(): return lax.ppermute(value, AXES, pairs)  11.9 us
    ppermute x6, waiting for transfers between devices, over_tiles(): return lax.ppermute(value, AXES, pairs)  7.87 us
    ppermute x6, starting transfers between devices, with_ocean(): return lax.ppermute(value, AXES, pairs)  7.09 us
    ppermute x3, starting transfers between devices, band_shift(): return lax.ppermute(value, AXES, pairs)  6.35 us
    pallas_call x1, Pallas kernels, regrid(): pl.pallas_call(functools.partial(regrid_body, count, comp_count), out_sha...  5.59 us
    ppermute x3, waiting for transfers between devices, band_shift(): return lax.ppermute(value, AXES, pairs)  5.14 us
  transfers between devices with their start and end apart: 21, of which 9 were waited for; matrix products, arithmetic and copies ran while one was open for 1% of the time, Pallas kernels for 2%

profile of v4, /device:TPU:1, one launch (start us, length us, event | category | flops | bytes accessed | tf_op | source)
XLA Modules:
  0.0 96.0 jit_solution(2228147483557784574)
XLA Ops:
  0.6 0.0 copy-start
  0.6 3.4 %copy-done = f32[128,128,128]{2,1,0:T(8,128)S(1)} copy-done((f32[128,128,128]{2,1,0:T(8,128)S(1)}, f32[128,128,128]{2,1,0:T(8,128)}, u32[]{:S(2)}) %copy-start) | copy-done | bytes 8388632
  4.1 0.7 edges.1
  4.8 4.0 %collective-permute-start = (bf16[2,128,128]{2,1,0:T(8,128)(2,1)S(1)}, bf16[2,128,128]{2,1,0:T(8,128)(2,1)S(1)}, u32[]{:S(2)}, u32[]{:S(2)}) collective-permute-start(bf16[2,128,128]{2,1,0:T(8,128)(2,1)S(1)} %get-tuple-element.26), channel_id=1, source_target_pairs={{0,2},{1,3},{2,4},{3,5},{4,6},{5,7},{6,8},{7,9},{8,10},{9,11},{10,... | collective-permute-start | bytes 196616 | tf_op jit(solution)/shard_map/ppermute | solution.py:740
  8.8 1.3 %collective-permute-start.1 = (bf16[2,128,128]{2,1,0:T(8,128)(2,1)S(1)}, bf16[2,128,128]{2,1,0:T(8,128)(2,1)S(1)}, u32[]{:S(2)}, u32[]{:S(2)}) collective-permute-start(bf16[2,128,128]{2,1,0:T(8,128)(2,1)S(1)} %get-tuple-element.27), channel_id=1, source_target_pairs={{2,0},{3,1},{4,2},{5,3},{6,4},{7,5},{8,6},{9,7},{10,8},{11,9},{12,... | collective-permute-start | bytes 196616 | tf_op jit(solution)/shard_map/ppermute | solution.py:740
  10.1 0.2 copy.19
  10.3 0.3 fusion.4
  10.6 0.2 convert_reduce_fusion
  10.8 0.2 select_reduce_fusion
  10.9 0.1 copy.20.refs_1_
  11.1 4.0 %collective-permute-done.1.low_rows.refs_5_ = bf16[2,128,128]{2,1,0:T(8,128)(2,1)S(1)} collective-permute-done((bf16[2,128,128]{2,1,0:T(8,128)(2,1)S(1)}, bf16[2,128,128]{2,1,0:T(8,128)(2,1)S(1)}, u32[]{:S(2)}, u32[]{:S(2)}) %collective-permute-start.1) | collective-permute-done | bytes 65568 | tf_op jit(solution)/shard_map/ppermute | solution.py:740
  15.2 1.0 %collective-permute-start.2 = (f32[4,144,128]{2,1,0:T(8,128)S(1)}, f32[4,144,128]{2,1,0:T(8,128)S(1)}, u32[]{:S(2)}, u32[]{:S(2)}) collective-permute-start(f32[4,144,128]{2,1,0:T(8,128)S(1)} %frame.1), channel_id=1, source_target_pairs={{0,1},{1,0},{2,3},{3,2},{4,5},{5,4},{6,7},{7,6},{8,9},{9,8},{10,11... | collective-permute-start | bytes 884744 | tf_op jit(solution)/shard_map/ppermute | solution.py:740
  16.2 0.1 pad_add_fusion.refs_0_.flags
  16.3 1.1 %collective-permute-done.2.refs_6_.refs_7_ = f32[4,144,128]{2,1,0:T(8,128)S(1)} collective-permute-done((f32[4,144,128]{2,1,0:T(8,128)S(1)}, f32[4,144,128]{2,1,0:T(8,128)S(1)}, u32[]{:S(2)}, u32[]{:S(2)}) %collective-permute-start.2) | collective-permute-done | bytes 294944 | tf_op jit(solution)/shard_map/ppermute | solution.py:740
  17.4 19.0 %advance.1 = (f32[128,128,128]{2,1,0:T(8,128)}, f32[128,128]{1,0:T(8,128)S(1)}, bf16[128,128]{1,0:T(8,128)(2,1)S(1)}, bf16[272,256]{1,0:T(8,128)(2,1)S(1)}, bf16...) custom-call(s32[4]{0:T(128)S(1)} %pad_add_fusion.refs_0_.flags, ...), custom_call_target="tpu_custom_call" | custom-call | flops 2147483648 | bytes 16777216 | tf_op jit(solution)/shard_map/advance/pallas_call | solution.py:359
  36.4 3.7 %collective-permute-start.3 = (bf16[272,256]{1,0:T(8,128)(2,1)S(1)}, bf16[272,256]{1,0:T(8,128)(2,1)S(1)}, u32[]{:S(2)}, u32[]{:S(2)}) collective-permute-start(bf16[272,256]{1,0:T(8,128)(2,1)S(1)} %get-tuple-element.31), channel_id=1, source_target_pairs={{0,8},{1,9},{2,10},{3,11},{4,12},{5,13},{6,14},{7,15},{8,16},{9,17... | collective-permute-start | bytes 417800 | tf_op jit(solution)/shard_map/ppermute | solution.py:781
  40.2 2.8 %collective-permute-start.4 = (bf16[272,256]{1,0:T(8,128)(2,1)S(1)}, bf16[272,256]{1,0:T(8,128)(2,1)S(1)}, u32[]{:S(2)}, u32[]{:S(2)}) collective-permute-start(bf16[272,256]{1,0:T(8,128)(2,1)S(1)} %get-tuple-element.32), channel_id=1, source_target_pairs={{0,16},{1,17},{2,18},{3,19},{4,20},{5,21},{6,22},{7,23},{8,24},{9,... | collective-permute-start | bytes 417800 | tf_op jit(solution)/shard_map/ppermute | solution.py:781
  43.0 1.9 %collective-permute-start.5 = (bf16[272,256]{1,0:T(8,128)(2,1)S(1)}, bf16[272,256]{1,0:T(8,128)(2,1)S(1)}, u32[]{:S(2)}, u32[]{:S(2)}) collective-permute-start(bf16[272,256]{1,0:T(8,128)(2,1)S(1)} %get-tuple-element.33), channel_id=1, source_target_pairs={{0,24},{1,25},{2,26},{3,27},{4,28},{5,29},{6,30},{7,31},{8,0},{9,1... | collective-permute-start | bytes 417800 | tf_op jit(solution)/shard_map/ppermute | solution.py:781
  44.9 1.3 %collective-permute-start.9 = (bf16[128,128]{1,0:T(8,128)(2,1)S(1)}, bf16[128,128]{1,0:T(8,128)(2,1)S(1)}, u32[]{:S(2)}, u32[]{:S(2)}) collective-permute-start(bf16[128,128]{1,0:T(8,128)(2,1)S(1)} %get-tuple-element.38.refs_7_), channel_id=1, source_target_pairs={{24,0},{25,1},{26,2},{27,3},{28,4},{29,5},{30,6},{31,7}} | collective-permute-start | bytes 98312 | tf_op jit(solution)/shard_map/ppermute | solution.py:799
  46.2 0.7 collective-permute-start.10
  46.9 0.7 collective-permute-start.11
  47.6 0.8 collective-permute-done.4.refs_2_
  48.4 1.1 %collective-permute-done.5.refs_3_ = bf16[272,256]{1,0:T(8,128)(2,1)S(1)} collective-permute-done((bf16[272,256]{1,0:T(8,128)(2,1)S(1)}, bf16[272,256]{1,0:T(8,128)(2,1)S(1)}, u32[]{:S(2)}, u32[]{:S(2)}) %collective-permute-start.5) | collective-permute-done | bytes 139296 | tf_op jit(solution)/shard_map/ppermute | solution.py:781
  49.4 0.7 regroup.1
  50.1 1.1 %collective-permute-start.6 = (bf16[208,256]{1,0:T(8,128)(2,1)S(1)}, bf16[208,256]{1,0:T(8,128)(2,1)S(1)}, u32[]{:S(2)}, u32[]{:S(2)}) collective-permute-start(bf16[208,256]{1,0:T(8,128)(2,1)S(1)} %get-tuple-element.35), channel_id=1, source_target_pairs={{0,1},{1,2},{2,3},{3,4},{4,5},{5,6},{6,7},{7,0},{8,9},{9,10},{10,1... | collective-permute-start | bytes 319496 | tf_op jit(solution)/shard_map/ppermute | solution.py:791
  51.2 1.3 %collective-permute-start.7 = (bf16[208,256]{1,0:T(8,128)(2,1)S(1)}, bf16[208,256]{1,0:T(8,128)(2,1)S(1)}, u32[]{:S(2)}, u32[]{:S(2)}) collective-permute-start(bf16[208,256]{1,0:T(8,128)(2,1)S(1)} %get-tuple-element.36), channel_id=1, source_target_pairs={{0,2},{1,3},{2,4},{3,5},{4,6},{5,7},{6,0},{7,1},{8,10},{9,11},{10,... | collective-permute-start | bytes 319496 | tf_op jit(solution)/shard_map/ppermute | solution.py:791
  52.5 4.5 %collective-permute-start.8 = (bf16[208,256]{1,0:T(8,128)(2,1)S(1)}, bf16[208,256]{1,0:T(8,128)(2,1)S(1)}, u32[]{:S(2)}, u32[]{:S(2)}) collective-permute-start(bf16[208,256]{1,0:T(8,128)(2,1)S(1)} %get-tuple-element.37), channel_id=1, source_target_pairs={{0,3},{1,4},{2,5},{3,6},{4,7},{5,0},{6,1},{7,2},{8,11},{9,12},{10,... | collective-permute-start | bytes 319496 | tf_op jit(solution)/shard_map/ppermute | solution.py:791
  57.0 0.1 slice_reduce_fusion.ocean_first
  57.2 1.7 %collective-permute-done.7.refs_2_ = bf16[208,256]{1,0:T(8,128)(2,1)S(1)} collective-permute-done((bf16[208,256]{1,0:T(8,128)(2,1)S(1)}, bf16[208,256]{1,0:T(8,128)(2,1)S(1)}, u32[]{:S(2)}, u32[]{:S(2)}) %collective-permute-start.7) | collective-permute-done | bytes 106528 | tf_op jit(solution)/shard_map/ppermute | solution.py:791
  58.9 2.8 %collective-permute-done.8.refs_3_ = bf16[208,256]{1,0:T(8,128)(2,1)S(1)} collective-permute-done((bf16[208,256]{1,0:T(8,128)(2,1)S(1)}, bf16[208,256]{1,0:T(8,128)(2,1)S(1)}, u32[]{:S(2)}, u32[]{:S(2)}) %collective-permute-start.8) | collective-permute-done | bytes 106528 | tf_op jit(solution)/shard_map/ppermute | solution.py:791
  61.7 5.6 %regrid.1 = (f32[2,128,128]{2,1,0:T(8,128)S(1)}, f32[128,128]{1,0:T(8,128)S(1)}, bf16[256,128]{1,0:T(8,128)(2,1)S(1)}) custom-call(s32[4]{0:T(128)S(1)} %pad_add_fusion.refs_0_.flags, f32[8]{0:T(128)S(1)} %slice_reduce_fusion.ocean_first, bf16[208,256]{1,0:T(8,128)(2,1)S(1)} %get-tuple-element.34.refs_0_, ...), custom_call_target="tpu_custom_call" | custom-call | flops 2147483648 | bytes 2097152 | tf_op jit(solution)/shard_map/regrid/pallas_call | solution.py:509
  67.3 1.3 %collective-permute-start.15 = (f32[128,128]{1,0:T(8,128)S(1)}, f32[128,128]{1,0:T(8,128)S(1)}, u32[]{:S(2)}, u32[]{:S(2)}) collective-permute-start(f32[128,128]{1,0:T(8,128)S(1)} %get-tuple-element.42.refs_0_), channel_id=1, source_target_pairs={{0,8},{1,9},{2,10},{3,11},{4,12},{5,13},{6,14},{7,15},{8,16},{9,17... | collective-permute-start | bytes 196616 | tf_op jit(solution)/shard_map/ppermute | solution.py:781
  68.6 0.1 copy.21
  68.7 3.1 %collective-permute-start.12 = (f32[2,128,128]{2,1,0:T(8,128)S(1)}, f32[2,128,128]{2,1,0:T(8,128)S(1)}, u32[]{:S(2)}, u32[]{:S(2)}) collective-permute-start(f32[2,128,128]{2,1,0:T(8,128)S(1)} %get-tuple-element.40.refs_3_), channel_id=1, source_target_pairs={{0,24},{1,25},{2,26},{3,27},{4,28},{5,29},{6,30},{7,31}} | collective-permute-start | bytes 393224 | tf_op jit(solution)/shard_map/ppermute | solution.py:799
  71.9 0.7 collective-permute-start.13
  72.5 0.7 collective-permute-start.14
  73.2 1.6 %collective-permute-start.16 = (f32[128,128]{1,0:T(8,128)S(1)}, f32[128,128]{1,0:T(8,128)S(1)}, u32[]{:S(2)}, u32[]{:S(2)}) collective-permute-start(f32[128,128]{1,0:T(8,128)S(1)} %get-tuple-element.42.refs_0_), channel_id=1, source_target_pairs={{0,16},{1,17},{2,18},{3,19},{4,20},{5,21},{6,22},{7,23},{8,24},{9,... | collective-permute-start | bytes 196616 | tf_op jit(solution)/shard_map/ppermute | solution.py:781
  74.8 0.6 collective-permute-start.17
  75.4 0.1 add_select_fusion.refs_4_
  75.5 1.0 %collective-permute-done.16.refs_2_ = f32[128,128]{1,0:T(8,128)S(1)} collective-permute-done((f32[128,128]{1,0:T(8,128)S(1)}, f32[128,128]{1,0:T(8,128)S(1)}, u32[]{:S(2)}, u32[]{:S(2)}) %collective-permute-start.16) | collective-permute-done | bytes 65568 | tf_op jit(solution)/shard_map/ppermute | solution.py:781
  76.5 1.5 %collective-permute-done.17.refs_3_ = f32[128,128]{1,0:T(8,128)S(1)} collective-permute-done((f32[128,128]{1,0:T(8,128)S(1)}, f32[128,128]{1,0:T(8,128)S(1)}, u32[]{:S(2)}, u32[]{:S(2)}) %collective-permute-start.17) | collective-permute-done | bytes 65568 | tf_op jit(solution)/shard_map/ppermute | solution.py:781
  77.9 0.2 pick.1
  78.1 5.6 %collective-permute-start.18 = (f32[64,128]{1,0:T(8,128)S(1)}, f32[64,128]{1,0:T(8,128)S(1)}, u32[]{:S(2)}, u32[]{:S(2)}) collective-permute-start(f32[64,128]{1,0:T(8,128)S(1)} %get-tuple-element.45), channel_id=1, source_target_pairs={{0,7},{1,0},{2,1},{3,2},{4,3},{5,4},{6,5},{7,6},{8,15},{9,8},{10,9... | collective-permute-start | bytes 98312 | tf_op jit(solution)/shard_map/ppermute | solution.py:791
  83.7 3.7 %collective-permute-start.19 = (f32[64,128]{1,0:T(8,128)S(1)}, f32[64,128]{1,0:T(8,128)S(1)}, u32[]{:S(2)}, u32[]{:S(2)}) collective-permute-start(f32[64,128]{1,0:T(8,128)S(1)} %get-tuple-element.46), channel_id=1, source_target_pairs={{0,6},{1,7},{2,0},{3,1},{4,2},{5,3},{6,4},{7,5},{8,14},{9,15},{10,... | collective-permute-start | bytes 98312 | tf_op jit(solution)/shard_map/ppermute | solution.py:791
  87.4 1.9 %collective-permute-start.20 = (f32[64,128]{1,0:T(8,128)S(1)}, f32[64,128]{1,0:T(8,128)S(1)}, u32[]{:S(2)}, u32[]{:S(2)}) collective-permute-start(f32[64,128]{1,0:T(8,128)S(1)} %get-tuple-element.47), channel_id=1, source_target_pairs={{0,5},{1,6},{2,7},{3,0},{4,1},{5,2},{6,3},{7,4},{8,13},{9,14},{10,... | collective-permute-start | bytes 98312 | tf_op jit(solution)/shard_map/ppermute | solution.py:791
  89.4 0.8 update.1
  90.2 3.3 %collective-permute-done.20.refs_3_ = f32[64,128]{1,0:T(8,128)S(1)} collective-permute-done((f32[64,128]{1,0:T(8,128)S(1)}, f32[64,128]{1,0:T(8,128)S(1)}, u32[]{:S(2)}, u32[]{:S(2)}) %collective-permute-start.20) | collective-permute-done | bytes 32800 | tf_op jit(solution)/shard_map/ppermute | solution.py:791
  93.6 2.4 %returned.1 = f32[128,128]{1,0:T(8,128)} custom-call(s32[4]{0:T(128)S(1)} %pad_add_fusion.refs_0_.flags, f32[64,128]{1,0:T(8,128)S(1)} %get-tuple-element.44.refs_0_, f32[64,128]{1,0:T(8,128)S(1)} %collective-permute-done.18.refs_1_, f32[64,128]{1,0:T(8,128)S(1)} %collective-permute-done.19.refs_2_, f32[64,128]{1,0:T(8,128)S(1)} %collective-permute-done.20.refs_3_, ...), custom_call_target="tpu_custom_call" | custom-call | tf_op jit(solution)/shard_map/returned/pallas_call | solution.py:694
  (33 shorter events, 0.1 us)
Async XLA Ops:
  0.6 3.4 %copy-start = (f32[128,128,128]{2,1,0:T(8,128)S(1)}, f32[128,128,128]{2,1,0:T(8,128)}, u32[]{:S(2)}) copy-start(f32[128,128,128]{2,1,0:T(8,128)} %refs_3_.1) | copy-start | bytes 25165828
  4.0 6.1 %copy-start.7 = (s32[128,1,2,3]{0,2,3,1:T(2,128)S(1)}, s32[128,1,2,3]{0,2,3,1:T(2,128)}, u32[]{:S(2)}) copy-start(s32[128,1,2,3]{0,2,3,1:T(2,128)} %param.11) | copy-start | bytes 9220
  4.0 12.3 %copy-start.6 = (s32[128,128]{1,0:T(8,128)S(1)}, s32[128,128]{1,0:T(8,128)}, u32[]{:S(2)}) copy-start(s32[128,128]{1,0:T(8,128)} %param.10) | copy-start | bytes 196612
  4.0 13.4 %copy-start.2 = (f32[128,128]{1,0:T(8,128)S(1)}, f32[128,128]{1,0:T(8,128)}, u32[]{:S(2)}) copy-start(f32[128,128]{1,0:T(8,128)} %refs_10_.1) | copy-start | bytes 196612
  4.0 13.4 %copy-start.3 = (f32[128,128]{1,0:T(8,128)S(1)}, f32[128,128]{1,0:T(8,128)}, u32[]{:S(2)}) copy-start(f32[128,128]{1,0:T(8,128)} %refs_11_.1) | copy-start | bytes 196612
  4.0 13.4 %copy-start.5 = (f32[128,8]{0,1:T(8,128)S(1)}, f32[128,8]{0,1:T(8,128)}, u32[]{:S(2)}) copy-start(f32[128,8]{0,1:T(8,128)} %param.14) | copy-start | bytes 12292
  4.0 53.0 %copy-start.4 = (f32[8,128]{1,0:T(8,128)S(1)}, f32[8,128]{1,0:T(8,128)}, u32[]{:S(2)}) copy-start(f32[8,128]{1,0:T(8,128)} %refs_5_.1) | copy-start | bytes 12292
  4.0 57.7 %copy-start.1 = (bf16[32,128,128]{2,1,0:T(8,128)(2,1)S(1)}, bf16[32,128,128]{2,1,0:T(8,128)(2,1)}, u32[]{:S(2)}) copy-start(bf16[32,128,128]{2,1,0:T(8,128)(2,1)} %refs_6_.1) | copy-start | bytes 3145732
  4.8 6.4 %collective-permute-start = (bf16[2,128,128]{2,1,0:T(8,128)(2,1)S(1)}, bf16[2,128,128]{2,1,0:T(8,128)(2,1)S(1)}, u32[]{:S(2)}, u32[]{:S(2)}) collective-permute-start(bf16[2,128,128]{2,1,0:T(8,128)(2,1)S(1)} %get-tuple-element.26), channel_id=1, source_target_pairs={{0,2},{1,3},{2,4},{3,5},{4,6},{5,7},{6,8},{7,9},{8,10},{9,11},{10,... | collective-permute-start | bytes 196616 | tf_op jit(solution)/shard_map/ppermute | solution.py:740
  8.8 6.4 %collective-permute-start.1 = (bf16[2,128,128]{2,1,0:T(8,128)(2,1)S(1)}, bf16[2,128,128]{2,1,0:T(8,128)(2,1)S(1)}, u32[]{:S(2)}, u32[]{:S(2)}) collective-permute-start(bf16[2,128,128]{2,1,0:T(8,128)(2,1)S(1)} %get-tuple-element.27), channel_id=1, source_target_pairs={{2,0},{3,1},{4,2},{5,3},{6,4},{7,5},{8,6},{9,7},{10,8},{11,9},{12,... | collective-permute-start | bytes 196616 | tf_op jit(solution)/shard_map/ppermute | solution.py:740
  15.2 2.2 %collective-permute-start.2 = (f32[4,144,128]{2,1,0:T(8,128)S(1)}, f32[4,144,128]{2,1,0:T(8,128)S(1)}, u32[]{:S(2)}, u32[]{:S(2)}) collective-permute-start(f32[4,144,128]{2,1,0:T(8,128)S(1)} %frame.1), channel_id=1, source_target_pairs={{0,1},{1,0},{2,3},{3,2},{4,5},{5,4},{6,7},{7,6},{8,9},{9,8},{10,11... | collective-permute-start | bytes 884744 | tf_op jit(solution)/shard_map/ppermute | solution.py:740
  36.4 10.5 %collective-permute-start.3 = (bf16[272,256]{1,0:T(8,128)(2,1)S(1)}, bf16[272,256]{1,0:T(8,128)(2,1)S(1)}, u32[]{:S(2)}, u32[]{:S(2)}) collective-permute-start(bf16[272,256]{1,0:T(8,128)(2,1)S(1)} %get-tuple-element.31), channel_id=1, source_target_pairs={{0,8},{1,9},{2,10},{3,11},{4,12},{5,13},{6,14},{7,15},{8,16},{9,17... | collective-permute-start | bytes 417800 | tf_op jit(solution)/shard_map/ppermute | solution.py:781
  40.2 8.2 %collective-permute-start.4 = (bf16[272,256]{1,0:T(8,128)(2,1)S(1)}, bf16[272,256]{1,0:T(8,128)(2,1)S(1)}, u32[]{:S(2)}, u32[]{:S(2)}) collective-permute-start(bf16[272,256]{1,0:T(8,128)(2,1)S(1)} %get-tuple-element.32), channel_id=1, source_target_pairs={{0,16},{1,17},{2,18},{3,19},{4,20},{5,21},{6,22},{7,23},{8,24},{9,... | collective-permute-start | bytes 417800 | tf_op jit(solution)/shard_map/ppermute | solution.py:781
  43.0 6.4 %collective-permute-start.5 = (bf16[272,256]{1,0:T(8,128)(2,1)S(1)}, bf16[272,256]{1,0:T(8,128)(2,1)S(1)}, u32[]{:S(2)}, u32[]{:S(2)}) collective-permute-start(bf16[272,256]{1,0:T(8,128)(2,1)S(1)} %get-tuple-element.33), channel_id=1, source_target_pairs={{0,24},{1,25},{2,26},{3,27},{4,28},{5,29},{6,30},{7,31},{8,0},{9,1... | collective-permute-start | bytes 417800 | tf_op jit(solution)/shard_map/ppermute | solution.py:781
  44.9 7.6 %collective-permute-start.9 = (bf16[128,128]{1,0:T(8,128)(2,1)S(1)}, bf16[128,128]{1,0:T(8,128)(2,1)S(1)}, u32[]{:S(2)}, u32[]{:S(2)}) collective-permute-start(bf16[128,128]{1,0:T(8,128)(2,1)S(1)} %get-tuple-element.38.refs_7_), channel_id=1, source_target_pairs={{24,0},{25,1},{26,2},{27,3},{28,4},{29,5},{30,6},{31,7}} | collective-permute-start | bytes 98312 | tf_op jit(solution)/shard_map/ppermute | solution.py:799
  46.2 10.9 %collective-permute-start.10 = (bf16[128,128]{1,0:T(8,128)(2,1)S(1)}, bf16[128,128]{1,0:T(8,128)(2,1)S(1)}, u32[]{:S(2)}, u32[]{:S(2)}) collective-permute-start(bf16[128,128]{1,0:T(8,128)(2,1)S(1)} %get-tuple-element.38.refs_7_), channel_id=1, source_target_pairs={{24,8},{25,9},{26,10},{27,11},{28,12},{29,13},{30,14},{31,15}} | collective-permute-start | bytes 98312 | tf_op jit(solution)/shard_map/ppermute | solution.py:799
  46.9 10.2 %collective-permute-start.11 = (bf16[128,128]{1,0:T(8,128)(2,1)S(1)}, bf16[128,128]{1,0:T(8,128)(2,1)S(1)}, u32[]{:S(2)}, u32[]{:S(2)}) collective-permute-start(bf16[128,128]{1,0:T(8,128)(2,1)S(1)} %get-tuple-element.38.refs_7_), channel_id=1, source_target_pairs={{24,16},{25,17},{26,18},{27,19},{28,20},{29,21},{30,22},{31,23}} | collective-permute-start | bytes 98312 | tf_op jit(solution)/shard_map/ppermute | solution.py:799
  50.1 7.0 %collective-permute-start.6 = (bf16[208,256]{1,0:T(8,128)(2,1)S(1)}, bf16[208,256]{1,0:T(8,128)(2,1)S(1)}, u32[]{:S(2)}, u32[]{:S(2)}) collective-permute-start(bf16[208,256]{1,0:T(8,128)(2,1)S(1)} %get-tuple-element.35), channel_id=1, source_target_pairs={{0,1},{1,2},{2,3},{3,4},{4,5},{5,6},{6,7},{7,0},{8,9},{9,10},{10,1... | collective-permute-start | bytes 319496 | tf_op jit(solution)/shard_map/ppermute | solution.py:791
  51.2 7.7 %collective-permute-start.7 = (bf16[208,256]{1,0:T(8,128)(2,1)S(1)}, bf16[208,256]{1,0:T(8,128)(2,1)S(1)}, u32[]{:S(2)}, u32[]{:S(2)}) collective-permute-start(bf16[208,256]{1,0:T(8,128)(2,1)S(1)} %get-tuple-element.36), channel_id=1, source_target_pairs={{0,2},{1,3},{2,4},{3,5},{4,6},{5,7},{6,0},{7,1},{8,10},{9,11},{10,... | collective-permute-start | bytes 319496 | tf_op jit(solution)/shard_map/ppermute | solution.py:791
  52.5 9.2 %collective-permute-start.8 = (bf16[208,256]{1,0:T(8,128)(2,1)S(1)}, bf16[208,256]{1,0:T(8,128)(2,1)S(1)}, u32[]{:S(2)}, u32[]{:S(2)}) collective-permute-start(bf16[208,256]{1,0:T(8,128)(2,1)S(1)} %get-tuple-element.37), channel_id=1, source_target_pairs={{0,3},{1,4},{2,5},{3,6},{4,7},{5,0},{6,1},{7,2},{8,11},{9,12},{10,... | collective-permute-start | bytes 319496 | tf_op jit(solution)/shard_map/ppermute | solution.py:791
  67.3 7.5 %collective-permute-start.15 = (f32[128,128]{1,0:T(8,128)S(1)}, f32[128,128]{1,0:T(8,128)S(1)}, u32[]{:S(2)}, u32[]{:S(2)}) collective-permute-start(f32[128,128]{1,0:T(8,128)S(1)} %get-tuple-element.42.refs_0_), channel_id=1, source_target_pairs={{0,8},{1,9},{2,10},{3,11},{4,12},{5,13},{6,14},{7,15},{8,16},{9,17... | collective-permute-start | bytes 196616 | tf_op jit(solution)/shard_map/ppermute | solution.py:781
  68.7 18.7 %collective-permute-start.12 = (f32[2,128,128]{2,1,0:T(8,128)S(1)}, f32[2,128,128]{2,1,0:T(8,128)S(1)}, u32[]{:S(2)}, u32[]{:S(2)}) collective-permute-start(f32[2,128,128]{2,1,0:T(8,128)S(1)} %get-tuple-element.40.refs_3_), channel_id=1, source_target_pairs={{0,24},{1,25},{2,26},{3,27},{4,28},{5,29},{6,30},{7,31}} | collective-permute-start | bytes 393224 | tf_op jit(solution)/shard_map/ppermute | solution.py:799
  71.9 17.5 %collective-permute-start.13 = (f32[2,128,128]{2,1,0:T(8,128)S(1)}, f32[2,128,128]{2,1,0:T(8,128)S(1)}, u32[]{:S(2)}, u32[]{:S(2)}) collective-permute-start(f32[2,128,128]{2,1,0:T(8,128)S(1)} %get-tuple-element.40.refs_3_), channel_id=1, source_target_pairs={{8,24},{9,25},{10,26},{11,27},{12,28},{13,29},{14,30},{15,31}} | collective-permute-start | bytes 393224 | tf_op jit(solution)/shard_map/ppermute | solution.py:799
  72.5 16.8 %collective-permute-start.14 = (f32[2,128,128]{2,1,0:T(8,128)S(1)}, f32[2,128,128]{2,1,0:T(8,128)S(1)}, u32[]{:S(2)}, u32[]{:S(2)}) collective-permute-start(f32[2,128,128]{2,1,0:T(8,128)S(1)} %get-tuple-element.40.refs_3_), channel_id=1, source_target_pairs={{16,24},{17,25},{18,26},{19,27},{20,28},{21,29},{22,30},{23,31}} | collective-permute-start | bytes 393224 | tf_op jit(solution)/shard_map/ppermute | solution.py:799
  73.2 3.3 %collective-permute-start.16 = (f32[128,128]{1,0:T(8,128)S(1)}, f32[128,128]{1,0:T(8,128)S(1)}, u32[]{:S(2)}, u32[]{:S(2)}) collective-permute-start(f32[128,128]{1,0:T(8,128)S(1)} %get-tuple-element.42.refs_0_), channel_id=1, source_target_pairs={{0,16},{1,17},{2,18},{3,19},{4,20},{5,21},{6,22},{7,23},{8,24},{9,... | collective-permute-start | bytes 196616 | tf_op jit(solution)/shard_map/ppermute | solution.py:781
  74.8 3.1 %collective-permute-start.17 = (f32[128,128]{1,0:T(8,128)S(1)}, f32[128,128]{1,0:T(8,128)S(1)}, u32[]{:S(2)}, u32[]{:S(2)}) collective-permute-start(f32[128,128]{1,0:T(8,128)S(1)} %get-tuple-element.42.refs_0_), channel_id=1, source_target_pairs={{0,24},{1,25},{2,26},{3,27},{4,28},{5,29},{6,30},{7,31},{8,0},{9,1... | collective-permute-start | bytes 196616 | tf_op jit(solution)/shard_map/ppermute | solution.py:781
  78.1 12.1 %collective-permute-start.18 = (f32[64,128]{1,0:T(8,128)S(1)}, f32[64,128]{1,0:T(8,128)S(1)}, u32[]{:S(2)}, u32[]{:S(2)}) collective-permute-start(f32[64,128]{1,0:T(8,128)S(1)} %get-tuple-element.45), channel_id=1, source_target_pairs={{0,7},{1,0},{2,1},{3,2},{4,3},{5,4},{6,5},{7,6},{8,15},{9,8},{10,9... | collective-permute-start | bytes 98312 | tf_op jit(solution)/shard_map/ppermute | solution.py:791
  83.7 6.5 %collective-permute-start.19 = (f32[64,128]{1,0:T(8,128)S(1)}, f32[64,128]{1,0:T(8,128)S(1)}, u32[]{:S(2)}, u32[]{:S(2)}) collective-permute-start(f32[64,128]{1,0:T(8,128)S(1)} %get-tuple-element.46), channel_id=1, source_target_pairs={{0,6},{1,7},{2,0},{3,1},{4,2},{5,3},{6,4},{7,5},{8,14},{9,15},{10,... | collective-permute-start | bytes 98312 | tf_op jit(solution)/shard_map/ppermute | solution.py:791
  87.4 6.1 %collective-permute-start.20 = (f32[64,128]{1,0:T(8,128)S(1)}, f32[64,128]{1,0:T(8,128)S(1)}, u32[]{:S(2)}, u32[]{:S(2)}) collective-permute-start(f32[64,128]{1,0:T(8,128)S(1)} %get-tuple-element.47), channel_id=1, source_target_pairs={{0,5},{1,6},{2,7},{3,0},{4,1},{5,2},{6,3},{7,4},{8,13},{9,14},{10,... | collective-permute-start | bytes 98312 | tf_op jit(solution)/shard_map/ppermute | solution.py:791

commit v5 on v4

--- a/solution.py
+++ b/solution.py
@@ -13,6 +13,7 @@
 F32 = jnp.float32
 BF16 = jnp.bfloat16
 EDGE = 8
+STRIP = 16
 CHUNK = 8
 AXES = ("comp", "lat", "lon")
 
@@ -71,7 +72,7 @@
             pltpu.VMEM((rows, EDGE, levels), F32),
             pltpu.SemaphoreType.DMA((4,)),
         ],
-        compiler_params=pltpu.CompilerParams(vmem_limit_bytes=16 * MIB),
+        compiler_params=pltpu.CompilerParams(vmem_limit_bytes=50 * MIB),
         name="edges",
     )(state)
 
@@ -105,15 +106,13 @@
     (flags, source_column, labels, state, up_rows, low_rows, left_in, right_in, own_sides) = refs[:9]
     (mask, mix_atm, mix_ocn, flux_map) = refs[9:13]
     out, surface, sea_copy = refs[13:16]
-    packed = refs[16 : 16 + comp_count]
-    (values, moved, halo_moved, smooth, pairs, mixed, later_smooth, later_pairs, later_mixed) = refs[
-        16 + comp_count : 25 + comp_count
-    ]
-    (weights, flux_weights, fluxes, staged, top, in_sems, out_sems) = refs[25 + comp_count :]
+    packed = refs[16]
+    (values, moved, halo_moved, smooth, pairs, later_smooth, later_pairs) = refs[17:24]
+    (weights, flux_weights, fluxes, staged, top, in_sems, out_sems) = refs[24:]
     left_cols = left_in.at[left_at : left_at + 2]
     right_cols = right_in.at[right_at : right_at + 2]
-    first = (smooth, pairs, mixed)
-    second = (later_smooth, later_pairs, later_mixed)
+    first = (smooth, pairs)
+    second = (later_smooth, later_pairs)
     rows, cols, levels = state.shape
     chunks = rows // CHUNK
     inner = pl.ds(EDGE, cols)
@@ -170,6 +169,19 @@
         refs[0][row] = line
         refs[1][row * cols : (row + 1) * cols, :] = side_by_side(line)
 
+    def stage_rows(refs, ref, start, count):
+        for col in range(0, cols, STRIP):
+            left = EDGE + col
+            block = ref[pl.ds(start - 1, count + 2), left : left + STRIP, :]
+            near = ref[pl.ds(start, count), left - 1 : left - 1 + STRIP, :]
+            far = ref[pl.ds(start, count), left + 1 : left + 1 + STRIP, :]
+            for row in range(count):
+                total = (block[row + 1] + (block[row] + block[row + 2])) + (near[row] + far[row])
+                line = SMOOTHING * total
+                refs[0][row, col : col + STRIP, :] = line
+                spot = row * cols + col
+                refs[1][spot : spot + STRIP, :] = side_by_side(line)
+
     def note_top(q, lines):
         lanes = lax.broadcasted_iota(jnp.int32, (cols, levels), 1)
         kept = lines[0]
@@ -179,19 +191,12 @@
         top[...] = jnp.where(lanes // CHUNK == q, turned, top[...])
 
     def mix_rows(refs, count):
-        refs[2][: count * cols, :] = dot_nn(refs[1][: count * cols, :], weights[...])
-
-    def finish(refs, row):
-        part = refs[2][row * cols : (row + 1) * cols, :]
-        return refs[0][row] + PHYSICS * jnp.tanh(part[:, :levels] + part[:, levels:])
-
-    def gather_row(ref, i):
-        here = ref[i, EDGE : EDGE + cols, :] + (
-            ref[i - 1, EDGE : EDGE + cols, :] + ref[i + 1, EDGE : EDGE + cols, :]
-        )
-        return here + (
-            ref[i, EDGE - 1 : EDGE - 1 + cols, :] + ref[i, EDGE + 1 : EDGE + 1 + cols, :]
-        )
+        both = dot_nn(refs[1][: count * cols, :], weights[...])
+        both = both[:, :levels] + both[:, levels:]
+        return [
+            refs[0][row] + PHYSICS * jnp.tanh(both[row * cols : (row + 1) * cols, :])
+            for row in range(count)
+        ]
 
     @pl.when(jnp.logical_not(ocean))
     def atmosphere():
@@ -205,9 +210,8 @@
                 + nearest[s][EDGE + 1 : EDGE + 1 + rows, :]
             )
             stage(first, s, total + (beyond[s][EDGE : EDGE + rows, :] + within[s][...]))
-        mix_rows(first, 2)
-        for s in range(2):
-            halo_moved[s] = finish(first, s)
+        for s, line in enumerate(mix_rows(first, 2)):
+            halo_moved[s] = line
 
         def moved_sides(r, _):
             moved[r + 1, EDGE - 1 : EDGE, :] = halo_moved[0, pl.ds(r, 1), :]
@@ -217,32 +221,26 @@
         lax.fori_loop(0, rows, moved_sides, 0, unroll=8)
         fetch(0).wait()
         fetch(1).wait()
-        for row in range(2):
-            stage(second, row, gather_row(values, row + 1))
-        mix_rows(second, 2)
-        moved[0, EDGE : EDGE + cols, :] = finish(second, 0)
-        moved[1, EDGE : EDGE + cols, :] = finish(second, 1)
+        stage_rows(second, values, 1, 2)
+        for row, line in enumerate(mix_rows(second, 2)):
+            moved[row, EDGE : EDGE + cols, :] = line
 
         @pl.when(flags[1] == 0)
         def _():
             moved[0, EDGE : EDGE + cols, :] = jnp.zeros((cols, levels), F32)
 
         def begin_first(q):
-            for row in range(CHUNK):
-                stage(first, row, gather_row(values, q * CHUNK + row + 3))
-            mix_rows(first, CHUNK)
+            stage_rows(first, values, q * CHUNK + 3, CHUNK)
 
         def end_first(q):
-            for row in range(CHUNK):
-                moved[q * CHUNK + row + 2, EDGE : EDGE + cols, :] = finish(first, row)
+            for row, line in enumerate(mix_rows(first, CHUNK)):
+                moved[q * CHUNK + row + 2, EDGE : EDGE + cols, :] = line
 
         def begin_second(q):
-            for row in range(CHUNK):
-                stage(second, row, gather_row(moved, q * CHUNK + row + 1))
+            stage_rows(second, moved, q * CHUNK + 1, CHUNK)
 
         def end_second(q, slot):
-            for row in range(CHUNK):
-                line = finish(second, row)
+            for row, line in enumerate(mix_rows(second, CHUNK)):
                 staged[slot, row] = line
                 both = line + moved[q * CHUNK + row + 1, EDGE : EDGE + cols, :]
                 later_pairs[row * cols : (row + 1) * cols, :] = side_by_side(both)
@@ -274,7 +272,6 @@
             begin_first(q)
             begin_second(q - 1)
             end_first(q)
-            mix_rows(second, CHUNK)
             end_second(q - 1, slot)
             return 0
 
@@ -287,21 +284,19 @@
         last = chunks - 1
         put(last - 2, last % 2).wait()
         begin_second(last)
-        mix_rows(second, CHUNK)
         end_second(last, last % 2)
         put(last - 1, (last - 1) % 2).wait()
         put(last, last % 2).wait()
         spots = lax.broadcasted_iota(jnp.int32, (source_column.shape[0], rows), 1)
         placing = jnp.where(source_column[...] == spots, 1.0, 0.0).astype(BF16)
         share = flux_count // comp_count
-        for shift in range(comp_count):
-            begin_field = lax.rem(flags[3] + shift, comp_count) * share
+        for c in range(comp_count):
             for f in range(share):
-                field = fluxes[pl.ds(begin_field + f, rows, stride=flux_count), :].astype(BF16)
-                packed[shift][: placing.shape[0], f * cols : (f + 1) * cols] = dot_nn(
+                field = fluxes[pl.ds(c * share + f, rows, stride=flux_count), :].astype(BF16)
+                packed[c, : placing.shape[0], f * cols : (f + 1) * cols] = dot_nn(
                     placing, field
                 ).astype(BF16)
-            packed[shift][placing.shape[0] :, :] = labels[...]
+            packed[c, placing.shape[0] :, :] = labels[...]
         surface[...] = top[...].T
 
     @pl.when(ocean)
@@ -318,9 +313,7 @@
             def _():
                 fetch(q + 1).wait()
 
-            for row in range(CHUNK):
-                stage(first, row, gather_row(values, base + row + 2))
-            mix_rows(first, CHUNK)
+            stage_rows(first, values, base + 2, CHUNK)
             slot = q % 2
 
             @pl.when(q >= 2)
@@ -328,10 +321,10 @@
                 put(q - 2, slot).wait()
 
             sea = dot_nn(mask[pl.ds(pl.multiple_of(base, CHUNK), CHUNK), :].T, spreader)
-            for row in range(CHUNK):
+            for row, line in enumerate(mix_rows(first, CHUNK)):
                 chosen = sea[:, row * levels : (row + 1) * levels] > 0.5
                 before = values[base + row + 2, EDGE : EDGE + cols, :]
-                staged[slot, row] = jnp.where(chosen, finish(first, row), before)
+                staged[slot, row] = jnp.where(chosen, line, before)
             put(q, slot).start()
             note_top(q, [staged[slot, row] for row in range(CHUNK)])
             return 0
@@ -340,8 +333,7 @@
         put(chunks - 2, (chunks - 2) % 2).wait()
         put(chunks - 1, (chunks - 1) % 2).wait()
         surface[...] = top[...].T
-        for shift in range(comp_count):
-            packed[shift][...] = jnp.zeros(packed[shift].shape, BF16)
+        packed[...] = jnp.zeros(packed.shape, BF16)
 
 
 def advance(
@@ -353,7 +345,7 @@
     smem = pl.BlockSpec(memory_space=pltpu.SMEM)
     hbm = pl.BlockSpec(memory_space=pltpu.HBM)
     entry = jax.ShapeDtypeStruct(
-        (source_column.shape[0] + labels.shape[0], fluxes // comp_count * cols), BF16
+        (comp_count, source_column.shape[0] + labels.shape[0], fluxes // comp_count * cols), BF16
     )
     cells = rows * cols
     return pl.pallas_call(
@@ -362,20 +354,18 @@
             jax.ShapeDtypeStruct(state.shape, F32),
             jax.ShapeDtypeStruct((rows, cols), F32),
             jax.ShapeDtypeStruct((rows, cols), BF16),
-        )
-        + (entry,) * comp_count,
+            entry,
+        ),
         in_specs=[smem, vmem, vmem, hbm] + [vmem] * (len(halos) + 4),
-        out_specs=(hbm,) + (vmem,) * (2 + comp_count),
+        out_specs=(hbm, vmem, vmem, vmem),
         scratch_shapes=[
             pltpu.VMEM((rows + 4, cols + 2 * EDGE, levels), F32),
             pltpu.VMEM((rows + 2, cols + 2 * EDGE, levels), F32),
             pltpu.VMEM((2, rows, levels), F32),
             pltpu.VMEM((CHUNK, cols, levels), F32),
             pltpu.VMEM((CHUNK * cols, 2 * levels), BF16),
-            pltpu.VMEM((CHUNK * cols, 2 * levels), F32),
             pltpu.VMEM((CHUNK, cols, levels), F32),
             pltpu.VMEM((CHUNK * cols, 2 * levels), BF16),
-            pltpu.VMEM((CHUNK * cols, 2 * levels), F32),
             pltpu.VMEM((2 * levels, 2 * levels), BF16),
             pltpu.VMEM((2 * fluxes, 2 * levels), BF16),
             pltpu.VMEM((rows * fluxes, cols), F32),
@@ -396,43 +386,34 @@
 LABEL_ROWS = 16
 
 
-def regroup_kernel(count, flags, *refs):
-    slabs, blocks = refs[:-count], refs[-count:]
-    sources = len(slabs) - 1
+def regroup_kernel(slabs, *blocks):
+    sources = slabs.shape[0] - 1
     capacity = (blocks[0].shape[0] - LABEL_ROWS) // sources
-    size = count * capacity
-
-    def chosen(c, start, stop):
-        shift = lax.rem(flags[3] - c + len(slabs), len(slabs))
-        value = slabs[0][start:stop, :].astype(F32)
-        for s in range(1, len(slabs)):
-            value = jnp.where(shift == s, slabs[s][start:stop, :].astype(F32), value)
-        return value
-
-    heads = [chosen(c, size, size + LABEL_ROWS) for c in range(sources)]
+    size = len(blocks) * capacity
+    heads = [slabs[c, size : size + LABEL_ROWS, :].astype(F32) for c in range(sources)]
     lines = [head[i : i + 1] for i in range(2) for head in heads]
     spare = jnp.zeros((LABEL_ROWS - len(lines), heads[0].shape[1]), F32)
     labels = jnp.concatenate(lines + [spare], axis=0).astype(BF16)
-    for n in range(count):
+    for n, block in enumerate(blocks):
         for c in range(sources):
-            blocks[n][c * capacity : (c + 1) * capacity, :] = chosen(
-                c, n * capacity, (n + 1) * capacity
-            ).astype(BF16)
-        blocks[n][sources * capacity :, :] = labels
-
-
-def regroup(flags, slabs, count):
-    rows, width = slabs[0].shape
-    size = (rows - LABEL_ROWS) // count * (len(slabs) - 1) + LABEL_ROWS
+            block[c * capacity : (c + 1) * capacity, :] = slabs[
+                c, n * capacity : (n + 1) * capacity, :
+            ]
+        block[sources * capacity :, :] = labels
+
+
+def regroup(slabs, count):
+    comps, rows, width = slabs.shape
+    size = (rows - LABEL_ROWS) // count * (comps - 1) + LABEL_ROWS
     vmem = pl.BlockSpec(memory_space=pltpu.VMEM)
     return pl.pallas_call(
-        functools.partial(regroup_kernel, count),
+        regroup_kernel,
         out_shape=(jax.ShapeDtypeStruct((size, width), BF16),) * count,
-        in_specs=[pl.BlockSpec(memory_space=pltpu.SMEM)] + [vmem] * len(slabs),
+        in_specs=[vmem],
         out_specs=(vmem,) * count,
         compiler_params=pltpu.CompilerParams(vmem_limit_bytes=16 * MIB),
         name="regroup",
-    )(flags, *slabs)
+    )(slabs)
 
 
 def regrid_body(count, comp_count, flags, ocean_first, *refs):
@@ -491,7 +472,9 @@
     for c in range(sources):
         sea = sea + jnp.where(flags[3] == c, seas[c][...].astype(F32), 0.0)
     base = jnp.where(flags[0] == 1, surface[...], 0.0)
-    shared[...] = base + jnp.where(sea > 0.5, change, 0.0)
+    value = base + jnp.where(sea > 0.5, change, 0.0)
+    for c in range(comp_count):
+        shared[c] = value
 
 
 def regrid(flags, ocean_first, blocks, seas, weights, surface, mask):
@@ -510,7 +493,7 @@
         functools.partial(regrid_body, count, comp_count),
         out_shape=(
             jax.ShapeDtypeStruct((share, rows, cols), F32),
-            jax.ShapeDtypeStruct((rows, cols), F32),
+            jax.ShapeDtypeStruct((comp_count, rows, cols), F32),
             jax.ShapeDtypeStruct((size, rows), BF16),
         ),
         in_specs=[smem, smem] + [vmem] * (count + comp_count + 3),
@@ -530,13 +513,10 @@
     )(flags, ocean_first, *blocks, *seas, weights, surface, mask)
 
 
-def pick_kernel(count, *refs):
-    parts = refs[:count]
-    hits, surface = refs[count : count + 2]
-    picked = refs[count + 2 :]
-    now = parts[0][...]
-    for part in parts[1:]:
-        now = now + part[...]
+def pick_kernel(parts, hits, surface, *picked):
+    now = parts[0]
+    for c in range(1, parts.shape[0]):
+        now = now + parts[c]
     surface[...] = now
     pair = jnp.concatenate(split_two(now), axis=0)
     size = picked[0].shape[0]
@@ -546,18 +526,18 @@
 
 
 def pick(parts, hits, neighbours):
-    rows, cols = parts[0].shape
+    _, rows, cols = parts.shape
     size = hits.shape[0] // neighbours
     vmem = pl.BlockSpec(memory_space=pltpu.VMEM)
     return pl.pallas_call(
-        functools.partial(pick_kernel, len(parts)),
+        pick_kernel,
         out_shape=(jax.ShapeDtypeStruct((rows, cols), F32),)
         + (jax.ShapeDtypeStruct((size, cols), F32),) * neighbours,
-        in_specs=[vmem] * (len(parts) + 1),
+        in_specs=[vmem] * 2,
         out_specs=(vmem,) * (1 + neighbours),
         compiler_params=pltpu.CompilerParams(vmem_limit_bytes=16 * MIB),
         name="pick",
-    )(*parts, hits)
+    )(parts, hits)
 
 
 LINES = 8
@@ -772,13 +752,8 @@
     sources = jnp.sum(jnp.where(placing, (positions // intersections)[None, :], 0), axis=1)
     packed_labels = jnp.sum(jnp.where(placing, labels[None, :], 0), axis=1)
 
-    def over_comp(value, shift, last):
-        pairs = [
-            (c * tile_count + t, (c + shift) % comp_count * tile_count + t)
-            for c in range(comp_count if last else comp_count - 1)
-            for t in range(tile_count)
-        ]
-        return lax.ppermute(value, AXES, pairs)
+    def over_comp(value):
+        return lax.all_to_all(value, "comp", split_axis=0, concat_axis=0, tiled=True)
 
     def over_tiles(value, offset, comps):
         if offset % tile_count == 0:
@@ -806,16 +781,15 @@
         flags, sources[:, None], label_lines, state, halos, mask, mix_atm, mix_ocn, flux_map.T,
         comp_count, left_at, right_at,
     )
-    moved, surface, sea_copy, packed = moved[0], moved[1], moved[2], moved[3:]
-    slabs = [packed[0]] + [over_comp(packed[s], s, False) for s in range(1, comp_count)]
+    moved, surface, sea_copy, packed = moved
+    slabs = over_comp(packed)
     seas = [with_ocean(sea_copy, c, True) for c in range(ocean_comp)] + [sea_copy]
-    blocks = regroup(flags, slabs, neighbours)
+    blocks = regroup(slabs, neighbours)
     blocks = [over_tiles(blocks[n], offsets[n], comp_count) for n in range(neighbours)]
     forcing, shared, hits = regrid(
         flags, ocean_map[:, 0], blocks, seas, regrid_weights, surface, mask
     )
-    parts = [shared] + [over_comp(shared, s, True) for s in range(1, comp_count)]
-    picks = pick(parts, hits, neighbours)
+    picks = pick(over_comp(shared), hits, neighbours)
     new_surface, picked = picks[0], picks[1:]
     arrived = [over_tiles(picked[n], -offsets[n], ocean_comp) for n in range(neighbours)]
     fields = [with_ocean(forcing, c, False) for c in range(ocean_comp)] + [forcing]

time: 96.4 us -> 97.5 us (1.011)
  waiting for transfers between devices: 17.3 us -> 25 us
  starting transfers between devices: 43.4 us -> 37.9 us
  local copies, waits for them, and re-layouts: 3.94 us -> 0.57 us
  Pallas kernels: 29.4 us -> 31.7 us
    ppermute x6 -> x0, starting transfers between devices: 11.9 us -> none  [over_comp(): return lax.ppermute(value, AXES, pairs)]
    all_to_all x0 -> x2, waiting for transfers between devices: none -> 11.2 us  [over_comp(): lax.all_to_all(value, 'comp', split_axis=0, concat_axis=0, tiled=True)]
    all_to_all x0 -> x2, starting transfers between devices: none -> 7.42 us  [over_comp(): lax.all_to_all(value, 'comp', split_axis=0, concat_axis=0, tiled=True)]
    ppermute x6 -> x0, waiting for transfers between devices: 4.33 us -> none  [over_comp(): return lax.ppermute(value, AXES, pairs)]
    unnamed x17 -> x15, local copies, waits for them, and re-layouts: 3.56 us -> 0.19 us
    ppermute x6, starting transfers between devices: 18.1 us -> 15.7 us  [over_tiles(): return lax.ppermute(value, AXES, pairs)]
    pallas_call x1, Pallas kernels: 19 us -> 20.3 us  [advance(): pl.pallas_call(functools.partial(advance_kernel, comp_count, left_at, rig...]
    ppermute x6, starting transfers between devices: 7.09 us -> 8.24 us  [with_ocean(): return lax.ppermute(value, AXES, pairs)]
  transfers between devices with their start and end apart: 21 -> 17, of which waited for: 9 -> 7; matrix products, arithmetic and copies ran while one was open for 1% -> 1% of each run, Pallas kernels for 2% -> 1%
where the time goes in v5:
time: 97.5 us; the launch traced here: 97 us
  starting transfers between devices  37.9 us (39%)
  Pallas kernels  31.7 us (33%)
  waiting for transfers between devices  25 us (26%)
  between operations  1.02 us (1%)
    pallas_call x1, Pallas kernels, advance(): pl.pallas_call(functools.partial(advance_kernel, comp_count, left_at, rig...  20.3 us
    ppermute x6, starting transfers between devices, over_tiles(): return lax.ppermute(value, AXES, pairs)  15.7 us
    all_to_all x2, waiting for transfers between devices, over_comp(): lax.all_to_all(value, 'comp', split_axis=0, concat_axis=0, tiled=True)  11.2 us
    ppermute x6, waiting for transfers between devices, over_tiles(): return lax.ppermute(value, AXES, pairs)  8.73 us
    ppermute x6, starting transfers between devices, with_ocean(): return lax.ppermute(value, AXES, pairs)  8.24 us
    all_to_all x2, starting transfers between devices, over_comp(): lax.all_to_all(value, 'comp', split_axis=0, concat_axis=0, tiled=True)  7.42 us
    ppermute x3, starting transfers between devices, band_shift(): return lax.ppermute(value, AXES, pairs)  6.48 us
    pallas_call x1, Pallas kernels, regrid(): pl.pallas_call(functools.partial(regrid_body, count, comp_count), out_sha...  6.29 us
  transfers between devices with their start and end apart: 17, of which 7 were waited for; matrix products, arithmetic and copies ran while one was open for 1% of the time, Pallas kernels for 1%

profile of v5, /device:TPU:1, one launch (start us, length us, event | category | flops | bytes accessed | tf_op | source)
XLA Modules:
  0.0 97.0 jit_solution(5020857400056646572)
XLA Ops:
  0.7 1.6 %edges.1 = (bf16[2,128,128]{2,1,0:T(8,128)(2,1)S(1)}, bf16[2,128,128]{2,1,0:T(8,128)(2,1)S(1)}, f32[4,128,128]{2,1,0:T(8,128)S(1)}) custom-call(f32[128,128,128]{2,1,0:T(8,128)} %refs_3_.1), custom_call_target="tpu_custom_call" | custom-call | tf_op jit(solution)/shard_map/edges/pallas_call | solution.py:63
  2.3 0.0 copy-start.3
  2.3 0.0 copy-start
  2.3 4.2 %collective-permute-start = (bf16[2,128,128]{2,1,0:T(8,128)(2,1)S(1)}, bf16[2,128,128]{2,1,0:T(8,128)(2,1)S(1)}, u32[]{:S(2)}, u32[]{:S(2)}) collective-permute-start(bf16[2,128,128]{2,1,0:T(8,128)(2,1)S(1)} %get-tuple-element.23), channel_id=1, source_target_pairs={{0,2},{1,3},{2,4},{3,5},{4,6},{5,7},{6,8},{7,9},{8,10},{9,11},{10,... | collective-permute-start | bytes 196616 | tf_op jit(solution)/shard_map/ppermute | solution.py:720
  6.5 1.3 %collective-permute-start.1 = (bf16[2,128,128]{2,1,0:T(8,128)(2,1)S(1)}, bf16[2,128,128]{2,1,0:T(8,128)(2,1)S(1)}, u32[]{:S(2)}, u32[]{:S(2)}) collective-permute-start(bf16[2,128,128]{2,1,0:T(8,128)(2,1)S(1)} %get-tuple-element.24), channel_id=1, source_target_pairs={{2,0},{3,1},{4,2},{5,3},{6,4},{7,5},{8,6},{9,7},{10,8},{11,9},{12,... | collective-permute-start | bytes 196616 | tf_op jit(solution)/shard_map/ppermute | solution.py:720
  7.8 0.2 copy.19
  8.0 0.3 fusion.4
  8.2 0.2 convert_reduce_fusion
  8.4 0.2 select_reduce_fusion
  8.7 0.1 copy.20.refs_1_
  8.8 0.0 collective-permute-done.up_rows.refs_4_
  8.8 4.0 %collective-permute-done.1.low_rows.refs_5_ = bf16[2,128,128]{2,1,0:T(8,128)(2,1)S(1)} collective-permute-done((bf16[2,128,128]{2,1,0:T(8,128)(2,1)S(1)}, bf16[2,128,128]{2,1,0:T(8,128)(2,1)S(1)}, u32[]{:S(2)}, u32[]{:S(2)}) %collective-permute-start.1) | collective-permute-done | bytes 65568 | tf_op jit(solution)/shard_map/ppermute | solution.py:720
  12.9 1.0 %collective-permute-start.2 = (f32[4,144,128]{2,1,0:T(8,128)S(1)}, f32[4,144,128]{2,1,0:T(8,128)S(1)}, u32[]{:S(2)}, u32[]{:S(2)}) collective-permute-start(f32[4,144,128]{2,1,0:T(8,128)S(1)} %frame.1), channel_id=1, source_target_pairs={{0,1},{1,0},{2,3},{3,2},{4,5},{5,4},{6,7},{7,6},{8,9},{9,8},{10,11... | collective-permute-start | bytes 884744 | tf_op jit(solution)/shard_map/ppermute | solution.py:720
  13.9 0.1 pad_add_fusion.refs_0_.flags
  14.0 1.1 %collective-permute-done.2.refs_6_.refs_7_ = f32[4,144,128]{2,1,0:T(8,128)S(1)} collective-permute-done((f32[4,144,128]{2,1,0:T(8,128)S(1)}, f32[4,144,128]{2,1,0:T(8,128)S(1)}, u32[]{:S(2)}, u32[]{:S(2)}) %collective-permute-start.2) | collective-permute-done | bytes 294944 | tf_op jit(solution)/shard_map/ppermute | solution.py:720
  15.1 20.3 %advance.1 = (f32[128,128,128]{2,1,0:T(8,128)}, f32[128,128]{1,0:T(8,128)S(1)}, bf16[128,128]{1,0:T(8,128)(2,1)S(1)}, bf16[4,272,256]{2,1,0:T(8,128)(2,1)}) custom-call(s32[4]{0:T(128)S(1)} %pad_add_fusion.refs_0_.flags, s32[256,1]{1,0:T(8,128)S(1)} %copy.20.refs_1_, bf16[16,256]{1,0:T(8,128)(2,1)S(1)} %fusion.9.refs_2_, f32[128,128,128]{2,1,0:T(8,128)} %refs_3_.1, ...), custom_call_target="tpu_custom_call" | custom-call | flops 2147483648 | bytes 16777216 | tf_op jit(solution)/shard_map/advance/pallas_call | solution.py:351
  35.4 4.0 %all-to-all-start = ((bf16[4,272,256]{2,1,0:T(8,128)(2,1)}), bf16[4,272,256]{2,1,0:T(8,128)(2,1)S(1)}, u32[]{:S(2)}, u32[]{:S(2)}) async-start(bf16[4,272,256]{2,1,0:T(8,128)(2,1)} %get-tuple-element.27), calls=%async_computation | async-start | bytes 1114112 | tf_op jit(solution)/shard_map/all_to_all | solution.py:756
  39.4 1.3 %collective-permute-start.6 = (bf16[128,128]{1,0:T(8,128)(2,1)S(1)}, bf16[128,128]{1,0:T(8,128)(2,1)S(1)}, u32[]{:S(2)}, u32[]{:S(2)}) collective-permute-start(bf16[128,128]{1,0:T(8,128)(2,1)S(1)} %get-tuple-element.32.refs_7_), channel_id=1, source_target_pairs={{24,0},{25,1},{26,2},{27,3},{28,4},{29,5},{30,6},{31,7}} | collective-permute-start | bytes 98312 | tf_op jit(solution)/shard_map/ppermute | solution.py:774
  40.7 0.7 collective-permute-start.7
  41.4 0.7 collective-permute-start.8
  42.0 7.1 %all-to-all-done.slabs = bf16[4,272,256]{2,1,0:T(8,128)(2,1)S(1)} async-done(((bf16[4,272,256]{2,1,0:T(8,128)(2,1)}), bf16[4,272,256]{2,1,0:T(8,128)(2,1)S(1)}, u32[]{:S(2)}, u32[]{:S(2)}) %all-to-all-start) | async-done | bytes 557088 | tf_op jit(solution)/shard_map/all_to_all | solution.py:756
  49.1 0.1 collective-permute-start.3
  49.3 1.3 %collective-permute-start.4 = (bf16[208,256]{1,0:T(8,128)(2,1)S(1)}, bf16[208,256]{1,0:T(8,128)(2,1)S(1)}, u32[]{:S(2)}, u32[]{:S(2)}) collective-permute-start(bf16[208,256]{1,0:T(8,128)(2,1)S(1)} %get-tuple-element.30), channel_id=1, source_target_pairs={{0,2},{1,3},{2,4},{3,5},{4,6},{5,7},{6,0},{7,1},{8,10},{9,11},{10,... | collective-permute-start | bytes 319496 | tf_op jit(solution)/shard_map/ppermute | solution.py:766
  50.6 0.0 collective-permute-done.6.refs_4_
  50.6 4.3 %collective-permute-start.5 = (bf16[208,256]{1,0:T(8,128)(2,1)S(1)}, bf16[208,256]{1,0:T(8,128)(2,1)S(1)}, u32[]{:S(2)}, u32[]{:S(2)}) collective-permute-start(bf16[208,256]{1,0:T(8,128)(2,1)S(1)} %get-tuple-element.31), channel_id=1, source_target_pairs={{0,3},{1,4},{2,5},{3,6},{4,7},{5,0},{6,1},{7,2},{8,11},{9,12},{10,... | collective-permute-start | bytes 319496 | tf_op jit(solution)/shard_map/ppermute | solution.py:766
  54.8 0.1 slice_reduce_fusion.ocean_first
  55.0 0.1 copy.21
  55.1 0.0 collective-permute-done.7.refs_5_
  55.1 0.0 collective-permute-done.8.refs_6_
  55.1 3.0 %collective-permute-done.4.refs_2_ = bf16[208,256]{1,0:T(8,128)(2,1)S(1)} collective-permute-done((bf16[208,256]{1,0:T(8,128)(2,1)S(1)}, bf16[208,256]{1,0:T(8,128)(2,1)S(1)}, u32[]{:S(2)}, u32[]{:S(2)}) %collective-permute-start.4) | collective-permute-done | bytes 106528 | tf_op jit(solution)/shard_map/ppermute | solution.py:766
  58.1 2.1 %collective-permute-done.5.refs_3_ = bf16[208,256]{1,0:T(8,128)(2,1)S(1)} collective-permute-done((bf16[208,256]{1,0:T(8,128)(2,1)S(1)}, bf16[208,256]{1,0:T(8,128)(2,1)S(1)}, u32[]{:S(2)}, u32[]{:S(2)}) %collective-permute-start.5) | collective-permute-done | bytes 106528 | tf_op jit(solution)/shard_map/ppermute | solution.py:766
  60.2 6.3 %regrid.1 = (f32[2,128,128]{2,1,0:T(8,128)S(1)}, f32[4,128,128]{2,1,0:T(8,128)}, bf16[256,128]{1,0:T(8,128)(2,1)S(1)}) custom-call(s32[4]{0:T(128)S(1)} %pad_add_fusion.refs_0_.flags, f32[8]{0:T(128)S(1)} %slice_reduce_fusion.ocean_first, bf16[208,256]{1,0:T(8,128)(2,1)S(1)} %get-tuple-element.28.refs_0_, ...), custom_call_target="tpu_custom_call" | custom-call | flops 2147483648 | bytes 2097152 | tf_op jit(solution)/shard_map/regrid/pallas_call | solution.py:492
  66.5 0.7 collective-permute-start.10
  67.1 0.7 collective-permute-start.11
  67.8 4.3 %collective-permute-start.9 = (f32[2,128,128]{2,1,0:T(8,128)S(1)}, f32[2,128,128]{2,1,0:T(8,128)S(1)}, u32[]{:S(2)}, u32[]{:S(2)}) collective-permute-start(f32[2,128,128]{2,1,0:T(8,128)S(1)} %get-tuple-element.34.refs_3_), channel_id=1, source_target_pairs={{0,24},{1,25},{2,26},{3,27},{4,28},{5,29},{6,30},{7,31}} | collective-permute-start | bytes 393224 | tf_op jit(solution)/shard_map/ppermute | solution.py:774
  72.1 3.4 %all-to-all-start.1 = ((f32[4,128,128]{2,1,0:T(8,128)}), f32[4,128,128]{2,1,0:T(8,128)S(1)}, u32[]{:S(2)}, u32[]{:S(2)}) async-start(f32[4,128,128]{2,1,0:T(8,128)} %get-tuple-element.36), calls=%async_computation.1 | async-start | bytes 524288 | tf_op jit(solution)/shard_map/all_to_all | solution.py:756
  75.6 0.1 add_select_fusion.refs_4_
  75.6 4.1 %all-to-all-done.1.parts = f32[4,128,128]{2,1,0:T(8,128)S(1)} async-done(((f32[4,128,128]{2,1,0:T(8,128)}), f32[4,128,128]{2,1,0:T(8,128)S(1)}, u32[]{:S(2)}, u32[]{:S(2)}) %all-to-all-start.1) | async-done | bytes 262176 | tf_op jit(solution)/shard_map/all_to_all | solution.py:756
  79.7 0.2 pick.1
  79.9 5.1 %collective-permute-start.12 = (f32[64,128]{1,0:T(8,128)S(1)}, f32[64,128]{1,0:T(8,128)S(1)}, u32[]{:S(2)}, u32[]{:S(2)}) collective-permute-start(f32[64,128]{1,0:T(8,128)S(1)} %get-tuple-element.39), channel_id=1, source_target_pairs={{0,7},{1,0},{2,1},{3,2},{4,3},{5,4},{6,5},{7,6},{8,15},{9,8},{10,9... | collective-permute-start | bytes 98312 | tf_op jit(solution)/shard_map/ppermute | solution.py:766
  85.0 3.0 %collective-permute-start.13 = (f32[64,128]{1,0:T(8,128)S(1)}, f32[64,128]{1,0:T(8,128)S(1)}, u32[]{:S(2)}, u32[]{:S(2)}) collective-permute-start(f32[64,128]{1,0:T(8,128)S(1)} %get-tuple-element.40), channel_id=1, source_target_pairs={{0,6},{1,7},{2,0},{3,1},{4,2},{5,3},{6,4},{7,5},{8,14},{9,15},{10,... | collective-permute-start | bytes 98312 | tf_op jit(solution)/shard_map/ppermute | solution.py:766
  88.1 0.0 collective-permute-done.10.refs_1_
  88.1 1.9 %collective-permute-start.14 = (f32[64,128]{1,0:T(8,128)S(1)}, f32[64,128]{1,0:T(8,128)S(1)}, u32[]{:S(2)}, u32[]{:S(2)}) collective-permute-start(f32[64,128]{1,0:T(8,128)S(1)} %get-tuple-element.41), channel_id=1, source_target_pairs={{0,5},{1,6},{2,7},{3,0},{4,1},{5,2},{6,3},{7,4},{8,13},{9,14},{10,... | collective-permute-start | bytes 98312 | tf_op jit(solution)/shard_map/ppermute | solution.py:766
  90.0 0.0 collective-permute-done.9.refs_0_
  90.0 0.8 update.1
  90.9 0.0 collective-permute-done.12.refs_1_
  90.9 3.7 %collective-permute-done.14.refs_3_ = f32[64,128]{1,0:T(8,128)S(1)} collective-permute-done((f32[64,128]{1,0:T(8,128)S(1)}, f32[64,128]{1,0:T(8,128)S(1)}, u32[]{:S(2)}, u32[]{:S(2)}) %collective-permute-start.14) | collective-permute-done | bytes 32800 | tf_op jit(solution)/shard_map/ppermute | solution.py:766
  94.6 2.4 %returned.1 = f32[128,128]{1,0:T(8,128)} custom-call(s32[4]{0:T(128)S(1)} %pad_add_fusion.refs_0_.flags, f32[64,128]{1,0:T(8,128)S(1)} %get-tuple-element.38.refs_0_, f32[64,128]{1,0:T(8,128)S(1)} %collective-permute-done.12.refs_1_, f32[64,128]{1,0:T(8,128)S(1)} %collective-permute-done.13.refs_2_, f32[64,128]{1,0:T(8,128)S(1)} %collective-permute-done.14.refs_3_, ...), custom_call_target="tpu_custom_call" | custom-call | tf_op jit(solution)/shard_map/returned/pallas_call | solution.py:674
  (23 shorter events, 0.2 us)
Async XLA Ops:
  0.6 7.2 %copy-start.6 = (s32[128,1,2,3]{0,2,3,1:T(2,128)S(1)}, s32[128,1,2,3]{0,2,3,1:T(2,128)}, u32[]{:S(2)}) copy-start(s32[128,1,2,3]{0,2,3,1:T(2,128)} %param.11) | copy-start | bytes 9220
  0.6 13.3 %copy-start.5 = (s32[128,128]{1,0:T(8,128)S(1)}, s32[128,128]{1,0:T(8,128)}, u32[]{:S(2)}) copy-start(s32[128,128]{1,0:T(8,128)} %param.10) | copy-start | bytes 196612
  0.7 14.4 %copy-start.4 = (f32[128,8]{0,1:T(8,128)S(1)}, f32[128,8]{0,1:T(8,128)}, u32[]{:S(2)}) copy-start(f32[128,8]{0,1:T(8,128)} %param.14) | copy-start | bytes 12292
  0.7 14.4 %copy-start.1 = (f32[128,128]{1,0:T(8,128)S(1)}, f32[128,128]{1,0:T(8,128)}, u32[]{:S(2)}) copy-start(f32[128,128]{1,0:T(8,128)} %refs_10_.1) | copy-start | bytes 196612
  0.7 14.4 %copy-start.2 = (f32[128,128]{1,0:T(8,128)S(1)}, f32[128,128]{1,0:T(8,128)}, u32[]{:S(2)}) copy-start(f32[128,128]{1,0:T(8,128)} %refs_11_.1) | copy-start | bytes 196612
  2.3 52.6 %copy-start.3 = (f32[8,128]{1,0:T(8,128)S(1)}, f32[8,128]{1,0:T(8,128)}, u32[]{:S(2)}) copy-start(f32[8,128]{1,0:T(8,128)} %refs_5_.1) | copy-start | bytes 12292
  2.3 57.9 %copy-start = (bf16[32,128,128]{2,1,0:T(8,128)(2,1)S(1)}, bf16[32,128,128]{2,1,0:T(8,128)(2,1)}, u32[]{:S(2)}) copy-start(bf16[32,128,128]{2,1,0:T(8,128)(2,1)} %refs_6_.1) | copy-start | bytes 3145732
  2.3 6.5 %collective-permute-start = (bf16[2,128,128]{2,1,0:T(8,128)(2,1)S(1)}, bf16[2,128,128]{2,1,0:T(8,128)(2,1)S(1)}, u32[]{:S(2)}, u32[]{:S(2)}) collective-permute-start(bf16[2,128,128]{2,1,0:T(8,128)(2,1)S(1)} %get-tuple-element.23), channel_id=1, source_target_pairs={{0,2},{1,3},{2,4},{3,5},{4,6},{5,7},{6,8},{7,9},{8,10},{9,11},{10,... | collective-permute-start | bytes 196616 | tf_op jit(solution)/shard_map/ppermute | solution.py:720
  6.5 6.4 %collective-permute-start.1 = (bf16[2,128,128]{2,1,0:T(8,128)(2,1)S(1)}, bf16[2,128,128]{2,1,0:T(8,128)(2,1)S(1)}, u32[]{:S(2)}, u32[]{:S(2)}) collective-permute-start(bf16[2,128,128]{2,1,0:T(8,128)(2,1)S(1)} %get-tuple-element.24), channel_id=1, source_target_pairs={{2,0},{3,1},{4,2},{5,3},{6,4},{7,5},{8,6},{9,7},{10,8},{11,9},{12,... | collective-permute-start | bytes 196616 | tf_op jit(solution)/shard_map/ppermute | solution.py:720
  12.9 2.2 %collective-permute-start.2 = (f32[4,144,128]{2,1,0:T(8,128)S(1)}, f32[4,144,128]{2,1,0:T(8,128)S(1)}, u32[]{:S(2)}, u32[]{:S(2)}) collective-permute-start(f32[4,144,128]{2,1,0:T(8,128)S(1)} %frame.1), channel_id=1, source_target_pairs={{0,1},{1,0},{2,3},{3,2},{4,5},{5,4},{6,7},{7,6},{8,9},{9,8},{10,11... | collective-permute-start | bytes 884744 | tf_op jit(solution)/shard_map/ppermute | solution.py:720
  35.4 13.7 %all-to-all-start = ((bf16[4,272,256]{2,1,0:T(8,128)(2,1)}), bf16[4,272,256]{2,1,0:T(8,128)(2,1)S(1)}, u32[]{:S(2)}, u32[]{:S(2)}) async-start(bf16[4,272,256]{2,1,0:T(8,128)(2,1)} %get-tuple-element.27), calls=%async_computation | async-start | bytes 1114112 | tf_op jit(solution)/shard_map/all_to_all | solution.py:756
  39.4 11.1 %collective-permute-start.6 = (bf16[128,128]{1,0:T(8,128)(2,1)S(1)}, bf16[128,128]{1,0:T(8,128)(2,1)S(1)}, u32[]{:S(2)}, u32[]{:S(2)}) collective-permute-start(bf16[128,128]{1,0:T(8,128)(2,1)S(1)} %get-tuple-element.32.refs_7_), channel_id=1, source_target_pairs={{24,0},{25,1},{26,2},{27,3},{28,4},{29,5},{30,6},{31,7}} | collective-permute-start | bytes 98312 | tf_op jit(solution)/shard_map/ppermute | solution.py:774
  40.7 14.4 %collective-permute-start.7 = (bf16[128,128]{1,0:T(8,128)(2,1)S(1)}, bf16[128,128]{1,0:T(8,128)(2,1)S(1)}, u32[]{:S(2)}, u32[]{:S(2)}) collective-permute-start(bf16[128,128]{1,0:T(8,128)(2,1)S(1)} %get-tuple-element.32.refs_7_), channel_id=1, source_target_pairs={{24,8},{25,9},{26,10},{27,11},{28,12},{29,13},{30,14},{31,15}} | collective-permute-start | bytes 98312 | tf_op jit(solution)/shard_map/ppermute | solution.py:774
  41.4 13.7 %collective-permute-start.8 = (bf16[128,128]{1,0:T(8,128)(2,1)S(1)}, bf16[128,128]{1,0:T(8,128)(2,1)S(1)}, u32[]{:S(2)}, u32[]{:S(2)}) collective-permute-start(bf16[128,128]{1,0:T(8,128)(2,1)S(1)} %get-tuple-element.32.refs_7_), channel_id=1, source_target_pairs={{24,16},{25,17},{26,18},{27,19},{28,20},{29,21},{30,22},{31,23}} | collective-permute-start | bytes 98312 | tf_op jit(solution)/shard_map/ppermute | solution.py:774
  49.1 6.0 %collective-permute-start.3 = (bf16[208,256]{1,0:T(8,128)(2,1)S(1)}, bf16[208,256]{1,0:T(8,128)(2,1)S(1)}, u32[]{:S(2)}, u32[]{:S(2)}) collective-permute-start(bf16[208,256]{1,0:T(8,128)(2,1)S(1)} %get-tuple-element.29), channel_id=1, source_target_pairs={{0,1},{1,2},{2,3},{3,4},{4,5},{5,6},{6,7},{7,0},{8,9},{9,10},{10,1... | collective-permute-start | bytes 319496 | tf_op jit(solution)/shard_map/ppermute | solution.py:766
  49.3 8.9 %collective-permute-start.4 = (bf16[208,256]{1,0:T(8,128)(2,1)S(1)}, bf16[208,256]{1,0:T(8,128)(2,1)S(1)}, u32[]{:S(2)}, u32[]{:S(2)}) collective-permute-start(bf16[208,256]{1,0:T(8,128)(2,1)S(1)} %get-tuple-element.30), channel_id=1, source_target_pairs={{0,2},{1,3},{2,4},{3,5},{4,6},{5,7},{6,0},{7,1},{8,10},{9,11},{10,... | collective-permute-start | bytes 319496 | tf_op jit(solution)/shard_map/ppermute | solution.py:766
  50.6 9.6 %collective-permute-start.5 = (bf16[208,256]{1,0:T(8,128)(2,1)S(1)}, bf16[208,256]{1,0:T(8,128)(2,1)S(1)}, u32[]{:S(2)}, u32[]{:S(2)}) collective-permute-start(bf16[208,256]{1,0:T(8,128)(2,1)S(1)} %get-tuple-element.31), channel_id=1, source_target_pairs={{0,3},{1,4},{2,5},{3,6},{4,7},{5,0},{6,1},{7,2},{8,11},{9,12},{10,... | collective-permute-start | bytes 319496 | tf_op jit(solution)/shard_map/ppermute | solution.py:766
  66.5 21.6 %collective-permute-start.10 = (f32[2,128,128]{2,1,0:T(8,128)S(1)}, f32[2,128,128]{2,1,0:T(8,128)S(1)}, u32[]{:S(2)}, u32[]{:S(2)}) collective-permute-start(f32[2,128,128]{2,1,0:T(8,128)S(1)} %get-tuple-element.34.refs_3_), channel_id=1, source_target_pairs={{8,24},{9,25},{10,26},{11,27},{12,28},{13,29},{14,30},{15,31}} | collective-permute-start | bytes 393224 | tf_op jit(solution)/shard_map/ppermute | solution.py:774
  67.1 22.9 %collective-permute-start.11 = (f32[2,128,128]{2,1,0:T(8,128)S(1)}, f32[2,128,128]{2,1,0:T(8,128)S(1)}, u32[]{:S(2)}, u32[]{:S(2)}) collective-permute-start(f32[2,128,128]{2,1,0:T(8,128)S(1)} %get-tuple-element.34.refs_3_), channel_id=1, source_target_pairs={{16,24},{17,25},{18,26},{19,27},{20,28},{21,29},{22,30},{23,31}} | collective-permute-start | bytes 393224 | tf_op jit(solution)/shard_map/ppermute | solution.py:774
  67.8 22.2 %collective-permute-start.9 = (f32[2,128,128]{2,1,0:T(8,128)S(1)}, f32[2,128,128]{2,1,0:T(8,128)S(1)}, u32[]{:S(2)}, u32[]{:S(2)}) collective-permute-start(f32[2,128,128]{2,1,0:T(8,128)S(1)} %get-tuple-element.34.refs_3_), channel_id=1, source_target_pairs={{0,24},{1,25},{2,26},{3,27},{4,28},{5,29},{6,30},{7,31}} | collective-permute-start | bytes 393224 | tf_op jit(solution)/shard_map/ppermute | solution.py:774
  72.1 7.6 %all-to-all-start.1 = ((f32[4,128,128]{2,1,0:T(8,128)}), f32[4,128,128]{2,1,0:T(8,128)S(1)}, u32[]{:S(2)}, u32[]{:S(2)}) async-start(f32[4,128,128]{2,1,0:T(8,128)} %get-tuple-element.36), calls=%async_computation.1 | async-start | bytes 524288 | tf_op jit(solution)/shard_map/all_to_all | solution.py:756
  79.9 10.9 %collective-permute-start.12 = (f32[64,128]{1,0:T(8,128)S(1)}, f32[64,128]{1,0:T(8,128)S(1)}, u32[]{:S(2)}, u32[]{:S(2)}) collective-permute-start(f32[64,128]{1,0:T(8,128)S(1)} %get-tuple-element.39), channel_id=1, source_target_pairs={{0,7},{1,0},{2,1},{3,2},{4,3},{5,4},{6,5},{7,6},{8,15},{9,8},{10,9... | collective-permute-start | bytes 98312 | tf_op jit(solution)/shard_map/ppermute | solution.py:766
  85.0 5.9 %collective-permute-start.13 = (f32[64,128]{1,0:T(8,128)S(1)}, f32[64,128]{1,0:T(8,128)S(1)}, u32[]{:S(2)}, u32[]{:S(2)}) collective-permute-start(f32[64,128]{1,0:T(8,128)S(1)} %get-tuple-element.40), channel_id=1, source_target_pairs={{0,6},{1,7},{2,0},{3,1},{4,2},{5,3},{6,4},{7,5},{8,14},{9,15},{10,... | collective-permute-start | bytes 98312 | tf_op jit(solution)/shard_map/ppermute | solution.py:766
  88.1 6.5 %collective-permute-start.14 = (f32[64,128]{1,0:T(8,128)S(1)}, f32[64,128]{1,0:T(8,128)S(1)}, u32[]{:S(2)}, u32[]{:S(2)}) collective-permute-start(f32[64,128]{1,0:T(8,128)S(1)} %get-tuple-element.41), channel_id=1, source_target_pairs={{0,5},{1,6},{2,7},{3,0},{4,1},{5,2},{6,3},{7,4},{8,13},{9,14},{10,... | collective-permute-start | bytes 98312 | tf_op jit(solution)/shard_map/ppermute | solution.py:766

commit v6 on v5

--- a/solution.py
+++ b/solution.py
@@ -107,12 +107,12 @@
     (mask, mix_atm, mix_ocn, flux_map) = refs[9:13]
     out, surface, sea_copy = refs[13:16]
     packed = refs[16]
-    (values, moved, halo_moved, smooth, pairs, later_smooth, later_pairs) = refs[17:24]
-    (weights, flux_weights, fluxes, staged, top, in_sems, out_sems) = refs[24:]
+    (values, moved, halo_moved, smooth, pairs, mixed, later_smooth, later_pairs, later_mixed) = refs[17:26]
+    (weights, flux_weights, fluxes, staged, top, in_sems, out_sems) = refs[26:]
     left_cols = left_in.at[left_at : left_at + 2]
     right_cols = right_in.at[right_at : right_at + 2]
-    first = (smooth, pairs)
-    second = (later_smooth, later_pairs)
+    first = (smooth, pairs, mixed)
+    second = (later_smooth, later_pairs, later_mixed)
     rows, cols, levels = state.shape
     chunks = rows // CHUNK
     inner = pl.ds(EDGE, cols)
@@ -191,12 +191,11 @@
         top[...] = jnp.where(lanes // CHUNK == q, turned, top[...])
 
     def mix_rows(refs, count):
-        both = dot_nn(refs[1][: count * cols, :], weights[...])
-        both = both[:, :levels] + both[:, levels:]
-        return [
-            refs[0][row] + PHYSICS * jnp.tanh(both[row * cols : (row + 1) * cols, :])
-            for row in range(count)
-        ]
+        refs[2][: count * cols, :] = dot_nn(refs[1][: count * cols, :], weights[...])
+
+    def finish(refs, row):
+        part = refs[2][row * cols : (row + 1) * cols, :]
+        return refs[0][row] + PHYSICS * jnp.tanh(part[:, :levels] + part[:, levels:])
 
     @pl.when(jnp.logical_not(ocean))
     def atmosphere():
@@ -210,8 +209,9 @@
                 + nearest[s][EDGE + 1 : EDGE + 1 + rows, :]
             )
             stage(first, s, total + (beyond[s][EDGE : EDGE + rows, :] + within[s][...]))
-        for s, line in enumerate(mix_rows(first, 2)):
-            halo_moved[s] = line
+        mix_rows(first, 2)
+        for s in range(2):
+            halo_moved[s] = finish(first, s)
 
         def moved_sides(r, _):
             moved[r + 1, EDGE - 1 : EDGE, :] = halo_moved[0, pl.ds(r, 1), :]
@@ -222,8 +222,9 @@
         fetch(0).wait()
         fetch(1).wait()
         stage_rows(second, values, 1, 2)
-        for row, line in enumerate(mix_rows(second, 2)):
-            moved[row, EDGE : EDGE + cols, :] = line
+        mix_rows(second, 2)
+        for row in range(2):
+            moved[row, EDGE : EDGE + cols, :] = finish(second, row)
 
         @pl.when(flags[1] == 0)
         def _():
@@ -231,16 +232,18 @@
 
         def begin_first(q):
             stage_rows(first, values, q * CHUNK + 3, CHUNK)
+            mix_rows(first, CHUNK)
 
         def end_first(q):
-            for row, line in enumerate(mix_rows(first, CHUNK)):
-                moved[q * CHUNK + row + 2, EDGE : EDGE + cols, :] = line
+            for row in range(CHUNK):
+                moved[q * CHUNK + row + 2, EDGE : EDGE + cols, :] = finish(first, row)
 
         def begin_second(q):
             stage_rows(second, moved, q * CHUNK + 1, CHUNK)
 
         def end_second(q, slot):
-            for row, line in enumerate(mix_rows(second, CHUNK)):
+            for row in range(CHUNK):
+                line = finish(second, row)
                 staged[slot, row] = line
                 both = line + moved[q * CHUNK + row + 1, EDGE : EDGE + cols, :]
                 later_pairs[row * cols : (row + 1) * cols, :] = side_by_side(both)
@@ -272,6 +275,7 @@
             begin_first(q)
             begin_second(q - 1)
             end_first(q)
+            mix_rows(second, CHUNK)
             end_second(q - 1, slot)
             return 0
 
@@ -284,6 +288,7 @@
         last = chunks - 1
         put(last - 2, last % 2).wait()
         begin_second(last)
+        mix_rows(second, CHUNK)
         end_second(last, last % 2)
         put(last - 1, (last - 1) % 2).wait()
         put(last, last % 2).wait()
@@ -314,6 +319,7 @@
                 fetch(q + 1).wait()
 
             stage_rows(first, values, base + 2, CHUNK)
+            mix_rows(first, CHUNK)
             slot = q % 2
 
             @pl.when(q >= 2)
@@ -321,10 +327,10 @@
                 put(q - 2, slot).wait()
 
             sea = dot_nn(mask[pl.ds(pl.multiple_of(base, CHUNK), CHUNK), :].T, spreader)
-            for row, line in enumerate(mix_rows(first, CHUNK)):
+            for row in range(CHUNK):
                 chosen = sea[:, row * levels : (row + 1) * levels] > 0.5
                 before = values[base + row + 2, EDGE : EDGE + cols, :]
-                staged[slot, row] = jnp.where(chosen, line, before)
+                staged[slot, row] = jnp.where(chosen, finish(first, row), before)
             put(q, slot).start()
             note_top(q, [staged[slot, row] for row in range(CHUNK)])
             return 0
@@ -364,8 +370,10 @@
             pltpu.VMEM((2, rows, levels), F32),
             pltpu.VMEM((CHUNK, cols, levels), F32),
             pltpu.VMEM((CHUNK * cols, 2 * levels), BF16),
+            pltpu.VMEM((CHUNK * cols, 2 * levels), F32),
             pltpu.VMEM((CHUNK, cols, levels), F32),
             pltpu.VMEM((CHUNK * cols, 2 * levels), BF16),
+            pltpu.VMEM((CHUNK * cols, 2 * levels), F32),
             pltpu.VMEM((2 * levels, 2 * levels), BF16),
             pltpu.VMEM((2 * fluxes, 2 * levels), BF16),
             pltpu.VMEM((rows * fluxes, cols), F32),
@@ -419,10 +427,10 @@
 def regrid_body(count, comp_count, flags, ocean_first, *refs):
     blocks = refs[:count]
     seas = refs[count : count + comp_count]
-    weights, surface, mask, forcing, shared, hits, entries, chosen, binned = refs[count + comp_count :]
+    weights, surface, mask, shared, hits, entries, chosen, binned = refs[count + comp_count :]
     sources = comp_count - 1
     rows, cols = mask.shape
-    share = forcing.shape[0]
+    share = shared.shape[0] - 1
     weight_count = weights.shape[0]
     capacity = (blocks[0].shape[0] - LABEL_ROWS) // sources
     size = count * capacity
@@ -464,17 +472,15 @@
             part = dot_nn(jnp.concatenate([h for h, _ in halves], axis=1), wide) + dot_nn(
                 jnp.concatenate([l for _, l in halves], axis=1), wide
             )
-            forcing[f] = part if g == 0 else forcing[f] + part
-    change = ocean_first[flags[3] * share] * forcing[0]
+            shared[f] = part if g == 0 else shared[f] + part
+    change = ocean_first[flags[3] * share] * shared[0]
     for f in range(1, share):
-        change = change + ocean_first[flags[3] * share + f] * forcing[f]
+        change = change + ocean_first[flags[3] * share + f] * shared[f]
     sea = jnp.where(flags[0] == 1, seas[sources][...].astype(F32), 0.0)
     for c in range(sources):
         sea = sea + jnp.where(flags[3] == c, seas[c][...].astype(F32), 0.0)
     base = jnp.where(flags[0] == 1, surface[...], 0.0)
-    value = base + jnp.where(sea > 0.5, change, 0.0)
-    for c in range(comp_count):
-        shared[c] = value
+    shared[share] = base + jnp.where(sea > 0.5, change, 0.0)
 
 
 def regrid(flags, ocean_first, blocks, seas, weights, surface, mask):
@@ -492,12 +498,11 @@
     return pl.pallas_call(
         functools.partial(regrid_body, count, comp_count),
         out_shape=(
-            jax.ShapeDtypeStruct((share, rows, cols), F32),
-            jax.ShapeDtypeStruct((comp_count, rows, cols), F32),
+            jax.ShapeDtypeStruct((share + 1, rows, cols), F32),
             jax.ShapeDtypeStruct((size, rows), BF16),
         ),
         in_specs=[smem, smem] + [vmem] * (count + comp_count + 3),
-        out_specs=(vmem, vmem, vmem),
+        out_specs=(vmem, vmem),
         scratch_shapes=[
             pltpu.VMEM((total, width), BF16),
             pltpu.VMEM((BATCH * rows, total), BF16),
@@ -513,10 +518,14 @@
     )(flags, ocean_first, *blocks, *seas, weights, surface, mask)
 
 
-def pick_kernel(parts, hits, surface, *picked):
-    now = parts[0]
-    for c in range(1, parts.shape[0]):
-        now = now + parts[c]
+def pick_kernel(count, *refs):
+    parts = refs[:count]
+    hits, surface = refs[count : count + 2]
+    picked = refs[count + 2 :]
+    share = parts[0].shape[0] - 1
+    now = parts[0][share]
+    for part in parts[1:]:
+        now = now + part[share]
     surface[...] = now
     pair = jnp.concatenate(split_two(now), axis=0)
     size = picked[0].shape[0]
@@ -526,18 +535,18 @@
 
 
 def pick(parts, hits, neighbours):
-    _, rows, cols = parts.shape
+    _, rows, cols = parts[0].shape
     size = hits.shape[0] // neighbours
     vmem = pl.BlockSpec(memory_space=pltpu.VMEM)
     return pl.pallas_call(
-        pick_kernel,
+        functools.partial(pick_kernel, len(parts)),
         out_shape=(jax.ShapeDtypeStruct((rows, cols), F32),)
         + (jax.ShapeDtypeStruct((size, cols), F32),) * neighbours,
-        in_specs=[vmem] * 2,
+        in_specs=[vmem] * (len(parts) + 1),
         out_specs=(vmem,) * (1 + neighbours),
         compiler_params=pltpu.CompilerParams(vmem_limit_bytes=16 * MIB),
         name="pick",
-    )(parts, hits)
+    )(*parts, hits)
 
 
 LINES = 8
@@ -547,7 +556,7 @@
     parts = refs[:groups]
     mask, ocean_map, out, token, held, table, wide, in_sems, out_sems = refs[groups:]
     rows, cols, levels = state.shape
-    share = parts[0].shape[0]
+    share = parts[0].shape[0] - 1
     flux_count = groups * share
     chunks = rows // LINES
     depth = LINES * flux_count
@@ -755,6 +764,14 @@
     def over_comp(value):
         return lax.all_to_all(value, "comp", split_axis=0, concat_axis=0, tiled=True)
 
+    def shifted_comp(value, shift):
+        pairs = [
+            (c * tile_count + t, (c + shift) % comp_count * tile_count + t)
+            for c in range(comp_count)
+            for t in range(tile_count)
+        ]
+        return lax.ppermute(value, AXES, pairs)
+
     def over_tiles(value, offset, comps):
         if offset % tile_count == 0:
             return value
@@ -765,12 +782,10 @@
         ]
         return lax.ppermute(value, AXES, pairs)
 
-    def with_ocean(value, comp, back):
+    def from_ocean(value, comp):
         pairs = [
-            (comp * tile_count + t, ocean_comp * tile_count + t) for t in range(tile_count)
+            (ocean_comp * tile_count + t, comp * tile_count + t) for t in range(tile_count)
         ]
-        if back:
-            pairs = [(there, here) for here, there in pairs]
         return lax.ppermute(value, AXES, pairs)
 
     label_lines = jnp.stack([packed_labels // rows, packed_labels % rows]).astype(BF16)
@@ -783,16 +798,17 @@
     )
     moved, surface, sea_copy, packed = moved
     slabs = over_comp(packed)
-    seas = [with_ocean(sea_copy, c, True) for c in range(ocean_comp)] + [sea_copy]
+    seas = [from_ocean(sea_copy, c) for c in range(ocean_comp)] + [sea_copy]
     blocks = regroup(slabs, neighbours)
     blocks = [over_tiles(blocks[n], offsets[n], comp_count) for n in range(neighbours)]
-    forcing, shared, hits = regrid(
+    shared, hits = regrid(
         flags, ocean_map[:, 0], blocks, seas, regrid_weights, surface, mask
     )
-    picks = pick(over_comp(shared), hits, neighbours)
+    parts = [shared] + [shifted_comp(shared, s) for s in range(1, comp_count)]
+    picks = pick(parts, hits, neighbours)
     new_surface, picked = picks[0], picks[1:]
     arrived = [over_tiles(picked[n], -offsets[n], ocean_comp) for n in range(neighbours)]
-    fields = [with_ocean(forcing, c, False) for c in range(ocean_comp)] + [forcing]
+    fields = parts[:0:-1] + parts[:1]
     final_state, token = update(flags, moved, fields, mask, ocean_map)
     weight_column = (packed_labels // rows)[:, None]
     surface_out = returned(

time: 97.5 us -> 92.4 us (0.948)
  starting transfers between devices: 37.9 us -> 31.7 us
  waiting for transfers between devices: 25 us -> 27.9 us
  Pallas kernels: 31.7 us -> 30.1 us
    ppermute x6, waiting for transfers between devices: 0.02 us -> 7.54 us  [the longest x3 7.53 us: shifted_comp(): return lax.ppermute(value, AXES, pairs)]
    all_to_all x2 -> x1, waiting for transfers between devices: 11.2 us -> 7.07 us  [over_comp(): lax.all_to_all(value, 'comp', split_axis=0, concat_axis=0, tiled=True)]
    ppermute x6, starting transfers between devices: 8.24 us -> 4.57 us  [the longest x3 2.61 us: from_ocean(): return lax.ppermute(value, AXES, pairs)]
    all_to_all x2 -> x1, starting transfers between devices: 7.42 us -> 4 us  [over_comp(): lax.all_to_all(value, 'comp', split_axis=0, concat_axis=0, tiled=True)]
  transfers between devices with their start and end apart: 17 -> 16, of which waited for: 7 -> 9; matrix products, arithmetic and copies ran while one was open for 1% -> 1% of each run, Pallas kernels for 1% -> 1%
where the time goes in v6:
time: 92.4 us; the launch traced here: 92 us
  starting transfers between devices  31.7 us (34%)
  Pallas kernels  30.1 us (33%)
  waiting for transfers between devices  27.9 us (30%)
  between operations  0.96 us (1%)
    pallas_call x1, Pallas kernels, advance(): pl.pallas_call(functools.partial(advance_kernel, comp_count, left_at, rig...  19.4 us
    ppermute x6, starting transfers between devices, over_tiles(): return lax.ppermute(value, AXES, pairs)  16.7 us
    ppermute x6, waiting for transfers between devices, over_tiles(): return lax.ppermute(value, AXES, pairs)  8.12 us
    ppermute x3, waiting for transfers between devices, shifted_comp(): return lax.ppermute(value, AXES, pairs)  7.53 us
    all_to_all x1, waiting for transfers between devices, over_comp(): lax.all_to_all(value, 'comp', split_axis=0, concat_axis=0, tiled=True)  7.07 us
    ppermute x3, starting transfers between devices, band_shift(): return lax.ppermute(value, AXES, pairs)  6.48 us
    pallas_call x1, Pallas kernels, regrid(): pl.pallas_call(functools.partial(regrid_body, count, comp_count), out_sha...  5.6 us
    ppermute x3, waiting for transfers between devices, band_shift(): return lax.ppermute(value, AXES, pairs)  5.13 us
  transfers between devices with their start and end apart: 16, of which 9 were waited for; matrix products, arithmetic and copies ran while one was open for 1% of the time, Pallas kernels for 1%

profile of v6, /device:TPU:1, one launch (start us, length us, event | category | flops | bytes accessed | tf_op | source)
XLA Modules:
  0.0 92.0 jit_solution(17913477474780975513)
XLA Ops:
  0.7 1.6 %edges.1 = (bf16[2,128,128]{2,1,0:T(8,128)(2,1)S(1)}, bf16[2,128,128]{2,1,0:T(8,128)(2,1)S(1)}, f32[4,128,128]{2,1,0:T(8,128)S(1)}) custom-call(f32[128,128,128]{2,1,0:T(8,128)} %refs_3_.1), custom_call_target="tpu_custom_call" | custom-call | tf_op jit(solution)/shard_map/edges/pallas_call | solution.py:63
  2.3 0.0 copy-start.3
  2.3 0.0 copy-start
  2.3 4.2 %collective-permute-start = (bf16[2,128,128]{2,1,0:T(8,128)(2,1)S(1)}, bf16[2,128,128]{2,1,0:T(8,128)(2,1)S(1)}, u32[]{:S(2)}, u32[]{:S(2)}) collective-permute-start(bf16[2,128,128]{2,1,0:T(8,128)(2,1)S(1)} %get-tuple-element.22), channel_id=1, source_target_pairs={{0,2},{1,3},{2,4},{3,5},{4,6},{5,7},{6,8},{7,9},{8,10},{9,11},{10,... | collective-permute-start | bytes 196616 | tf_op jit(solution)/shard_map/ppermute | solution.py:729
  6.5 1.3 %collective-permute-start.1 = (bf16[2,128,128]{2,1,0:T(8,128)(2,1)S(1)}, bf16[2,128,128]{2,1,0:T(8,128)(2,1)S(1)}, u32[]{:S(2)}, u32[]{:S(2)}) collective-permute-start(bf16[2,128,128]{2,1,0:T(8,128)(2,1)S(1)} %get-tuple-element.23), channel_id=1, source_target_pairs={{2,0},{3,1},{4,2},{5,3},{6,4},{7,5},{8,6},{9,7},{10,8},{11,9},{12,... | collective-permute-start | bytes 196616 | tf_op jit(solution)/shard_map/ppermute | solution.py:729
  7.8 0.2 copy.19
  8.0 0.3 fusion.4
  8.3 0.2 convert_reduce_fusion
  8.5 0.2 select_reduce_fusion
  8.6 0.1 copy.20.refs_1_
  8.8 0.0 collective-permute-done.up_rows.refs_4_
  8.8 4.0 %collective-permute-done.1.low_rows.refs_5_ = bf16[2,128,128]{2,1,0:T(8,128)(2,1)S(1)} collective-permute-done((bf16[2,128,128]{2,1,0:T(8,128)(2,1)S(1)}, bf16[2,128,128]{2,1,0:T(8,128)(2,1)S(1)}, u32[]{:S(2)}, u32[]{:S(2)}) %collective-permute-start.1) | collective-permute-done | bytes 65568 | tf_op jit(solution)/shard_map/ppermute | solution.py:729
  12.9 1.0 %collective-permute-start.2 = (f32[4,144,128]{2,1,0:T(8,128)S(1)}, f32[4,144,128]{2,1,0:T(8,128)S(1)}, u32[]{:S(2)}, u32[]{:S(2)}) collective-permute-start(f32[4,144,128]{2,1,0:T(8,128)S(1)} %frame.1), channel_id=1, source_target_pairs={{0,1},{1,0},{2,3},{3,2},{4,5},{5,4},{6,7},{7,6},{8,9},{9,8},{10,11... | collective-permute-start | bytes 884744 | tf_op jit(solution)/shard_map/ppermute | solution.py:729
  13.9 0.1 pad_add_fusion.refs_0_.flags
  14.0 1.1 %collective-permute-done.2.refs_6_.refs_7_ = f32[4,144,128]{2,1,0:T(8,128)S(1)} collective-permute-done((f32[4,144,128]{2,1,0:T(8,128)S(1)}, f32[4,144,128]{2,1,0:T(8,128)S(1)}, u32[]{:S(2)}, u32[]{:S(2)}) %collective-permute-start.2) | collective-permute-done | bytes 294944 | tf_op jit(solution)/shard_map/ppermute | solution.py:729
  15.1 19.4 %advance.1 = (f32[128,128,128]{2,1,0:T(8,128)}, f32[128,128]{1,0:T(8,128)S(1)}, bf16[128,128]{1,0:T(8,128)(2,1)S(1)}, bf16[4,272,256]{2,1,0:T(8,128)(2,1)}) custom-call(s32[4]{0:T(128)S(1)} %pad_add_fusion.refs_0_.flags, s32[256,1]{1,0:T(8,128)S(1)} %copy.20.refs_1_, bf16[16,256]{1,0:T(8,128)(2,1)S(1)} %fusion.9.refs_2_, f32[128,128,128]{2,1,0:T(8,128)} %refs_3_.1, ...), custom_call_target="tpu_custom_call" | custom-call | flops 2147483648 | bytes 16777216 | tf_op jit(solution)/shard_map/advance/pallas_call | solution.py:357
  34.5 4.0 %all-to-all-start = ((bf16[4,272,256]{2,1,0:T(8,128)(2,1)}), bf16[4,272,256]{2,1,0:T(8,128)(2,1)S(1)}, u32[]{:S(2)}, u32[]{:S(2)}) async-start(bf16[4,272,256]{2,1,0:T(8,128)(2,1)} %get-tuple-element.26), calls=%async_computation | async-start | bytes 1114112 | tf_op jit(solution)/shard_map/all_to_all | solution.py:765
  38.5 1.3 %collective-permute-start.6 = (bf16[128,128]{1,0:T(8,128)(2,1)S(1)}, bf16[128,128]{1,0:T(8,128)(2,1)S(1)}, u32[]{:S(2)}, u32[]{:S(2)}) collective-permute-start(bf16[128,128]{1,0:T(8,128)(2,1)S(1)} %get-tuple-element.31.refs_7_), channel_id=1, source_target_pairs={{24,0},{25,1},{26,2},{27,3},{28,4},{29,5},{30,6},{31,7}} | collective-permute-start | bytes 98312 | tf_op jit(solution)/shard_map/ppermute | solution.py:789
  39.8 0.7 collective-permute-start.7
  40.5 0.7 collective-permute-start.8
  41.2 7.1 %all-to-all-done.slabs = bf16[4,272,256]{2,1,0:T(8,128)(2,1)S(1)} async-done(((bf16[4,272,256]{2,1,0:T(8,128)(2,1)}), bf16[4,272,256]{2,1,0:T(8,128)(2,1)S(1)}, u32[]{:S(2)}, u32[]{:S(2)}) %all-to-all-start) | async-done | bytes 557088 | tf_op jit(solution)/shard_map/all_to_all | solution.py:765
  48.3 0.1 collective-permute-start.3
  48.4 1.3 %collective-permute-start.4 = (bf16[208,256]{1,0:T(8,128)(2,1)S(1)}, bf16[208,256]{1,0:T(8,128)(2,1)S(1)}, u32[]{:S(2)}, u32[]{:S(2)}) collective-permute-start(bf16[208,256]{1,0:T(8,128)(2,1)S(1)} %get-tuple-element.29), channel_id=1, source_target_pairs={{0,2},{1,3},{2,4},{3,5},{4,6},{5,7},{6,0},{7,1},{8,10},{9,11},{10,... | collective-permute-start | bytes 319496 | tf_op jit(solution)/shard_map/ppermute | solution.py:783
  49.7 0.0 collective-permute-done.6.refs_4_
  49.7 4.3 %collective-permute-start.5 = (bf16[208,256]{1,0:T(8,128)(2,1)S(1)}, bf16[208,256]{1,0:T(8,128)(2,1)S(1)}, u32[]{:S(2)}, u32[]{:S(2)}) collective-permute-start(bf16[208,256]{1,0:T(8,128)(2,1)S(1)} %get-tuple-element.30), channel_id=1, source_target_pairs={{0,3},{1,4},{2,5},{3,6},{4,7},{5,0},{6,1},{7,2},{8,11},{9,12},{10,... | collective-permute-start | bytes 319496 | tf_op jit(solution)/shard_map/ppermute | solution.py:783
  54.0 0.1 slice_reduce_fusion.ocean_first
  54.1 0.1 copy.21
  54.2 0.0 collective-permute-done.7.refs_5_
  54.2 0.0 collective-permute-done.8.refs_6_
  54.2 0.0 collective-permute-done.3.refs_1_
  54.2 2.9 %collective-permute-done.4.refs_2_ = bf16[208,256]{1,0:T(8,128)(2,1)S(1)} collective-permute-done((bf16[208,256]{1,0:T(8,128)(2,1)S(1)}, bf16[208,256]{1,0:T(8,128)(2,1)S(1)}, u32[]{:S(2)}, u32[]{:S(2)}) %collective-permute-start.4) | collective-permute-done | bytes 106528 | tf_op jit(solution)/shard_map/ppermute | solution.py:783
  57.2 2.1 %collective-permute-done.5.refs_3_ = bf16[208,256]{1,0:T(8,128)(2,1)S(1)} collective-permute-done((bf16[208,256]{1,0:T(8,128)(2,1)S(1)}, bf16[208,256]{1,0:T(8,128)(2,1)S(1)}, u32[]{:S(2)}, u32[]{:S(2)}) %collective-permute-start.5) | collective-permute-done | bytes 106528 | tf_op jit(solution)/shard_map/ppermute | solution.py:783
  59.3 5.6 %regrid.1 = (f32[3,128,128]{2,1,0:T(8,128)S(1)}, bf16[256,128]{1,0:T(8,128)(2,1)S(1)}) custom-call(s32[4]{0:T(128)S(1)} %pad_add_fusion.refs_0_.flags, f32[8]{0:T(128)S(1)} %slice_reduce_fusion.ocean_first, bf16[208,256]{1,0:T(8,128)(2,1)S(1)} %get-tuple-element.27.refs_0_, bf16[208,256]{1,0:T(8,128)(2,1)S(1)} %collective-permute-done.3.refs_1_, ...), custom_call_target="tpu_custom_call" | custom-call | flops 2147483648 | bytes 2097152 | tf_op jit(solution)/shard_map/regrid/pallas_call | solution.py:498
  64.9 1.2 %collective-permute-start.9 = (f32[3,128,128]{2,1,0:T(8,128)S(1)}, f32[3,128,128]{2,1,0:T(8,128)S(1)}, u32[]{:S(2)}, u32[]{:S(2)}) collective-permute-start(f32[3,128,128]{2,1,0:T(8,128)S(1)} %get-tuple-element.33.refs_3_.refs_0_), channel_id=1, source_target_pairs={{0,24},{1,25},{2,26},{3,27},{4,28},{5,29},{6,30},{7,31},{8,0},{9,1... | collective-permute-start | bytes 589832 | tf_op jit(solution)/shard_map/ppermute | solution.py:773
  66.1 0.6 collective-permute-start.10
  66.6 0.2 collective-permute-start.11
  66.8 0.1 add_select_fusion.refs_4_
  66.9 2.5 %collective-permute-done.9.refs_0_.refs_3_ = f32[3,128,128]{2,1,0:T(8,128)S(1)} collective-permute-done((f32[3,128,128]{2,1,0:T(8,128)S(1)}, f32[3,128,128]{2,1,0:T(8,128)S(1)}, u32[]{:S(2)}, u32[]{:S(2)}) %collective-permute-start.9) | collective-permute-done | bytes 196640 | tf_op jit(solution)/shard_map/ppermute | solution.py:773
  69.5 2.2 %collective-permute-done.10.refs_1_.refs_2_ = f32[3,128,128]{2,1,0:T(8,128)S(1)} collective-permute-done((f32[3,128,128]{2,1,0:T(8,128)S(1)}, f32[3,128,128]{2,1,0:T(8,128)S(1)}, u32[]{:S(2)}, u32[]{:S(2)}) %collective-permute-start.10) | collective-permute-done | bytes 196640 | tf_op jit(solution)/shard_map/ppermute | solution.py:773
  71.7 2.8 %collective-permute-done.11.refs_2_.refs_1_ = f32[3,128,128]{2,1,0:T(8,128)S(1)} collective-permute-done((f32[3,128,128]{2,1,0:T(8,128)S(1)}, f32[3,128,128]{2,1,0:T(8,128)S(1)}, u32[]{:S(2)}, u32[]{:S(2)}) %collective-permute-start.11) | collective-permute-done | bytes 196640 | tf_op jit(solution)/shard_map/ppermute | solution.py:773
  74.5 0.2 pick.1
  74.6 5.1 %collective-permute-start.12 = (f32[64,128]{1,0:T(8,128)S(1)}, f32[64,128]{1,0:T(8,128)S(1)}, u32[]{:S(2)}, u32[]{:S(2)}) collective-permute-start(f32[64,128]{1,0:T(8,128)S(1)} %get-tuple-element.37), channel_id=1, source_target_pairs={{0,7},{1,0},{2,1},{3,2},{4,3},{5,4},{6,5},{7,6},{8,15},{9,8},{10,9... | collective-permute-start | bytes 98312 | tf_op jit(solution)/shard_map/ppermute | solution.py:783
  79.7 3.7 %collective-permute-start.13 = (f32[64,128]{1,0:T(8,128)S(1)}, f32[64,128]{1,0:T(8,128)S(1)}, u32[]{:S(2)}, u32[]{:S(2)}) collective-permute-start(f32[64,128]{1,0:T(8,128)S(1)} %get-tuple-element.38), channel_id=1, source_target_pairs={{0,6},{1,7},{2,0},{3,1},{4,2},{5,3},{6,4},{7,5},{8,14},{9,15},{10,... | collective-permute-start | bytes 98312 | tf_op jit(solution)/shard_map/ppermute | solution.py:783
  83.5 2.2 %collective-permute-start.14 = (f32[64,128]{1,0:T(8,128)S(1)}, f32[64,128]{1,0:T(8,128)S(1)}, u32[]{:S(2)}, u32[]{:S(2)}) collective-permute-start(f32[64,128]{1,0:T(8,128)S(1)} %get-tuple-element.39), channel_id=1, source_target_pairs={{0,5},{1,6},{2,7},{3,0},{4,1},{5,2},{6,3},{7,4},{8,13},{9,14},{10,... | collective-permute-start | bytes 98312 | tf_op jit(solution)/shard_map/ppermute | solution.py:783
  85.6 0.8 update.1
  86.5 0.0 collective-permute-done.13.refs_2_
  86.5 3.1 %collective-permute-done.14.refs_3_ = f32[64,128]{1,0:T(8,128)S(1)} collective-permute-done((f32[64,128]{1,0:T(8,128)S(1)}, f32[64,128]{1,0:T(8,128)S(1)}, u32[]{:S(2)}, u32[]{:S(2)}) %collective-permute-start.14) | collective-permute-done | bytes 32800 | tf_op jit(solution)/shard_map/ppermute | solution.py:783
  89.6 2.4 %returned.1 = f32[128,128]{1,0:T(8,128)} custom-call(s32[4]{0:T(128)S(1)} %pad_add_fusion.refs_0_.flags, f32[64,128]{1,0:T(8,128)S(1)} %get-tuple-element.36.refs_0_, f32[64,128]{1,0:T(8,128)S(1)} %collective-permute-done.12.refs_1_, f32[64,128]{1,0:T(8,128)S(1)} %collective-permute-done.13.refs_2_, f32[64,128]{1,0:T(8,128)S(1)} %collective-permute-done.14.refs_3_, ...), custom_call_target="tpu_custom_call" | custom-call | tf_op jit(solution)/shard_map/returned/pallas_call | solution.py:683
  (21 shorter events, 0.1 us)
Async XLA Ops:
  0.6 7.2 %copy-start.6 = (s32[128,1,2,3]{0,2,3,1:T(2,128)S(1)}, s32[128,1,2,3]{0,2,3,1:T(2,128)}, u32[]{:S(2)}) copy-start(s32[128,1,2,3]{0,2,3,1:T(2,128)} %param.11) | copy-start | bytes 9220
  0.6 13.3 %copy-start.5 = (s32[128,128]{1,0:T(8,128)S(1)}, s32[128,128]{1,0:T(8,128)}, u32[]{:S(2)}) copy-start(s32[128,128]{1,0:T(8,128)} %param.10) | copy-start | bytes 196612
  0.7 14.5 %copy-start.1 = (f32[128,128]{1,0:T(8,128)S(1)}, f32[128,128]{1,0:T(8,128)}, u32[]{:S(2)}) copy-start(f32[128,128]{1,0:T(8,128)} %refs_10_.1) | copy-start | bytes 196612
  0.7 14.4 %copy-start.2 = (f32[128,128]{1,0:T(8,128)S(1)}, f32[128,128]{1,0:T(8,128)}, u32[]{:S(2)}) copy-start(f32[128,128]{1,0:T(8,128)} %refs_11_.1) | copy-start | bytes 196612
  0.7 14.4 %copy-start.4 = (f32[128,8]{0,1:T(8,128)S(1)}, f32[128,8]{0,1:T(8,128)}, u32[]{:S(2)}) copy-start(f32[128,8]{0,1:T(8,128)} %param.14) | copy-start | bytes 12292
  2.3 51.7 %copy-start.3 = (f32[8,128]{1,0:T(8,128)S(1)}, f32[8,128]{1,0:T(8,128)}, u32[]{:S(2)}) copy-start(f32[8,128]{1,0:T(8,128)} %refs_5_.1) | copy-start | bytes 12292
  2.3 57.0 %copy-start = (bf16[32,128,128]{2,1,0:T(8,128)(2,1)S(1)}, bf16[32,128,128]{2,1,0:T(8,128)(2,1)}, u32[]{:S(2)}) copy-start(bf16[32,128,128]{2,1,0:T(8,128)(2,1)} %refs_6_.1) | copy-start | bytes 3145732
  2.3 6.5 %collective-permute-start = (bf16[2,128,128]{2,1,0:T(8,128)(2,1)S(1)}, bf16[2,128,128]{2,1,0:T(8,128)(2,1)S(1)}, u32[]{:S(2)}, u32[]{:S(2)}) collective-permute-start(bf16[2,128,128]{2,1,0:T(8,128)(2,1)S(1)} %get-tuple-element.22), channel_id=1, source_target_pairs={{0,2},{1,3},{2,4},{3,5},{4,6},{5,7},{6,8},{7,9},{8,10},{9,11},{10,... | collective-permute-start | bytes 196616 | tf_op jit(solution)/shard_map/ppermute | solution.py:729
  6.5 6.4 %collective-permute-start.1 = (bf16[2,128,128]{2,1,0:T(8,128)(2,1)S(1)}, bf16[2,128,128]{2,1,0:T(8,128)(2,1)S(1)}, u32[]{:S(2)}, u32[]{:S(2)}) collective-permute-start(bf16[2,128,128]{2,1,0:T(8,128)(2,1)S(1)} %get-tuple-element.23), channel_id=1, source_target_pairs={{2,0},{3,1},{4,2},{5,3},{6,4},{7,5},{8,6},{9,7},{10,8},{11,9},{12,... | collective-permute-start | bytes 196616 | tf_op jit(solution)/shard_map/ppermute | solution.py:729
  12.9 2.2 %collective-permute-start.2 = (f32[4,144,128]{2,1,0:T(8,128)S(1)}, f32[4,144,128]{2,1,0:T(8,128)S(1)}, u32[]{:S(2)}, u32[]{:S(2)}) collective-permute-start(f32[4,144,128]{2,1,0:T(8,128)S(1)} %frame.1), channel_id=1, source_target_pairs={{0,1},{1,0},{2,3},{3,2},{4,5},{5,4},{6,7},{7,6},{8,9},{9,8},{10,11... | collective-permute-start | bytes 884744 | tf_op jit(solution)/shard_map/ppermute | solution.py:729
  34.5 13.7 %all-to-all-start = ((bf16[4,272,256]{2,1,0:T(8,128)(2,1)}), bf16[4,272,256]{2,1,0:T(8,128)(2,1)S(1)}, u32[]{:S(2)}, u32[]{:S(2)}) async-start(bf16[4,272,256]{2,1,0:T(8,128)(2,1)} %get-tuple-element.26), calls=%async_computation | async-start | bytes 1114112 | tf_op jit(solution)/shard_map/all_to_all | solution.py:765
  38.5 11.2 %collective-permute-start.6 = (bf16[128,128]{1,0:T(8,128)(2,1)S(1)}, bf16[128,128]{1,0:T(8,128)(2,1)S(1)}, u32[]{:S(2)}, u32[]{:S(2)}) collective-permute-start(bf16[128,128]{1,0:T(8,128)(2,1)S(1)} %get-tuple-element.31.refs_7_), channel_id=1, source_target_pairs={{24,0},{25,1},{26,2},{27,3},{28,4},{29,5},{30,6},{31,7}} | collective-permute-start | bytes 98312 | tf_op jit(solution)/shard_map/ppermute | solution.py:789
  39.8 14.4 %collective-permute-start.7 = (bf16[128,128]{1,0:T(8,128)(2,1)S(1)}, bf16[128,128]{1,0:T(8,128)(2,1)S(1)}, u32[]{:S(2)}, u32[]{:S(2)}) collective-permute-start(bf16[128,128]{1,0:T(8,128)(2,1)S(1)} %get-tuple-element.31.refs_7_), channel_id=1, source_target_pairs={{24,8},{25,9},{26,10},{27,11},{28,12},{29,13},{30,14},{31,15}} | collective-permute-start | bytes 98312 | tf_op jit(solution)/shard_map/ppermute | solution.py:789
  40.5 13.7 %collective-permute-start.8 = (bf16[128,128]{1,0:T(8,128)(2,1)S(1)}, bf16[128,128]{1,0:T(8,128)(2,1)S(1)}, u32[]{:S(2)}, u32[]{:S(2)}) collective-permute-start(bf16[128,128]{1,0:T(8,128)(2,1)S(1)} %get-tuple-element.31.refs_7_), channel_id=1, source_target_pairs={{24,16},{25,17},{26,18},{27,19},{28,20},{29,21},{30,22},{31,23}} | collective-permute-start | bytes 98312 | tf_op jit(solution)/shard_map/ppermute | solution.py:789
  48.3 6.0 %collective-permute-start.3 = (bf16[208,256]{1,0:T(8,128)(2,1)S(1)}, bf16[208,256]{1,0:T(8,128)(2,1)S(1)}, u32[]{:S(2)}, u32[]{:S(2)}) collective-permute-start(bf16[208,256]{1,0:T(8,128)(2,1)S(1)} %get-tuple-element.28), channel_id=1, source_target_pairs={{0,1},{1,2},{2,3},{3,4},{4,5},{5,6},{6,7},{7,0},{8,9},{9,10},{10,1... | collective-permute-start | bytes 319496 | tf_op jit(solution)/shard_map/ppermute | solution.py:783
  48.4 8.8 %collective-permute-start.4 = (bf16[208,256]{1,0:T(8,128)(2,1)S(1)}, bf16[208,256]{1,0:T(8,128)(2,1)S(1)}, u32[]{:S(2)}, u32[]{:S(2)}) collective-permute-start(bf16[208,256]{1,0:T(8,128)(2,1)S(1)} %get-tuple-element.29), channel_id=1, source_target_pairs={{0,2},{1,3},{2,4},{3,5},{4,6},{5,7},{6,0},{7,1},{8,10},{9,11},{10,... | collective-permute-start | bytes 319496 | tf_op jit(solution)/shard_map/ppermute | solution.py:783
  49.7 9.6 %collective-permute-start.5 = (bf16[208,256]{1,0:T(8,128)(2,1)S(1)}, bf16[208,256]{1,0:T(8,128)(2,1)S(1)}, u32[]{:S(2)}, u32[]{:S(2)}) collective-permute-start(bf16[208,256]{1,0:T(8,128)(2,1)S(1)} %get-tuple-element.30), channel_id=1, source_target_pairs={{0,3},{1,4},{2,5},{3,6},{4,7},{5,0},{6,1},{7,2},{8,11},{9,12},{10,... | collective-permute-start | bytes 319496 | tf_op jit(solution)/shard_map/ppermute | solution.py:783
  64.9 4.6 %collective-permute-start.9 = (f32[3,128,128]{2,1,0:T(8,128)S(1)}, f32[3,128,128]{2,1,0:T(8,128)S(1)}, u32[]{:S(2)}, u32[]{:S(2)}) collective-permute-start(f32[3,128,128]{2,1,0:T(8,128)S(1)} %get-tuple-element.33.refs_3_.refs_0_), channel_id=1, source_target_pairs={{0,24},{1,25},{2,26},{3,27},{4,28},{5,29},{6,30},{7,31},{8,0},{9,1... | collective-permute-start | bytes 589832 | tf_op jit(solution)/shard_map/ppermute | solution.py:773
  66.1 5.6 %collective-permute-start.10 = (f32[3,128,128]{2,1,0:T(8,128)S(1)}, f32[3,128,128]{2,1,0:T(8,128)S(1)}, u32[]{:S(2)}, u32[]{:S(2)}) collective-permute-start(f32[3,128,128]{2,1,0:T(8,128)S(1)} %get-tuple-element.33.refs_3_.refs_0_), channel_id=1, source_target_pairs={{0,16},{1,17},{2,18},{3,19},{4,20},{5,21},{6,22},{7,23},{8,24},{9,... | collective-permute-start | bytes 589832 | tf_op jit(solution)/shard_map/ppermute | solution.py:773
  66.6 7.8 %collective-permute-start.11 = (f32[3,128,128]{2,1,0:T(8,128)S(1)}, f32[3,128,128]{2,1,0:T(8,128)S(1)}, u32[]{:S(2)}, u32[]{:S(2)}) collective-permute-start(f32[3,128,128]{2,1,0:T(8,128)S(1)} %get-tuple-element.33.refs_3_.refs_0_), channel_id=1, source_target_pairs={{0,8},{1,9},{2,10},{3,11},{4,12},{5,13},{6,14},{7,15},{8,16},{9,17... | collective-permute-start | bytes 589832 | tf_op jit(solution)/shard_map/ppermute | solution.py:773
  74.6 11.9 %collective-permute-start.12 = (f32[64,128]{1,0:T(8,128)S(1)}, f32[64,128]{1,0:T(8,128)S(1)}, u32[]{:S(2)}, u32[]{:S(2)}) collective-permute-start(f32[64,128]{1,0:T(8,128)S(1)} %get-tuple-element.37), channel_id=1, source_target_pairs={{0,7},{1,0},{2,1},{3,2},{4,3},{5,4},{6,5},{7,6},{8,15},{9,8},{10,9... | collective-permute-start | bytes 98312 | tf_op jit(solution)/shard_map/ppermute | solution.py:783
  79.7 6.8 %collective-permute-start.13 = (f32[64,128]{1,0:T(8,128)S(1)}, f32[64,128]{1,0:T(8,128)S(1)}, u32[]{:S(2)}, u32[]{:S(2)}) collective-permute-start(f32[64,128]{1,0:T(8,128)S(1)} %get-tuple-element.38), channel_id=1, source_target_pairs={{0,6},{1,7},{2,0},{3,1},{4,2},{5,3},{6,4},{7,5},{8,14},{9,15},{10,... | collective-permute-start | bytes 98312 | tf_op jit(solution)/shard_map/ppermute | solution.py:783
  83.5 6.1 %collective-permute-start.14 = (f32[64,128]{1,0:T(8,128)S(1)}, f32[64,128]{1,0:T(8,128)S(1)}, u32[]{:S(2)}, u32[]{:S(2)}) collective-permute-start(f32[64,128]{1,0:T(8,128)S(1)} %get-tuple-element.39), channel_id=1, source_target_pairs={{0,5},{1,6},{2,7},{3,0},{4,1},{5,2},{6,3},{7,4},{8,13},{9,14},{10,... | collective-permute-start | bytes 98312 | tf_op jit(solution)/shard_map/ppermute | solution.py:783

commit v7 on v6

--- a/solution.py
+++ b/solution.py
@@ -13,7 +13,7 @@
 F32 = jnp.float32
 BF16 = jnp.bfloat16
 EDGE = 8
-STRIP = 16
+AHEAD = 4
 CHUNK = 8
 AXES = ("comp", "lat", "lon")
 
@@ -134,7 +134,7 @@
         fetch(q).start()
         return 0
 
-    lax.fori_loop(0, chunks, begin, 0)
+    lax.fori_loop(0, AHEAD, begin, 0)
     ocean = flags[0] == 1
     mix = jnp.where(ocean, mix_ocn[...], mix_atm[...])
     mix_high, mix_low = split_two(mix)
@@ -157,12 +157,19 @@
         values[r, EDGE - 1 : EDGE, :] = left_cols[1, i : i + 1, :]
         values[r, EDGE + cols : EDGE + cols + 1, :] = right_cols[0, i : i + 1, :]
 
-    def side_cells(r, _):
-        values[r + 2, EDGE - 1 : EDGE, :] = left_cols[1, pl.ds(r + EDGE, 1), :]
-        values[r + 2, EDGE + cols : EDGE + cols + 1, :] = right_cols[0, pl.ds(r + EDGE, 1), :]
-        return 0
-
-    lax.fori_loop(0, rows, side_cells, 0, unroll=8)
+    def side_cells(start, count):
+        for row in range(count):
+            values[start + row + 2, EDGE - 1 : EDGE, :] = left_cols[1, pl.ds(start + row + EDGE, 1), :]
+            values[start + row + 2, EDGE + cols : EDGE + cols + 1, :] = right_cols[
+                0, pl.ds(start + row + EDGE, 1), :
+            ]
+
+    def moved_sides(start, count):
+        for row in range(count):
+            moved[start + row + 1, EDGE - 1 : EDGE, :] = halo_moved[0, pl.ds(start + row, 1), :]
+            moved[start + row + 1, EDGE + cols : EDGE + cols + 1, :] = halo_moved[
+                1, pl.ds(start + row, 1), :
+            ]
 
     def stage(refs, row, total):
         line = SMOOTHING * total
@@ -170,17 +177,13 @@
         refs[1][row * cols : (row + 1) * cols, :] = side_by_side(line)
 
     def stage_rows(refs, ref, start, count):
-        for col in range(0, cols, STRIP):
-            left = EDGE + col
-            block = ref[pl.ds(start - 1, count + 2), left : left + STRIP, :]
-            near = ref[pl.ds(start, count), left - 1 : left - 1 + STRIP, :]
-            far = ref[pl.ds(start, count), left + 1 : left + 1 + STRIP, :]
-            for row in range(count):
-                total = (block[row + 1] + (block[row] + block[row + 2])) + (near[row] + far[row])
-                line = SMOOTHING * total
-                refs[0][row, col : col + STRIP, :] = line
-                spot = row * cols + col
-                refs[1][spot : spot + STRIP, :] = side_by_side(line)
+        for row in range(count):
+            i = start + row
+            here = ref[i, EDGE : EDGE + cols, :] + (
+                ref[i - 1, EDGE : EDGE + cols, :] + ref[i + 1, EDGE : EDGE + cols, :]
+            )
+            near = ref[i, EDGE - 1 : EDGE - 1 + cols, :] + ref[i, EDGE + 1 : EDGE + 1 + cols, :]
+            stage(refs, row, here + near)
 
     def note_top(q, lines):
         lanes = lax.broadcasted_iota(jnp.int32, (cols, levels), 1)
@@ -213,12 +216,7 @@
         for s in range(2):
             halo_moved[s] = finish(first, s)
 
-        def moved_sides(r, _):
-            moved[r + 1, EDGE - 1 : EDGE, :] = halo_moved[0, pl.ds(r, 1), :]
-            moved[r + 1, EDGE + cols : EDGE + cols + 1, :] = halo_moved[1, pl.ds(r, 1), :]
-            return 0
-
-        lax.fori_loop(0, rows, moved_sides, 0, unroll=8)
+        side_cells(0, 1)
         fetch(0).wait()
         fetch(1).wait()
         stage_rows(second, values, 1, 2)
@@ -231,6 +229,7 @@
             moved[0, EDGE : EDGE + cols, :] = jnp.zeros((cols, levels), F32)
 
         def begin_first(q):
+            side_cells(jnp.minimum(q * CHUNK + 1, rows - CHUNK), CHUNK)
             stage_rows(first, values, q * CHUNK + 3, CHUNK)
             mix_rows(first, CHUNK)
 
@@ -239,6 +238,7 @@
                 moved[q * CHUNK + row + 2, EDGE : EDGE + cols, :] = finish(first, row)
 
         def begin_second(q):
+            moved_sides(q * CHUNK, CHUNK)
             stage_rows(second, moved, q * CHUNK + 1, CHUNK)
 
         def end_second(q, slot):
@@ -258,6 +258,7 @@
                 block = jnp.where(sea > 0.5, block, 0.0)
                 fluxes[pl.ds(pl.multiple_of(r * flux_count, flux_count), flux_count), :] = block
 
+        fetch(AHEAD).start()
         begin_first(0)
         end_first(0)
 
@@ -265,6 +266,10 @@
             @pl.when(q + 1 < chunks)
             def _():
                 fetch(q + 1).wait()
+
+            @pl.when(q + AHEAD < chunks)
+            def _():
+                fetch(q + AHEAD).start()
 
             slot = (q - 1) % 2
 
@@ -290,8 +295,6 @@
         begin_second(last)
         mix_rows(second, CHUNK)
         end_second(last, last % 2)
-        put(last - 1, (last - 1) % 2).wait()
-        put(last, last % 2).wait()
         spots = lax.broadcasted_iota(jnp.int32, (source_column.shape[0], rows), 1)
         placing = jnp.where(source_column[...] == spots, 1.0, 0.0).astype(BF16)
         share = flux_count // comp_count
@@ -302,6 +305,8 @@
                     placing, field
                 ).astype(BF16)
             packed[c, placing.shape[0] :, :] = labels[...]
+        put(last - 1, (last - 1) % 2).wait()
+        put(last, last % 2).wait()
         surface[...] = top[...].T
 
     @pl.when(ocean)
@@ -318,6 +323,11 @@
             def _():
                 fetch(q + 1).wait()
 
+            @pl.when(q + AHEAD < chunks)
+            def _():
+                fetch(q + AHEAD).start()
+
+            side_cells(base, CHUNK)
             stage_rows(first, values, base + 2, CHUNK)
             mix_rows(first, CHUNK)
             slot = q % 2
@@ -427,10 +437,10 @@
 def regrid_body(count, comp_count, flags, ocean_first, *refs):
     blocks = refs[:count]
     seas = refs[count : count + comp_count]
-    weights, surface, mask, shared, hits, entries, chosen, binned = refs[count + comp_count :]
+    weights, surface, mask, forcing, shared, hits, entries, chosen, binned = refs[count + comp_count :]
     sources = comp_count - 1
     rows, cols = mask.shape
-    share = shared.shape[0] - 1
+    share = forcing.shape[0]
     weight_count = weights.shape[0]
     capacity = (blocks[0].shape[0] - LABEL_ROWS) // sources
     size = count * capacity
@@ -464,23 +474,35 @@
             chosen[i * rows : (i + 1) * rows, :] = by_target * by_weight[w : w + 1, :]
         binned[...] = dot_nn(chosen[...], entries[...])
         wide = weights[g * BATCH : (g + 1) * BATCH].reshape(BATCH * cols, cols)
-        for f in range(share):
-            halves = [
+        halves = [
+            [
                 split_two(binned[i * rows : (i + 1) * rows, f * cols : (f + 1) * cols])
                 for i in range(BATCH)
             ]
-            part = dot_nn(jnp.concatenate([h for h, _ in halves], axis=1), wide) + dot_nn(
-                jnp.concatenate([l for _, l in halves], axis=1), wide
-            )
-            shared[f] = part if g == 0 else shared[f] + part
-    change = ocean_first[flags[3] * share] * shared[0]
+            for f in range(share)
+        ]
+        stacked = jnp.concatenate(
+            [
+                jnp.concatenate([half[k] for half in halves[f]], axis=1)
+                for k in range(2)
+                for f in range(share)
+            ],
+            axis=0,
+        )
+        product = dot_nn(stacked, wide)
+        for f in range(share):
+            part = product[f * rows : (f + 1) * rows] + product[
+                (share + f) * rows : (share + f + 1) * rows
+            ]
+            forcing[f] = part if g == 0 else forcing[f] + part
+    change = ocean_first[flags[3] * share] * forcing[0]
     for f in range(1, share):
-        change = change + ocean_first[flags[3] * share + f] * shared[f]
+        change = change + ocean_first[flags[3] * share + f] * forcing[f]
     sea = jnp.where(flags[0] == 1, seas[sources][...].astype(F32), 0.0)
     for c in range(sources):
         sea = sea + jnp.where(flags[3] == c, seas[c][...].astype(F32), 0.0)
     base = jnp.where(flags[0] == 1, surface[...], 0.0)
-    shared[share] = base + jnp.where(sea > 0.5, change, 0.0)
+    shared[...] = base + jnp.where(sea > 0.5, change, 0.0)
 
 
 def regrid(flags, ocean_first, blocks, seas, weights, surface, mask):
@@ -498,11 +520,12 @@
     return pl.pallas_call(
         functools.partial(regrid_body, count, comp_count),
         out_shape=(
-            jax.ShapeDtypeStruct((share + 1, rows, cols), F32),
+            jax.ShapeDtypeStruct((share, rows, cols), F32),
+            jax.ShapeDtypeStruct((rows, cols), F32),
             jax.ShapeDtypeStruct((size, rows), BF16),
         ),
         in_specs=[smem, smem] + [vmem] * (count + comp_count + 3),
-        out_specs=(vmem, vmem),
+        out_specs=(vmem, vmem, vmem),
         scratch_shapes=[
             pltpu.VMEM((total, width), BF16),
             pltpu.VMEM((BATCH * rows, total), BF16),
@@ -522,10 +545,9 @@
     parts = refs[:count]
     hits, surface = refs[count : count + 2]
     picked = refs[count + 2 :]
-    share = parts[0].shape[0] - 1
-    now = parts[0][share]
+    now = parts[0][...]
     for part in parts[1:]:
-        now = now + part[share]
+        now = now + part[...]
     surface[...] = now
     pair = jnp.concatenate(split_two(now), axis=0)
     size = picked[0].shape[0]
@@ -535,7 +557,7 @@
 
 
 def pick(parts, hits, neighbours):
-    _, rows, cols = parts[0].shape
+    rows, cols = parts[0].shape
     size = hits.shape[0] // neighbours
     vmem = pl.BlockSpec(memory_space=pltpu.VMEM)
     return pl.pallas_call(
@@ -556,7 +578,7 @@
     parts = refs[:groups]
     mask, ocean_map, out, token, held, table, wide, in_sems, out_sems = refs[groups:]
     rows, cols, levels = state.shape
-    share = parts[0].shape[0] - 1
+    share = parts[0].shape[0]
     flux_count = groups * share
     chunks = rows // LINES
     depth = LINES * flux_count
@@ -788,6 +810,12 @@
         ]
         return lax.ppermute(value, AXES, pairs)
 
+    def to_ocean(value, comp):
+        pairs = [
+            (comp * tile_count + t, ocean_comp * tile_count + t) for t in range(tile_count)
+        ]
+        return lax.ppermute(value, AXES, pairs)
+
     label_lines = jnp.stack([packed_labels // rows, packed_labels % rows]).astype(BF16)
     label_lines = jnp.pad(label_lines, ((0, LABEL_ROWS - 2), (0, 0)))
 
@@ -801,14 +829,15 @@
     seas = [from_ocean(sea_copy, c) for c in range(ocean_comp)] + [sea_copy]
     blocks = regroup(slabs, neighbours)
     blocks = [over_tiles(blocks[n], offsets[n], comp_count) for n in range(neighbours)]
-    shared, hits = regrid(
+    forcing, shared, hits = regrid(
         flags, ocean_map[:, 0], blocks, seas, regrid_weights, surface, mask
     )
     parts = [shared] + [shifted_comp(shared, s) for s in range(1, comp_count)]
+    parts[1], forcing = lax.optimization_barrier((parts[1], forcing))
     picks = pick(parts, hits, neighbours)
     new_surface, picked = picks[0], picks[1:]
     arrived = [over_tiles(picked[n], -offsets[n], ocean_comp) for n in range(neighbours)]
-    fields = parts[:0:-1] + parts[:1]
+    fields = [to_ocean(forcing, c) for c in range(ocean_comp)] + [forcing]
     final_state, token = update(flags, moved, fields, mask, ocean_map)
     weight_column = (packed_labels // rows)[:, None]
     surface_out = returned(

time: 92.4 us -> 88.4 us (0.957)
  waiting for transfers between devices: 27.9 us -> 21.8 us
  starting transfers between devices: 31.7 us -> 35.1 us
  Pallas kernels: 30.1 us -> 28.6 us
    ppermute x3, waiting for transfers between devices: 7.53 us -> 1.11 us  [shifted_comp(): return lax.ppermute(value, AXES, pairs)]
    ppermute x0 -> x3, starting transfers between devices: none -> 3.38 us  [to_ocean(): return lax.ppermute(value, AXES, pairs)]
    pallas_call x1, Pallas kernels: 5.6 us -> 4.1 us  [regrid(): pl.pallas_call(functools.partial(regrid_body, count, comp_count), out_sha...]
    ppermute x3, starting transfers between devices: 1.96 us -> 2.93 us  [shifted_comp(): return lax.ppermute(value, AXES, pairs)]
    ppermute x6, starting transfers between devices: 16.7 us -> 15.7 us  [over_tiles(): return lax.ppermute(value, AXES, pairs)]
  transfers between devices with their start and end apart: 16 -> 19, of which waited for: 9 -> 7; matrix products, arithmetic and copies ran while one was open for 1% -> 2% of each run, Pallas kernels for 1% -> 1%
where the time goes in v7:
time: 88.4 us; the launch traced here: 88 us
  starting transfers between devices  35.1 us (40%)
  Pallas kernels  28.6 us (32%)
  waiting for transfers between devices  21.8 us (25%)
  between operations  1.02 us (1%)
    pallas_call x1, Pallas kernels, advance(): pl.pallas_call(functools.partial(advance_kernel, comp_count, left_at, rig...  19.4 us
    ppermute x6, starting transfers between devices, over_tiles(): return lax.ppermute(value, AXES, pairs)  15.7 us
    ppermute x6, waiting for transfers between devices, over_tiles(): return lax.ppermute(value, AXES, pairs)  8.51 us
    all_to_all x1, waiting for transfers between devices, over_comp(): lax.all_to_all(value, 'comp', split_axis=0, concat_axis=0, tiled=True)  7.07 us
    ppermute x3, starting transfers between devices, band_shift(): return lax.ppermute(value, AXES, pairs)  6.48 us
    ppermute x3, waiting for transfers between devices, band_shift(): return lax.ppermute(value, AXES, pairs)  5.13 us
    pallas_call x1, Pallas kernels, regrid(): pl.pallas_call(functools.partial(regrid_body, count, comp_count), out_sha...  4.1 us
    all_to_all x1, starting transfers between devices, over_comp(): lax.all_to_all(value, 'comp', split_axis=0, concat_axis=0, tiled=True)  4.01 us
  transfers between devices with their start and end apart: 19, of which 7 were waited for; matrix products, arithmetic and copies ran while one was open for 2% of the time, Pallas kernels for 1%

profile of v7, /device:TPU:1, one launch (start us, length us, event | category | flops | bytes accessed | tf_op | source)
XLA Modules:
  0.0 88.0 jit_solution(10955672614964356156)
XLA Ops:
  0.7 1.6 %edges.1 = (bf16[2,128,128]{2,1,0:T(8,128)(2,1)S(1)}, bf16[2,128,128]{2,1,0:T(8,128)(2,1)S(1)}, f32[4,128,128]{2,1,0:T(8,128)S(1)}) custom-call(f32[128,128,128]{2,1,0:T(8,128)} %refs_3_.1), custom_call_target="tpu_custom_call" | custom-call | tf_op jit(solution)/shard_map/edges/pallas_call | solution.py:63
  2.3 0.0 copy-start.3
  2.3 0.0 copy-start
  2.3 4.2 %collective-permute-start = (bf16[2,128,128]{2,1,0:T(8,128)(2,1)S(1)}, bf16[2,128,128]{2,1,0:T(8,128)(2,1)S(1)}, u32[]{:S(2)}, u32[]{:S(2)}) collective-permute-start(bf16[2,128,128]{2,1,0:T(8,128)(2,1)S(1)} %get-tuple-element.25), channel_id=1, source_target_pairs={{0,2},{1,3},{2,4},{3,5},{4,6},{5,7},{6,8},{7,9},{8,10},{9,11},{10,... | collective-permute-start | bytes 196616 | tf_op jit(solution)/shard_map/ppermute | solution.py:751
  6.5 1.3 %collective-permute-start.1 = (bf16[2,128,128]{2,1,0:T(8,128)(2,1)S(1)}, bf16[2,128,128]{2,1,0:T(8,128)(2,1)S(1)}, u32[]{:S(2)}, u32[]{:S(2)}) collective-permute-start(bf16[2,128,128]{2,1,0:T(8,128)(2,1)S(1)} %get-tuple-element.26), channel_id=1, source_target_pairs={{2,0},{3,1},{4,2},{5,3},{6,4},{7,5},{8,6},{9,7},{10,8},{11,9},{12,... | collective-permute-start | bytes 196616 | tf_op jit(solution)/shard_map/ppermute | solution.py:751
  7.8 0.2 copy.19
  8.0 0.3 fusion.4
  8.2 0.2 convert_reduce_fusion
  8.4 0.2 select_reduce_fusion
  8.7 0.1 copy.20.refs_1_
  8.8 0.0 collective-permute-done.up_rows.refs_4_
  8.8 4.0 %collective-permute-done.1.low_rows.refs_5_ = bf16[2,128,128]{2,1,0:T(8,128)(2,1)S(1)} collective-permute-done((bf16[2,128,128]{2,1,0:T(8,128)(2,1)S(1)}, bf16[2,128,128]{2,1,0:T(8,128)(2,1)S(1)}, u32[]{:S(2)}, u32[]{:S(2)}) %collective-permute-start.1) | collective-permute-done | bytes 65568 | tf_op jit(solution)/shard_map/ppermute | solution.py:751
  12.9 1.0 %collective-permute-start.2 = (f32[4,144,128]{2,1,0:T(8,128)S(1)}, f32[4,144,128]{2,1,0:T(8,128)S(1)}, u32[]{:S(2)}, u32[]{:S(2)}) collective-permute-start(f32[4,144,128]{2,1,0:T(8,128)S(1)} %frame.1), channel_id=1, source_target_pairs={{0,1},{1,0},{2,3},{3,2},{4,5},{5,4},{6,7},{7,6},{8,9},{9,8},{10,11... | collective-permute-start | bytes 884744 | tf_op jit(solution)/shard_map/ppermute | solution.py:751
  13.9 0.1 pad_add_fusion.refs_0_.flags
  14.0 1.1 %collective-permute-done.2.refs_6_.refs_7_ = f32[4,144,128]{2,1,0:T(8,128)S(1)} collective-permute-done((f32[4,144,128]{2,1,0:T(8,128)S(1)}, f32[4,144,128]{2,1,0:T(8,128)S(1)}, u32[]{:S(2)}, u32[]{:S(2)}) %collective-permute-start.2) | collective-permute-done | bytes 294944 | tf_op jit(solution)/shard_map/ppermute | solution.py:751
  15.1 19.4 %advance.1 = (f32[128,128,128]{2,1,0:T(8,128)}, f32[128,128]{1,0:T(8,128)S(1)}, bf16[128,128]{1,0:T(8,128)(2,1)S(1)}, bf16[4,272,256]{2,1,0:T(8,128)(2,1)}) custom-call(s32[4]{0:T(128)S(1)} %pad_add_fusion.refs_0_.flags, s32[256,1]{1,0:T(8,128)S(1)} %copy.20.refs_1_, bf16[16,256]{1,0:T(8,128)(2,1)S(1)} %fusion.9.refs_2_, f32[128,128,128]{2,1,0:T(8,128)} %refs_3_.1, ...), custom_call_target="tpu_custom_call" | custom-call | flops 2147483648 | bytes 16777216 | tf_op jit(solution)/shard_map/advance/pallas_call | solution.py:367
  34.5 4.0 %all-to-all-start = ((bf16[4,272,256]{2,1,0:T(8,128)(2,1)}), bf16[4,272,256]{2,1,0:T(8,128)(2,1)S(1)}, u32[]{:S(2)}, u32[]{:S(2)}) async-start(bf16[4,272,256]{2,1,0:T(8,128)(2,1)} %get-tuple-element.29), calls=%async_computation | async-start | bytes 1114112 | tf_op jit(solution)/shard_map/all_to_all | solution.py:787
  38.5 1.3 %collective-permute-start.6 = (bf16[128,128]{1,0:T(8,128)(2,1)S(1)}, bf16[128,128]{1,0:T(8,128)(2,1)S(1)}, u32[]{:S(2)}, u32[]{:S(2)}) collective-permute-start(bf16[128,128]{1,0:T(8,128)(2,1)S(1)} %get-tuple-element.34.refs_7_), channel_id=1, source_target_pairs={{24,0},{25,1},{26,2},{27,3},{28,4},{29,5},{30,6},{31,7}} | collective-permute-start | bytes 98312 | tf_op jit(solution)/shard_map/ppermute | solution.py:811
  39.8 0.7 collective-permute-start.7
  40.5 0.7 collective-permute-start.8
  41.2 7.1 %all-to-all-done.slabs = bf16[4,272,256]{2,1,0:T(8,128)(2,1)S(1)} async-done(((bf16[4,272,256]{2,1,0:T(8,128)(2,1)}), bf16[4,272,256]{2,1,0:T(8,128)(2,1)S(1)}, u32[]{:S(2)}, u32[]{:S(2)}) %all-to-all-start) | async-done | bytes 557088 | tf_op jit(solution)/shard_map/all_to_all | solution.py:787
  48.3 0.1 collective-permute-start.3
  48.4 1.3 %collective-permute-start.4 = (bf16[208,256]{1,0:T(8,128)(2,1)S(1)}, bf16[208,256]{1,0:T(8,128)(2,1)S(1)}, u32[]{:S(2)}, u32[]{:S(2)}) collective-permute-start(bf16[208,256]{1,0:T(8,128)(2,1)S(1)} %get-tuple-element.32), channel_id=1, source_target_pairs={{0,2},{1,3},{2,4},{3,5},{4,6},{5,7},{6,0},{7,1},{8,10},{9,11},{10,... | collective-permute-start | bytes 319496 | tf_op jit(solution)/shard_map/ppermute | solution.py:805
  49.7 0.0 collective-permute-done.6.refs_4_
  49.7 4.3 %collective-permute-start.5 = (bf16[208,256]{1,0:T(8,128)(2,1)S(1)}, bf16[208,256]{1,0:T(8,128)(2,1)S(1)}, u32[]{:S(2)}, u32[]{:S(2)}) collective-permute-start(bf16[208,256]{1,0:T(8,128)(2,1)S(1)} %get-tuple-element.33), channel_id=1, source_target_pairs={{0,3},{1,4},{2,5},{3,6},{4,7},{5,0},{6,1},{7,2},{8,11},{9,12},{10,... | collective-permute-start | bytes 319496 | tf_op jit(solution)/shard_map/ppermute | solution.py:805
  54.0 0.1 slice_reduce_fusion.ocean_first
  54.1 3.1 %collective-permute-done.4.refs_2_ = bf16[208,256]{1,0:T(8,128)(2,1)S(1)} collective-permute-done((bf16[208,256]{1,0:T(8,128)(2,1)S(1)}, bf16[208,256]{1,0:T(8,128)(2,1)S(1)}, u32[]{:S(2)}, u32[]{:S(2)}) %collective-permute-start.4) | collective-permute-done | bytes 106528 | tf_op jit(solution)/shard_map/ppermute | solution.py:805
  57.2 2.1 %collective-permute-done.5.refs_3_ = bf16[208,256]{1,0:T(8,128)(2,1)S(1)} collective-permute-done((bf16[208,256]{1,0:T(8,128)(2,1)S(1)}, bf16[208,256]{1,0:T(8,128)(2,1)S(1)}, u32[]{:S(2)}, u32[]{:S(2)}) %collective-permute-start.5) | collective-permute-done | bytes 106528 | tf_op jit(solution)/shard_map/ppermute | solution.py:805
  59.3 4.1 %regrid.1 = (f32[2,128,128]{2,1,0:T(8,128)S(1)}, f32[128,128]{1,0:T(8,128)S(1)}, bf16[256,128]{1,0:T(8,128)(2,1)S(1)}) custom-call(s32[4]{0:T(128)S(1)} %pad_add_fusion.refs_0_.flags, f32[8]{0:T(128)S(1)} %slice_reduce_fusion.ocean_first, bf16[208,256]{1,0:T(8,128)(2,1)S(1)} %get-tuple-element.30.refs_0_, ...), custom_call_target="tpu_custom_call" | custom-call | flops 2147483648 | bytes 2097152 | tf_op jit(solution)/shard_map/regrid/pallas_call | solution.py:520
  63.4 0.6 collective-permute-start.9
  64.0 0.1 copy.21
  64.1 1.0 %collective-permute-start.13 = (f32[128,128]{1,0:T(8,128)S(1)}, f32[128,128]{1,0:T(8,128)S(1)}, u32[]{:S(2)}, u32[]{:S(2)}) collective-permute-start(f32[128,128]{1,0:T(8,128)S(1)} %get-tuple-element.36.refs_0_), channel_id=1, source_target_pairs={{0,16},{1,17},{2,18},{3,19},{4,20},{5,21},{6,22},{7,23},{8,24},{9,... | collective-permute-start | bytes 196616 | tf_op jit(solution)/shard_map/ppermute | solution.py:795
  65.1 1.4 %collective-permute-start.14 = (f32[128,128]{1,0:T(8,128)S(1)}, f32[128,128]{1,0:T(8,128)S(1)}, u32[]{:S(2)}, u32[]{:S(2)}) collective-permute-start(f32[128,128]{1,0:T(8,128)S(1)} %get-tuple-element.36.refs_0_), channel_id=1, source_target_pairs={{0,24},{1,25},{2,26},{3,27},{4,28},{5,29},{6,30},{7,31},{8,0},{9,1... | collective-permute-start | bytes 196616 | tf_op jit(solution)/shard_map/ppermute | solution.py:795
  66.5 1.1 %collective-permute-done.9.refs_1_ = f32[128,128]{1,0:T(8,128)S(1)} collective-permute-done((f32[128,128]{1,0:T(8,128)S(1)}, f32[128,128]{1,0:T(8,128)S(1)}, u32[]{:S(2)}, u32[]{:S(2)}) %collective-permute-start.9) | collective-permute-done | bytes 65568 | tf_op jit(solution)/shard_map/ppermute | solution.py:795
  67.6 2.0 %collective-permute-start.10 = (f32[2,128,128]{2,1,0:T(8,128)S(1)}, f32[2,128,128]{2,1,0:T(8,128)S(1)}, u32[]{:S(2)}, u32[]{:S(2)}) collective-permute-start(f32[2,128,128]{2,1,0:T(8,128)S(1)} %get-tuple-element.38.refs_3_), channel_id=1, source_target_pairs={{0,24},{1,25},{2,26},{3,27},{4,28},{5,29},{6,30},{7,31}} | collective-permute-start | bytes 393224 | tf_op jit(solution)/shard_map/ppermute | solution.py:817
  69.6 0.7 collective-permute-start.11
  70.3 0.7 collective-permute-start.12
  71.0 0.1 add_select_fusion.refs_4_
  71.1 0.0 collective-permute-done.13.refs_2_
  71.1 0.2 pick.1
  71.3 5.4 %collective-permute-start.15 = (f32[64,128]{1,0:T(8,128)S(1)}, f32[64,128]{1,0:T(8,128)S(1)}, u32[]{:S(2)}, u32[]{:S(2)}) collective-permute-start(f32[64,128]{1,0:T(8,128)S(1)} %get-tuple-element.43), channel_id=1, source_target_pairs={{0,7},{1,0},{2,1},{3,2},{4,3},{5,4},{6,5},{7,6},{8,15},{9,8},{10,9... | collective-permute-start | bytes 98312 | tf_op jit(solution)/shard_map/ppermute | solution.py:805
  76.7 2.7 %collective-permute-start.16 = (f32[64,128]{1,0:T(8,128)S(1)}, f32[64,128]{1,0:T(8,128)S(1)}, u32[]{:S(2)}, u32[]{:S(2)}) collective-permute-start(f32[64,128]{1,0:T(8,128)S(1)} %get-tuple-element.44), channel_id=1, source_target_pairs={{0,6},{1,7},{2,0},{3,1},{4,2},{5,3},{6,4},{7,5},{8,14},{9,15},{10,... | collective-permute-start | bytes 98312 | tf_op jit(solution)/shard_map/ppermute | solution.py:805
  79.4 0.0 collective-permute-done.10.refs_0_
  79.4 1.9 %collective-permute-start.17 = (f32[64,128]{1,0:T(8,128)S(1)}, f32[64,128]{1,0:T(8,128)S(1)}, u32[]{:S(2)}, u32[]{:S(2)}) collective-permute-start(f32[64,128]{1,0:T(8,128)S(1)} %get-tuple-element.45), channel_id=1, source_target_pairs={{0,5},{1,6},{2,7},{3,0},{4,1},{5,2},{6,3},{7,4},{8,13},{9,14},{10,... | collective-permute-start | bytes 98312 | tf_op jit(solution)/shard_map/ppermute | solution.py:805
  81.4 0.0 collective-permute-done.12.refs_2_
  81.4 0.8 update.1
  82.3 3.3 %collective-permute-done.17.refs_3_ = f32[64,128]{1,0:T(8,128)S(1)} collective-permute-done((f32[64,128]{1,0:T(8,128)S(1)}, f32[64,128]{1,0:T(8,128)S(1)}, u32[]{:S(2)}, u32[]{:S(2)}) %collective-permute-start.17) | collective-permute-done | bytes 32800 | tf_op jit(solution)/shard_map/ppermute | solution.py:805
  85.6 2.4 %returned.1 = f32[128,128]{1,0:T(8,128)} custom-call(s32[4]{0:T(128)S(1)} %pad_add_fusion.refs_0_.flags, f32[64,128]{1,0:T(8,128)S(1)} %get-tuple-element.42.refs_0_, f32[64,128]{1,0:T(8,128)S(1)} %collective-permute-done.15.refs_1_, f32[64,128]{1,0:T(8,128)S(1)} %collective-permute-done.16.refs_2_, f32[64,128]{1,0:T(8,128)S(1)} %collective-permute-done.17.refs_3_, ...), custom_call_target="tpu_custom_call" | custom-call | tf_op jit(solution)/shard_map/returned/pallas_call | solution.py:705
  (27 shorter events, 0.2 us)
Async XLA Ops:
  0.6 7.2 %copy-start.6 = (s32[128,1,2,3]{0,2,3,1:T(2,128)S(1)}, s32[128,1,2,3]{0,2,3,1:T(2,128)}, u32[]{:S(2)}) copy-start(s32[128,1,2,3]{0,2,3,1:T(2,128)} %param.11) | copy-start | bytes 9220
  0.6 13.3 %copy-start.5 = (s32[128,128]{1,0:T(8,128)S(1)}, s32[128,128]{1,0:T(8,128)}, u32[]{:S(2)}) copy-start(s32[128,128]{1,0:T(8,128)} %param.10) | copy-start | bytes 196612
  0.7 14.4 %copy-start.4 = (f32[128,8]{0,1:T(8,128)S(1)}, f32[128,8]{0,1:T(8,128)}, u32[]{:S(2)}) copy-start(f32[128,8]{0,1:T(8,128)} %param.14) | copy-start | bytes 12292
  0.7 14.4 %copy-start.1 = (f32[128,128]{1,0:T(8,128)S(1)}, f32[128,128]{1,0:T(8,128)}, u32[]{:S(2)}) copy-start(f32[128,128]{1,0:T(8,128)} %refs_10_.1) | copy-start | bytes 196612
  0.7 14.4 %copy-start.2 = (f32[128,128]{1,0:T(8,128)S(1)}, f32[128,128]{1,0:T(8,128)}, u32[]{:S(2)}) copy-start(f32[128,128]{1,0:T(8,128)} %refs_11_.1) | copy-start | bytes 196612
  2.3 51.7 %copy-start.3 = (f32[8,128]{1,0:T(8,128)S(1)}, f32[8,128]{1,0:T(8,128)}, u32[]{:S(2)}) copy-start(f32[8,128]{1,0:T(8,128)} %refs_5_.1) | copy-start | bytes 12292
  2.3 57.0 %copy-start = (bf16[32,128,128]{2,1,0:T(8,128)(2,1)S(1)}, bf16[32,128,128]{2,1,0:T(8,128)(2,1)}, u32[]{:S(2)}) copy-start(bf16[32,128,128]{2,1,0:T(8,128)(2,1)} %refs_6_.1) | copy-start | bytes 3145732
  2.3 6.5 %collective-permute-start = (bf16[2,128,128]{2,1,0:T(8,128)(2,1)S(1)}, bf16[2,128,128]{2,1,0:T(8,128)(2,1)S(1)}, u32[]{:S(2)}, u32[]{:S(2)}) collective-permute-start(bf16[2,128,128]{2,1,0:T(8,128)(2,1)S(1)} %get-tuple-element.25), channel_id=1, source_target_pairs={{0,2},{1,3},{2,4},{3,5},{4,6},{5,7},{6,8},{7,9},{8,10},{9,11},{10,... | collective-permute-start | bytes 196616 | tf_op jit(solution)/shard_map/ppermute | solution.py:751
  6.5 6.4 %collective-permute-start.1 = (bf16[2,128,128]{2,1,0:T(8,128)(2,1)S(1)}, bf16[2,128,128]{2,1,0:T(8,128)(2,1)S(1)}, u32[]{:S(2)}, u32[]{:S(2)}) collective-permute-start(bf16[2,128,128]{2,1,0:T(8,128)(2,1)S(1)} %get-tuple-element.26), channel_id=1, source_target_pairs={{2,0},{3,1},{4,2},{5,3},{6,4},{7,5},{8,6},{9,7},{10,8},{11,9},{12,... | collective-permute-start | bytes 196616 | tf_op jit(solution)/shard_map/ppermute | solution.py:751
  12.9 2.2 %collective-permute-start.2 = (f32[4,144,128]{2,1,0:T(8,128)S(1)}, f32[4,144,128]{2,1,0:T(8,128)S(1)}, u32[]{:S(2)}, u32[]{:S(2)}) collective-permute-start(f32[4,144,128]{2,1,0:T(8,128)S(1)} %frame.1), channel_id=1, source_target_pairs={{0,1},{1,0},{2,3},{3,2},{4,5},{5,4},{6,7},{7,6},{8,9},{9,8},{10,11... | collective-permute-start | bytes 884744 | tf_op jit(solution)/shard_map/ppermute | solution.py:751
  34.5 13.7 %all-to-all-start = ((bf16[4,272,256]{2,1,0:T(8,128)(2,1)}), bf16[4,272,256]{2,1,0:T(8,128)(2,1)S(1)}, u32[]{:S(2)}, u32[]{:S(2)}) async-start(bf16[4,272,256]{2,1,0:T(8,128)(2,1)} %get-tuple-element.29), calls=%async_computation | async-start | bytes 1114112 | tf_op jit(solution)/shard_map/all_to_all | solution.py:787
  38.5 11.1 %collective-permute-start.6 = (bf16[128,128]{1,0:T(8,128)(2,1)S(1)}, bf16[128,128]{1,0:T(8,128)(2,1)S(1)}, u32[]{:S(2)}, u32[]{:S(2)}) collective-permute-start(bf16[128,128]{1,0:T(8,128)(2,1)S(1)} %get-tuple-element.34.refs_7_), channel_id=1, source_target_pairs={{24,0},{25,1},{26,2},{27,3},{28,4},{29,5},{30,6},{31,7}} | collective-permute-start | bytes 98312 | tf_op jit(solution)/shard_map/ppermute | solution.py:811
  39.8 14.3 %collective-permute-start.7 = (bf16[128,128]{1,0:T(8,128)(2,1)S(1)}, bf16[128,128]{1,0:T(8,128)(2,1)S(1)}, u32[]{:S(2)}, u32[]{:S(2)}) collective-permute-start(bf16[128,128]{1,0:T(8,128)(2,1)S(1)} %get-tuple-element.34.refs_7_), channel_id=1, source_target_pairs={{24,8},{25,9},{26,10},{27,11},{28,12},{29,13},{30,14},{31,15}} | collective-permute-start | bytes 98312 | tf_op jit(solution)/shard_map/ppermute | solution.py:811
  40.5 13.6 %collective-permute-start.8 = (bf16[128,128]{1,0:T(8,128)(2,1)S(1)}, bf16[128,128]{1,0:T(8,128)(2,1)S(1)}, u32[]{:S(2)}, u32[]{:S(2)}) collective-permute-start(bf16[128,128]{1,0:T(8,128)(2,1)S(1)} %get-tuple-element.34.refs_7_), channel_id=1, source_target_pairs={{24,16},{25,17},{26,18},{27,19},{28,20},{29,21},{30,22},{31,23}} | collective-permute-start | bytes 98312 | tf_op jit(solution)/shard_map/ppermute | solution.py:811
  48.3 5.8 %collective-permute-start.3 = (bf16[208,256]{1,0:T(8,128)(2,1)S(1)}, bf16[208,256]{1,0:T(8,128)(2,1)S(1)}, u32[]{:S(2)}, u32[]{:S(2)}) collective-permute-start(bf16[208,256]{1,0:T(8,128)(2,1)S(1)} %get-tuple-element.31), channel_id=1, source_target_pairs={{0,1},{1,2},{2,3},{3,4},{4,5},{5,6},{6,7},{7,0},{8,9},{9,10},{10,1... | collective-permute-start | bytes 319496 | tf_op jit(solution)/shard_map/ppermute | solution.py:805
  48.4 8.8 %collective-permute-start.4 = (bf16[208,256]{1,0:T(8,128)(2,1)S(1)}, bf16[208,256]{1,0:T(8,128)(2,1)S(1)}, u32[]{:S(2)}, u32[]{:S(2)}) collective-permute-start(bf16[208,256]{1,0:T(8,128)(2,1)S(1)} %get-tuple-element.32), channel_id=1, source_target_pairs={{0,2},{1,3},{2,4},{3,5},{4,6},{5,7},{6,0},{7,1},{8,10},{9,11},{10,... | collective-permute-start | bytes 319496 | tf_op jit(solution)/shard_map/ppermute | solution.py:805
  49.7 9.6 %collective-permute-start.5 = (bf16[208,256]{1,0:T(8,128)(2,1)S(1)}, bf16[208,256]{1,0:T(8,128)(2,1)S(1)}, u32[]{:S(2)}, u32[]{:S(2)}) collective-permute-start(bf16[208,256]{1,0:T(8,128)(2,1)S(1)} %get-tuple-element.33), channel_id=1, source_target_pairs={{0,3},{1,4},{2,5},{3,6},{4,7},{5,0},{6,1},{7,2},{8,11},{9,12},{10,... | collective-permute-start | bytes 319496 | tf_op jit(solution)/shard_map/ppermute | solution.py:805
  63.4 4.2 %collective-permute-start.9 = (f32[128,128]{1,0:T(8,128)S(1)}, f32[128,128]{1,0:T(8,128)S(1)}, u32[]{:S(2)}, u32[]{:S(2)}) collective-permute-start(f32[128,128]{1,0:T(8,128)S(1)} %get-tuple-element.36.refs_0_), channel_id=1, source_target_pairs={{0,8},{1,9},{2,10},{3,11},{4,12},{5,13},{6,14},{7,15},{8,16},{9,17... | collective-permute-start | bytes 196616 | tf_op jit(solution)/shard_map/ppermute | solution.py:795
  64.1 7.0 %collective-permute-start.13 = (f32[128,128]{1,0:T(8,128)S(1)}, f32[128,128]{1,0:T(8,128)S(1)}, u32[]{:S(2)}, u32[]{:S(2)}) collective-permute-start(f32[128,128]{1,0:T(8,128)S(1)} %get-tuple-element.36.refs_0_), channel_id=1, source_target_pairs={{0,16},{1,17},{2,18},{3,19},{4,20},{5,21},{6,22},{7,23},{8,24},{9,... | collective-permute-start | bytes 196616 | tf_op jit(solution)/shard_map/ppermute | solution.py:795
  65.1 6.0 %collective-permute-start.14 = (f32[128,128]{1,0:T(8,128)S(1)}, f32[128,128]{1,0:T(8,128)S(1)}, u32[]{:S(2)}, u32[]{:S(2)}) collective-permute-start(f32[128,128]{1,0:T(8,128)S(1)} %get-tuple-element.36.refs_0_), channel_id=1, source_target_pairs={{0,24},{1,25},{2,26},{3,27},{4,28},{5,29},{6,30},{7,31},{8,0},{9,1... | collective-permute-start | bytes 196616 | tf_op jit(solution)/shard_map/ppermute | solution.py:795
  67.6 11.9 %collective-permute-start.10 = (f32[2,128,128]{2,1,0:T(8,128)S(1)}, f32[2,128,128]{2,1,0:T(8,128)S(1)}, u32[]{:S(2)}, u32[]{:S(2)}) collective-permute-start(f32[2,128,128]{2,1,0:T(8,128)S(1)} %get-tuple-element.38.refs_3_), channel_id=1, source_target_pairs={{0,24},{1,25},{2,26},{3,27},{4,28},{5,29},{6,30},{7,31}} | collective-permute-start | bytes 393224 | tf_op jit(solution)/shard_map/ppermute | solution.py:817
  69.6 11.7 %collective-permute-start.11 = (f32[2,128,128]{2,1,0:T(8,128)S(1)}, f32[2,128,128]{2,1,0:T(8,128)S(1)}, u32[]{:S(2)}, u32[]{:S(2)}) collective-permute-start(f32[2,128,128]{2,1,0:T(8,128)S(1)} %get-tuple-element.38.refs_3_), channel_id=1, source_target_pairs={{8,24},{9,25},{10,26},{11,27},{12,28},{13,29},{14,30},{15,31}} | collective-permute-start | bytes 393224 | tf_op jit(solution)/shard_map/ppermute | solution.py:817
  70.3 11.1 %collective-permute-start.12 = (f32[2,128,128]{2,1,0:T(8,128)S(1)}, f32[2,128,128]{2,1,0:T(8,128)S(1)}, u32[]{:S(2)}, u32[]{:S(2)}) collective-permute-start(f32[2,128,128]{2,1,0:T(8,128)S(1)} %get-tuple-element.38.refs_3_), channel_id=1, source_target_pairs={{16,24},{17,25},{18,26},{19,27},{20,28},{21,29},{22,30},{23,31}} | collective-permute-start | bytes 393224 | tf_op jit(solution)/shard_map/ppermute | solution.py:817
  71.3 11.0 %collective-permute-start.15 = (f32[64,128]{1,0:T(8,128)S(1)}, f32[64,128]{1,0:T(8,128)S(1)}, u32[]{:S(2)}, u32[]{:S(2)}) collective-permute-start(f32[64,128]{1,0:T(8,128)S(1)} %get-tuple-element.43), channel_id=1, source_target_pairs={{0,7},{1,0},{2,1},{3,2},{4,3},{5,4},{6,5},{7,6},{8,15},{9,8},{10,9... | collective-permute-start | bytes 98312 | tf_op jit(solution)/shard_map/ppermute | solution.py:805
  76.7 5.5 %collective-permute-start.16 = (f32[64,128]{1,0:T(8,128)S(1)}, f32[64,128]{1,0:T(8,128)S(1)}, u32[]{:S(2)}, u32[]{:S(2)}) collective-permute-start(f32[64,128]{1,0:T(8,128)S(1)} %get-tuple-element.44), channel_id=1, source_target_pairs={{0,6},{1,7},{2,0},{3,1},{4,2},{5,3},{6,4},{7,5},{8,14},{9,15},{10,... | collective-permute-start | bytes 98312 | tf_op jit(solution)/shard_map/ppermute | solution.py:805
  79.4 6.1 %collective-permute-start.17 = (f32[64,128]{1,0:T(8,128)S(1)}, f32[64,128]{1,0:T(8,128)S(1)}, u32[]{:S(2)}, u32[]{:S(2)}) collective-permute-start(f32[64,128]{1,0:T(8,128)S(1)} %get-tuple-element.45), channel_id=1, source_target_pairs={{0,5},{1,6},{2,7},{3,0},{4,1},{5,2},{6,3},{7,4},{8,13},{9,14},{10,... | collective-permute-start | bytes 98312 | tf_op jit(solution)/shard_map/ppermute | solution.py:805

commit v8 on v7

--- a/solution.py
+++ b/solution.py
@@ -103,12 +103,12 @@
 
 
 def advance_kernel(comp_count, left_at, right_at, *refs):
-    (flags, source_column, labels, state, up_rows, low_rows, left_in, right_in, own_sides) = refs[:9]
-    (mask, mix_atm, mix_ocn, flux_map) = refs[9:13]
-    out, surface, sea_copy = refs[13:16]
-    packed = refs[16]
-    (values, moved, halo_moved, smooth, pairs, mixed, later_smooth, later_pairs, later_mixed) = refs[17:26]
-    (weights, flux_weights, fluxes, staged, top, in_sems, out_sems) = refs[26:]
+    (flags, ocean_first, source_column, labels, state, up_rows, low_rows, left_in, right_in) = refs[:9]
+    (own_sides, mask, mix_atm, mix_ocn, flux_map) = refs[9:14]
+    out, surface, packed = refs[14:17]
+    phi = refs[17:-16]
+    (values, moved, halo_moved, smooth, pairs, mixed, later_smooth, later_pairs, later_mixed) = refs[-16:-7]
+    (weights, flux_weights, fluxes, staged, top, in_sems, out_sems) = refs[-7:]
     left_cols = left_in.at[left_at : left_at + 2]
     right_cols = right_in.at[right_at : right_at + 2]
     first = (smooth, pairs, mixed)
@@ -142,7 +142,6 @@
     weights[levels:, :levels] = mix_high
     weights[:levels, levels:] = mix_low
     weights[levels:, levels:] = mix_low
-    sea_copy[...] = mask[...].astype(BF16)
     map_high, map_low = split_two(flux_map[...])
     flux_weights[...] = jnp.concatenate(
         [
@@ -298,13 +297,21 @@
         spots = lax.broadcasted_iota(jnp.int32, (source_column.shape[0], rows), 1)
         placing = jnp.where(source_column[...] == spots, 1.0, 0.0).astype(BF16)
         share = flux_count // comp_count
+        size = placing.shape[0]
+        total = jnp.zeros((size, cols), F32)
         for c in range(comp_count):
             for f in range(share):
-                field = fluxes[pl.ds(c * share + f, rows, stride=flux_count), :].astype(BF16)
-                packed[c, : placing.shape[0], f * cols : (f + 1) * cols] = dot_nn(
-                    placing, field
-                ).astype(BF16)
-            packed[c, placing.shape[0] :, :] = labels[...]
+                index = c * share + f
+                field = fluxes[pl.ds(index, rows, stride=flux_count), :].astype(BF16)
+                value = dot_nn(placing, field)
+                packed[c, :size, f * cols : (f + 1) * cols] = value.astype(BF16)
+                total = total + ocean_first[index] * value
+            packed[c, size:, :] = labels[...]
+        total = side_by_side(total)
+        capacity = size // len(phi)
+        for n, block in enumerate(phi):
+            block[:capacity, :] = total[n * capacity : (n + 1) * capacity, :]
+            block[capacity:, :] = labels[...]
         put(last - 1, (last - 1) % 2).wait()
         put(last, last % 2).wait()
         surface[...] = top[...].T
@@ -350,10 +357,13 @@
         put(chunks - 1, (chunks - 1) % 2).wait()
         surface[...] = top[...].T
         packed[...] = jnp.zeros(packed.shape, BF16)
+        for block in phi:
+            block[...] = jnp.zeros(block.shape, BF16)
 
 
 def advance(
-    flags, source_column, labels, state, halos, mask, mix_atm, mix_ocn, flux_map_t, comp_count, left_at, right_at
+    flags, ocean_first, source_column, labels, state, halos, mask, mix_atm, mix_ocn, flux_map_t,
+    comp_count, neighbours, left_at, right_at,
 ):
     rows, cols, levels = state.shape
     fluxes = flux_map_t.shape[0]
@@ -363,17 +373,20 @@
     entry = jax.ShapeDtypeStruct(
         (comp_count, source_column.shape[0] + labels.shape[0], fluxes // comp_count * cols), BF16
     )
+    block = jax.ShapeDtypeStruct(
+        (source_column.shape[0] // neighbours + labels.shape[0], 2 * cols), BF16
+    )
     cells = rows * cols
     return pl.pallas_call(
         functools.partial(advance_kernel, comp_count, left_at, right_at),
         out_shape=(
             jax.ShapeDtypeStruct(state.shape, F32),
             jax.ShapeDtypeStruct((rows, cols), F32),
-            jax.ShapeDtypeStruct((rows, cols), BF16),
             entry,
-        ),
-        in_specs=[smem, vmem, vmem, hbm] + [vmem] * (len(halos) + 4),
-        out_specs=(hbm, vmem, vmem, vmem),
+        )
+        + (block,) * neighbours,
+        in_specs=[smem, smem, vmem, vmem, hbm] + [vmem] * (len(halos) + 4),
+        out_specs=(hbm, vmem, vmem) + (vmem,) * neighbours,
         scratch_shapes=[
             pltpu.VMEM((rows + 4, cols + 2 * EDGE, levels), F32),
             pltpu.VMEM((rows + 2, cols + 2 * EDGE, levels), F32),
@@ -397,7 +410,7 @@
             flops=8 * cells * levels * levels, bytes_accessed=8 * cells * levels, transcendentals=0
         ),
         name="advance",
-    )(flags, source_column, labels, state, *halos, mask, mix_atm, mix_ocn, flux_map_t)
+    )(flags, ocean_first, source_column, labels, state, *halos, mask, mix_atm, mix_ocn, flux_map_t)
 
 
 BATCH = 8
@@ -434,40 +447,101 @@
     )(slabs)
 
 
-def regrid_body(count, comp_count, flags, ocean_first, *refs):
+def label_lines_of(blocks, start, lines):
+    width = blocks[0].shape[1]
+    capacity = width // len(blocks)
+    lanes = lax.broadcasted_iota(jnp.int32, (LABEL_ROWS, width), 1) // capacity
+    labels = jnp.zeros((LABEL_ROWS, width), F32)
+    for n, block in enumerate(blocks):
+        labels = jnp.where(lanes == n, block[start:, :].astype(F32), labels)
+    labels = labels.astype(jnp.int32)
+    join = lambda first: jnp.concatenate([labels[first + c : first + c + 1] for c in range(lines)], axis=1)
+    return join(0), join(lines)
+
+
+def selectors(weight_line, target_line, weight_count, rows):
+    total = target_line.shape[1]
+    spots = lax.broadcasted_iota(jnp.int32, (rows, total), 0)
+    by_target = jnp.where(target_line == spots, 1.0, 0.0)
+    numbers = lax.broadcasted_iota(jnp.int32, (weight_count, total), 0)
+    by_weight = jnp.where(weight_line == numbers, 1.0, 0.0).astype(BF16)
+    return by_target, by_weight
+
+
+def project_kernel(count, flags, *refs):
     blocks = refs[:count]
-    seas = refs[count : count + comp_count]
-    weights, surface, mask, forcing, shared, hits, entries, chosen, binned = refs[count + comp_count :]
-    sources = comp_count - 1
+    weights, surface, mask, shared, hits, entries, chosen = refs[count:]
     rows, cols = mask.shape
-    share = forcing.shape[0]
     weight_count = weights.shape[0]
+    capacity = blocks[0].shape[0] - LABEL_ROWS
+    for n in range(count):
+        entries[n * capacity : (n + 1) * capacity, :] = blocks[n][:capacity, :]
+    weight_line, target_line = label_lines_of(blocks, capacity, 1)
+    by_target, by_weight = selectors(weight_line, target_line, weight_count, rows)
+    hits[...] = by_target.T.astype(BF16)
+    by_target = by_target.astype(BF16)
+    change = jnp.zeros((rows, cols), F32)
+    for g in range(weight_count // BATCH):
+        for i in range(BATCH):
+            w = g * BATCH + i
+            chosen[i * rows : (i + 1) * rows, :] = by_target * by_weight[w : w + 1, :]
+        both = dot_nn(chosen[...], entries[...])
+        both = both[:, :cols] + both[:, cols:]
+        wide = weights[g * BATCH : (g + 1) * BATCH].reshape(BATCH * cols, cols)
+        halves = [split_two(both[i * rows : (i + 1) * rows, :]) for i in range(BATCH)]
+        stacked = jnp.concatenate(
+            [jnp.concatenate([half[k] for half in halves], axis=1) for k in range(2)], axis=0
+        )
+        product = dot_nn(stacked, wide)
+        change = change + (product[:rows] + product[rows:])
+    shared[0] = jnp.where(flags[0] == 1, surface[...], change)
+    shared[1] = mask[...]
+
+
+def project(flags, blocks, weights, surface, mask):
+    rows, cols = mask.shape
+    count = len(blocks)
+    height, width = blocks[0].shape
+    total = count * (height - LABEL_ROWS)
+    vmem = pl.BlockSpec(memory_space=pltpu.VMEM)
+    smem = pl.BlockSpec(memory_space=pltpu.SMEM)
+    return pl.pallas_call(
+        functools.partial(project_kernel, count),
+        out_shape=(
+            jax.ShapeDtypeStruct((2, rows, cols), F32),
+            jax.ShapeDtypeStruct((total, rows), BF16),
+        ),
+        in_specs=[smem] + [vmem] * (count + 3),
+        out_specs=(vmem, vmem),
+        scratch_shapes=[
+            pltpu.VMEM((total, width), BF16),
+            pltpu.VMEM((BATCH * rows, total), BF16),
+        ],
+        compiler_params=pltpu.CompilerParams(vmem_limit_bytes=32 * MIB),
+        cost_estimate=pl.CostEstimate(
+            flops=2 * weights.shape[0] * rows * (width * total + 2 * cols * cols),
+            bytes_accessed=2 * MIB,
+            transcendentals=0,
+        ),
+        name="project",
+    )(flags, *blocks, weights, surface, mask)
+
+
+def regrid_kernel(sources, *refs):
+    blocks = refs[:-5]
+    weights, forcing, entries, chosen, binned = refs[-5:]
+    share, rows, cols = forcing.shape
+    weight_count = weights.shape[0]
+    count = len(blocks)
     capacity = (blocks[0].shape[0] - LABEL_ROWS) // sources
     size = count * capacity
-    total = sources * size
-    width = blocks[0].shape[1]
     for c in range(sources):
         for n in range(count):
             start = c * size + n * capacity
             entries[start : start + capacity, :] = blocks[n][c * capacity : (c + 1) * capacity, :]
-    lanes = lax.broadcasted_iota(jnp.int32, (LABEL_ROWS, width), 1) // capacity
-    labels = jnp.zeros((LABEL_ROWS, width), F32)
-    for n in range(count):
-        labels = jnp.where(lanes == n, blocks[n][sources * capacity :, :].astype(F32), labels)
-    labels = labels.astype(jnp.int32)
-    weight_line = jnp.concatenate([labels[c : c + 1, :size] for c in range(sources)], axis=1)
-    target_line = jnp.concatenate(
-        [labels[sources + c : sources + c + 1, :size] for c in range(sources)], axis=1
-    )
-    spots = lax.broadcasted_iota(jnp.int32, (rows, total), 0)
-    by_target = jnp.where(target_line == spots, 1.0, 0.0)
-    own = by_target[:, :size]
-    for c in range(1, sources):
-        own = jnp.where(flags[3] == c, by_target[:, c * size : (c + 1) * size], own)
-    hits[...] = own.T.astype(BF16)
+    weight_line, target_line = label_lines_of(blocks, sources * capacity, sources)
+    by_target, by_weight = selectors(weight_line, target_line, weight_count, rows)
     by_target = by_target.astype(BF16)
-    numbers = lax.broadcasted_iota(jnp.int32, (weight_count, total), 0)
-    by_weight = jnp.where(weight_line == numbers, 1.0, 0.0).astype(BF16)
     for g in range(weight_count // BATCH):
         for i in range(BATCH):
             w = g * BATCH + i
@@ -495,37 +569,20 @@
                 (share + f) * rows : (share + f + 1) * rows
             ]
             forcing[f] = part if g == 0 else forcing[f] + part
-    change = ocean_first[flags[3] * share] * forcing[0]
-    for f in range(1, share):
-        change = change + ocean_first[flags[3] * share + f] * forcing[f]
-    sea = jnp.where(flags[0] == 1, seas[sources][...].astype(F32), 0.0)
-    for c in range(sources):
-        sea = sea + jnp.where(flags[3] == c, seas[c][...].astype(F32), 0.0)
-    base = jnp.where(flags[0] == 1, surface[...], 0.0)
-    shared[...] = base + jnp.where(sea > 0.5, change, 0.0)
-
-
-def regrid(flags, ocean_first, blocks, seas, weights, surface, mask):
-    comp_count = len(seas)
+
+
+def regrid(blocks, comp_count, weights, rows):
     sources = comp_count - 1
-    rows, cols = mask.shape
-    count = len(blocks)
+    weight_count, cols, _ = weights.shape
     height, width = blocks[0].shape
-    size = (height - LABEL_ROWS) // sources * count
-    total = size * sources
+    total = (height - LABEL_ROWS) * len(blocks)
     share = width // cols
-    weight_count = weights.shape[0]
     vmem = pl.BlockSpec(memory_space=pltpu.VMEM)
-    smem = pl.BlockSpec(memory_space=pltpu.SMEM)
     return pl.pallas_call(
-        functools.partial(regrid_body, count, comp_count),
-        out_shape=(
-            jax.ShapeDtypeStruct((share, rows, cols), F32),
-            jax.ShapeDtypeStruct((rows, cols), F32),
-            jax.ShapeDtypeStruct((size, rows), BF16),
-        ),
-        in_specs=[smem, smem] + [vmem] * (count + comp_count + 3),
-        out_specs=(vmem, vmem, vmem),
+        functools.partial(regrid_kernel, sources),
+        out_shape=jax.ShapeDtypeStruct((share, rows, cols), F32),
+        in_specs=[vmem] * (len(blocks) + 1),
+        out_specs=vmem,
         scratch_shapes=[
             pltpu.VMEM((total, width), BF16),
             pltpu.VMEM((BATCH * rows, total), BF16),
@@ -538,16 +595,23 @@
             transcendentals=0,
         ),
         name="regrid",
-    )(flags, ocean_first, *blocks, *seas, weights, surface, mask)
-
-
-def pick_kernel(count, *refs):
+    )(*blocks, weights)
+
+
+def pick_kernel(count, flags, *refs):
     parts = refs[:count]
     hits, surface = refs[count : count + 2]
     picked = refs[count + 2 :]
-    now = parts[0][...]
-    for part in parts[1:]:
-        now = now + part[...]
+    from_ocean = lax.rem(flags[3] + 1, count)
+    base = jnp.zeros(surface.shape, F32)
+    sea = base
+    change = base
+    for shift in range(count):
+        is_base = from_ocean == shift
+        base = base + jnp.where(is_base, parts[shift][0], 0.0)
+        sea = sea + jnp.where(is_base, parts[shift][1], 0.0)
+        change = change + jnp.where(is_base, 0.0, parts[shift][0])
+    now = base + jnp.where(sea > 0.5, change, 0.0)
     surface[...] = now
     pair = jnp.concatenate(split_two(now), axis=0)
     size = picked[0].shape[0]
@@ -556,19 +620,19 @@
         picked[n][...] = dot_nn(jnp.concatenate([some, some], axis=1), pair)
 
 
-def pick(parts, hits, neighbours):
-    rows, cols = parts[0].shape
+def pick(flags, parts, hits, neighbours):
+    _, rows, cols = parts[0].shape
     size = hits.shape[0] // neighbours
     vmem = pl.BlockSpec(memory_space=pltpu.VMEM)
     return pl.pallas_call(
         functools.partial(pick_kernel, len(parts)),
         out_shape=(jax.ShapeDtypeStruct((rows, cols), F32),)
         + (jax.ShapeDtypeStruct((size, cols), F32),) * neighbours,
-        in_specs=[vmem] * (len(parts) + 1),
+        in_specs=[pl.BlockSpec(memory_space=pltpu.SMEM)] + [vmem] * (len(parts) + 1),
         out_specs=(vmem,) * (1 + neighbours),
         compiler_params=pltpu.CompilerParams(vmem_limit_bytes=16 * MIB),
         name="pick",
-    )(*parts, hits)
+    )(flags, *parts, hits)
 
 
 LINES = 8
@@ -804,12 +868,6 @@
         ]
         return lax.ppermute(value, AXES, pairs)
 
-    def from_ocean(value, comp):
-        pairs = [
-            (ocean_comp * tile_count + t, comp * tile_count + t) for t in range(tile_count)
-        ]
-        return lax.ppermute(value, AXES, pairs)
-
     def to_ocean(value, comp):
         pairs = [
             (comp * tile_count + t, ocean_comp * tile_count + t) for t in range(tile_count)
@@ -821,20 +879,18 @@
 
     halos = (up_rows, low_rows, left_cols, right_cols, sides)
     moved = advance(
-        flags, sources[:, None], label_lines, state, halos, mask, mix_atm, mix_ocn, flux_map.T,
-        comp_count, left_at, right_at,
+        flags, ocean_map[:, 0], sources[:, None], label_lines, state, halos, mask, mix_atm, mix_ocn,
+        flux_map.T, comp_count, neighbours, left_at, right_at,
     )
-    moved, surface, sea_copy, packed = moved
-    slabs = over_comp(packed)
-    seas = [from_ocean(sea_copy, c) for c in range(ocean_comp)] + [sea_copy]
-    blocks = regroup(slabs, neighbours)
+    moved, surface, packed, phi = moved[0], moved[1], moved[2], moved[3:]
+    phi = [over_tiles(phi[n], offsets[n], ocean_comp) for n in range(neighbours)]
+    phi[1], packed = lax.optimization_barrier((phi[1], packed))
+    shared, hits = project(flags, phi, regrid_weights, surface, mask)
+    parts = [shared] + [shifted_comp(shared, s) for s in range(1, comp_count)]
+    picks = pick(flags, parts, hits, neighbours)
+    blocks = regroup(over_comp(packed), neighbours)
     blocks = [over_tiles(blocks[n], offsets[n], comp_count) for n in range(neighbours)]
-    forcing, shared, hits = regrid(
-        flags, ocean_map[:, 0], blocks, seas, regrid_weights, surface, mask
-    )
-    parts = [shared] + [shifted_comp(shared, s) for s in range(1, comp_count)]
-    parts[1], forcing = lax.optimization_barrier((parts[1], forcing))
-    picks = pick(parts, hits, neighbours)
+    forcing = regrid(blocks, comp_count, regrid_weights, rows)
     new_surface, picked = picks[0], picks[1:]
     arrived = [over_tiles(picked[n], -offsets[n], ocean_comp) for n in range(neighbours)]
     fields = [to_ocean(forcing, c) for c in range(ocean_comp)] + [forcing]

time: 88.4 us -> 88.5 us (level)
  waiting for transfers between devices: 21.8 us -> 10.8 us
  starting transfers between devices: 35.1 us -> 44.1 us
  Pallas kernels: 28.6 us -> 30.8 us
    ppermute x6 -> x9, starting transfers between devices: 15.7 us -> 26.2 us  [over_tiles(): return lax.ppermute(value, AXES, pairs)]
    all_to_all x1, waiting for transfers between devices: 7.07 us -> 0.01 us  [over_comp(): lax.all_to_all(value, 'comp', split_axis=0, concat_axis=0, tiled=True)]
    ppermute x6 -> x9, waiting for transfers between devices: 8.51 us -> 5.74 us  [over_tiles(): return lax.ppermute(value, AXES, pairs)]
    ppermute x3 -> x0, starting transfers between devices: 2.61 us -> none  [from_ocean(): return lax.ppermute(value, AXES, pairs)]
    pallas_call x1 -> x2, Pallas kernels: 4.1 us -> 5.65 us  [the longest x1 3.55 us: regrid(): pl.pallas_call(functools.partial(regrid_kernel, sources), out_shape=jax.S...]
    ppermute x3, waiting for transfers between devices: 1.11 us -> 0.01 us  [shifted_comp(): return lax.ppermute(value, AXES, pairs)]
    ppermute x3, starting transfers between devices: 3.38 us -> 4.45 us  [to_ocean(): return lax.ppermute(value, AXES, pairs)]
  transfers between devices with their start and end apart: 19 -> 19, of which waited for: 7 -> 5; matrix products, arithmetic and copies ran while one was open for 2% -> 2% of each run, Pallas kernels for 1% -> 8%
where the time goes in v8:
time: 88.5 us; the launch traced here: 88 us
  starting transfers between devices  44.1 us (50%)
  Pallas kernels  30.8 us (35%)
  waiting for transfers between devices  10.8 us (12%)
  between operations  1.07 us (1%)
    ppermute x9, starting transfers between devices, over_tiles(): return lax.ppermute(value, AXES, pairs)  26.2 us
    pallas_call x1, Pallas kernels, advance(): pl.pallas_call(functools.partial(advance_kernel, comp_count, left_at, rig...  19.4 us
    ppermute x3, starting transfers between devices, band_shift(): return lax.ppermute(value, AXES, pairs)  6.48 us
    ppermute x9, waiting for transfers between devices, over_tiles(): return lax.ppermute(value, AXES, pairs)  5.74 us
    ppermute x3, waiting for transfers between devices, band_shift(): return lax.ppermute(value, AXES, pairs)  5.01 us
    ppermute x3, starting transfers between devices, to_ocean(): return lax.ppermute(value, AXES, pairs)  4.45 us
    pallas_call x1, Pallas kernels, regrid(): pl.pallas_call(functools.partial(regrid_kernel, sources), out_shape=jax.S...  3.55 us
    all_to_all x1, starting transfers between devices, over_comp(): lax.all_to_all(value, 'comp', split_axis=0, concat_axis=0, tiled=True)  3.47 us
  transfers between devices with their start and end apart: 19, of which 5 were waited for; matrix products, arithmetic and copies ran while one was open for 2% of the time, Pallas kernels for 8%

profile of v8, /device:TPU:1, one launch (start us, length us, event | category | flops | bytes accessed | tf_op | source)
XLA Modules:
  0.0 88.0 jit_solution(14427513278031139606)
XLA Ops:
  0.7 1.6 %edges.1 = (bf16[2,128,128]{2,1,0:T(8,128)(2,1)S(1)}, bf16[2,128,128]{2,1,0:T(8,128)(2,1)S(1)}, f32[4,128,128]{2,1,0:T(8,128)S(1)}) custom-call(f32[128,128,128]{2,1,0:T(8,128)} %refs_4_.3), custom_call_target="tpu_custom_call" | custom-call | tf_op jit(solution)/shard_map/edges/pallas_call | solution.py:63
  2.3 0.0 copy-start
  2.3 4.2 %collective-permute-start = (bf16[2,128,128]{2,1,0:T(8,128)(2,1)S(1)}, bf16[2,128,128]{2,1,0:T(8,128)(2,1)S(1)}, u32[]{:S(2)}, u32[]{:S(2)}) collective-permute-start(bf16[2,128,128]{2,1,0:T(8,128)(2,1)S(1)} %get-tuple-element.27), channel_id=1, source_target_pairs={{0,2},{1,3},{2,4},{3,5},{4,6},{5,7},{6,8},{7,9},{8,10},{9,11},{10,... | collective-permute-start | bytes 196616 | tf_op jit(solution)/shard_map/ppermute | solution.py:815
  6.5 1.3 %collective-permute-start.1 = (bf16[2,128,128]{2,1,0:T(8,128)(2,1)S(1)}, bf16[2,128,128]{2,1,0:T(8,128)(2,1)S(1)}, u32[]{:S(2)}, u32[]{:S(2)}) collective-permute-start(bf16[2,128,128]{2,1,0:T(8,128)(2,1)S(1)} %get-tuple-element.28), channel_id=1, source_target_pairs={{2,0},{3,1},{4,2},{5,3},{6,4},{7,5},{8,6},{9,7},{10,8},{11,9},{12,... | collective-permute-start | bytes 196616 | tf_op jit(solution)/shard_map/ppermute | solution.py:815
  7.8 0.2 copy.19
  8.0 0.3 fusion.4
  8.3 0.2 convert_reduce_fusion
  8.5 0.2 select_reduce_fusion
  8.6 0.1 copy.20.refs_2_
  8.8 0.1 slice_reduce_fusion.refs_1_
  8.9 0.0 collective-permute-done.up_rows.refs_5_
  8.9 3.9 %collective-permute-done.1.low_rows.refs_6_ = bf16[2,128,128]{2,1,0:T(8,128)(2,1)S(1)} collective-permute-done((bf16[2,128,128]{2,1,0:T(8,128)(2,1)S(1)}, bf16[2,128,128]{2,1,0:T(8,128)(2,1)S(1)}, u32[]{:S(2)}, u32[]{:S(2)}) %collective-permute-start.1) | collective-permute-done | bytes 65568 | tf_op jit(solution)/shard_map/ppermute | solution.py:815
  12.9 1.0 %collective-permute-start.2 = (f32[4,144,128]{2,1,0:T(8,128)S(1)}, f32[4,144,128]{2,1,0:T(8,128)S(1)}, u32[]{:S(2)}, u32[]{:S(2)}) collective-permute-start(f32[4,144,128]{2,1,0:T(8,128)S(1)} %frame.1), channel_id=1, source_target_pairs={{0,1},{1,0},{2,3},{3,2},{4,5},{5,4},{6,7},{7,6},{8,9},{9,8},{10,11... | collective-permute-start | bytes 884744 | tf_op jit(solution)/shard_map/ppermute | solution.py:815
  13.9 0.1 pad_add_fusion.refs_0_.flags
  14.0 1.1 %collective-permute-done.2.refs_7_.refs_8_ = f32[4,144,128]{2,1,0:T(8,128)S(1)} collective-permute-done((f32[4,144,128]{2,1,0:T(8,128)S(1)}, f32[4,144,128]{2,1,0:T(8,128)S(1)}, u32[]{:S(2)}, u32[]{:S(2)}) %collective-permute-start.2) | collective-permute-done | bytes 294944 | tf_op jit(solution)/shard_map/ppermute | solution.py:815
  15.1 19.4 %advance.1 = (f32[128,128,128]{2,1,0:T(8,128)}, f32[128,128]{1,0:T(8,128)S(1)}, bf16[4,272,256]{2,1,0:T(8,128)(2,1)}, bf16[80,256]{1,0:T(8,128)(2,1)S(1)}, bf16[...) custom-call(s32[4]{0:T(128)S(1)} %pad_add_fusion.refs_0_.flags, ...), custom_call_target="tpu_custom_call" | custom-call | flops 2147483648 | bytes 16777216 | tf_op jit(solution)/shard_map/advance/pallas_call | solution.py:380
  34.6 3.3 %collective-permute-start.3 = (bf16[80,256]{1,0:T(8,128)(2,1)S(1)}, bf16[80,256]{1,0:T(8,128)(2,1)S(1)}, u32[]{:S(2)}, u32[]{:S(2)}) collective-permute-start(bf16[80,256]{1,0:T(8,128)(2,1)S(1)} %get-tuple-element.31), channel_id=1, source_target_pairs={{0,1},{1,2},{2,3},{3,4},{4,5},{5,6},{6,7},{7,0},{8,9},{9,10},{10,1... | collective-permute-start | bytes 122888 | tf_op jit(solution)/shard_map/ppermute | solution.py:869
  37.8 1.1 %collective-permute-done.3.refs_1_ = bf16[80,256]{1,0:T(8,128)(2,1)S(1)} collective-permute-done((bf16[80,256]{1,0:T(8,128)(2,1)S(1)}, bf16[80,256]{1,0:T(8,128)(2,1)S(1)}, u32[]{:S(2)}, u32[]{:S(2)}) %collective-permute-start.3) | collective-permute-done | bytes 40992 | tf_op jit(solution)/shard_map/ppermute | solution.py:869
  38.9 3.5 %all-to-all-start = ((bf16[4,272,256]{2,1,0:T(8,128)(2,1)}), bf16[4,272,256]{2,1,0:T(8,128)(2,1)S(1)}, u32[]{:S(2)}, u32[]{:S(2)}) async-start(bf16[4,272,256]{2,1,0:T(8,128)(2,1)} %get-tuple-element.33), calls=%async_computation | async-start | bytes 1114112 | tf_op jit(solution)/shard_map/all_to_all | solution.py:851
  42.4 3.2 %collective-permute-start.10 = (bf16[80,256]{1,0:T(8,128)(2,1)S(1)}, bf16[80,256]{1,0:T(8,128)(2,1)S(1)}, u32[]{:S(2)}, u32[]{:S(2)}) collective-permute-start(bf16[80,256]{1,0:T(8,128)(2,1)S(1)} %get-tuple-element.41), channel_id=1, source_target_pairs={{0,2},{1,3},{2,4},{3,5},{4,6},{5,7},{6,0},{7,1},{8,10},{9,11},{10,... | collective-permute-start | bytes 122888 | tf_op jit(solution)/shard_map/ppermute | solution.py:869
  45.6 8.0 %collective-permute-start.11 = (bf16[80,256]{1,0:T(8,128)(2,1)S(1)}, bf16[80,256]{1,0:T(8,128)(2,1)S(1)}, u32[]{:S(2)}, u32[]{:S(2)}) collective-permute-start(bf16[80,256]{1,0:T(8,128)(2,1)S(1)} %get-tuple-element.42), channel_id=1, source_target_pairs={{0,3},{1,4},{2,5},{3,6},{4,7},{5,0},{6,1},{7,2},{8,11},{9,12},{10,... | collective-permute-start | bytes 122888 | tf_op jit(solution)/shard_map/ppermute | solution.py:869
  53.6 0.1 collective-permute-start.4
  53.7 1.6 %collective-permute-start.5 = (bf16[208,256]{1,0:T(8,128)(2,1)S(1)}, bf16[208,256]{1,0:T(8,128)(2,1)S(1)}, u32[]{:S(2)}, u32[]{:S(2)}) collective-permute-start(bf16[208,256]{1,0:T(8,128)(2,1)S(1)} %get-tuple-element.36), channel_id=1, source_target_pairs={{0,2},{1,3},{2,4},{3,5},{4,6},{5,7},{6,0},{7,1},{8,10},{9,11},{10,... | collective-permute-start | bytes 319496 | tf_op jit(solution)/shard_map/ppermute | solution.py:869
  55.3 1.7 %collective-permute-start.6 = (bf16[208,256]{1,0:T(8,128)(2,1)S(1)}, bf16[208,256]{1,0:T(8,128)(2,1)S(1)}, u32[]{:S(2)}, u32[]{:S(2)}) collective-permute-start(bf16[208,256]{1,0:T(8,128)(2,1)S(1)} %get-tuple-element.37), channel_id=1, source_target_pairs={{0,3},{1,4},{2,5},{3,6},{4,7},{5,0},{6,1},{7,2},{8,11},{9,12},{10,... | collective-permute-start | bytes 319496 | tf_op jit(solution)/shard_map/ppermute | solution.py:869
  57.0 0.1 copy.21
  57.2 0.0 collective-permute-done.10.refs_2_
  57.2 0.0 collective-permute-done.11.refs_3_
  57.2 2.1 %project.1 = (f32[2,128,128]{2,1,0:T(8,128)S(1)}, bf16[256,128]{1,0:T(8,128)(2,1)S(1)}) custom-call(s32[4]{0:T(128)S(1)} %pad_add_fusion.refs_0_.flags, bf16[80,256]{1,0:T(8,128)(2,1)S(1)} %get-tuple-element.39.refs_0_, bf16[80,256]{1,0:T(8,128)(2,1)S(1)} %collective-permute-done.3.refs_1_, bf16[80,256]{1,0:T(8,128)(2,1)S(1)} %collective-permute-done.10.refs_2_, ...), custom_call_target="tpu_custom_call" | custom-call | flops 805306368 | bytes 2097152 | tf_op jit(solution)/shard_map/project/pallas_call | solution.py:508
  59.3 1.3 %collective-permute-start.12 = (f32[2,128,128]{2,1,0:T(8,128)S(1)}, f32[2,128,128]{2,1,0:T(8,128)S(1)}, u32[]{:S(2)}, u32[]{:S(2)}) collective-permute-start(f32[2,128,128]{2,1,0:T(8,128)S(1)} %get-tuple-element.44.refs_0_), channel_id=1, source_target_pairs={{0,8},{1,9},{2,10},{3,11},{4,12},{5,13},{6,14},{7,15},{8,16},{9,17... | collective-permute-start | bytes 393224 | tf_op jit(solution)/shard_map/ppermute | solution.py:859
  60.6 0.2 collective-permute-start.13
  60.8 0.0 collective-permute-done.4.refs_1_
  60.8 1.9 %collective-permute-start.14 = (f32[2,128,128]{2,1,0:T(8,128)S(1)}, f32[2,128,128]{2,1,0:T(8,128)S(1)}, u32[]{:S(2)}, u32[]{:S(2)}) collective-permute-start(f32[2,128,128]{2,1,0:T(8,128)S(1)} %get-tuple-element.44.refs_0_), channel_id=1, source_target_pairs={{0,24},{1,25},{2,26},{3,27},{4,28},{5,29},{6,30},{7,31},{8,0},{9,1... | collective-permute-start | bytes 393224 | tf_op jit(solution)/shard_map/ppermute | solution.py:859
  62.8 1.1 %collective-permute-done.6.refs_3_ = bf16[208,256]{1,0:T(8,128)(2,1)S(1)} collective-permute-done((bf16[208,256]{1,0:T(8,128)(2,1)S(1)}, bf16[208,256]{1,0:T(8,128)(2,1)S(1)}, u32[]{:S(2)}, u32[]{:S(2)}) %collective-permute-start.6) | collective-permute-done | bytes 106528 | tf_op jit(solution)/shard_map/ppermute | solution.py:869
  63.9 3.6 %regrid.1.refs_3_ = f32[2,128,128]{2,1,0:T(8,128)S(1)} custom-call(bf16[208,256]{1,0:T(8,128)(2,1)S(1)} %get-tuple-element.34.refs_0_, bf16[208,256]{1,0:T(8,128)(2,1)S(1)} %collective-permute-done.4.refs_1_, bf16[208,256]{1,0:T(8,128)(2,1)S(1)} %collective-permute-done.5.refs_2_, bf16[208,256]{1,0:T(8,128)(2,1)S(1)} %collective-permute-done.6.refs_3_, ...), custom_call_target="tpu_custom_call" | custom-call | flops 2147483648 | bytes 2097152 | tf_op jit(solution)/shard_map/regrid/pallas_call | solution.py:581
  67.5 3.1 %collective-permute-start.7 = (f32[2,128,128]{2,1,0:T(8,128)S(1)}, f32[2,128,128]{2,1,0:T(8,128)S(1)}, u32[]{:S(2)}, u32[]{:S(2)}) collective-permute-start(f32[2,128,128]{2,1,0:T(8,128)S(1)} %regrid.1.refs_3_), channel_id=1, source_target_pairs={{0,24},{1,25},{2,26},{3,27},{4,28},{5,29},{6,30},{7,31}} | collective-permute-start | bytes 393224 | tf_op jit(solution)/shard_map/ppermute | solution.py:875
  70.6 0.7 collective-permute-start.8
  71.3 0.0 collective-permute-done.12.refs_1_
  71.3 0.7 collective-permute-start.9
  72.0 0.1 add_select_fusion.refs_4_
  72.0 0.0 collective-permute-done.13.refs_2_
  72.1 0.0 collective-permute-done.14.refs_3_
  72.1 0.8 pick.1
  72.8 4.5 %collective-permute-start.15 = (f32[64,128]{1,0:T(8,128)S(1)}, f32[64,128]{1,0:T(8,128)S(1)}, u32[]{:S(2)}, u32[]{:S(2)}) collective-permute-start(f32[64,128]{1,0:T(8,128)S(1)} %get-tuple-element.47), channel_id=1, source_target_pairs={{0,7},{1,0},{2,1},{3,2},{4,3},{5,4},{6,5},{7,6},{8,15},{9,8},{10,9... | collective-permute-start | bytes 98312 | tf_op jit(solution)/shard_map/ppermute | solution.py:869
  77.3 1.9 %collective-permute-start.16 = (f32[64,128]{1,0:T(8,128)S(1)}, f32[64,128]{1,0:T(8,128)S(1)}, u32[]{:S(2)}, u32[]{:S(2)}) collective-permute-start(f32[64,128]{1,0:T(8,128)S(1)} %get-tuple-element.48), channel_id=1, source_target_pairs={{0,6},{1,7},{2,0},{3,1},{4,2},{5,3},{6,4},{7,5},{8,14},{9,15},{10,... | collective-permute-start | bytes 98312 | tf_op jit(solution)/shard_map/ppermute | solution.py:869
  79.3 2.0 %collective-permute-start.17 = (f32[64,128]{1,0:T(8,128)S(1)}, f32[64,128]{1,0:T(8,128)S(1)}, u32[]{:S(2)}, u32[]{:S(2)}) collective-permute-start(f32[64,128]{1,0:T(8,128)S(1)} %get-tuple-element.49), channel_id=1, source_target_pairs={{0,5},{1,6},{2,7},{3,0},{4,1},{5,2},{6,3},{7,4},{8,13},{9,14},{10,... | collective-permute-start | bytes 98312 | tf_op jit(solution)/shard_map/ppermute | solution.py:869
  81.3 0.8 update.1
  82.1 3.5 %collective-permute-done.17.refs_3_ = f32[64,128]{1,0:T(8,128)S(1)} collective-permute-done((f32[64,128]{1,0:T(8,128)S(1)}, f32[64,128]{1,0:T(8,128)S(1)}, u32[]{:S(2)}, u32[]{:S(2)}) %collective-permute-start.17) | collective-permute-done | bytes 32800 | tf_op jit(solution)/shard_map/ppermute | solution.py:869
  85.6 2.4 %returned.1 = f32[128,128]{1,0:T(8,128)} custom-call(s32[4]{0:T(128)S(1)} %pad_add_fusion.refs_0_.flags, f32[64,128]{1,0:T(8,128)S(1)} %get-tuple-element.46.refs_0_, f32[64,128]{1,0:T(8,128)S(1)} %collective-permute-done.15.refs_1_, f32[64,128]{1,0:T(8,128)S(1)} %collective-permute-done.16.refs_2_, f32[64,128]{1,0:T(8,128)S(1)} %collective-permute-done.17.refs_3_, ...), custom_call_target="tpu_custom_call" | custom-call | tf_op jit(solution)/shard_map/returned/pallas_call | solution.py:769
  (28 shorter events, 0.2 us)
Async XLA Ops:
  0.6 7.2 %copy-start.6 = (s32[128,1,2,3]{0,2,3,1:T(2,128)S(1)}, s32[128,1,2,3]{0,2,3,1:T(2,128)}, u32[]{:S(2)}) copy-start(s32[128,1,2,3]{0,2,3,1:T(2,128)} %param.11) | copy-start | bytes 9220
  0.6 8.2 %copy-start.3 = (f32[8,128]{1,0:T(8,128)S(1)}, f32[8,128]{1,0:T(8,128)}, u32[]{:S(2)}) copy-start(f32[8,128]{1,0:T(8,128)} %refs_5_.1) | copy-start | bytes 12292
  0.7 13.3 %copy-start.5 = (s32[128,128]{1,0:T(8,128)S(1)}, s32[128,128]{1,0:T(8,128)}, u32[]{:S(2)}) copy-start(s32[128,128]{1,0:T(8,128)} %param.10) | copy-start | bytes 196612
  0.7 14.4 %copy-start.1 = (f32[128,128]{1,0:T(8,128)S(1)}, f32[128,128]{1,0:T(8,128)}, u32[]{:S(2)}) copy-start(f32[128,128]{1,0:T(8,128)} %refs_11_.1) | copy-start | bytes 196612
  0.7 14.4 %copy-start.2 = (f32[128,128]{1,0:T(8,128)S(1)}, f32[128,128]{1,0:T(8,128)}, u32[]{:S(2)}) copy-start(f32[128,128]{1,0:T(8,128)} %refs_12_.1) | copy-start | bytes 196612
  0.7 14.4 %copy-start.4 = (f32[128,8]{0,1:T(8,128)S(1)}, f32[128,8]{0,1:T(8,128)}, u32[]{:S(2)}) copy-start(f32[128,8]{0,1:T(8,128)} %param.14) | copy-start | bytes 12292
  2.3 54.9 %copy-start = (bf16[32,128,128]{2,1,0:T(8,128)(2,1)S(1)}, bf16[32,128,128]{2,1,0:T(8,128)(2,1)}, u32[]{:S(2)}) copy-start(bf16[32,128,128]{2,1,0:T(8,128)(2,1)} %refs_6_.1) | copy-start | bytes 3145732
  2.3 6.6 %collective-permute-start = (bf16[2,128,128]{2,1,0:T(8,128)(2,1)S(1)}, bf16[2,128,128]{2,1,0:T(8,128)(2,1)S(1)}, u32[]{:S(2)}, u32[]{:S(2)}) collective-permute-start(bf16[2,128,128]{2,1,0:T(8,128)(2,1)S(1)} %get-tuple-element.27), channel_id=1, source_target_pairs={{0,2},{1,3},{2,4},{3,5},{4,6},{5,7},{6,8},{7,9},{8,10},{9,11},{10,... | collective-permute-start | bytes 196616 | tf_op jit(solution)/shard_map/ppermute | solution.py:815
  6.5 6.4 %collective-permute-start.1 = (bf16[2,128,128]{2,1,0:T(8,128)(2,1)S(1)}, bf16[2,128,128]{2,1,0:T(8,128)(2,1)S(1)}, u32[]{:S(2)}, u32[]{:S(2)}) collective-permute-start(bf16[2,128,128]{2,1,0:T(8,128)(2,1)S(1)} %get-tuple-element.28), channel_id=1, source_target_pairs={{2,0},{3,1},{4,2},{5,3},{6,4},{7,5},{8,6},{9,7},{10,8},{11,9},{12,... | collective-permute-start | bytes 196616 | tf_op jit(solution)/shard_map/ppermute | solution.py:815
  12.9 2.2 %collective-permute-start.2 = (f32[4,144,128]{2,1,0:T(8,128)S(1)}, f32[4,144,128]{2,1,0:T(8,128)S(1)}, u32[]{:S(2)}, u32[]{:S(2)}) collective-permute-start(f32[4,144,128]{2,1,0:T(8,128)S(1)} %frame.1), channel_id=1, source_target_pairs={{0,1},{1,0},{2,3},{3,2},{4,5},{5,4},{6,7},{7,6},{8,9},{9,8},{10,11... | collective-permute-start | bytes 884744 | tf_op jit(solution)/shard_map/ppermute | solution.py:815
  34.6 4.4 %collective-permute-start.3 = (bf16[80,256]{1,0:T(8,128)(2,1)S(1)}, bf16[80,256]{1,0:T(8,128)(2,1)S(1)}, u32[]{:S(2)}, u32[]{:S(2)}) collective-permute-start(bf16[80,256]{1,0:T(8,128)(2,1)S(1)} %get-tuple-element.31), channel_id=1, source_target_pairs={{0,1},{1,2},{2,3},{3,4},{4,5},{5,6},{6,7},{7,0},{8,9},{9,10},{10,1... | collective-permute-start | bytes 122888 | tf_op jit(solution)/shard_map/ppermute | solution.py:869
  38.9 14.7 %all-to-all-start = ((bf16[4,272,256]{2,1,0:T(8,128)(2,1)}), bf16[4,272,256]{2,1,0:T(8,128)(2,1)S(1)}, u32[]{:S(2)}, u32[]{:S(2)}) async-start(bf16[4,272,256]{2,1,0:T(8,128)(2,1)} %get-tuple-element.33), calls=%async_computation | async-start | bytes 1114112 | tf_op jit(solution)/shard_map/all_to_all | solution.py:851
  42.4 14.8 %collective-permute-start.10 = (bf16[80,256]{1,0:T(8,128)(2,1)S(1)}, bf16[80,256]{1,0:T(8,128)(2,1)S(1)}, u32[]{:S(2)}, u32[]{:S(2)}) collective-permute-start(bf16[80,256]{1,0:T(8,128)(2,1)S(1)} %get-tuple-element.41), channel_id=1, source_target_pairs={{0,2},{1,3},{2,4},{3,5},{4,6},{5,7},{6,0},{7,1},{8,10},{9,11},{10,... | collective-permute-start | bytes 122888 | tf_op jit(solution)/shard_map/ppermute | solution.py:869
  45.6 11.6 %collective-permute-start.11 = (bf16[80,256]{1,0:T(8,128)(2,1)S(1)}, bf16[80,256]{1,0:T(8,128)(2,1)S(1)}, u32[]{:S(2)}, u32[]{:S(2)}) collective-permute-start(bf16[80,256]{1,0:T(8,128)(2,1)S(1)} %get-tuple-element.42), channel_id=1, source_target_pairs={{0,3},{1,4},{2,5},{3,6},{4,7},{5,0},{6,1},{7,2},{8,11},{9,12},{10,... | collective-permute-start | bytes 122888 | tf_op jit(solution)/shard_map/ppermute | solution.py:869
  53.6 7.2 %collective-permute-start.4 = (bf16[208,256]{1,0:T(8,128)(2,1)S(1)}, bf16[208,256]{1,0:T(8,128)(2,1)S(1)}, u32[]{:S(2)}, u32[]{:S(2)}) collective-permute-start(bf16[208,256]{1,0:T(8,128)(2,1)S(1)} %get-tuple-element.35), channel_id=1, source_target_pairs={{0,1},{1,2},{2,3},{3,4},{4,5},{5,6},{6,7},{7,0},{8,9},{9,10},{10,1... | collective-permute-start | bytes 319496 | tf_op jit(solution)/shard_map/ppermute | solution.py:869
  53.7 9.1 %collective-permute-start.5 = (bf16[208,256]{1,0:T(8,128)(2,1)S(1)}, bf16[208,256]{1,0:T(8,128)(2,1)S(1)}, u32[]{:S(2)}, u32[]{:S(2)}) collective-permute-start(bf16[208,256]{1,0:T(8,128)(2,1)S(1)} %get-tuple-element.36), channel_id=1, source_target_pairs={{0,2},{1,3},{2,4},{3,5},{4,6},{5,7},{6,0},{7,1},{8,10},{9,11},{10,... | collective-permute-start | bytes 319496 | tf_op jit(solution)/shard_map/ppermute | solution.py:869
  55.3 8.6 %collective-permute-start.6 = (bf16[208,256]{1,0:T(8,128)(2,1)S(1)}, bf16[208,256]{1,0:T(8,128)(2,1)S(1)}, u32[]{:S(2)}, u32[]{:S(2)}) collective-permute-start(bf16[208,256]{1,0:T(8,128)(2,1)S(1)} %get-tuple-element.37), channel_id=1, source_target_pairs={{0,3},{1,4},{2,5},{3,6},{4,7},{5,0},{6,1},{7,2},{8,11},{9,12},{10,... | collective-permute-start | bytes 319496 | tf_op jit(solution)/shard_map/ppermute | solution.py:869
  59.3 12.0 %collective-permute-start.12 = (f32[2,128,128]{2,1,0:T(8,128)S(1)}, f32[2,128,128]{2,1,0:T(8,128)S(1)}, u32[]{:S(2)}, u32[]{:S(2)}) collective-permute-start(f32[2,128,128]{2,1,0:T(8,128)S(1)} %get-tuple-element.44.refs_0_), channel_id=1, source_target_pairs={{0,8},{1,9},{2,10},{3,11},{4,12},{5,13},{6,14},{7,15},{8,16},{9,17... | collective-permute-start | bytes 393224 | tf_op jit(solution)/shard_map/ppermute | solution.py:859
  60.6 11.5 %collective-permute-start.13 = (f32[2,128,128]{2,1,0:T(8,128)S(1)}, f32[2,128,128]{2,1,0:T(8,128)S(1)}, u32[]{:S(2)}, u32[]{:S(2)}) collective-permute-start(f32[2,128,128]{2,1,0:T(8,128)S(1)} %get-tuple-element.44.refs_0_), channel_id=1, source_target_pairs={{0,16},{1,17},{2,18},{3,19},{4,20},{5,21},{6,22},{7,23},{8,24},{9,... | collective-permute-start | bytes 393224 | tf_op jit(solution)/shard_map/ppermute | solution.py:859
  60.8 11.2 %collective-permute-start.14 = (f32[2,128,128]{2,1,0:T(8,128)S(1)}, f32[2,128,128]{2,1,0:T(8,128)S(1)}, u32[]{:S(2)}, u32[]{:S(2)}) collective-permute-start(f32[2,128,128]{2,1,0:T(8,128)S(1)} %get-tuple-element.44.refs_0_), channel_id=1, source_target_pairs={{0,24},{1,25},{2,26},{3,27},{4,28},{5,29},{6,30},{7,31},{8,0},{9,1... | collective-permute-start | bytes 393224 | tf_op jit(solution)/shard_map/ppermute | solution.py:859
  67.5 11.8 %collective-permute-start.7 = (f32[2,128,128]{2,1,0:T(8,128)S(1)}, f32[2,128,128]{2,1,0:T(8,128)S(1)}, u32[]{:S(2)}, u32[]{:S(2)}) collective-permute-start(f32[2,128,128]{2,1,0:T(8,128)S(1)} %regrid.1.refs_3_), channel_id=1, source_target_pairs={{0,24},{1,25},{2,26},{3,27},{4,28},{5,29},{6,30},{7,31}} | collective-permute-start | bytes 393224 | tf_op jit(solution)/shard_map/ppermute | solution.py:875
  70.6 10.6 %collective-permute-start.8 = (f32[2,128,128]{2,1,0:T(8,128)S(1)}, f32[2,128,128]{2,1,0:T(8,128)S(1)}, u32[]{:S(2)}, u32[]{:S(2)}) collective-permute-start(f32[2,128,128]{2,1,0:T(8,128)S(1)} %regrid.1.refs_3_), channel_id=1, source_target_pairs={{8,24},{9,25},{10,26},{11,27},{12,28},{13,29},{14,30},{15,31}} | collective-permute-start | bytes 393224 | tf_op jit(solution)/shard_map/ppermute | solution.py:875
  71.3 10.0 %collective-permute-start.9 = (f32[2,128,128]{2,1,0:T(8,128)S(1)}, f32[2,128,128]{2,1,0:T(8,128)S(1)}, u32[]{:S(2)}, u32[]{:S(2)}) collective-permute-start(f32[2,128,128]{2,1,0:T(8,128)S(1)} %regrid.1.refs_3_), channel_id=1, source_target_pairs={{16,24},{17,25},{18,26},{19,27},{20,28},{21,29},{22,30},{23,31}} | collective-permute-start | bytes 393224 | tf_op jit(solution)/shard_map/ppermute | solution.py:875
  72.8 9.3 %collective-permute-start.15 = (f32[64,128]{1,0:T(8,128)S(1)}, f32[64,128]{1,0:T(8,128)S(1)}, u32[]{:S(2)}, u32[]{:S(2)}) collective-permute-start(f32[64,128]{1,0:T(8,128)S(1)} %get-tuple-element.47), channel_id=1, source_target_pairs={{0,7},{1,0},{2,1},{3,2},{4,3},{5,4},{6,5},{7,6},{8,15},{9,8},{10,9... | collective-permute-start | bytes 98312 | tf_op jit(solution)/shard_map/ppermute | solution.py:869
  77.3 4.8 %collective-permute-start.16 = (f32[64,128]{1,0:T(8,128)S(1)}, f32[64,128]{1,0:T(8,128)S(1)}, u32[]{:S(2)}, u32[]{:S(2)}) collective-permute-start(f32[64,128]{1,0:T(8,128)S(1)} %get-tuple-element.48), channel_id=1, source_target_pairs={{0,6},{1,7},{2,0},{3,1},{4,2},{5,3},{6,4},{7,5},{8,14},{9,15},{10,... | collective-permute-start | bytes 98312 | tf_op jit(solution)/shard_map/ppermute | solution.py:869
  79.3 6.4 %collective-permute-start.17 = (f32[64,128]{1,0:T(8,128)S(1)}, f32[64,128]{1,0:T(8,128)S(1)}, u32[]{:S(2)}, u32[]{:S(2)}) collective-permute-start(f32[64,128]{1,0:T(8,128)S(1)} %get-tuple-element.49), channel_id=1, source_target_pairs={{0,5},{1,6},{2,7},{3,0},{4,1},{5,2},{6,3},{7,4},{8,13},{9,14},{10,... | collective-permute-start | bytes 98312 | tf_op jit(solution)/shard_map/ppermute | solution.py:869

commit v9 on v8

--- a/solution.py
+++ b/solution.py
@@ -884,11 +884,11 @@
     )
     moved, surface, packed, phi = moved[0], moved[1], moved[2], moved[3:]
     phi = [over_tiles(phi[n], offsets[n], ocean_comp) for n in range(neighbours)]
-    phi[1], packed = lax.optimization_barrier((phi[1], packed))
     shared, hits = project(flags, phi, regrid_weights, surface, mask)
+    slabs, shared = lax.optimization_barrier((over_comp(packed), shared))
     parts = [shared] + [shifted_comp(shared, s) for s in range(1, comp_count)]
     picks = pick(flags, parts, hits, neighbours)
-    blocks = regroup(over_comp(packed), neighbours)
+    blocks = regroup(slabs, neighbours)
     blocks = [over_tiles(blocks[n], offsets[n], comp_count) for n in range(neighbours)]
     forcing = regrid(blocks, comp_count, regrid_weights, rows)
     new_surface, picked = picks[0], picks[1:]

time: 88.5 us -> 88.4 us (level)
  starting transfers between devices: 44.1 us -> 42 us
  waiting for transfers between devices: 10.8 us -> 12.7 us
    ppermute x9, waiting for transfers between devices: 5.74 us -> 7.66 us  [over_tiles(): return lax.ppermute(value, AXES, pairs)]
    ppermute x3, starting transfers between devices: 4.45 us -> 2.64 us  [to_ocean(): return lax.ppermute(value, AXES, pairs)]
    ppermute x9, starting transfers between devices: 26.2 us -> 24.9 us  [over_tiles(): return lax.ppermute(value, AXES, pairs)]
  transfers between devices with their start and end apart: 19 -> 19, of which waited for: 5 -> 6; matrix products, arithmetic and copies ran while one was open for 2% -> 2% of each run, Pallas kernels for 8% -> 8%
where the time goes in v9:
time: 88.4 us; the launch traced here: 87.9 us
  starting transfers between devices  42 us (48%)
  Pallas kernels  30.8 us (35%)
  waiting for transfers between devices  12.7 us (14%)
  between operations  1.05 us (1%)
    ppermute x9, starting transfers between devices, over_tiles(): return lax.ppermute(value, AXES, pairs)  24.9 us
    pallas_call x1, Pallas kernels, advance(): pl.pallas_call(functools.partial(advance_kernel, comp_count, left_at, rig...  19.4 us
    ppermute x9, waiting for transfers between devices, over_tiles(): return lax.ppermute(value, AXES, pairs)  7.66 us
    ppermute x3, starting transfers between devices, band_shift(): return lax.ppermute(value, AXES, pairs)  6.35 us
    ppermute x3, waiting for transfers between devices, band_shift(): return lax.ppermute(value, AXES, pairs)  5.01 us
    ppermute x3, starting transfers between devices, shifted_comp(): return lax.ppermute(value, AXES, pairs)  4.16 us
    all_to_all x1, starting transfers between devices, over_comp(): lax.all_to_all(value, 'comp', split_axis=0, concat_axis=0, tiled=True)  4 us
    pallas_call x1, Pallas kernels, regrid(): pl.pallas_call(functools.partial(regrid_kernel, sources), out_shape=jax.S...  3.55 us
  transfers between devices with their start and end apart: 19, of which 6 were waited for; matrix products, arithmetic and copies ran while one was open for 2% of the time, Pallas kernels for 8%

profile of v9, /device:TPU:1, one launch (start us, length us, event | category | flops | bytes accessed | tf_op | source)
XLA Modules:
  0.0 87.9 jit_solution(16801409312113066713)
XLA Ops:
  0.7 1.6 %edges.1 = (bf16[2,128,128]{2,1,0:T(8,128)(2,1)S(1)}, bf16[2,128,128]{2,1,0:T(8,128)(2,1)S(1)}, f32[4,128,128]{2,1,0:T(8,128)S(1)}) custom-call(f32[128,128,128]{2,1,0:T(8,128)} %refs_4_.3), custom_call_target="tpu_custom_call" | custom-call | tf_op jit(solution)/shard_map/edges/pallas_call | solution.py:63
  2.3 4.0 %collective-permute-start = (bf16[2,128,128]{2,1,0:T(8,128)(2,1)S(1)}, bf16[2,128,128]{2,1,0:T(8,128)(2,1)S(1)}, u32[]{:S(2)}, u32[]{:S(2)}) collective-permute-start(bf16[2,128,128]{2,1,0:T(8,128)(2,1)S(1)} %get-tuple-element.27), channel_id=1, source_target_pairs={{0,2},{1,3},{2,4},{3,5},{4,6},{5,7},{6,8},{7,9},{8,10},{9,11},{10,... | collective-permute-start | bytes 196616 | tf_op jit(solution)/shard_map/ppermute | solution.py:815
  6.4 1.3 %collective-permute-start.1 = (bf16[2,128,128]{2,1,0:T(8,128)(2,1)S(1)}, bf16[2,128,128]{2,1,0:T(8,128)(2,1)S(1)}, u32[]{:S(2)}, u32[]{:S(2)}) collective-permute-start(bf16[2,128,128]{2,1,0:T(8,128)(2,1)S(1)} %get-tuple-element.28), channel_id=1, source_target_pairs={{2,0},{3,1},{4,2},{5,3},{6,4},{7,5},{8,6},{9,7},{10,8},{11,9},{12,... | collective-permute-start | bytes 196616 | tf_op jit(solution)/shard_map/ppermute | solution.py:815
  7.7 0.2 copy.19
  7.9 0.3 fusion.4
  8.1 0.2 convert_reduce_fusion
  8.3 0.2 select_reduce_fusion
  8.6 0.1 copy.20.refs_2_
  8.7 0.1 slice_reduce_fusion.refs_1_
  8.8 0.0 collective-permute-done.up_rows.refs_5_
  8.8 3.9 %collective-permute-done.1.low_rows.refs_6_ = bf16[2,128,128]{2,1,0:T(8,128)(2,1)S(1)} collective-permute-done((bf16[2,128,128]{2,1,0:T(8,128)(2,1)S(1)}, bf16[2,128,128]{2,1,0:T(8,128)(2,1)S(1)}, u32[]{:S(2)}, u32[]{:S(2)}) %collective-permute-start.1) | collective-permute-done | bytes 65568 | tf_op jit(solution)/shard_map/ppermute | solution.py:815
  12.8 1.0 %collective-permute-start.2 = (f32[4,144,128]{2,1,0:T(8,128)S(1)}, f32[4,144,128]{2,1,0:T(8,128)S(1)}, u32[]{:S(2)}, u32[]{:S(2)}) collective-permute-start(f32[4,144,128]{2,1,0:T(8,128)S(1)} %frame.1), channel_id=1, source_target_pairs={{0,1},{1,0},{2,3},{3,2},{4,5},{5,4},{6,7},{7,6},{8,9},{9,8},{10,11... | collective-permute-start | bytes 884744 | tf_op jit(solution)/shard_map/ppermute | solution.py:815
  13.8 0.1 pad_add_fusion.refs_0_.flags
  13.9 1.1 %collective-permute-done.2.refs_7_.refs_8_ = f32[4,144,128]{2,1,0:T(8,128)S(1)} collective-permute-done((f32[4,144,128]{2,1,0:T(8,128)S(1)}, f32[4,144,128]{2,1,0:T(8,128)S(1)}, u32[]{:S(2)}, u32[]{:S(2)}) %collective-permute-start.2) | collective-permute-done | bytes 294944 | tf_op jit(solution)/shard_map/ppermute | solution.py:815
  15.0 19.4 %advance.1 = (f32[128,128,128]{2,1,0:T(8,128)}, f32[128,128]{1,0:T(8,128)S(1)}, bf16[4,272,256]{2,1,0:T(8,128)(2,1)}, bf16[80,256]{1,0:T(8,128)(2,1)S(1)}, bf16[...) custom-call(s32[4]{0:T(128)S(1)} %pad_add_fusion.refs_0_.flags, ...), custom_call_target="tpu_custom_call" | custom-call | flops 2147483648 | bytes 16777216 | tf_op jit(solution)/shard_map/advance/pallas_call | solution.py:380
  34.4 4.0 %all-to-all-start = ((bf16[4,272,256]{2,1,0:T(8,128)(2,1)}), bf16[4,272,256]{2,1,0:T(8,128)(2,1)S(1)}, u32[]{:S(2)}, u32[]{:S(2)}) async-start(bf16[4,272,256]{2,1,0:T(8,128)(2,1)} %get-tuple-element.31), calls=%async_computation | async-start | bytes 1114112 | tf_op jit(solution)/shard_map/all_to_all | solution.py:851
  38.4 2.8 %collective-permute-start.3 = (bf16[80,256]{1,0:T(8,128)(2,1)S(1)}, bf16[80,256]{1,0:T(8,128)(2,1)S(1)}, u32[]{:S(2)}, u32[]{:S(2)}) collective-permute-start(bf16[80,256]{1,0:T(8,128)(2,1)S(1)} %get-tuple-element.33), channel_id=1, source_target_pairs={{0,1},{1,2},{2,3},{3,4},{4,5},{5,6},{6,7},{7,0},{8,9},{9,10},{10,1... | collective-permute-start | bytes 122888 | tf_op jit(solution)/shard_map/ppermute | solution.py:869
  41.2 3.2 %collective-permute-start.4 = (bf16[80,256]{1,0:T(8,128)(2,1)S(1)}, bf16[80,256]{1,0:T(8,128)(2,1)S(1)}, u32[]{:S(2)}, u32[]{:S(2)}) collective-permute-start(bf16[80,256]{1,0:T(8,128)(2,1)S(1)} %get-tuple-element.34), channel_id=1, source_target_pairs={{0,2},{1,3},{2,4},{3,5},{4,6},{5,7},{6,0},{7,1},{8,10},{9,11},{10,... | collective-permute-start | bytes 122888 | tf_op jit(solution)/shard_map/ppermute | solution.py:869
  44.4 5.6 %collective-permute-start.5 = (bf16[80,256]{1,0:T(8,128)(2,1)S(1)}, bf16[80,256]{1,0:T(8,128)(2,1)S(1)}, u32[]{:S(2)}, u32[]{:S(2)}) collective-permute-start(bf16[80,256]{1,0:T(8,128)(2,1)S(1)} %get-tuple-element.35), channel_id=1, source_target_pairs={{0,3},{1,4},{2,5},{3,6},{4,7},{5,0},{6,1},{7,2},{8,11},{9,12},{10,... | collective-permute-start | bytes 122888 | tf_op jit(solution)/shard_map/ppermute | solution.py:869
  50.1 0.0 collective-permute-done.3.refs_1_
  50.1 0.0 collective-permute-done.4.refs_2_
  50.1 1.5 %collective-permute-done.5.refs_3_ = bf16[80,256]{1,0:T(8,128)(2,1)S(1)} collective-permute-done((bf16[80,256]{1,0:T(8,128)(2,1)S(1)}, bf16[80,256]{1,0:T(8,128)(2,1)S(1)}, u32[]{:S(2)}, u32[]{:S(2)}) %collective-permute-start.5) | collective-permute-done | bytes 40992 | tf_op jit(solution)/shard_map/ppermute | solution.py:869
  51.6 2.1 %project.1 = (f32[2,128,128]{2,1,0:T(8,128)S(1)}, bf16[256,128]{1,0:T(8,128)(2,1)S(1)}) custom-call(s32[4]{0:T(128)S(1)} %pad_add_fusion.refs_0_.flags, bf16[80,256]{1,0:T(8,128)(2,1)S(1)} %get-tuple-element.32.refs_0_, bf16[80,256]{1,0:T(8,128)(2,1)S(1)} %collective-permute-done.3.refs_1_, bf16[80,256]{1,0:T(8,128)(2,1)S(1)} %collective-permute-done.4.refs_2_, ...), custom_call_target="tpu_custom_call" | custom-call | flops 805306368 | bytes 2097152 | tf_op jit(solution)/shard_map/project/pallas_call | solution.py:508
  53.8 0.5 collective-permute-start.6
  54.2 2.7 %collective-permute-start.7 = (bf16[208,256]{1,0:T(8,128)(2,1)S(1)}, bf16[208,256]{1,0:T(8,128)(2,1)S(1)}, u32[]{:S(2)}, u32[]{:S(2)}) collective-permute-start(bf16[208,256]{1,0:T(8,128)(2,1)S(1)} %get-tuple-element.41), channel_id=1, source_target_pairs={{0,2},{1,3},{2,4},{3,5},{4,6},{5,7},{6,0},{7,1},{8,10},{9,11},{10,... | collective-permute-start | bytes 319496 | tf_op jit(solution)/shard_map/ppermute | solution.py:869
  56.9 0.1 collective-permute-start.8
  56.9 0.1 copy.21
  57.1 2.0 %collective-permute-start.12 = (f32[2,128,128]{2,1,0:T(8,128)S(1)}, f32[2,128,128]{2,1,0:T(8,128)S(1)}, u32[]{:S(2)}, u32[]{:S(2)}) collective-permute-start(f32[2,128,128]{2,1,0:T(8,128)S(1)} %get-tuple-element.44.refs_0_), channel_id=1, source_target_pairs={{0,8},{1,9},{2,10},{3,11},{4,12},{5,13},{6,14},{7,15},{8,16},{9,17... | collective-permute-start | bytes 393224 | tf_op jit(solution)/shard_map/ppermute | solution.py:859
  59.1 0.0 collective-permute-start.13
  59.1 0.0 collective-permute-done.6.refs_1_
  59.1 2.1 %collective-permute-start.14 = (f32[2,128,128]{2,1,0:T(8,128)S(1)}, f32[2,128,128]{2,1,0:T(8,128)S(1)}, u32[]{:S(2)}, u32[]{:S(2)}) collective-permute-start(f32[2,128,128]{2,1,0:T(8,128)S(1)} %get-tuple-element.44.refs_0_), channel_id=1, source_target_pairs={{0,24},{1,25},{2,26},{3,27},{4,28},{5,29},{6,30},{7,31},{8,0},{9,1... | collective-permute-start | bytes 393224 | tf_op jit(solution)/shard_map/ppermute | solution.py:859
  61.2 0.9 collective-permute-done.7.refs_2_
  62.1 2.0 %collective-permute-done.8.refs_3_ = bf16[208,256]{1,0:T(8,128)(2,1)S(1)} collective-permute-done((bf16[208,256]{1,0:T(8,128)(2,1)S(1)}, bf16[208,256]{1,0:T(8,128)(2,1)S(1)}, u32[]{:S(2)}, u32[]{:S(2)}) %collective-permute-start.8) | collective-permute-done | bytes 106528 | tf_op jit(solution)/shard_map/ppermute | solution.py:869
  64.1 3.6 %regrid.1.refs_3_ = f32[2,128,128]{2,1,0:T(8,128)S(1)} custom-call(bf16[208,256]{1,0:T(8,128)(2,1)S(1)} %get-tuple-element.39.refs_0_, bf16[208,256]{1,0:T(8,128)(2,1)S(1)} %collective-permute-done.6.refs_1_, bf16[208,256]{1,0:T(8,128)(2,1)S(1)} %collective-permute-done.7.refs_2_, bf16[208,256]{1,0:T(8,128)(2,1)S(1)} %collective-permute-done.8.refs_3_, ...), custom_call_target="tpu_custom_call" | custom-call | flops 2147483648 | bytes 2097152 | tf_op jit(solution)/shard_map/regrid/pallas_call | solution.py:581
  67.6 0.7 collective-permute-start.10
  68.3 0.7 collective-permute-start.11
  69.0 0.0 collective-permute-done.12.refs_1_
  69.0 1.3 %collective-permute-start.9 = (f32[2,128,128]{2,1,0:T(8,128)S(1)}, f32[2,128,128]{2,1,0:T(8,128)S(1)}, u32[]{:S(2)}, u32[]{:S(2)}) collective-permute-start(f32[2,128,128]{2,1,0:T(8,128)S(1)} %regrid.1.refs_3_), channel_id=1, source_target_pairs={{0,24},{1,25},{2,26},{3,27},{4,28},{5,29},{6,30},{7,31}} | collective-permute-start | bytes 393224 | tf_op jit(solution)/shard_map/ppermute | solution.py:875
  70.3 0.1 add_select_fusion.refs_4_
  70.4 0.0 collective-permute-done.13.refs_2_
  70.4 0.0 collective-permute-done.14.refs_3_
  70.4 0.8 pick.1
  71.2 4.3 %collective-permute-start.15 = (f32[64,128]{1,0:T(8,128)S(1)}, f32[64,128]{1,0:T(8,128)S(1)}, u32[]{:S(2)}, u32[]{:S(2)}) collective-permute-start(f32[64,128]{1,0:T(8,128)S(1)} %get-tuple-element.47), channel_id=1, source_target_pairs={{0,7},{1,0},{2,1},{3,2},{4,3},{5,4},{6,5},{7,6},{8,15},{9,8},{10,9... | collective-permute-start | bytes 98312 | tf_op jit(solution)/shard_map/ppermute | solution.py:869
  75.4 3.9 %collective-permute-start.16 = (f32[64,128]{1,0:T(8,128)S(1)}, f32[64,128]{1,0:T(8,128)S(1)}, u32[]{:S(2)}, u32[]{:S(2)}) collective-permute-start(f32[64,128]{1,0:T(8,128)S(1)} %get-tuple-element.48), channel_id=1, source_target_pairs={{0,6},{1,7},{2,0},{3,1},{4,2},{5,3},{6,4},{7,5},{8,14},{9,15},{10,... | collective-permute-start | bytes 98312 | tf_op jit(solution)/shard_map/ppermute | solution.py:869
  79.4 1.9 %collective-permute-start.17 = (f32[64,128]{1,0:T(8,128)S(1)}, f32[64,128]{1,0:T(8,128)S(1)}, u32[]{:S(2)}, u32[]{:S(2)}) collective-permute-start(f32[64,128]{1,0:T(8,128)S(1)} %get-tuple-element.49), channel_id=1, source_target_pairs={{0,5},{1,6},{2,7},{3,0},{4,1},{5,2},{6,3},{7,4},{8,13},{9,14},{10,... | collective-permute-start | bytes 98312 | tf_op jit(solution)/shard_map/ppermute | solution.py:869
  81.3 0.8 update.1
  82.2 3.3 %collective-permute-done.17.refs_3_ = f32[64,128]{1,0:T(8,128)S(1)} collective-permute-done((f32[64,128]{1,0:T(8,128)S(1)}, f32[64,128]{1,0:T(8,128)S(1)}, u32[]{:S(2)}, u32[]{:S(2)}) %collective-permute-start.17) | collective-permute-done | bytes 32800 | tf_op jit(solution)/shard_map/ppermute | solution.py:869
  85.5 2.4 %returned.1 = f32[128,128]{1,0:T(8,128)} custom-call(s32[4]{0:T(128)S(1)} %pad_add_fusion.refs_0_.flags, f32[64,128]{1,0:T(8,128)S(1)} %get-tuple-element.46.refs_0_, f32[64,128]{1,0:T(8,128)S(1)} %collective-permute-done.15.refs_1_, f32[64,128]{1,0:T(8,128)S(1)} %collective-permute-done.16.refs_2_, f32[64,128]{1,0:T(8,128)S(1)} %collective-permute-done.17.refs_3_, ...), custom_call_target="tpu_custom_call" | custom-call | tf_op jit(solution)/shard_map/returned/pallas_call | solution.py:769
  (28 shorter events, 0.2 us)
Async XLA Ops:
  0.6 7.0 %copy-start.6 = (s32[128,1,2,3]{0,2,3,1:T(2,128)S(1)}, s32[128,1,2,3]{0,2,3,1:T(2,128)}, u32[]{:S(2)}) copy-start(s32[128,1,2,3]{0,2,3,1:T(2,128)} %param.11) | copy-start | bytes 9220
  0.6 8.1 %copy-start.3 = (f32[8,128]{1,0:T(8,128)S(1)}, f32[8,128]{1,0:T(8,128)}, u32[]{:S(2)}) copy-start(f32[8,128]{1,0:T(8,128)} %refs_5_.1) | copy-start | bytes 12292
  0.7 13.2 %copy-start.5 = (s32[128,128]{1,0:T(8,128)S(1)}, s32[128,128]{1,0:T(8,128)}, u32[]{:S(2)}) copy-start(s32[128,128]{1,0:T(8,128)} %param.10) | copy-start | bytes 196612
  0.7 14.3 %copy-start.4 = (f32[128,8]{0,1:T(8,128)S(1)}, f32[128,8]{0,1:T(8,128)}, u32[]{:S(2)}) copy-start(f32[128,8]{0,1:T(8,128)} %param.14) | copy-start | bytes 12292
  0.7 14.3 %copy-start.1 = (f32[128,128]{1,0:T(8,128)S(1)}, f32[128,128]{1,0:T(8,128)}, u32[]{:S(2)}) copy-start(f32[128,128]{1,0:T(8,128)} %refs_11_.1) | copy-start | bytes 196612
  0.7 14.3 %copy-start.2 = (f32[128,128]{1,0:T(8,128)S(1)}, f32[128,128]{1,0:T(8,128)}, u32[]{:S(2)}) copy-start(f32[128,128]{1,0:T(8,128)} %refs_12_.1) | copy-start | bytes 196612
  0.7 50.9 %copy-start = (bf16[32,128,128]{2,1,0:T(8,128)(2,1)S(1)}, bf16[32,128,128]{2,1,0:T(8,128)(2,1)}, u32[]{:S(2)}) copy-start(bf16[32,128,128]{2,1,0:T(8,128)(2,1)} %refs_6_.1) | copy-start | bytes 3145732
  2.3 6.5 %collective-permute-start = (bf16[2,128,128]{2,1,0:T(8,128)(2,1)S(1)}, bf16[2,128,128]{2,1,0:T(8,128)(2,1)S(1)}, u32[]{:S(2)}, u32[]{:S(2)}) collective-permute-start(bf16[2,128,128]{2,1,0:T(8,128)(2,1)S(1)} %get-tuple-element.27), channel_id=1, source_target_pairs={{0,2},{1,3},{2,4},{3,5},{4,6},{5,7},{6,8},{7,9},{8,10},{9,11},{10,... | collective-permute-start | bytes 196616 | tf_op jit(solution)/shard_map/ppermute | solution.py:815
  6.4 6.4 %collective-permute-start.1 = (bf16[2,128,128]{2,1,0:T(8,128)(2,1)S(1)}, bf16[2,128,128]{2,1,0:T(8,128)(2,1)S(1)}, u32[]{:S(2)}, u32[]{:S(2)}) collective-permute-start(bf16[2,128,128]{2,1,0:T(8,128)(2,1)S(1)} %get-tuple-element.28), channel_id=1, source_target_pairs={{2,0},{3,1},{4,2},{5,3},{6,4},{7,5},{8,6},{9,7},{10,8},{11,9},{12,... | collective-permute-start | bytes 196616 | tf_op jit(solution)/shard_map/ppermute | solution.py:815
  12.8 2.2 %collective-permute-start.2 = (f32[4,144,128]{2,1,0:T(8,128)S(1)}, f32[4,144,128]{2,1,0:T(8,128)S(1)}, u32[]{:S(2)}, u32[]{:S(2)}) collective-permute-start(f32[4,144,128]{2,1,0:T(8,128)S(1)} %frame.1), channel_id=1, source_target_pairs={{0,1},{1,0},{2,3},{3,2},{4,5},{5,4},{6,7},{7,6},{8,9},{9,8},{10,11... | collective-permute-start | bytes 884744 | tf_op jit(solution)/shard_map/ppermute | solution.py:815
  34.4 19.3 %all-to-all-start = ((bf16[4,272,256]{2,1,0:T(8,128)(2,1)}), bf16[4,272,256]{2,1,0:T(8,128)(2,1)S(1)}, u32[]{:S(2)}, u32[]{:S(2)}) async-start(bf16[4,272,256]{2,1,0:T(8,128)(2,1)} %get-tuple-element.31), calls=%async_computation | async-start | bytes 1114112 | tf_op jit(solution)/shard_map/all_to_all | solution.py:851
  38.4 11.6 %collective-permute-start.3 = (bf16[80,256]{1,0:T(8,128)(2,1)S(1)}, bf16[80,256]{1,0:T(8,128)(2,1)S(1)}, u32[]{:S(2)}, u32[]{:S(2)}) collective-permute-start(bf16[80,256]{1,0:T(8,128)(2,1)S(1)} %get-tuple-element.33), channel_id=1, source_target_pairs={{0,1},{1,2},{2,3},{3,4},{4,5},{5,6},{6,7},{7,0},{8,9},{9,10},{10,1... | collective-permute-start | bytes 122888 | tf_op jit(solution)/shard_map/ppermute | solution.py:869
  41.2 8.9 %collective-permute-start.4 = (bf16[80,256]{1,0:T(8,128)(2,1)S(1)}, bf16[80,256]{1,0:T(8,128)(2,1)S(1)}, u32[]{:S(2)}, u32[]{:S(2)}) collective-permute-start(bf16[80,256]{1,0:T(8,128)(2,1)S(1)} %get-tuple-element.34), channel_id=1, source_target_pairs={{0,2},{1,3},{2,4},{3,5},{4,6},{5,7},{6,0},{7,1},{8,10},{9,11},{10,... | collective-permute-start | bytes 122888 | tf_op jit(solution)/shard_map/ppermute | solution.py:869
  44.4 7.2 %collective-permute-start.5 = (bf16[80,256]{1,0:T(8,128)(2,1)S(1)}, bf16[80,256]{1,0:T(8,128)(2,1)S(1)}, u32[]{:S(2)}, u32[]{:S(2)}) collective-permute-start(bf16[80,256]{1,0:T(8,128)(2,1)S(1)} %get-tuple-element.35), channel_id=1, source_target_pairs={{0,3},{1,4},{2,5},{3,6},{4,7},{5,0},{6,1},{7,2},{8,11},{9,12},{10,... | collective-permute-start | bytes 122888 | tf_op jit(solution)/shard_map/ppermute | solution.py:869
  53.8 5.4 %collective-permute-start.6 = (bf16[208,256]{1,0:T(8,128)(2,1)S(1)}, bf16[208,256]{1,0:T(8,128)(2,1)S(1)}, u32[]{:S(2)}, u32[]{:S(2)}) collective-permute-start(bf16[208,256]{1,0:T(8,128)(2,1)S(1)} %get-tuple-element.40), channel_id=1, source_target_pairs={{0,1},{1,2},{2,3},{3,4},{4,5},{5,6},{6,7},{7,0},{8,9},{9,10},{10,1... | collective-permute-start | bytes 319496 | tf_op jit(solution)/shard_map/ppermute | solution.py:869
  54.2 7.9 %collective-permute-start.7 = (bf16[208,256]{1,0:T(8,128)(2,1)S(1)}, bf16[208,256]{1,0:T(8,128)(2,1)S(1)}, u32[]{:S(2)}, u32[]{:S(2)}) collective-permute-start(bf16[208,256]{1,0:T(8,128)(2,1)S(1)} %get-tuple-element.41), channel_id=1, source_target_pairs={{0,2},{1,3},{2,4},{3,5},{4,6},{5,7},{6,0},{7,1},{8,10},{9,11},{10,... | collective-permute-start | bytes 319496 | tf_op jit(solution)/shard_map/ppermute | solution.py:869
  56.9 7.2 %collective-permute-start.8 = (bf16[208,256]{1,0:T(8,128)(2,1)S(1)}, bf16[208,256]{1,0:T(8,128)(2,1)S(1)}, u32[]{:S(2)}, u32[]{:S(2)}) collective-permute-start(bf16[208,256]{1,0:T(8,128)(2,1)S(1)} %get-tuple-element.42), channel_id=1, source_target_pairs={{0,3},{1,4},{2,5},{3,6},{4,7},{5,0},{6,1},{7,2},{8,11},{9,12},{10,... | collective-permute-start | bytes 319496 | tf_op jit(solution)/shard_map/ppermute | solution.py:869
  57.1 11.9 %collective-permute-start.12 = (f32[2,128,128]{2,1,0:T(8,128)S(1)}, f32[2,128,128]{2,1,0:T(8,128)S(1)}, u32[]{:S(2)}, u32[]{:S(2)}) collective-permute-start(f32[2,128,128]{2,1,0:T(8,128)S(1)} %get-tuple-element.44.refs_0_), channel_id=1, source_target_pairs={{0,8},{1,9},{2,10},{3,11},{4,12},{5,13},{6,14},{7,15},{8,16},{9,17... | collective-permute-start | bytes 393224 | tf_op jit(solution)/shard_map/ppermute | solution.py:859
  59.1 11.3 %collective-permute-start.13 = (f32[2,128,128]{2,1,0:T(8,128)S(1)}, f32[2,128,128]{2,1,0:T(8,128)S(1)}, u32[]{:S(2)}, u32[]{:S(2)}) collective-permute-start(f32[2,128,128]{2,1,0:T(8,128)S(1)} %get-tuple-element.44.refs_0_), channel_id=1, source_target_pairs={{0,16},{1,17},{2,18},{3,19},{4,20},{5,21},{6,22},{7,23},{8,24},{9,... | collective-permute-start | bytes 393224 | tf_op jit(solution)/shard_map/ppermute | solution.py:859
  59.1 11.3 %collective-permute-start.14 = (f32[2,128,128]{2,1,0:T(8,128)S(1)}, f32[2,128,128]{2,1,0:T(8,128)S(1)}, u32[]{:S(2)}, u32[]{:S(2)}) collective-permute-start(f32[2,128,128]{2,1,0:T(8,128)S(1)} %get-tuple-element.44.refs_0_), channel_id=1, source_target_pairs={{0,24},{1,25},{2,26},{3,27},{4,28},{5,29},{6,30},{7,31},{8,0},{9,1... | collective-permute-start | bytes 393224 | tf_op jit(solution)/shard_map/ppermute | solution.py:859
  67.6 11.7 %collective-permute-start.10 = (f32[2,128,128]{2,1,0:T(8,128)S(1)}, f32[2,128,128]{2,1,0:T(8,128)S(1)}, u32[]{:S(2)}, u32[]{:S(2)}) collective-permute-start(f32[2,128,128]{2,1,0:T(8,128)S(1)} %regrid.1.refs_3_), channel_id=1, source_target_pairs={{8,24},{9,25},{10,26},{11,27},{12,28},{13,29},{14,30},{15,31}} | collective-permute-start | bytes 393224 | tf_op jit(solution)/shard_map/ppermute | solution.py:875
  68.3 13.0 %collective-permute-start.11 = (f32[2,128,128]{2,1,0:T(8,128)S(1)}, f32[2,128,128]{2,1,0:T(8,128)S(1)}, u32[]{:S(2)}, u32[]{:S(2)}) collective-permute-start(f32[2,128,128]{2,1,0:T(8,128)S(1)} %regrid.1.refs_3_), channel_id=1, source_target_pairs={{16,24},{17,25},{18,26},{19,27},{20,28},{21,29},{22,30},{23,31}} | collective-permute-start | bytes 393224 | tf_op jit(solution)/shard_map/ppermute | solution.py:875
  69.0 12.3 %collective-permute-start.9 = (f32[2,128,128]{2,1,0:T(8,128)S(1)}, f32[2,128,128]{2,1,0:T(8,128)S(1)}, u32[]{:S(2)}, u32[]{:S(2)}) collective-permute-start(f32[2,128,128]{2,1,0:T(8,128)S(1)} %regrid.1.refs_3_), channel_id=1, source_target_pairs={{0,24},{1,25},{2,26},{3,27},{4,28},{5,29},{6,30},{7,31}} | collective-permute-start | bytes 393224 | tf_op jit(solution)/shard_map/ppermute | solution.py:875
  71.2 11.0 %collective-permute-start.15 = (f32[64,128]{1,0:T(8,128)S(1)}, f32[64,128]{1,0:T(8,128)S(1)}, u32[]{:S(2)}, u32[]{:S(2)}) collective-permute-start(f32[64,128]{1,0:T(8,128)S(1)} %get-tuple-element.47), channel_id=1, source_target_pairs={{0,7},{1,0},{2,1},{3,2},{4,3},{5,4},{6,5},{7,6},{8,15},{9,8},{10,9... | collective-permute-start | bytes 98312 | tf_op jit(solution)/shard_map/ppermute | solution.py:869
  75.4 6.7 %collective-permute-start.16 = (f32[64,128]{1,0:T(8,128)S(1)}, f32[64,128]{1,0:T(8,128)S(1)}, u32[]{:S(2)}, u32[]{:S(2)}) collective-permute-start(f32[64,128]{1,0:T(8,128)S(1)} %get-tuple-element.48), channel_id=1, source_target_pairs={{0,6},{1,7},{2,0},{3,1},{4,2},{5,3},{6,4},{7,5},{8,14},{9,15},{10,... | collective-permute-start | bytes 98312 | tf_op jit(solution)/shard_map/ppermute | solution.py:869
  79.4 6.1 %collective-permute-start.17 = (f32[64,128]{1,0:T(8,128)S(1)}, f32[64,128]{1,0:T(8,128)S(1)}, u32[]{:S(2)}, u32[]{:S(2)}) collective-permute-start(f32[64,128]{1,0:T(8,128)S(1)} %get-tuple-element.49), channel_id=1, source_target_pairs={{0,5},{1,6},{2,7},{3,0},{4,1},{5,2},{6,3},{7,4},{8,13},{9,14},{10,... | collective-permute-start | bytes 98312 | tf_op jit(solution)/shard_map/ppermute | solution.py:869

commit v10 on v7

--- a/solution.py
+++ b/solution.py
@@ -108,7 +108,7 @@
     out, surface, sea_copy = refs[13:16]
     packed = refs[16]
     (values, moved, halo_moved, smooth, pairs, mixed, later_smooth, later_pairs, later_mixed) = refs[17:26]
-    (weights, flux_weights, fluxes, staged, top, in_sems, out_sems) = refs[26:]
+    (weights, flux_weights, flux_pairs, fluxes, staged, top, in_sems, out_sems) = refs[26:]
     left_cols = left_in.at[left_at : left_at + 2]
     right_cols = right_in.at[right_at : right_at + 2]
     first = (smooth, pairs, mixed)
@@ -246,10 +246,12 @@
                 line = finish(second, row)
                 staged[slot, row] = line
                 both = line + moved[q * CHUNK + row + 1, EDGE : EDGE + cols, :]
-                later_pairs[row * cols : (row + 1) * cols, :] = side_by_side(both)
+                flux_pairs[row * cols : (row + 1) * cols, :] = side_by_side(both)
             put(q, slot).start()
             note_top(q, [staged[slot, row] for row in range(CHUNK)])
-            flux = dot_nt(flux_weights[...], later_pairs[...])
+
+        def sum_fluxes(q):
+            flux = dot_nt(flux_weights[...], flux_pairs[...])
             flux = flux[:flux_count] + flux[flux_count:]
             for row in range(CHUNK):
                 r = q * CHUNK + row
@@ -259,6 +261,7 @@
                 fluxes[pl.ds(pl.multiple_of(r * flux_count, flux_count), flux_count), :] = block
 
         fetch(AHEAD).start()
+        flux_pairs[...] = jnp.zeros(flux_pairs.shape, BF16)
         begin_first(0)
         end_first(0)
 
@@ -277,10 +280,11 @@
             def _():
                 put(q - 3, slot).wait()
 
+            sum_fluxes(jnp.maximum(q - 2, 0))
             begin_first(q)
             begin_second(q - 1)
+            mix_rows(second, CHUNK)
             end_first(q)
-            mix_rows(second, CHUNK)
             end_second(q - 1, slot)
             return 0
 
@@ -292,9 +296,11 @@
 
         last = chunks - 1
         put(last - 2, last % 2).wait()
+        sum_fluxes(last - 1)
         begin_second(last)
         mix_rows(second, CHUNK)
         end_second(last, last % 2)
+        sum_fluxes(last)
         spots = lax.broadcasted_iota(jnp.int32, (source_column.shape[0], rows), 1)
         placing = jnp.where(source_column[...] == spots, 1.0, 0.0).astype(BF16)
         share = flux_count // comp_count
@@ -386,6 +392,7 @@
             pltpu.VMEM((CHUNK * cols, 2 * levels), F32),
             pltpu.VMEM((2 * levels, 2 * levels), BF16),
             pltpu.VMEM((2 * fluxes, 2 * levels), BF16),
+            pltpu.VMEM((CHUNK * cols, 2 * levels), BF16),
             pltpu.VMEM((rows * fluxes, cols), F32),
             pltpu.VMEM((2, CHUNK, cols, levels), F32),
             pltpu.VMEM((cols, levels), F32),

time: 88.4 us -> 86.3 us (0.976)
  Pallas kernels: 28.6 us -> 26.5 us
    pallas_call x1, Pallas kernels: 19.4 us -> 17.3 us  [advance(): pl.pallas_call(functools.partial(advance_kernel, comp_count, left_at, rig...]
where the time goes in v10:
time: 86.3 us; the launch traced here: 85.9 us
  starting transfers between devices  35.2 us (41%)
  Pallas kernels  26.5 us (31%)
  waiting for transfers between devices  21.8 us (25%)
  between operations  1.02 us (1%)
    pallas_call x1, Pallas kernels, advance(): pl.pallas_call(functools.partial(advance_kernel, comp_count, left_at, rig...  17.3 us
    ppermute x6, starting transfers between devices, over_tiles(): return lax.ppermute(value, AXES, pairs)  15.8 us
    ppermute x6, waiting for transfers between devices, over_tiles(): return lax.ppermute(value, AXES, pairs)  8.5 us
    all_to_all x1, waiting for transfers between devices, over_comp(): lax.all_to_all(value, 'comp', split_axis=0, concat_axis=0, tiled=True)  7.07 us
    ppermute x3, starting transfers between devices, band_shift(): return lax.ppermute(value, AXES, pairs)  6.48 us
    ppermute x3, waiting for transfers between devices, band_shift(): return lax.ppermute(value, AXES, pairs)  5.13 us
    pallas_call x1, Pallas kernels, regrid(): pl.pallas_call(functools.partial(regrid_body, count, comp_count), out_sha...  4.1 us
    all_to_all x1, starting transfers between devices, over_comp(): lax.all_to_all(value, 'comp', split_axis=0, concat_axis=0, tiled=True)  4 us
  transfers between devices with their start and end apart: 19, of which 7 were waited for; matrix products, arithmetic and copies ran while one was open for 2% of the time, Pallas kernels for 1%

profile of v10, /device:TPU:1, one launch (start us, length us, event | category | flops | bytes accessed | tf_op | source)
XLA Modules:
  0.0 85.9 jit_solution(958120807400664011)
XLA Ops:
  0.7 1.6 %edges.1 = (bf16[2,128,128]{2,1,0:T(8,128)(2,1)S(1)}, bf16[2,128,128]{2,1,0:T(8,128)(2,1)S(1)}, f32[4,128,128]{2,1,0:T(8,128)S(1)}) custom-call(f32[128,128,128]{2,1,0:T(8,128)} %refs_3_.1), custom_call_target="tpu_custom_call" | custom-call | tf_op jit(solution)/shard_map/edges/pallas_call | solution.py:63
  2.3 0.0 copy-start.3
  2.3 0.0 copy-start
  2.3 4.2 %collective-permute-start = (bf16[2,128,128]{2,1,0:T(8,128)(2,1)S(1)}, bf16[2,128,128]{2,1,0:T(8,128)(2,1)S(1)}, u32[]{:S(2)}, u32[]{:S(2)}) collective-permute-start(bf16[2,128,128]{2,1,0:T(8,128)(2,1)S(1)} %get-tuple-element.25), channel_id=1, source_target_pairs={{0,2},{1,3},{2,4},{3,5},{4,6},{5,7},{6,8},{7,9},{8,10},{9,11},{10,... | collective-permute-start | bytes 196616 | tf_op jit(solution)/shard_map/ppermute | solution.py:758
  6.5 1.3 %collective-permute-start.1 = (bf16[2,128,128]{2,1,0:T(8,128)(2,1)S(1)}, bf16[2,128,128]{2,1,0:T(8,128)(2,1)S(1)}, u32[]{:S(2)}, u32[]{:S(2)}) collective-permute-start(bf16[2,128,128]{2,1,0:T(8,128)(2,1)S(1)} %get-tuple-element.26), channel_id=1, source_target_pairs={{2,0},{3,1},{4,2},{5,3},{6,4},{7,5},{8,6},{9,7},{10,8},{11,9},{12,... | collective-permute-start | bytes 196616 | tf_op jit(solution)/shard_map/ppermute | solution.py:758
  7.8 0.2 copy.19
  8.0 0.3 fusion.4
  8.2 0.2 convert_reduce_fusion
  8.4 0.2 select_reduce_fusion
  8.7 0.1 copy.20.refs_1_
  8.8 0.0 collective-permute-done.up_rows.refs_4_
  8.8 4.0 %collective-permute-done.1.low_rows.refs_5_ = bf16[2,128,128]{2,1,0:T(8,128)(2,1)S(1)} collective-permute-done((bf16[2,128,128]{2,1,0:T(8,128)(2,1)S(1)}, bf16[2,128,128]{2,1,0:T(8,128)(2,1)S(1)}, u32[]{:S(2)}, u32[]{:S(2)}) %collective-permute-start.1) | collective-permute-done | bytes 65568 | tf_op jit(solution)/shard_map/ppermute | solution.py:758
  12.9 1.0 %collective-permute-start.2 = (f32[4,144,128]{2,1,0:T(8,128)S(1)}, f32[4,144,128]{2,1,0:T(8,128)S(1)}, u32[]{:S(2)}, u32[]{:S(2)}) collective-permute-start(f32[4,144,128]{2,1,0:T(8,128)S(1)} %frame.1), channel_id=1, source_target_pairs={{0,1},{1,0},{2,3},{3,2},{4,5},{5,4},{6,7},{7,6},{8,9},{9,8},{10,11... | collective-permute-start | bytes 884744 | tf_op jit(solution)/shard_map/ppermute | solution.py:758
  13.9 0.1 pad_add_fusion.refs_0_.flags
  14.0 1.1 %collective-permute-done.2.refs_6_.refs_7_ = f32[4,144,128]{2,1,0:T(8,128)S(1)} collective-permute-done((f32[4,144,128]{2,1,0:T(8,128)S(1)}, f32[4,144,128]{2,1,0:T(8,128)S(1)}, u32[]{:S(2)}, u32[]{:S(2)}) %collective-permute-start.2) | collective-permute-done | bytes 294944 | tf_op jit(solution)/shard_map/ppermute | solution.py:758
  15.1 17.3 %advance.1 = (f32[128,128,128]{2,1,0:T(8,128)}, f32[128,128]{1,0:T(8,128)S(1)}, bf16[128,128]{1,0:T(8,128)(2,1)S(1)}, bf16[4,272,256]{2,1,0:T(8,128)(2,1)}) custom-call(s32[4]{0:T(128)S(1)} %pad_add_fusion.refs_0_.flags, s32[256,1]{1,0:T(8,128)S(1)} %copy.20.refs_1_, bf16[16,256]{1,0:T(8,128)(2,1)S(1)} %fusion.9.refs_2_, f32[128,128,128]{2,1,0:T(8,128)} %refs_3_.1, ...), custom_call_target="tpu_custom_call" | custom-call | flops 2147483648 | bytes 16777216 | tf_op jit(solution)/shard_map/advance/pallas_call | solution.py:373
  32.4 4.0 %all-to-all-start = ((bf16[4,272,256]{2,1,0:T(8,128)(2,1)}), bf16[4,272,256]{2,1,0:T(8,128)(2,1)S(1)}, u32[]{:S(2)}, u32[]{:S(2)}) async-start(bf16[4,272,256]{2,1,0:T(8,128)(2,1)} %get-tuple-element.29), calls=%async_computation | async-start | bytes 1114112 | tf_op jit(solution)/shard_map/all_to_all | solution.py:794
  36.4 1.3 %collective-permute-start.6 = (bf16[128,128]{1,0:T(8,128)(2,1)S(1)}, bf16[128,128]{1,0:T(8,128)(2,1)S(1)}, u32[]{:S(2)}, u32[]{:S(2)}) collective-permute-start(bf16[128,128]{1,0:T(8,128)(2,1)S(1)} %get-tuple-element.34.refs_7_), channel_id=1, source_target_pairs={{24,0},{25,1},{26,2},{27,3},{28,4},{29,5},{30,6},{31,7}} | collective-permute-start | bytes 98312 | tf_op jit(solution)/shard_map/ppermute | solution.py:818
  37.7 0.7 collective-permute-start.7
  38.4 0.7 collective-permute-start.8
  39.1 7.1 %all-to-all-done.slabs = bf16[4,272,256]{2,1,0:T(8,128)(2,1)S(1)} async-done(((bf16[4,272,256]{2,1,0:T(8,128)(2,1)}), bf16[4,272,256]{2,1,0:T(8,128)(2,1)S(1)}, u32[]{:S(2)}, u32[]{:S(2)}) %all-to-all-start) | async-done | bytes 557088 | tf_op jit(solution)/shard_map/all_to_all | solution.py:794
  46.2 0.1 collective-permute-start.3
  46.3 1.3 %collective-permute-start.4 = (bf16[208,256]{1,0:T(8,128)(2,1)S(1)}, bf16[208,256]{1,0:T(8,128)(2,1)S(1)}, u32[]{:S(2)}, u32[]{:S(2)}) collective-permute-start(bf16[208,256]{1,0:T(8,128)(2,1)S(1)} %get-tuple-element.32), channel_id=1, source_target_pairs={{0,2},{1,3},{2,4},{3,5},{4,6},{5,7},{6,0},{7,1},{8,10},{9,11},{10,... | collective-permute-start | bytes 319496 | tf_op jit(solution)/shard_map/ppermute | solution.py:812
  47.6 0.0 collective-permute-done.6.refs_4_
  47.6 4.3 %collective-permute-start.5 = (bf16[208,256]{1,0:T(8,128)(2,1)S(1)}, bf16[208,256]{1,0:T(8,128)(2,1)S(1)}, u32[]{:S(2)}, u32[]{:S(2)}) collective-permute-start(bf16[208,256]{1,0:T(8,128)(2,1)S(1)} %get-tuple-element.33), channel_id=1, source_target_pairs={{0,3},{1,4},{2,5},{3,6},{4,7},{5,0},{6,1},{7,2},{8,11},{9,12},{10,... | collective-permute-start | bytes 319496 | tf_op jit(solution)/shard_map/ppermute | solution.py:812
  51.9 0.1 slice_reduce_fusion.ocean_first
  52.0 0.0 collective-permute-done.7.refs_5_
  52.0 0.0 collective-permute-done.8.refs_6_
  52.0 3.1 %collective-permute-done.4.refs_2_ = bf16[208,256]{1,0:T(8,128)(2,1)S(1)} collective-permute-done((bf16[208,256]{1,0:T(8,128)(2,1)S(1)}, bf16[208,256]{1,0:T(8,128)(2,1)S(1)}, u32[]{:S(2)}, u32[]{:S(2)}) %collective-permute-start.4) | collective-permute-done | bytes 106528 | tf_op jit(solution)/shard_map/ppermute | solution.py:812
  55.1 2.1 %collective-permute-done.5.refs_3_ = bf16[208,256]{1,0:T(8,128)(2,1)S(1)} collective-permute-done((bf16[208,256]{1,0:T(8,128)(2,1)S(1)}, bf16[208,256]{1,0:T(8,128)(2,1)S(1)}, u32[]{:S(2)}, u32[]{:S(2)}) %collective-permute-start.5) | collective-permute-done | bytes 106528 | tf_op jit(solution)/shard_map/ppermute | solution.py:812
  57.2 4.1 %regrid.1 = (f32[2,128,128]{2,1,0:T(8,128)S(1)}, f32[128,128]{1,0:T(8,128)S(1)}, bf16[256,128]{1,0:T(8,128)(2,1)S(1)}) custom-call(s32[4]{0:T(128)S(1)} %pad_add_fusion.refs_0_.flags, f32[8]{0:T(128)S(1)} %slice_reduce_fusion.ocean_first, bf16[208,256]{1,0:T(8,128)(2,1)S(1)} %get-tuple-element.30.refs_0_, ...), custom_call_target="tpu_custom_call" | custom-call | flops 2147483648 | bytes 2097152 | tf_op jit(solution)/shard_map/regrid/pallas_call | solution.py:527
  61.3 0.6 collective-permute-start.9
  61.9 0.1 copy.21
  62.0 1.0 %collective-permute-start.13 = (f32[128,128]{1,0:T(8,128)S(1)}, f32[128,128]{1,0:T(8,128)S(1)}, u32[]{:S(2)}, u32[]{:S(2)}) collective-permute-start(f32[128,128]{1,0:T(8,128)S(1)} %get-tuple-element.36.refs_0_), channel_id=1, source_target_pairs={{0,16},{1,17},{2,18},{3,19},{4,20},{5,21},{6,22},{7,23},{8,24},{9,... | collective-permute-start | bytes 196616 | tf_op jit(solution)/shard_map/ppermute | solution.py:802
  63.0 1.4 %collective-permute-start.14 = (f32[128,128]{1,0:T(8,128)S(1)}, f32[128,128]{1,0:T(8,128)S(1)}, u32[]{:S(2)}, u32[]{:S(2)}) collective-permute-start(f32[128,128]{1,0:T(8,128)S(1)} %get-tuple-element.36.refs_0_), channel_id=1, source_target_pairs={{0,24},{1,25},{2,26},{3,27},{4,28},{5,29},{6,30},{7,31},{8,0},{9,1... | collective-permute-start | bytes 196616 | tf_op jit(solution)/shard_map/ppermute | solution.py:802
  64.4 1.1 %collective-permute-done.9.refs_1_ = f32[128,128]{1,0:T(8,128)S(1)} collective-permute-done((f32[128,128]{1,0:T(8,128)S(1)}, f32[128,128]{1,0:T(8,128)S(1)}, u32[]{:S(2)}, u32[]{:S(2)}) %collective-permute-start.9) | collective-permute-done | bytes 65568 | tf_op jit(solution)/shard_map/ppermute | solution.py:802
  65.5 2.0 %collective-permute-start.10 = (f32[2,128,128]{2,1,0:T(8,128)S(1)}, f32[2,128,128]{2,1,0:T(8,128)S(1)}, u32[]{:S(2)}, u32[]{:S(2)}) collective-permute-start(f32[2,128,128]{2,1,0:T(8,128)S(1)} %get-tuple-element.38.refs_3_), channel_id=1, source_target_pairs={{0,24},{1,25},{2,26},{3,27},{4,28},{5,29},{6,30},{7,31}} | collective-permute-start | bytes 393224 | tf_op jit(solution)/shard_map/ppermute | solution.py:824
  67.5 0.7 collective-permute-start.11
  68.2 0.7 collective-permute-start.12
  68.9 0.1 add_select_fusion.refs_4_
  69.0 0.0 collective-permute-done.14.refs_3_
  69.0 0.2 pick.1
  69.2 5.4 %collective-permute-start.15 = (f32[64,128]{1,0:T(8,128)S(1)}, f32[64,128]{1,0:T(8,128)S(1)}, u32[]{:S(2)}, u32[]{:S(2)}) collective-permute-start(f32[64,128]{1,0:T(8,128)S(1)} %get-tuple-element.43), channel_id=1, source_target_pairs={{0,7},{1,0},{2,1},{3,2},{4,3},{5,4},{6,5},{7,6},{8,15},{9,8},{10,9... | collective-permute-start | bytes 98312 | tf_op jit(solution)/shard_map/ppermute | solution.py:812
  74.6 2.7 %collective-permute-start.16 = (f32[64,128]{1,0:T(8,128)S(1)}, f32[64,128]{1,0:T(8,128)S(1)}, u32[]{:S(2)}, u32[]{:S(2)}) collective-permute-start(f32[64,128]{1,0:T(8,128)S(1)} %get-tuple-element.44), channel_id=1, source_target_pairs={{0,6},{1,7},{2,0},{3,1},{4,2},{5,3},{6,4},{7,5},{8,14},{9,15},{10,... | collective-permute-start | bytes 98312 | tf_op jit(solution)/shard_map/ppermute | solution.py:812
  77.3 1.9 %collective-permute-start.17 = (f32[64,128]{1,0:T(8,128)S(1)}, f32[64,128]{1,0:T(8,128)S(1)}, u32[]{:S(2)}, u32[]{:S(2)}) collective-permute-start(f32[64,128]{1,0:T(8,128)S(1)} %get-tuple-element.45), channel_id=1, source_target_pairs={{0,5},{1,6},{2,7},{3,0},{4,1},{5,2},{6,3},{7,4},{8,13},{9,14},{10,... | collective-permute-start | bytes 98312 | tf_op jit(solution)/shard_map/ppermute | solution.py:812
  79.3 0.8 update.1
  80.2 3.3 %collective-permute-done.17.refs_3_ = f32[64,128]{1,0:T(8,128)S(1)} collective-permute-done((f32[64,128]{1,0:T(8,128)S(1)}, f32[64,128]{1,0:T(8,128)S(1)}, u32[]{:S(2)}, u32[]{:S(2)}) %collective-permute-start.17) | collective-permute-done | bytes 32800 | tf_op jit(solution)/shard_map/ppermute | solution.py:812
  83.5 2.4 %returned.1 = f32[128,128]{1,0:T(8,128)} custom-call(s32[4]{0:T(128)S(1)} %pad_add_fusion.refs_0_.flags, f32[64,128]{1,0:T(8,128)S(1)} %get-tuple-element.42.refs_0_, f32[64,128]{1,0:T(8,128)S(1)} %collective-permute-done.15.refs_1_, f32[64,128]{1,0:T(8,128)S(1)} %collective-permute-done.16.refs_2_, f32[64,128]{1,0:T(8,128)S(1)} %collective-permute-done.17.refs_3_, ...), custom_call_target="tpu_custom_call" | custom-call | tf_op jit(solution)/shard_map/returned/pallas_call | solution.py:712
  (27 shorter events, 0.2 us)
Async XLA Ops:
  0.6 7.2 %copy-start.6 = (s32[128,1,2,3]{0,2,3,1:T(2,128)S(1)}, s32[128,1,2,3]{0,2,3,1:T(2,128)}, u32[]{:S(2)}) copy-start(s32[128,1,2,3]{0,2,3,1:T(2,128)} %param.11) | copy-start | bytes 9220
  0.6 13.3 %copy-start.5 = (s32[128,128]{1,0:T(8,128)S(1)}, s32[128,128]{1,0:T(8,128)}, u32[]{:S(2)}) copy-start(s32[128,128]{1,0:T(8,128)} %param.10) | copy-start | bytes 196612
  0.7 14.4 %copy-start.4 = (f32[128,8]{0,1:T(8,128)S(1)}, f32[128,8]{0,1:T(8,128)}, u32[]{:S(2)}) copy-start(f32[128,8]{0,1:T(8,128)} %param.14) | copy-start | bytes 12292
  0.7 14.4 %copy-start.1 = (f32[128,128]{1,0:T(8,128)S(1)}, f32[128,128]{1,0:T(8,128)}, u32[]{:S(2)}) copy-start(f32[128,128]{1,0:T(8,128)} %refs_10_.1) | copy-start | bytes 196612
  0.7 14.4 %copy-start.2 = (f32[128,128]{1,0:T(8,128)S(1)}, f32[128,128]{1,0:T(8,128)}, u32[]{:S(2)}) copy-start(f32[128,128]{1,0:T(8,128)} %refs_11_.1) | copy-start | bytes 196612
  2.3 49.6 %copy-start.3 = (f32[8,128]{1,0:T(8,128)S(1)}, f32[8,128]{1,0:T(8,128)}, u32[]{:S(2)}) copy-start(f32[8,128]{1,0:T(8,128)} %refs_5_.1) | copy-start | bytes 12292
  2.3 54.9 %copy-start = (bf16[32,128,128]{2,1,0:T(8,128)(2,1)S(1)}, bf16[32,128,128]{2,1,0:T(8,128)(2,1)}, u32[]{:S(2)}) copy-start(bf16[32,128,128]{2,1,0:T(8,128)(2,1)} %refs_6_.1) | copy-start | bytes 3145732
  2.3 6.5 %collective-permute-start = (bf16[2,128,128]{2,1,0:T(8,128)(2,1)S(1)}, bf16[2,128,128]{2,1,0:T(8,128)(2,1)S(1)}, u32[]{:S(2)}, u32[]{:S(2)}) collective-permute-start(bf16[2,128,128]{2,1,0:T(8,128)(2,1)S(1)} %get-tuple-element.25), channel_id=1, source_target_pairs={{0,2},{1,3},{2,4},{3,5},{4,6},{5,7},{6,8},{7,9},{8,10},{9,11},{10,... | collective-permute-start | bytes 196616 | tf_op jit(solution)/shard_map/ppermute | solution.py:758
  6.5 6.4 %collective-permute-start.1 = (bf16[2,128,128]{2,1,0:T(8,128)(2,1)S(1)}, bf16[2,128,128]{2,1,0:T(8,128)(2,1)S(1)}, u32[]{:S(2)}, u32[]{:S(2)}) collective-permute-start(bf16[2,128,128]{2,1,0:T(8,128)(2,1)S(1)} %get-tuple-element.26), channel_id=1, source_target_pairs={{2,0},{3,1},{4,2},{5,3},{6,4},{7,5},{8,6},{9,7},{10,8},{11,9},{12,... | collective-permute-start | bytes 196616 | tf_op jit(solution)/shard_map/ppermute | solution.py:758
  12.9 2.2 %collective-permute-start.2 = (f32[4,144,128]{2,1,0:T(8,128)S(1)}, f32[4,144,128]{2,1,0:T(8,128)S(1)}, u32[]{:S(2)}, u32[]{:S(2)}) collective-permute-start(f32[4,144,128]{2,1,0:T(8,128)S(1)} %frame.1), channel_id=1, source_target_pairs={{0,1},{1,0},{2,3},{3,2},{4,5},{5,4},{6,7},{7,6},{8,9},{9,8},{10,11... | collective-permute-start | bytes 884744 | tf_op jit(solution)/shard_map/ppermute | solution.py:758
  32.4 13.7 %all-to-all-start = ((bf16[4,272,256]{2,1,0:T(8,128)(2,1)}), bf16[4,272,256]{2,1,0:T(8,128)(2,1)S(1)}, u32[]{:S(2)}, u32[]{:S(2)}) async-start(bf16[4,272,256]{2,1,0:T(8,128)(2,1)} %get-tuple-element.29), calls=%async_computation | async-start | bytes 1114112 | tf_op jit(solution)/shard_map/all_to_all | solution.py:794
  36.4 11.2 %collective-permute-start.6 = (bf16[128,128]{1,0:T(8,128)(2,1)S(1)}, bf16[128,128]{1,0:T(8,128)(2,1)S(1)}, u32[]{:S(2)}, u32[]{:S(2)}) collective-permute-start(bf16[128,128]{1,0:T(8,128)(2,1)S(1)} %get-tuple-element.34.refs_7_), channel_id=1, source_target_pairs={{24,0},{25,1},{26,2},{27,3},{28,4},{29,5},{30,6},{31,7}} | collective-permute-start | bytes 98312 | tf_op jit(solution)/shard_map/ppermute | solution.py:818
  37.7 14.3 %collective-permute-start.7 = (bf16[128,128]{1,0:T(8,128)(2,1)S(1)}, bf16[128,128]{1,0:T(8,128)(2,1)S(1)}, u32[]{:S(2)}, u32[]{:S(2)}) collective-permute-start(bf16[128,128]{1,0:T(8,128)(2,1)S(1)} %get-tuple-element.34.refs_7_), channel_id=1, source_target_pairs={{24,8},{25,9},{26,10},{27,11},{28,12},{29,13},{30,14},{31,15}} | collective-permute-start | bytes 98312 | tf_op jit(solution)/shard_map/ppermute | solution.py:818
  38.4 13.6 %collective-permute-start.8 = (bf16[128,128]{1,0:T(8,128)(2,1)S(1)}, bf16[128,128]{1,0:T(8,128)(2,1)S(1)}, u32[]{:S(2)}, u32[]{:S(2)}) collective-permute-start(bf16[128,128]{1,0:T(8,128)(2,1)S(1)} %get-tuple-element.34.refs_7_), channel_id=1, source_target_pairs={{24,16},{25,17},{26,18},{27,19},{28,20},{29,21},{30,22},{31,23}} | collective-permute-start | bytes 98312 | tf_op jit(solution)/shard_map/ppermute | solution.py:818
  46.2 5.8 %collective-permute-start.3 = (bf16[208,256]{1,0:T(8,128)(2,1)S(1)}, bf16[208,256]{1,0:T(8,128)(2,1)S(1)}, u32[]{:S(2)}, u32[]{:S(2)}) collective-permute-start(bf16[208,256]{1,0:T(8,128)(2,1)S(1)} %get-tuple-element.31), channel_id=1, source_target_pairs={{0,1},{1,2},{2,3},{3,4},{4,5},{5,6},{6,7},{7,0},{8,9},{9,10},{10,1... | collective-permute-start | bytes 319496 | tf_op jit(solution)/shard_map/ppermute | solution.py:812
  46.3 8.8 %collective-permute-start.4 = (bf16[208,256]{1,0:T(8,128)(2,1)S(1)}, bf16[208,256]{1,0:T(8,128)(2,1)S(1)}, u32[]{:S(2)}, u32[]{:S(2)}) collective-permute-start(bf16[208,256]{1,0:T(8,128)(2,1)S(1)} %get-tuple-element.32), channel_id=1, source_target_pairs={{0,2},{1,3},{2,4},{3,5},{4,6},{5,7},{6,0},{7,1},{8,10},{9,11},{10,... | collective-permute-start | bytes 319496 | tf_op jit(solution)/shard_map/ppermute | solution.py:812
  47.6 9.6 %collective-permute-start.5 = (bf16[208,256]{1,0:T(8,128)(2,1)S(1)}, bf16[208,256]{1,0:T(8,128)(2,1)S(1)}, u32[]{:S(2)}, u32[]{:S(2)}) collective-permute-start(bf16[208,256]{1,0:T(8,128)(2,1)S(1)} %get-tuple-element.33), channel_id=1, source_target_pairs={{0,3},{1,4},{2,5},{3,6},{4,7},{5,0},{6,1},{7,2},{8,11},{9,12},{10,... | collective-permute-start | bytes 319496 | tf_op jit(solution)/shard_map/ppermute | solution.py:812
  61.3 4.2 %collective-permute-start.9 = (f32[128,128]{1,0:T(8,128)S(1)}, f32[128,128]{1,0:T(8,128)S(1)}, u32[]{:S(2)}, u32[]{:S(2)}) collective-permute-start(f32[128,128]{1,0:T(8,128)S(1)} %get-tuple-element.36.refs_0_), channel_id=1, source_target_pairs={{0,8},{1,9},{2,10},{3,11},{4,12},{5,13},{6,14},{7,15},{8,16},{9,17... | collective-permute-start | bytes 196616 | tf_op jit(solution)/shard_map/ppermute | solution.py:802
  62.0 7.0 %collective-permute-start.13 = (f32[128,128]{1,0:T(8,128)S(1)}, f32[128,128]{1,0:T(8,128)S(1)}, u32[]{:S(2)}, u32[]{:S(2)}) collective-permute-start(f32[128,128]{1,0:T(8,128)S(1)} %get-tuple-element.36.refs_0_), channel_id=1, source_target_pairs={{0,16},{1,17},{2,18},{3,19},{4,20},{5,21},{6,22},{7,23},{8,24},{9,... | collective-permute-start | bytes 196616 | tf_op jit(solution)/shard_map/ppermute | solution.py:802
  63.0 6.0 %collective-permute-start.14 = (f32[128,128]{1,0:T(8,128)S(1)}, f32[128,128]{1,0:T(8,128)S(1)}, u32[]{:S(2)}, u32[]{:S(2)}) collective-permute-start(f32[128,128]{1,0:T(8,128)S(1)} %get-tuple-element.36.refs_0_), channel_id=1, source_target_pairs={{0,24},{1,25},{2,26},{3,27},{4,28},{5,29},{6,30},{7,31},{8,0},{9,1... | collective-permute-start | bytes 196616 | tf_op jit(solution)/shard_map/ppermute | solution.py:802
  65.5 11.9 %collective-permute-start.10 = (f32[2,128,128]{2,1,0:T(8,128)S(1)}, f32[2,128,128]{2,1,0:T(8,128)S(1)}, u32[]{:S(2)}, u32[]{:S(2)}) collective-permute-start(f32[2,128,128]{2,1,0:T(8,128)S(1)} %get-tuple-element.38.refs_3_), channel_id=1, source_target_pairs={{0,24},{1,25},{2,26},{3,27},{4,28},{5,29},{6,30},{7,31}} | collective-permute-start | bytes 393224 | tf_op jit(solution)/shard_map/ppermute | solution.py:824
  67.5 11.8 %collective-permute-start.11 = (f32[2,128,128]{2,1,0:T(8,128)S(1)}, f32[2,128,128]{2,1,0:T(8,128)S(1)}, u32[]{:S(2)}, u32[]{:S(2)}) collective-permute-start(f32[2,128,128]{2,1,0:T(8,128)S(1)} %get-tuple-element.38.refs_3_), channel_id=1, source_target_pairs={{8,24},{9,25},{10,26},{11,27},{12,28},{13,29},{14,30},{15,31}} | collective-permute-start | bytes 393224 | tf_op jit(solution)/shard_map/ppermute | solution.py:824
  68.2 11.1 %collective-permute-start.12 = (f32[2,128,128]{2,1,0:T(8,128)S(1)}, f32[2,128,128]{2,1,0:T(8,128)S(1)}, u32[]{:S(2)}, u32[]{:S(2)}) collective-permute-start(f32[2,128,128]{2,1,0:T(8,128)S(1)} %get-tuple-element.38.refs_3_), channel_id=1, source_target_pairs={{16,24},{17,25},{18,26},{19,27},{20,28},{21,29},{22,30},{23,31}} | collective-permute-start | bytes 393224 | tf_op jit(solution)/shard_map/ppermute | solution.py:824
  69.2 11.0 %collective-permute-start.15 = (f32[64,128]{1,0:T(8,128)S(1)}, f32[64,128]{1,0:T(8,128)S(1)}, u32[]{:S(2)}, u32[]{:S(2)}) collective-permute-start(f32[64,128]{1,0:T(8,128)S(1)} %get-tuple-element.43), channel_id=1, source_target_pairs={{0,7},{1,0},{2,1},{3,2},{4,3},{5,4},{6,5},{7,6},{8,15},{9,8},{10,9... | collective-permute-start | bytes 98312 | tf_op jit(solution)/shard_map/ppermute | solution.py:812
  74.6 5.5 %collective-permute-start.16 = (f32[64,128]{1,0:T(8,128)S(1)}, f32[64,128]{1,0:T(8,128)S(1)}, u32[]{:S(2)}, u32[]{:S(2)}) collective-permute-start(f32[64,128]{1,0:T(8,128)S(1)} %get-tuple-element.44), channel_id=1, source_target_pairs={{0,6},{1,7},{2,0},{3,1},{4,2},{5,3},{6,4},{7,5},{8,14},{9,15},{10,... | collective-permute-start | bytes 98312 | tf_op jit(solution)/shard_map/ppermute | solution.py:812
  77.3 6.1 %collective-permute-start.17 = (f32[64,128]{1,0:T(8,128)S(1)}, f32[64,128]{1,0:T(8,128)S(1)}, u32[]{:S(2)}, u32[]{:S(2)}) collective-permute-start(f32[64,128]{1,0:T(8,128)S(1)} %get-tuple-element.45), channel_id=1, source_target_pairs={{0,5},{1,6},{2,7},{3,0},{4,1},{5,2},{6,3},{7,4},{8,13},{9,14},{10,... | collective-permute-start | bytes 98312 | tf_op jit(solution)/shard_map/ppermute | solution.py:812

commit v11 on v10

--- a/solution.py
+++ b/solution.py
@@ -13,6 +13,7 @@
 F32 = jnp.float32
 BF16 = jnp.bfloat16
 EDGE = 8
+LINES = 8
 AHEAD = 4
 CHUNK = 8
 AXES = ("comp", "lat", "lon")
@@ -104,11 +105,10 @@
 
 def advance_kernel(comp_count, left_at, right_at, *refs):
     (flags, source_column, labels, state, up_rows, low_rows, left_in, right_in, own_sides) = refs[:9]
-    (mask, mix_atm, mix_ocn, flux_map) = refs[9:13]
-    out, surface, sea_copy = refs[13:16]
-    packed = refs[16]
-    (values, moved, halo_moved, smooth, pairs, mixed, later_smooth, later_pairs, later_mixed) = refs[17:26]
-    (weights, flux_weights, flux_pairs, fluxes, staged, top, in_sems, out_sems) = refs[26:]
+    (mask, mix_atm, mix_ocn, flux_map, ocean_map) = refs[9:14]
+    out, surface, sea_copy, packed, wide = refs[14:19]
+    (values, moved, halo_moved, smooth, pairs, mixed, later_smooth, later_pairs, later_mixed) = refs[19:28]
+    (weights, flux_weights, flux_pairs, fluxes, staged, top, table, in_sems, out_sems) = refs[28:]
     left_cols = left_in.at[left_at : left_at + 2]
     right_cols = right_in.at[right_at : right_at + 2]
     first = (smooth, pairs, mixed)
@@ -248,9 +248,9 @@
                 both = line + moved[q * CHUNK + row + 1, EDGE : EDGE + cols, :]
                 flux_pairs[row * cols : (row + 1) * cols, :] = side_by_side(both)
             put(q, slot).start()
-            note_top(q, [staged[slot, row] for row in range(CHUNK)])
 
         def sum_fluxes(q):
+            note_top(q, [staged[q % 2, row] for row in range(CHUNK)])
             flux = dot_nt(flux_weights[...], flux_pairs[...])
             flux = flux[:flux_count] + flux[flux_count:]
             for row in range(CHUNK):
@@ -262,6 +262,7 @@
 
         fetch(AHEAD).start()
         flux_pairs[...] = jnp.zeros(flux_pairs.shape, BF16)
+        staged[0] = jnp.zeros(staged.shape[1:], F32)
         begin_first(0)
         end_first(0)
 
@@ -356,10 +357,21 @@
         put(chunks - 1, (chunks - 1) % 2).wait()
         surface[...] = top[...].T
         packed[...] = jnp.zeros(packed.shape, BF16)
+        table[...] = jnp.zeros(table.shape, F32)
+        for line in range(LINES):
+            for f in range(flux_count):
+                spot = f * LINES + line
+                table[spot : spot + 1, line * levels : (line + 1) * levels] = ocean_map[f : f + 1]
+        high, low = split_two(table[...])
+        depth = table.shape[0]
+        wide[:depth] = high
+        wide[depth : 2 * depth] = high
+        wide[2 * depth :] = low
 
 
 def advance(
-    flags, source_column, labels, state, halos, mask, mix_atm, mix_ocn, flux_map_t, comp_count, left_at, right_at
+    flags, source_column, labels, state, halos, mask, mix_atm, mix_ocn, flux_map_t, ocean_map,
+    comp_count, left_at, right_at,
 ):
     rows, cols, levels = state.shape
     fluxes = flux_map_t.shape[0]
@@ -377,9 +389,10 @@
             jax.ShapeDtypeStruct((rows, cols), F32),
             jax.ShapeDtypeStruct((rows, cols), BF16),
             entry,
+            jax.ShapeDtypeStruct((3 * LINES * fluxes, LINES * levels), BF16),
         ),
-        in_specs=[smem, vmem, vmem, hbm] + [vmem] * (len(halos) + 4),
-        out_specs=(hbm, vmem, vmem, vmem),
+        in_specs=[smem, vmem, vmem, hbm] + [vmem] * (len(halos) + 5),
+        out_specs=(hbm, vmem, vmem, vmem, vmem),
         scratch_shapes=[
             pltpu.VMEM((rows + 4, cols + 2 * EDGE, levels), F32),
             pltpu.VMEM((rows + 2, cols + 2 * EDGE, levels), F32),
@@ -396,6 +409,7 @@
             pltpu.VMEM((rows * fluxes, cols), F32),
             pltpu.VMEM((2, CHUNK, cols, levels), F32),
             pltpu.VMEM((cols, levels), F32),
+            pltpu.VMEM((LINES * fluxes, LINES * levels), F32),
             pltpu.SemaphoreType.DMA((rows // CHUNK,)),
             pltpu.SemaphoreType.DMA((2,)),
         ],
@@ -404,7 +418,7 @@
             flops=8 * cells * levels * levels, bytes_accessed=8 * cells * levels, transcendentals=0
         ),
         name="advance",
-    )(flags, source_column, labels, state, *halos, mask, mix_atm, mix_ocn, flux_map_t)
+    )(flags, source_column, labels, state, *halos, mask, mix_atm, mix_ocn, flux_map_t, ocean_map)
 
 
 BATCH = 8
@@ -578,17 +592,13 @@
     )(*parts, hits)
 
 
-LINES = 8
-
-
 def update_kernel(groups, flags, state, *refs):
     parts = refs[:groups]
-    mask, ocean_map, out, token, held, table, wide, in_sems, out_sems = refs[groups:]
+    mask, wide, out, token, held, in_sems, out_sems = refs[groups:]
     rows, cols, levels = state.shape
     share = parts[0].shape[0]
     flux_count = groups * share
     chunks = rows // LINES
-    depth = LINES * flux_count
     token[...] = jnp.zeros(token.shape, F32)
 
     def fetch(q):
@@ -605,16 +615,6 @@
     def ocean():
         for q in range(chunks):
             fetch(q).start()
-        table[...] = jnp.zeros(table.shape, F32)
-        for line in range(LINES):
-            for f in range(flux_count):
-                spot = f * LINES + line
-                table[spot : spot + 1, line * levels : (line + 1) * levels] = ocean_map[f : f + 1]
-        high, low = split_two(table[...])
-        wide[:depth] = high
-        wide[depth : 2 * depth] = high
-        wide[2 * depth :] = low
-
         def one(q, _):
             start = pl.multiple_of(q * LINES, LINES)
             sea = mask[pl.ds(start, LINES), :] > 0.5
@@ -639,9 +639,9 @@
             put(q).wait()
 
 
-def update(flags, state, parts, mask, ocean_map):
+def update(flags, state, parts, mask, wide):
     rows, cols, levels = state.shape
-    depth = LINES * ocean_map.shape[0]
+    depth = wide.shape[0] // 3
     vmem = pl.BlockSpec(memory_space=pltpu.VMEM)
     smem = pl.BlockSpec(memory_space=pltpu.SMEM)
     hbm = pl.BlockSpec(memory_space=pltpu.HBM)
@@ -656,8 +656,6 @@
         input_output_aliases={1: 0},
         scratch_shapes=[
             pltpu.VMEM(state.shape, F32),
-            pltpu.VMEM((depth, LINES * levels), F32),
-            pltpu.VMEM((3 * depth, LINES * levels), BF16),
             pltpu.SemaphoreType.DMA((rows // LINES,)),
             pltpu.SemaphoreType.DMA((rows // LINES,)),
         ],
@@ -668,12 +666,12 @@
             transcendentals=0,
         ),
         name="update",
-    )(flags, state, *parts, mask, ocean_map)
+    )(flags, state, *parts, mask, wide)
 
 
 def returned_kernel(groups, flags, *refs):
     picked = refs[:groups]
-    weight_column, row_line, weights, mask, surface, new_surface, token, out, total = refs[groups:]
+    weight_line, row_line, weights, mask, surface, new_surface, token, out, total = refs[groups:]
     rows, cols = mask.shape
     weight_count = weights.shape[0]
 
@@ -684,29 +682,31 @@
     @pl.when(flags[0] == 0)
     def atmosphere():
         values = jnp.concatenate([p[...] for p in picked], axis=0)
-        pair = side_by_side(values)
-        which = jnp.broadcast_to(weight_column[...], values.shape)
-        total[...] = jnp.zeros(values.shape, F32)
+        turned = values.T
+        pair = jnp.concatenate(split_two(turned), axis=0)
+        total[...] = jnp.zeros(turned.shape, F32)
 
         def one(i, _):
-            both = jnp.concatenate([weights[2 * i], weights[2 * i + 1]], axis=0)
-            images = dot_nt(pair, jnp.concatenate([both, both], axis=1))
-            total[...] += jnp.where(which == 2 * i, images[:, :cols], 0.0) + jnp.where(
-                which == 2 * i + 1, images[:, cols:], 0.0
-            )
+            block = weights[pl.ds(4 * i, 4)].reshape(4 * cols, cols)
+            images = dot_nn(jnp.concatenate([block, block], axis=1), pair)
+            some = total[...]
+            for j in range(4):
+                chosen = weight_line[...] == 4 * i + j
+                some = some + jnp.where(chosen, images[j * cols : (j + 1) * cols, :], 0.0)
+            total[...] = some
             return 0
 
-        lax.fori_loop(0, weight_count // 2, one, 0, unroll=8)
+        lax.fori_loop(0, weight_count // 4, one, 0, unroll=2)
         spots = lax.broadcasted_iota(jnp.int32, (rows, values.shape[0]), 0)
         chosen = jnp.where(jnp.broadcast_to(row_line[...], spots.shape) == spots, 1.0, 0.0).astype(BF16)
         high, low = split_two(total[...])
-        back = dot_nn(chosen, high) + dot_nn(chosen, low)
+        back = dot_nt(chosen, high) + dot_nt(chosen, low)
         out[...] = jnp.where(mask[...] > 0.5, back, surface[...])
 
 
-def returned(flags, picked, weight_column, row_line, weights, mask, surface, new_surface, token):
+def returned(flags, picked, weight_line, row_line, weights, mask, surface, new_surface, token):
     rows, cols = mask.shape
-    entry_total = weight_column.shape[0]
+    entry_total = weight_line.shape[1]
     vmem = pl.BlockSpec(memory_space=pltpu.VMEM)
     smem = pl.BlockSpec(memory_space=pltpu.SMEM)
     return pl.pallas_call(
@@ -714,10 +714,10 @@
         out_shape=jax.ShapeDtypeStruct((rows, cols), F32),
         in_specs=[smem] + [vmem] * (len(picked) + 7),
         out_specs=vmem,
-        scratch_shapes=[pltpu.VMEM((entry_total, cols), F32)],
+        scratch_shapes=[pltpu.VMEM((cols, entry_total), F32)],
         compiler_params=pltpu.CompilerParams(vmem_limit_bytes=16 * MIB),
         name="returned",
-    )(flags, *picked, weight_column, row_line, weights, mask, surface, new_surface, token)
+    )(flags, *picked, weight_line, row_line, weights, mask, surface, new_surface, token)
 
 
 def local(
@@ -829,9 +829,9 @@
     halos = (up_rows, low_rows, left_cols, right_cols, sides)
     moved = advance(
         flags, sources[:, None], label_lines, state, halos, mask, mix_atm, mix_ocn, flux_map.T,
-        comp_count, left_at, right_at,
+        ocean_map, comp_count, left_at, right_at,
     )
-    moved, surface, sea_copy, packed = moved
+    moved, surface, sea_copy, packed, wide = moved
     slabs = over_comp(packed)
     seas = [from_ocean(sea_copy, c) for c in range(ocean_comp)] + [sea_copy]
     blocks = regroup(slabs, neighbours)
@@ -845,10 +845,10 @@
     new_surface, picked = picks[0], picks[1:]
     arrived = [over_tiles(picked[n], -offsets[n], ocean_comp) for n in range(neighbours)]
     fields = [to_ocean(forcing, c) for c in range(ocean_comp)] + [forcing]
-    final_state, token = update(flags, moved, fields, mask, ocean_map)
-    weight_column = (packed_labels // rows)[:, None]
+    final_state, token = update(flags, moved, fields, mask, wide)
+    weight_line = (packed_labels // rows)[None, :]
     surface_out = returned(
-        flags, arrived, weight_column, sources[None, :], regrid_weights, mask, surface, new_surface,
+        flags, arrived, weight_line, sources[None, :], regrid_weights, mask, surface, new_surface,
         token,
     )
     return (final_state, surface_out)

time: 86.3 us -> 92.8 us (1.075)
  waiting for transfers between devices: 21.8 us -> 26.7 us
  starting transfers between devices: 35.2 us -> 36.5 us
    ppermute x3, waiting for transfers between devices: 1.11 us -> 5.85 us  [shifted_comp(): return lax.ppermute(value, AXES, pairs)]
    ppermute x6, starting transfers between devices: 15.8 us -> 17.2 us  [over_tiles(): return lax.ppermute(value, AXES, pairs)]
    ppermute x3, starting transfers between devices: 2.93 us -> 1.45 us  [shifted_comp(): return lax.ppermute(value, AXES, pairs)]
    ppermute x3, starting transfers between devices: 3.39 us -> 4.73 us  [to_ocean(): return lax.ppermute(value, AXES, pairs)]
  transfers between devices with their start and end apart: 19 -> 19, of which waited for: 7 -> 9; matrix products, arithmetic and copies ran while one was open for 2% -> 1% of each run, Pallas kernels for 1% -> 1%
where the time goes in v11:
time: 92.8 us; the launch traced here: 92.3 us
  starting transfers between devices  36.5 us (39%)
  Pallas kernels  27.1 us (29%)
  waiting for transfers between devices  26.7 us (29%)
  between operations  1 us (1%)
    pallas_call x1, Pallas kernels, advance(): pl.pallas_call(functools.partial(advance_kernel, comp_count, left_at, rig...  17.6 us
    ppermute x6, starting transfers between devices, over_tiles(): return lax.ppermute(value, AXES, pairs)  17.2 us
    ppermute x6, waiting for transfers between devices, over_tiles(): return lax.ppermute(value, AXES, pairs)  8.87 us
    all_to_all x1, waiting for transfers between devices, over_comp(): lax.all_to_all(value, 'comp', split_axis=0, concat_axis=0, tiled=True)  6.72 us
    ppermute x3, starting transfers between devices, band_shift(): return lax.ppermute(value, AXES, pairs)  6.48 us
    ppermute x3, waiting for transfers between devices, shifted_comp(): return lax.ppermute(value, AXES, pairs)  5.85 us
    ppermute x3, waiting for transfers between devices, band_shift(): return lax.ppermute(value, AXES, pairs)  5.25 us
    ppermute x3, starting transfers between devices, to_ocean(): return lax.ppermute(value, AXES, pairs)  4.73 us
  transfers between devices with their start and end apart: 19, of which 9 were waited for; matrix products, arithmetic and copies ran while one was open for 1% of the time, Pallas kernels for 1%

profile of v11, /device:TPU:1, one launch (start us, length us, event | category | flops | bytes accessed | tf_op | source)
XLA Modules:
  0.0 92.3 jit_solution(11886231668622666569)
XLA Ops:
  0.7 1.6 %edges.1 = (bf16[2,128,128]{2,1,0:T(8,128)(2,1)S(1)}, bf16[2,128,128]{2,1,0:T(8,128)(2,1)S(1)}, f32[4,128,128]{2,1,0:T(8,128)S(1)}) custom-call(f32[128,128,128]{2,1,0:T(8,128)} %refs_3_.1), custom_call_target="tpu_custom_call" | custom-call | tf_op jit(solution)/shard_map/edges/pallas_call | solution.py:64
  2.3 0.0 copy-start
  2.3 4.2 %collective-permute-start = (bf16[2,128,128]{2,1,0:T(8,128)(2,1)S(1)}, bf16[2,128,128]{2,1,0:T(8,128)(2,1)S(1)}, u32[]{:S(2)}, u32[]{:S(2)}) collective-permute-start(bf16[2,128,128]{2,1,0:T(8,128)(2,1)S(1)} %get-tuple-element.26), channel_id=1, source_target_pairs={{0,2},{1,3},{2,4},{3,5},{4,6},{5,7},{6,8},{7,9},{8,10},{9,11},{10,... | collective-permute-start | bytes 196616 | tf_op jit(solution)/shard_map/ppermute | solution.py:758
  6.5 1.3 %collective-permute-start.1 = (bf16[2,128,128]{2,1,0:T(8,128)(2,1)S(1)}, bf16[2,128,128]{2,1,0:T(8,128)(2,1)S(1)}, u32[]{:S(2)}, u32[]{:S(2)}) collective-permute-start(bf16[2,128,128]{2,1,0:T(8,128)(2,1)S(1)} %get-tuple-element.27), channel_id=1, source_target_pairs={{2,0},{3,1},{4,2},{5,3},{6,4},{7,5},{8,6},{9,7},{10,8},{11,9},{12,... | collective-permute-start | bytes 196616 | tf_op jit(solution)/shard_map/ppermute | solution.py:758
  7.8 0.1 copy.14
  8.0 0.2 reshape.114
  8.2 0.2 convert_reduce_fusion
  8.3 0.2 select_reduce_fusion
  8.5 0.1 copy.15.refs_1_
  8.7 4.1 %collective-permute-done.1.low_rows.refs_5_ = bf16[2,128,128]{2,1,0:T(8,128)(2,1)S(1)} collective-permute-done((bf16[2,128,128]{2,1,0:T(8,128)(2,1)S(1)}, bf16[2,128,128]{2,1,0:T(8,128)(2,1)S(1)}, u32[]{:S(2)}, u32[]{:S(2)}) %collective-permute-start.1) | collective-permute-done | bytes 65568 | tf_op jit(solution)/shard_map/ppermute | solution.py:758
  12.9 1.0 %collective-permute-start.2 = (f32[4,144,128]{2,1,0:T(8,128)S(1)}, f32[4,144,128]{2,1,0:T(8,128)S(1)}, u32[]{:S(2)}, u32[]{:S(2)}) collective-permute-start(f32[4,144,128]{2,1,0:T(8,128)S(1)} %frame.1), channel_id=1, source_target_pairs={{0,1},{1,0},{2,3},{3,2},{4,5},{5,4},{6,7},{7,6},{8,9},{9,8},{10,11... | collective-permute-start | bytes 884744 | tf_op jit(solution)/shard_map/ppermute | solution.py:758
  13.9 0.1 pad_add_fusion.refs_0_.flags
  14.0 1.1 %collective-permute-done.2.refs_6_.refs_7_ = f32[4,144,128]{2,1,0:T(8,128)S(1)} collective-permute-done((f32[4,144,128]{2,1,0:T(8,128)S(1)}, f32[4,144,128]{2,1,0:T(8,128)S(1)}, u32[]{:S(2)}, u32[]{:S(2)}) %collective-permute-start.2) | collective-permute-done | bytes 294944 | tf_op jit(solution)/shard_map/ppermute | solution.py:758
  15.1 17.6 %advance.1 = (f32[128,128,128]{2,1,0:T(8,128)}, f32[128,128]{1,0:T(8,128)S(1)}, bf16[128,128]{1,0:T(8,128)(2,1)S(1)}, bf16[4,272,256]{2,1,0:T(8,128)(2,1)}, bf16[192,1024]{1,0:T(8,128)(2,1)S(1)}) custom-call(s32[4]{0:T(128)S(1)} %pad_add_fusion.refs_0_.flags, s32[256,1]{1,0:T(8,128)S(1)} %copy.15.refs_1_, bf16[16,256]{1,0:T(8,128)(2,1)S(1)} %fusion.3.refs_2_, ...), custom_call_target="tpu_custom_call" | custom-call | flops 2147483648 | bytes 16777216 | tf_op jit(solution)/shard_map/advance/pallas_call | solution.py:385
  32.7 4.0 %all-to-all-start = ((bf16[4,272,256]{2,1,0:T(8,128)(2,1)}), bf16[4,272,256]{2,1,0:T(8,128)(2,1)S(1)}, u32[]{:S(2)}, u32[]{:S(2)}) async-start(bf16[4,272,256]{2,1,0:T(8,128)(2,1)} %get-tuple-element.30), calls=%async_computation | async-start | bytes 1114112 | tf_op jit(solution)/shard_map/all_to_all | solution.py:794
  36.7 0.7 collective-permute-start.8
  37.4 0.7 collective-permute-start.7
  38.0 1.3 %collective-permute-start.6 = (bf16[128,128]{1,0:T(8,128)(2,1)S(1)}, bf16[128,128]{1,0:T(8,128)(2,1)S(1)}, u32[]{:S(2)}, u32[]{:S(2)}) collective-permute-start(bf16[128,128]{1,0:T(8,128)(2,1)S(1)} %get-tuple-element.35.refs_7_), channel_id=1, source_target_pairs={{24,0},{25,1},{26,2},{27,3},{28,4},{29,5},{30,6},{31,7}} | collective-permute-start | bytes 98312 | tf_op jit(solution)/shard_map/ppermute | solution.py:818
  39.3 6.7 %all-to-all-done.slabs = bf16[4,272,256]{2,1,0:T(8,128)(2,1)S(1)} async-done(((bf16[4,272,256]{2,1,0:T(8,128)(2,1)}), bf16[4,272,256]{2,1,0:T(8,128)(2,1)S(1)}, u32[]{:S(2)}, u32[]{:S(2)}) %all-to-all-start) | async-done | bytes 557088 | tf_op jit(solution)/shard_map/all_to_all | solution.py:794
  46.1 0.5 collective-permute-start.3
  46.5 1.3 %collective-permute-start.4 = (bf16[208,256]{1,0:T(8,128)(2,1)S(1)}, bf16[208,256]{1,0:T(8,128)(2,1)S(1)}, u32[]{:S(2)}, u32[]{:S(2)}) collective-permute-start(bf16[208,256]{1,0:T(8,128)(2,1)S(1)} %get-tuple-element.33), channel_id=1, source_target_pairs={{0,2},{1,3},{2,4},{3,5},{4,6},{5,7},{6,0},{7,1},{8,10},{9,11},{10,... | collective-permute-start | bytes 319496 | tf_op jit(solution)/shard_map/ppermute | solution.py:812
  47.8 0.0 collective-permute-done.8.refs_6_
  47.8 4.3 %collective-permute-start.5 = (bf16[208,256]{1,0:T(8,128)(2,1)S(1)}, bf16[208,256]{1,0:T(8,128)(2,1)S(1)}, u32[]{:S(2)}, u32[]{:S(2)}) collective-permute-start(bf16[208,256]{1,0:T(8,128)(2,1)S(1)} %get-tuple-element.34), channel_id=1, source_target_pairs={{0,3},{1,4},{2,5},{3,6},{4,7},{5,0},{6,1},{7,2},{8,11},{9,12},{10,... | collective-permute-start | bytes 319496 | tf_op jit(solution)/shard_map/ppermute | solution.py:812
  52.1 0.1 slice_reduce_fusion.ocean_first
  52.2 0.0 collective-permute-done.7.refs_5_
  52.3 3.1 %collective-permute-done.4.refs_2_ = bf16[208,256]{1,0:T(8,128)(2,1)S(1)} collective-permute-done((bf16[208,256]{1,0:T(8,128)(2,1)S(1)}, bf16[208,256]{1,0:T(8,128)(2,1)S(1)}, u32[]{:S(2)}, u32[]{:S(2)}) %collective-permute-start.4) | collective-permute-done | bytes 106528 | tf_op jit(solution)/shard_map/ppermute | solution.py:812
  55.4 2.1 %collective-permute-done.5.refs_3_ = bf16[208,256]{1,0:T(8,128)(2,1)S(1)} collective-permute-done((bf16[208,256]{1,0:T(8,128)(2,1)S(1)}, bf16[208,256]{1,0:T(8,128)(2,1)S(1)}, u32[]{:S(2)}, u32[]{:S(2)}) %collective-permute-start.5) | collective-permute-done | bytes 106528 | tf_op jit(solution)/shard_map/ppermute | solution.py:812
  57.5 4.1 %regrid.1 = (f32[2,128,128]{2,1,0:T(8,128)S(1)}, f32[128,128]{1,0:T(8,128)S(1)}, bf16[256,128]{1,0:T(8,128)(2,1)S(1)}) custom-call(s32[4]{0:T(128)S(1)} %pad_add_fusion.refs_0_.flags, f32[8]{0:T(128)S(1)} %slice_reduce_fusion.ocean_first, bf16[208,256]{1,0:T(8,128)(2,1)S(1)} %get-tuple-element.31.refs_0_, ...), custom_call_target="tpu_custom_call" | custom-call | flops 2147483648 | bytes 2097152 | tf_op jit(solution)/shard_map/regrid/pallas_call | solution.py:541
  61.6 0.6 collective-permute-start.9
  62.1 3.5 %collective-permute-done.9.refs_1_ = f32[128,128]{1,0:T(8,128)S(1)} collective-permute-done((f32[128,128]{1,0:T(8,128)S(1)}, f32[128,128]{1,0:T(8,128)S(1)}, u32[]{:S(2)}, u32[]{:S(2)}) %collective-permute-start.9) | collective-permute-done | bytes 65568 | tf_op jit(solution)/shard_map/ppermute | solution.py:802
  65.6 0.7 collective-permute-start.12
  66.3 0.7 collective-permute-start.11
  67.0 3.4 %collective-permute-start.10 = (f32[2,128,128]{2,1,0:T(8,128)S(1)}, f32[2,128,128]{2,1,0:T(8,128)S(1)}, u32[]{:S(2)}, u32[]{:S(2)}) collective-permute-start(f32[2,128,128]{2,1,0:T(8,128)S(1)} %get-tuple-element.39.refs_3_), channel_id=1, source_target_pairs={{0,24},{1,25},{2,26},{3,27},{4,28},{5,29},{6,30},{7,31}} | collective-permute-start | bytes 393224 | tf_op jit(solution)/shard_map/ppermute | solution.py:824
  70.4 0.1 collective-permute-start.14
  70.5 0.8 collective-permute-start.13
  71.3 2.3 %collective-permute-done.14.refs_3_ = f32[128,128]{1,0:T(8,128)S(1)} collective-permute-done((f32[128,128]{1,0:T(8,128)S(1)}, f32[128,128]{1,0:T(8,128)S(1)}, u32[]{:S(2)}, u32[]{:S(2)}) %collective-permute-start.14) | collective-permute-done | bytes 65568 | tf_op jit(solution)/shard_map/ppermute | solution.py:802
  73.6 0.1 collective-permute-done.13.refs_2_
  73.6 0.2 pick.1
  73.8 6.2 %collective-permute-start.15 = (f32[64,128]{1,0:T(8,128)S(1)}, f32[64,128]{1,0:T(8,128)S(1)}, u32[]{:S(2)}, u32[]{:S(2)}) collective-permute-start(f32[64,128]{1,0:T(8,128)S(1)} %get-tuple-element.45), channel_id=1, source_target_pairs={{0,7},{1,0},{2,1},{3,2},{4,3},{5,4},{6,5},{7,6},{8,15},{9,8},{10,9... | collective-permute-start | bytes 98312 | tf_op jit(solution)/shard_map/ppermute | solution.py:812
  80.1 3.1 %collective-permute-start.16 = (f32[64,128]{1,0:T(8,128)S(1)}, f32[64,128]{1,0:T(8,128)S(1)}, u32[]{:S(2)}, u32[]{:S(2)}) collective-permute-start(f32[64,128]{1,0:T(8,128)S(1)} %get-tuple-element.46), channel_id=1, source_target_pairs={{0,6},{1,7},{2,0},{3,1},{4,2},{5,3},{6,4},{7,5},{8,14},{9,15},{10,... | collective-permute-start | bytes 98312 | tf_op jit(solution)/shard_map/ppermute | solution.py:812
  83.1 1.9 %collective-permute-start.17 = (f32[64,128]{1,0:T(8,128)S(1)}, f32[64,128]{1,0:T(8,128)S(1)}, u32[]{:S(2)}, u32[]{:S(2)}) collective-permute-start(f32[64,128]{1,0:T(8,128)S(1)} %get-tuple-element.47), channel_id=1, source_target_pairs={{0,5},{1,6},{2,7},{3,0},{4,1},{5,2},{6,3},{7,4},{8,13},{9,14},{10,... | collective-permute-start | bytes 98312 | tf_op jit(solution)/shard_map/ppermute | solution.py:812
  85.1 0.0 collective-permute-done.11.refs_1_
  85.1 0.0 collective-permute-done.10.refs_0_
  85.1 0.8 update.1
  85.9 0.0 collective-permute-done.15.refs_1_
  85.9 0.0 collective-permute-done.16.refs_2_
  86.0 3.7 %collective-permute-done.17.refs_3_ = f32[64,128]{1,0:T(8,128)S(1)} collective-permute-done((f32[64,128]{1,0:T(8,128)S(1)}, f32[64,128]{1,0:T(8,128)S(1)}, u32[]{:S(2)}, u32[]{:S(2)}) %collective-permute-start.17) | collective-permute-done | bytes 32800 | tf_op jit(solution)/shard_map/ppermute | solution.py:812
  89.6 2.7 %returned.1 = f32[128,128]{1,0:T(8,128)} custom-call(s32[4]{0:T(128)S(1)} %pad_add_fusion.refs_0_.flags, f32[64,128]{1,0:T(8,128)S(1)} %get-tuple-element.44.refs_0_, f32[64,128]{1,0:T(8,128)S(1)} %collective-permute-done.15.refs_1_, f32[64,128]{1,0:T(8,128)S(1)} %collective-permute-done.16.refs_2_, f32[64,128]{1,0:T(8,128)S(1)} %collective-permute-done.17.refs_3_, ...), custom_call_target="tpu_custom_call" | custom-call | tf_op jit(solution)/shard_map/returned/pallas_call | solution.py:712
  (26 shorter events, 0.2 us)
Async XLA Ops:
  0.6 7.2 %copy-start.6 = (s32[128,1,2,3]{0,2,3,1:T(2,128)S(1)}, s32[128,1,2,3]{0,2,3,1:T(2,128)}, u32[]{:S(2)}) copy-start(s32[128,1,2,3]{0,2,3,1:T(2,128)} %param.11) | copy-start | bytes 9220
  0.6 13.3 %copy-start.5 = (s32[128,128]{1,0:T(8,128)S(1)}, s32[128,128]{1,0:T(8,128)}, u32[]{:S(2)}) copy-start(s32[128,128]{1,0:T(8,128)} %param.10) | copy-start | bytes 196612
  0.7 14.4 %copy-start.3 = (f32[8,128]{1,0:T(8,128)S(1)}, f32[8,128]{1,0:T(8,128)}, u32[]{:S(2)}) copy-start(f32[8,128]{1,0:T(8,128)} %refs_13_.1) | copy-start | bytes 12292
  0.7 14.4 %copy-start.4 = (f32[128,8]{0,1:T(8,128)S(1)}, f32[128,8]{0,1:T(8,128)}, u32[]{:S(2)}) copy-start(f32[128,8]{0,1:T(8,128)} %param.14) | copy-start | bytes 12292
  0.7 14.4 %copy-start.2 = (f32[128,128]{1,0:T(8,128)S(1)}, f32[128,128]{1,0:T(8,128)}, u32[]{:S(2)}) copy-start(f32[128,128]{1,0:T(8,128)} %refs_11_.1) | copy-start | bytes 196612
  0.7 14.4 %copy-start.1 = (f32[128,128]{1,0:T(8,128)S(1)}, f32[128,128]{1,0:T(8,128)}, u32[]{:S(2)}) copy-start(f32[128,128]{1,0:T(8,128)} %refs_10_.1) | copy-start | bytes 196612
  2.3 55.2 %copy-start = (bf16[32,128,128]{2,1,0:T(8,128)(2,1)S(1)}, bf16[32,128,128]{2,1,0:T(8,128)(2,1)}, u32[]{:S(2)}) copy-start(bf16[32,128,128]{2,1,0:T(8,128)(2,1)} %refs_6_.1) | copy-start | bytes 3145732
  2.3 6.4 %collective-permute-start = (bf16[2,128,128]{2,1,0:T(8,128)(2,1)S(1)}, bf16[2,128,128]{2,1,0:T(8,128)(2,1)S(1)}, u32[]{:S(2)}, u32[]{:S(2)}) collective-permute-start(bf16[2,128,128]{2,1,0:T(8,128)(2,1)S(1)} %get-tuple-element.26), channel_id=1, source_target_pairs={{0,2},{1,3},{2,4},{3,5},{4,6},{5,7},{6,8},{7,9},{8,10},{9,11},{10,... | collective-permute-start | bytes 196616 | tf_op jit(solution)/shard_map/ppermute | solution.py:758
  6.5 6.4 %collective-permute-start.1 = (bf16[2,128,128]{2,1,0:T(8,128)(2,1)S(1)}, bf16[2,128,128]{2,1,0:T(8,128)(2,1)S(1)}, u32[]{:S(2)}, u32[]{:S(2)}) collective-permute-start(bf16[2,128,128]{2,1,0:T(8,128)(2,1)S(1)} %get-tuple-element.27), channel_id=1, source_target_pairs={{2,0},{3,1},{4,2},{5,3},{6,4},{7,5},{8,6},{9,7},{10,8},{11,9},{12,... | collective-permute-start | bytes 196616 | tf_op jit(solution)/shard_map/ppermute | solution.py:758
  12.9 2.2 %collective-permute-start.2 = (f32[4,144,128]{2,1,0:T(8,128)S(1)}, f32[4,144,128]{2,1,0:T(8,128)S(1)}, u32[]{:S(2)}, u32[]{:S(2)}) collective-permute-start(f32[4,144,128]{2,1,0:T(8,128)S(1)} %frame.1), channel_id=1, source_target_pairs={{0,1},{1,0},{2,3},{3,2},{4,5},{5,4},{6,7},{7,6},{8,9},{9,8},{10,11... | collective-permute-start | bytes 884744 | tf_op jit(solution)/shard_map/ppermute | solution.py:758
  32.7 13.3 %all-to-all-start = ((bf16[4,272,256]{2,1,0:T(8,128)(2,1)}), bf16[4,272,256]{2,1,0:T(8,128)(2,1)S(1)}, u32[]{:S(2)}, u32[]{:S(2)}) async-start(bf16[4,272,256]{2,1,0:T(8,128)(2,1)} %get-tuple-element.30), calls=%async_computation | async-start | bytes 1114112 | tf_op jit(solution)/shard_map/all_to_all | solution.py:794
  36.7 11.1 %collective-permute-start.8 = (bf16[128,128]{1,0:T(8,128)(2,1)S(1)}, bf16[128,128]{1,0:T(8,128)(2,1)S(1)}, u32[]{:S(2)}, u32[]{:S(2)}) collective-permute-start(bf16[128,128]{1,0:T(8,128)(2,1)S(1)} %get-tuple-element.35.refs_7_), channel_id=1, source_target_pairs={{24,16},{25,17},{26,18},{27,19},{28,20},{29,21},{30,22},{31,23}} | collective-permute-start | bytes 98312 | tf_op jit(solution)/shard_map/ppermute | solution.py:818
  37.4 14.9 %collective-permute-start.7 = (bf16[128,128]{1,0:T(8,128)(2,1)S(1)}, bf16[128,128]{1,0:T(8,128)(2,1)S(1)}, u32[]{:S(2)}, u32[]{:S(2)}) collective-permute-start(bf16[128,128]{1,0:T(8,128)(2,1)S(1)} %get-tuple-element.35.refs_7_), channel_id=1, source_target_pairs={{24,8},{25,9},{26,10},{27,11},{28,12},{29,13},{30,14},{31,15}} | collective-permute-start | bytes 98312 | tf_op jit(solution)/shard_map/ppermute | solution.py:818
  38.0 14.2 %collective-permute-start.6 = (bf16[128,128]{1,0:T(8,128)(2,1)S(1)}, bf16[128,128]{1,0:T(8,128)(2,1)S(1)}, u32[]{:S(2)}, u32[]{:S(2)}) collective-permute-start(bf16[128,128]{1,0:T(8,128)(2,1)S(1)} %get-tuple-element.35.refs_7_), channel_id=1, source_target_pairs={{24,0},{25,1},{26,2},{27,3},{28,4},{29,5},{30,6},{31,7}} | collective-permute-start | bytes 98312 | tf_op jit(solution)/shard_map/ppermute | solution.py:818
  46.1 6.2 %collective-permute-start.3 = (bf16[208,256]{1,0:T(8,128)(2,1)S(1)}, bf16[208,256]{1,0:T(8,128)(2,1)S(1)}, u32[]{:S(2)}, u32[]{:S(2)}) collective-permute-start(bf16[208,256]{1,0:T(8,128)(2,1)S(1)} %get-tuple-element.32), channel_id=1, source_target_pairs={{0,1},{1,2},{2,3},{3,4},{4,5},{5,6},{6,7},{7,0},{8,9},{9,10},{10,1... | collective-permute-start | bytes 319496 | tf_op jit(solution)/shard_map/ppermute | solution.py:812
  46.5 8.8 %collective-permute-start.4 = (bf16[208,256]{1,0:T(8,128)(2,1)S(1)}, bf16[208,256]{1,0:T(8,128)(2,1)S(1)}, u32[]{:S(2)}, u32[]{:S(2)}) collective-permute-start(bf16[208,256]{1,0:T(8,128)(2,1)S(1)} %get-tuple-element.33), channel_id=1, source_target_pairs={{0,2},{1,3},{2,4},{3,5},{4,6},{5,7},{6,0},{7,1},{8,10},{9,11},{10,... | collective-permute-start | bytes 319496 | tf_op jit(solution)/shard_map/ppermute | solution.py:812
  47.8 9.6 %collective-permute-start.5 = (bf16[208,256]{1,0:T(8,128)(2,1)S(1)}, bf16[208,256]{1,0:T(8,128)(2,1)S(1)}, u32[]{:S(2)}, u32[]{:S(2)}) collective-permute-start(bf16[208,256]{1,0:T(8,128)(2,1)S(1)} %get-tuple-element.34), channel_id=1, source_target_pairs={{0,3},{1,4},{2,5},{3,6},{4,7},{5,0},{6,1},{7,2},{8,11},{9,12},{10,... | collective-permute-start | bytes 319496 | tf_op jit(solution)/shard_map/ppermute | solution.py:812
  61.6 4.1 %collective-permute-start.9 = (f32[128,128]{1,0:T(8,128)S(1)}, f32[128,128]{1,0:T(8,128)S(1)}, u32[]{:S(2)}, u32[]{:S(2)}) collective-permute-start(f32[128,128]{1,0:T(8,128)S(1)} %get-tuple-element.37.refs_0_), channel_id=1, source_target_pairs={{0,8},{1,9},{2,10},{3,11},{4,12},{5,13},{6,14},{7,15},{8,16},{9,17... | collective-permute-start | bytes 196616 | tf_op jit(solution)/shard_map/ppermute | solution.py:802
  65.6 17.5 %collective-permute-start.12 = (f32[2,128,128]{2,1,0:T(8,128)S(1)}, f32[2,128,128]{2,1,0:T(8,128)S(1)}, u32[]{:S(2)}, u32[]{:S(2)}) collective-permute-start(f32[2,128,128]{2,1,0:T(8,128)S(1)} %get-tuple-element.39.refs_3_), channel_id=1, source_target_pairs={{16,24},{17,25},{18,26},{19,27},{20,28},{21,29},{22,30},{23,31}} | collective-permute-start | bytes 393224 | tf_op jit(solution)/shard_map/ppermute | solution.py:824
  66.3 18.8 %collective-permute-start.11 = (f32[2,128,128]{2,1,0:T(8,128)S(1)}, f32[2,128,128]{2,1,0:T(8,128)S(1)}, u32[]{:S(2)}, u32[]{:S(2)}) collective-permute-start(f32[2,128,128]{2,1,0:T(8,128)S(1)} %get-tuple-element.39.refs_3_), channel_id=1, source_target_pairs={{8,24},{9,25},{10,26},{11,27},{12,28},{13,29},{14,30},{15,31}} | collective-permute-start | bytes 393224 | tf_op jit(solution)/shard_map/ppermute | solution.py:824
  67.0 18.1 %collective-permute-start.10 = (f32[2,128,128]{2,1,0:T(8,128)S(1)}, f32[2,128,128]{2,1,0:T(8,128)S(1)}, u32[]{:S(2)}, u32[]{:S(2)}) collective-permute-start(f32[2,128,128]{2,1,0:T(8,128)S(1)} %get-tuple-element.39.refs_3_), channel_id=1, source_target_pairs={{0,24},{1,25},{2,26},{3,27},{4,28},{5,29},{6,30},{7,31}} | collective-permute-start | bytes 393224 | tf_op jit(solution)/shard_map/ppermute | solution.py:824
  70.4 3.2 %collective-permute-start.14 = (f32[128,128]{1,0:T(8,128)S(1)}, f32[128,128]{1,0:T(8,128)S(1)}, u32[]{:S(2)}, u32[]{:S(2)}) collective-permute-start(f32[128,128]{1,0:T(8,128)S(1)} %get-tuple-element.37.refs_0_), channel_id=1, source_target_pairs={{0,24},{1,25},{2,26},{3,27},{4,28},{5,29},{6,30},{7,31},{8,0},{9,1... | collective-permute-start | bytes 196616 | tf_op jit(solution)/shard_map/ppermute | solution.py:802
  70.5 3.2 %collective-permute-start.13 = (f32[128,128]{1,0:T(8,128)S(1)}, f32[128,128]{1,0:T(8,128)S(1)}, u32[]{:S(2)}, u32[]{:S(2)}) collective-permute-start(f32[128,128]{1,0:T(8,128)S(1)} %get-tuple-element.37.refs_0_), channel_id=1, source_target_pairs={{0,16},{1,17},{2,18},{3,19},{4,20},{5,21},{6,22},{7,23},{8,24},{9,... | collective-permute-start | bytes 196616 | tf_op jit(solution)/shard_map/ppermute | solution.py:802
  73.8 12.1 %collective-permute-start.15 = (f32[64,128]{1,0:T(8,128)S(1)}, f32[64,128]{1,0:T(8,128)S(1)}, u32[]{:S(2)}, u32[]{:S(2)}) collective-permute-start(f32[64,128]{1,0:T(8,128)S(1)} %get-tuple-element.45), channel_id=1, source_target_pairs={{0,7},{1,0},{2,1},{3,2},{4,3},{5,4},{6,5},{7,6},{8,15},{9,8},{10,9... | collective-permute-start | bytes 98312 | tf_op jit(solution)/shard_map/ppermute | solution.py:812
  80.1 5.9 %collective-permute-start.16 = (f32[64,128]{1,0:T(8,128)S(1)}, f32[64,128]{1,0:T(8,128)S(1)}, u32[]{:S(2)}, u32[]{:S(2)}) collective-permute-start(f32[64,128]{1,0:T(8,128)S(1)} %get-tuple-element.46), channel_id=1, source_target_pairs={{0,6},{1,7},{2,0},{3,1},{4,2},{5,3},{6,4},{7,5},{8,14},{9,15},{10,... | collective-permute-start | bytes 98312 | tf_op jit(solution)/shard_map/ppermute | solution.py:812
  83.1 6.5 %collective-permute-start.17 = (f32[64,128]{1,0:T(8,128)S(1)}, f32[64,128]{1,0:T(8,128)S(1)}, u32[]{:S(2)}, u32[]{:S(2)}) collective-permute-start(f32[64,128]{1,0:T(8,128)S(1)} %get-tuple-element.47), channel_id=1, source_target_pairs={{0,5},{1,6},{2,7},{3,0},{4,1},{5,2},{6,3},{7,4},{8,13},{9,14},{10,... | collective-permute-start | bytes 98312 | tf_op jit(solution)/shard_map/ppermute | solution.py:812

commit v12 on v10

--- a/solution.py
+++ b/solution.py
@@ -103,12 +103,11 @@
 
 
 def advance_kernel(comp_count, left_at, right_at, *refs):
-    (flags, source_column, labels, state, up_rows, low_rows, left_in, right_in, own_sides) = refs[:9]
-    (mask, mix_atm, mix_ocn, flux_map) = refs[9:13]
-    out, surface, sea_copy = refs[13:16]
-    packed = refs[16]
-    (values, moved, halo_moved, smooth, pairs, mixed, later_smooth, later_pairs, later_mixed) = refs[17:26]
-    (weights, flux_weights, flux_pairs, fluxes, staged, top, in_sems, out_sems) = refs[26:]
+    (flags, labels, state, up_rows, low_rows, left_in, right_in, own_sides) = refs[:8]
+    (mask, mix_atm, mix_ocn, flux_map) = refs[8:12]
+    out, surface, sea_copy, packed = refs[12:16]
+    (values, moved, halo_moved, smooth, pairs, mixed, later_smooth, later_pairs, later_mixed) = refs[16:25]
+    (weights, flux_weights, flux_pairs, fluxes, staged, top, in_sems, out_sems) = refs[25:]
     left_cols = left_in.at[left_at : left_at + 2]
     right_cols = right_in.at[right_at : right_at + 2]
     first = (smooth, pairs, mixed)
@@ -301,16 +300,12 @@
         mix_rows(second, CHUNK)
         end_second(last, last % 2)
         sum_fluxes(last)
-        spots = lax.broadcasted_iota(jnp.int32, (source_column.shape[0], rows), 1)
-        placing = jnp.where(source_column[...] == spots, 1.0, 0.0).astype(BF16)
         share = flux_count // comp_count
         for c in range(comp_count):
             for f in range(share):
-                field = fluxes[pl.ds(c * share + f, rows, stride=flux_count), :].astype(BF16)
-                packed[c, : placing.shape[0], f * cols : (f + 1) * cols] = dot_nn(
-                    placing, field
-                ).astype(BF16)
-            packed[c, placing.shape[0] :, :] = labels[...]
+                field = fluxes[pl.ds(c * share + f, rows, stride=flux_count), :]
+                packed[c, :rows, f * cols : (f + 1) * cols] = field.astype(BF16)
+            packed[c, rows:, :] = labels[...]
         put(last - 1, (last - 1) % 2).wait()
         put(last, last % 2).wait()
         surface[...] = top[...].T
@@ -359,7 +354,7 @@
 
 
 def advance(
-    flags, source_column, labels, state, halos, mask, mix_atm, mix_ocn, flux_map_t, comp_count, left_at, right_at
+    flags, labels, state, halos, mask, mix_atm, mix_ocn, flux_map_t, comp_count, left_at, right_at
 ):
     rows, cols, levels = state.shape
     fluxes = flux_map_t.shape[0]
@@ -367,7 +362,7 @@
     smem = pl.BlockSpec(memory_space=pltpu.SMEM)
     hbm = pl.BlockSpec(memory_space=pltpu.HBM)
     entry = jax.ShapeDtypeStruct(
-        (comp_count, source_column.shape[0] + labels.shape[0], fluxes // comp_count * cols), BF16
+        (comp_count, rows + labels.shape[0], fluxes // comp_count * cols), BF16
     )
     cells = rows * cols
     return pl.pallas_call(
@@ -378,7 +373,7 @@
             jax.ShapeDtypeStruct((rows, cols), BF16),
             entry,
         ),
-        in_specs=[smem, vmem, vmem, hbm] + [vmem] * (len(halos) + 4),
+        in_specs=[smem, vmem, hbm] + [vmem] * (len(halos) + 4),
         out_specs=(hbm, vmem, vmem, vmem),
         scratch_shapes=[
             pltpu.VMEM((rows + 4, cols + 2 * EDGE, levels), F32),
@@ -404,7 +399,7 @@
             flops=8 * cells * levels * levels, bytes_accessed=8 * cells * levels, transcendentals=0
         ),
         name="advance",
-    )(flags, source_column, labels, state, *halos, mask, mix_atm, mix_ocn, flux_map_t)
+    )(flags, labels, state, *halos, mask, mix_atm, mix_ocn, flux_map_t)
 
 
 BATCH = 8
@@ -414,22 +409,25 @@
 def regroup_kernel(slabs, *blocks):
     sources = slabs.shape[0] - 1
     capacity = (blocks[0].shape[0] - LABEL_ROWS) // sources
+    rows = slabs.shape[1] - LABEL_ROWS
     size = len(blocks) * capacity
-    heads = [slabs[c, size : size + LABEL_ROWS, :].astype(F32) for c in range(sources)]
+    heads = [slabs[c, rows:, :].astype(F32) for c in range(sources)]
     lines = [head[i : i + 1] for i in range(2) for head in heads]
     spare = jnp.zeros((LABEL_ROWS - len(lines), heads[0].shape[1]), F32)
     labels = jnp.concatenate(lines + [spare], axis=0).astype(BF16)
-    for n, block in enumerate(blocks):
-        for c in range(sources):
-            block[c * capacity : (c + 1) * capacity, :] = slabs[
-                c, n * capacity : (n + 1) * capacity, :
-            ]
+    spots = lax.broadcasted_iota(jnp.int32, (rows, size), 0).astype(F32)
+    for c in range(sources):
+        placing = jnp.where(heads[c][2:3, :size] == spots, 1.0, 0.0).T.astype(BF16)
+        packed = dot_nn(placing, slabs[c, :rows, :]).astype(BF16)
+        for n, block in enumerate(blocks):
+            block[c * capacity : (c + 1) * capacity, :] = packed[n * capacity : (n + 1) * capacity, :]
+    for block in blocks:
         block[sources * capacity :, :] = labels
 
 
-def regroup(slabs, count):
+def regroup(slabs, count, entry_total):
     comps, rows, width = slabs.shape
-    size = (rows - LABEL_ROWS) // count * (comps - 1) + LABEL_ROWS
+    size = entry_total // count * (comps - 1) + LABEL_ROWS
     vmem = pl.BlockSpec(memory_space=pltpu.VMEM)
     return pl.pallas_call(
         regroup_kernel,
@@ -823,18 +821,18 @@
         ]
         return lax.ppermute(value, AXES, pairs)
 
-    label_lines = jnp.stack([packed_labels // rows, packed_labels % rows]).astype(BF16)
-    label_lines = jnp.pad(label_lines, ((0, LABEL_ROWS - 2), (0, 0)))
+    label_lines = jnp.stack([packed_labels // rows, packed_labels % rows, sources]).astype(BF16)
+    label_lines = jnp.pad(label_lines, ((0, LABEL_ROWS - 3), (0, 0)))
 
     halos = (up_rows, low_rows, left_cols, right_cols, sides)
     moved = advance(
-        flags, sources[:, None], label_lines, state, halos, mask, mix_atm, mix_ocn, flux_map.T,
+        flags, label_lines, state, halos, mask, mix_atm, mix_ocn, flux_map.T,
         comp_count, left_at, right_at,
     )
     moved, surface, sea_copy, packed = moved
     slabs = over_comp(packed)
     seas = [from_ocean(sea_copy, c) for c in range(ocean_comp)] + [sea_copy]
-    blocks = regroup(slabs, neighbours)
+    blocks = regroup(slabs, neighbours, entry_total)
     blocks = [over_tiles(blocks[n], offsets[n], comp_count) for n in range(neighbours)]
     forcing, shared, hits = regrid(
         flags, ocean_map[:, 0], blocks, seas, regrid_weights, surface, mask

time: 86.3 us -> 83.6 us (0.969)
  waiting for transfers between devices: 21.8 us -> 19.5 us
    all_to_all x1, waiting for transfers between devices: 7.07 us -> 4.21 us  [over_comp(): lax.all_to_all(value, 'comp', split_axis=0, concat_axis=0, tiled=True)]
  transfers between devices with their start and end apart: 19 -> 19, of which waited for: 7 -> 7; matrix products, arithmetic and copies ran while one was open for 2% -> 1% of each run, Pallas kernels for 1% -> 2%
where the time goes in v12:
time: 83.6 us; the launch traced here: 83.2 us
  starting transfers between devices  34.6 us (41%)
  Pallas kernels  26.8 us (32%)
  waiting for transfers between devices  19.5 us (23%)
  between operations  1.03 us (1%)
    pallas_call x1, Pallas kernels, advance(): pl.pallas_call(functools.partial(advance_kernel, comp_count, left_at, rig...  17.3 us
    ppermute x6, starting transfers between devices, over_tiles(): return lax.ppermute(value, AXES, pairs)  15.7 us
    ppermute x6, waiting for transfers between devices, over_tiles(): return lax.ppermute(value, AXES, pairs)  8.53 us
    ppermute x3, starting transfers between devices, band_shift(): return lax.ppermute(value, AXES, pairs)  6.35 us
    ppermute x3, waiting for transfers between devices, band_shift(): return lax.ppermute(value, AXES, pairs)  5.26 us
    all_to_all x1, waiting for transfers between devices, over_comp(): lax.all_to_all(value, 'comp', split_axis=0, concat_axis=0, tiled=True)  4.21 us
    pallas_call x1, Pallas kernels, regrid(): pl.pallas_call(functools.partial(regrid_body, count, comp_count), out_sha...  4.1 us
    all_to_all x1, starting transfers between devices, over_comp(): lax.all_to_all(value, 'comp', split_axis=0, concat_axis=0, tiled=True)  4 us
  transfers between devices with their start and end apart: 19, of which 7 were waited for; matrix products, arithmetic and copies ran while one was open for 1% of the time, Pallas kernels for 2%

profile of v12, /device:TPU:1, one launch (start us, length us, event | category | flops | bytes accessed | tf_op | source)
XLA Modules:
  0.0 83.2 jit_solution(13912145880236459373)
XLA Ops:
  0.7 1.6 %edges.1 = (bf16[2,128,128]{2,1,0:T(8,128)(2,1)S(1)}, bf16[2,128,128]{2,1,0:T(8,128)(2,1)S(1)}, f32[4,128,128]{2,1,0:T(8,128)S(1)}) custom-call(f32[128,128,128]{2,1,0:T(8,128)} %refs_2_.1), custom_call_target="tpu_custom_call" | custom-call | tf_op jit(solution)/shard_map/edges/pallas_call | solution.py:63
  2.3 4.0 %collective-permute-start = (bf16[2,128,128]{2,1,0:T(8,128)(2,1)S(1)}, bf16[2,128,128]{2,1,0:T(8,128)(2,1)S(1)}, u32[]{:S(2)}, u32[]{:S(2)}) collective-permute-start(bf16[2,128,128]{2,1,0:T(8,128)(2,1)S(1)} %get-tuple-element.25), channel_id=1, source_target_pairs={{0,2},{1,3},{2,4},{3,5},{4,6},{5,7},{6,8},{7,9},{8,10},{9,11},{10,... | collective-permute-start | bytes 196616 | tf_op jit(solution)/shard_map/ppermute | solution.py:756
  6.4 1.3 %collective-permute-start.1 = (bf16[2,128,128]{2,1,0:T(8,128)(2,1)S(1)}, bf16[2,128,128]{2,1,0:T(8,128)(2,1)S(1)}, u32[]{:S(2)}, u32[]{:S(2)}) collective-permute-start(bf16[2,128,128]{2,1,0:T(8,128)(2,1)S(1)} %get-tuple-element.26), channel_id=1, source_target_pairs={{2,0},{3,1},{4,2},{5,3},{6,4},{7,5},{8,6},{9,7},{10,8},{11,9},{12,... | collective-permute-start | bytes 196616 | tf_op jit(solution)/shard_map/ppermute | solution.py:756
  7.7 0.2 copy.18
  7.9 0.3 fusion.4
  8.1 0.2 convert_reduce_fusion
  8.3 0.2 select_reduce_fusion.1
  8.6 0.0 collective-permute-done.up_rows.refs_3_
  8.6 4.1 %collective-permute-done.1.low_rows.refs_4_ = bf16[2,128,128]{2,1,0:T(8,128)(2,1)S(1)} collective-permute-done((bf16[2,128,128]{2,1,0:T(8,128)(2,1)S(1)}, bf16[2,128,128]{2,1,0:T(8,128)(2,1)S(1)}, u32[]{:S(2)}, u32[]{:S(2)}) %collective-permute-start.1) | collective-permute-done | bytes 65568 | tf_op jit(solution)/shard_map/ppermute | solution.py:756
  12.8 1.0 %collective-permute-start.2 = (f32[4,144,128]{2,1,0:T(8,128)S(1)}, f32[4,144,128]{2,1,0:T(8,128)S(1)}, u32[]{:S(2)}, u32[]{:S(2)}) collective-permute-start(f32[4,144,128]{2,1,0:T(8,128)S(1)} %frame.1), channel_id=1, source_target_pairs={{0,1},{1,0},{2,3},{3,2},{4,5},{5,4},{6,7},{7,6},{8,9},{9,8},{10,11... | collective-permute-start | bytes 884744 | tf_op jit(solution)/shard_map/ppermute | solution.py:756
  13.8 0.1 pad_add_fusion.refs_0_.flags
  13.9 1.1 %collective-permute-done.2.refs_5_.refs_6_ = f32[4,144,128]{2,1,0:T(8,128)S(1)} collective-permute-done((f32[4,144,128]{2,1,0:T(8,128)S(1)}, f32[4,144,128]{2,1,0:T(8,128)S(1)}, u32[]{:S(2)}, u32[]{:S(2)}) %collective-permute-start.2) | collective-permute-done | bytes 294944 | tf_op jit(solution)/shard_map/ppermute | solution.py:756
  15.0 17.3 %advance.1 = (f32[128,128,128]{2,1,0:T(8,128)}, f32[128,128]{1,0:T(8,128)S(1)}, bf16[128,128]{1,0:T(8,128)(2,1)S(1)}, bf16[4,144,256]{2,1,0:T(8,128)(2,1)}) custom-call(s32[4]{0:T(128)S(1)} %pad_add_fusion.refs_0_.flags, bf16[16,256]{1,0:T(8,128)(2,1)S(1)} %fusion.11.refs_1_, f32[128,128,128]{2,1,0:T(8,128)} %refs_2_.1, ...), custom_call_target="tpu_custom_call" | custom-call | flops 2147483648 | bytes 16777216 | tf_op jit(solution)/shard_map/advance/pallas_call | solution.py:368
  32.3 4.0 %all-to-all-start = ((bf16[4,144,256]{2,1,0:T(8,128)(2,1)}), bf16[4,144,256]{2,1,0:T(8,128)(2,1)S(1)}, u32[]{:S(2)}, u32[]{:S(2)}) async-start(bf16[4,144,256]{2,1,0:T(8,128)(2,1)} %get-tuple-element.29), calls=%async_computation | async-start | bytes 589824 | tf_op jit(solution)/shard_map/all_to_all | solution.py:792
  36.3 1.3 %collective-permute-start.6 = (bf16[128,128]{1,0:T(8,128)(2,1)S(1)}, bf16[128,128]{1,0:T(8,128)(2,1)S(1)}, u32[]{:S(2)}, u32[]{:S(2)}) collective-permute-start(bf16[128,128]{1,0:T(8,128)(2,1)S(1)} %get-tuple-element.34.refs_7_), channel_id=1, source_target_pairs={{24,0},{25,1},{26,2},{27,3},{28,4},{29,5},{30,6},{31,7}} | collective-permute-start | bytes 98312 | tf_op jit(solution)/shard_map/ppermute | solution.py:816
  37.6 0.7 collective-permute-start.7
  38.3 0.7 collective-permute-start.8
  39.0 4.2 %all-to-all-done.slabs = bf16[4,144,256]{2,1,0:T(8,128)(2,1)S(1)} async-done(((bf16[4,144,256]{2,1,0:T(8,128)(2,1)}), bf16[4,144,256]{2,1,0:T(8,128)(2,1)S(1)}, u32[]{:S(2)}, u32[]{:S(2)}) %all-to-all-start) | async-done | bytes 294944 | tf_op jit(solution)/shard_map/all_to_all | solution.py:792
  43.2 0.3 regroup.1
  43.5 0.2 collective-permute-start.3
  43.7 1.3 %collective-permute-start.4 = (bf16[208,256]{1,0:T(8,128)(2,1)S(1)}, bf16[208,256]{1,0:T(8,128)(2,1)S(1)}, u32[]{:S(2)}, u32[]{:S(2)}) collective-permute-start(bf16[208,256]{1,0:T(8,128)(2,1)S(1)} %get-tuple-element.32), channel_id=1, source_target_pairs={{0,2},{1,3},{2,4},{3,5},{4,6},{5,7},{6,0},{7,1},{8,10},{9,11},{10,... | collective-permute-start | bytes 319496 | tf_op jit(solution)/shard_map/ppermute | solution.py:810
  45.0 0.0 collective-permute-done.6.refs_4_
  45.0 4.1 %collective-permute-start.5 = (bf16[208,256]{1,0:T(8,128)(2,1)S(1)}, bf16[208,256]{1,0:T(8,128)(2,1)S(1)}, u32[]{:S(2)}, u32[]{:S(2)}) collective-permute-start(bf16[208,256]{1,0:T(8,128)(2,1)S(1)} %get-tuple-element.33), channel_id=1, source_target_pairs={{0,3},{1,4},{2,5},{3,6},{4,7},{5,0},{6,1},{7,2},{8,11},{9,12},{10,... | collective-permute-start | bytes 319496 | tf_op jit(solution)/shard_map/ppermute | solution.py:810
  49.2 0.1 slice_reduce_fusion.ocean_first
  49.3 0.0 collective-permute-done.7.refs_5_
  49.3 3.2 %collective-permute-done.4.refs_2_ = bf16[208,256]{1,0:T(8,128)(2,1)S(1)} collective-permute-done((bf16[208,256]{1,0:T(8,128)(2,1)S(1)}, bf16[208,256]{1,0:T(8,128)(2,1)S(1)}, u32[]{:S(2)}, u32[]{:S(2)}) %collective-permute-start.4) | collective-permute-done | bytes 106528 | tf_op jit(solution)/shard_map/ppermute | solution.py:810
  52.5 2.1 %collective-permute-done.5.refs_3_ = bf16[208,256]{1,0:T(8,128)(2,1)S(1)} collective-permute-done((bf16[208,256]{1,0:T(8,128)(2,1)S(1)}, bf16[208,256]{1,0:T(8,128)(2,1)S(1)}, u32[]{:S(2)}, u32[]{:S(2)}) %collective-permute-start.5) | collective-permute-done | bytes 106528 | tf_op jit(solution)/shard_map/ppermute | solution.py:810
  54.5 4.1 %regrid.1 = (f32[2,128,128]{2,1,0:T(8,128)S(1)}, f32[128,128]{1,0:T(8,128)S(1)}, bf16[256,128]{1,0:T(8,128)(2,1)S(1)}) custom-call(s32[4]{0:T(128)S(1)} %pad_add_fusion.refs_0_.flags, f32[8]{0:T(128)S(1)} %slice_reduce_fusion.ocean_first, bf16[208,256]{1,0:T(8,128)(2,1)S(1)} %get-tuple-element.30.refs_0_, ...), custom_call_target="tpu_custom_call" | custom-call | flops 2147483648 | bytes 2097152 | tf_op jit(solution)/shard_map/regrid/pallas_call | solution.py:525
  58.6 0.6 collective-permute-start.9
  59.2 0.1 copy.19
  59.4 0.9 %collective-permute-start.13 = (f32[128,128]{1,0:T(8,128)S(1)}, f32[128,128]{1,0:T(8,128)S(1)}, u32[]{:S(2)}, u32[]{:S(2)}) collective-permute-start(f32[128,128]{1,0:T(8,128)S(1)} %get-tuple-element.36.refs_0_), channel_id=1, source_target_pairs={{0,16},{1,17},{2,18},{3,19},{4,20},{5,21},{6,22},{7,23},{8,24},{9,... | collective-permute-start | bytes 196616 | tf_op jit(solution)/shard_map/ppermute | solution.py:800
  60.3 1.0 %collective-permute-start.14 = (f32[128,128]{1,0:T(8,128)S(1)}, f32[128,128]{1,0:T(8,128)S(1)}, u32[]{:S(2)}, u32[]{:S(2)}) collective-permute-start(f32[128,128]{1,0:T(8,128)S(1)} %get-tuple-element.36.refs_0_), channel_id=1, source_target_pairs={{0,24},{1,25},{2,26},{3,27},{4,28},{5,29},{6,30},{7,31},{8,0},{9,1... | collective-permute-start | bytes 196616 | tf_op jit(solution)/shard_map/ppermute | solution.py:800
  61.4 1.5 %collective-permute-done.9.refs_1_ = f32[128,128]{1,0:T(8,128)S(1)} collective-permute-done((f32[128,128]{1,0:T(8,128)S(1)}, f32[128,128]{1,0:T(8,128)S(1)}, u32[]{:S(2)}, u32[]{:S(2)}) %collective-permute-start.9) | collective-permute-done | bytes 65568 | tf_op jit(solution)/shard_map/ppermute | solution.py:800
  62.8 2.0 %collective-permute-start.10 = (f32[2,128,128]{2,1,0:T(8,128)S(1)}, f32[2,128,128]{2,1,0:T(8,128)S(1)}, u32[]{:S(2)}, u32[]{:S(2)}) collective-permute-start(f32[2,128,128]{2,1,0:T(8,128)S(1)} %get-tuple-element.38.refs_3_), channel_id=1, source_target_pairs={{0,24},{1,25},{2,26},{3,27},{4,28},{5,29},{6,30},{7,31}} | collective-permute-start | bytes 393224 | tf_op jit(solution)/shard_map/ppermute | solution.py:822
  64.8 0.7 collective-permute-start.11
  65.5 0.7 collective-permute-start.12
  66.2 0.1 add_select_fusion.refs_4_
  66.3 0.0 collective-permute-done.13.refs_2_
  66.3 0.2 pick.1
  66.5 5.8 %collective-permute-start.15 = (f32[64,128]{1,0:T(8,128)S(1)}, f32[64,128]{1,0:T(8,128)S(1)}, u32[]{:S(2)}, u32[]{:S(2)}) collective-permute-start(f32[64,128]{1,0:T(8,128)S(1)} %get-tuple-element.43), channel_id=1, source_target_pairs={{0,7},{1,0},{2,1},{3,2},{4,3},{5,4},{6,5},{7,6},{8,15},{9,8},{10,9... | collective-permute-start | bytes 98312 | tf_op jit(solution)/shard_map/ppermute | solution.py:810
  72.3 2.3 %collective-permute-start.16 = (f32[64,128]{1,0:T(8,128)S(1)}, f32[64,128]{1,0:T(8,128)S(1)}, u32[]{:S(2)}, u32[]{:S(2)}) collective-permute-start(f32[64,128]{1,0:T(8,128)S(1)} %get-tuple-element.44), channel_id=1, source_target_pairs={{0,6},{1,7},{2,0},{3,1},{4,2},{5,3},{6,4},{7,5},{8,14},{9,15},{10,... | collective-permute-start | bytes 98312 | tf_op jit(solution)/shard_map/ppermute | solution.py:810
  74.6 0.0 collective-permute-done.10.refs_0_
  74.6 1.9 %collective-permute-start.17 = (f32[64,128]{1,0:T(8,128)S(1)}, f32[64,128]{1,0:T(8,128)S(1)}, u32[]{:S(2)}, u32[]{:S(2)}) collective-permute-start(f32[64,128]{1,0:T(8,128)S(1)} %get-tuple-element.45), channel_id=1, source_target_pairs={{0,5},{1,6},{2,7},{3,0},{4,1},{5,2},{6,3},{7,4},{8,13},{9,14},{10,... | collective-permute-start | bytes 98312 | tf_op jit(solution)/shard_map/ppermute | solution.py:810
  76.6 0.0 collective-permute-done.12.refs_2_
  76.6 0.8 %update.1 = (f32[128,128,128]{2,1,0:T(8,128)}, f32[8,128]{1,0:T(8,128)S(1)}) custom-call(s32[4]{0:T(128)S(1)} %pad_add_fusion.refs_0_.flags, f32[128,128,128]{2,1,0:T(8,128)} %get-tuple-element.28.state, f32[2,128,128]{2,1,0:T(8,128)S(1)} %collective-permute-done.10.refs_0_, ...), custom_call_target="tpu_custom_call", output_to_operand_aliasing={{0}: (1, {})} | custom-call | flops 805306368 | bytes 16777216 | tf_op jit(solution)/shard_map/update/pallas_call | solution.py:646
  77.4 0.0 collective-permute-done.15.refs_1_
  77.5 3.3 %collective-permute-done.17.refs_3_ = f32[64,128]{1,0:T(8,128)S(1)} collective-permute-done((f32[64,128]{1,0:T(8,128)S(1)}, f32[64,128]{1,0:T(8,128)S(1)}, u32[]{:S(2)}, u32[]{:S(2)}) %collective-permute-start.17) | collective-permute-done | bytes 32800 | tf_op jit(solution)/shard_map/ppermute | solution.py:810
  80.8 2.4 %returned.1 = f32[128,128]{1,0:T(8,128)} custom-call(s32[4]{0:T(128)S(1)} %pad_add_fusion.refs_0_.flags, f32[64,128]{1,0:T(8,128)S(1)} %get-tuple-element.42.refs_0_, f32[64,128]{1,0:T(8,128)S(1)} %collective-permute-done.15.refs_1_, f32[64,128]{1,0:T(8,128)S(1)} %collective-permute-done.16.refs_2_, f32[64,128]{1,0:T(8,128)S(1)} %collective-permute-done.17.refs_3_, ...), custom_call_target="tpu_custom_call" | custom-call | tf_op jit(solution)/shard_map/returned/pallas_call | solution.py:710
  (27 shorter events, 0.1 us)
Async XLA Ops:
  0.6 7.0 %copy-start.6 = (s32[128,1,2,3]{0,2,3,1:T(2,128)S(1)}, s32[128,1,2,3]{0,2,3,1:T(2,128)}, u32[]{:S(2)}) copy-start(s32[128,1,2,3]{0,2,3,1:T(2,128)} %param.11) | copy-start | bytes 9220
  0.6 13.2 %copy-start.5 = (s32[128,128]{1,0:T(8,128)S(1)}, s32[128,128]{1,0:T(8,128)}, u32[]{:S(2)}) copy-start(s32[128,128]{1,0:T(8,128)} %param.10) | copy-start | bytes 196612
  0.7 14.3 %copy-start.4 = (f32[128,8]{0,1:T(8,128)S(1)}, f32[128,8]{0,1:T(8,128)}, u32[]{:S(2)}) copy-start(f32[128,8]{0,1:T(8,128)} %param.14) | copy-start | bytes 12292
  0.7 14.3 %copy-start.1 = (f32[128,128]{1,0:T(8,128)S(1)}, f32[128,128]{1,0:T(8,128)}, u32[]{:S(2)}) copy-start(f32[128,128]{1,0:T(8,128)} %refs_9_.1) | copy-start | bytes 196612
  0.7 14.3 %copy-start.2 = (f32[128,128]{1,0:T(8,128)S(1)}, f32[128,128]{1,0:T(8,128)}, u32[]{:S(2)}) copy-start(f32[128,128]{1,0:T(8,128)} %refs_10_.1) | copy-start | bytes 196612
  0.7 48.5 %copy-start.3 = (f32[8,128]{1,0:T(8,128)S(1)}, f32[8,128]{1,0:T(8,128)}, u32[]{:S(2)}) copy-start(f32[8,128]{1,0:T(8,128)} %refs_5_.1) | copy-start | bytes 12292
  0.7 53.8 %copy-start = (bf16[32,128,128]{2,1,0:T(8,128)(2,1)S(1)}, bf16[32,128,128]{2,1,0:T(8,128)(2,1)}, u32[]{:S(2)}) copy-start(bf16[32,128,128]{2,1,0:T(8,128)(2,1)} %refs_6_.1) | copy-start | bytes 3145732
  2.3 6.3 %collective-permute-start = (bf16[2,128,128]{2,1,0:T(8,128)(2,1)S(1)}, bf16[2,128,128]{2,1,0:T(8,128)(2,1)S(1)}, u32[]{:S(2)}, u32[]{:S(2)}) collective-permute-start(bf16[2,128,128]{2,1,0:T(8,128)(2,1)S(1)} %get-tuple-element.25), channel_id=1, source_target_pairs={{0,2},{1,3},{2,4},{3,5},{4,6},{5,7},{6,8},{7,9},{8,10},{9,11},{10,... | collective-permute-start | bytes 196616 | tf_op jit(solution)/shard_map/ppermute | solution.py:756
  6.4 6.4 %collective-permute-start.1 = (bf16[2,128,128]{2,1,0:T(8,128)(2,1)S(1)}, bf16[2,128,128]{2,1,0:T(8,128)(2,1)S(1)}, u32[]{:S(2)}, u32[]{:S(2)}) collective-permute-start(bf16[2,128,128]{2,1,0:T(8,128)(2,1)S(1)} %get-tuple-element.26), channel_id=1, source_target_pairs={{2,0},{3,1},{4,2},{5,3},{6,4},{7,5},{8,6},{9,7},{10,8},{11,9},{12,... | collective-permute-start | bytes 196616 | tf_op jit(solution)/shard_map/ppermute | solution.py:756
  12.8 2.2 %collective-permute-start.2 = (f32[4,144,128]{2,1,0:T(8,128)S(1)}, f32[4,144,128]{2,1,0:T(8,128)S(1)}, u32[]{:S(2)}, u32[]{:S(2)}) collective-permute-start(f32[4,144,128]{2,1,0:T(8,128)S(1)} %frame.1), channel_id=1, source_target_pairs={{0,1},{1,0},{2,3},{3,2},{4,5},{5,4},{6,7},{7,6},{8,9},{9,8},{10,11... | collective-permute-start | bytes 884744 | tf_op jit(solution)/shard_map/ppermute | solution.py:756
  32.3 10.8 %all-to-all-start = ((bf16[4,144,256]{2,1,0:T(8,128)(2,1)}), bf16[4,144,256]{2,1,0:T(8,128)(2,1)S(1)}, u32[]{:S(2)}, u32[]{:S(2)}) async-start(bf16[4,144,256]{2,1,0:T(8,128)(2,1)} %get-tuple-element.29), calls=%async_computation | async-start | bytes 589824 | tf_op jit(solution)/shard_map/all_to_all | solution.py:792
  36.3 8.7 %collective-permute-start.6 = (bf16[128,128]{1,0:T(8,128)(2,1)S(1)}, bf16[128,128]{1,0:T(8,128)(2,1)S(1)}, u32[]{:S(2)}, u32[]{:S(2)}) collective-permute-start(bf16[128,128]{1,0:T(8,128)(2,1)S(1)} %get-tuple-element.34.refs_7_), channel_id=1, source_target_pairs={{24,0},{25,1},{26,2},{27,3},{28,4},{29,5},{30,6},{31,7}} | collective-permute-start | bytes 98312 | tf_op jit(solution)/shard_map/ppermute | solution.py:816
  37.6 11.7 %collective-permute-start.7 = (bf16[128,128]{1,0:T(8,128)(2,1)S(1)}, bf16[128,128]{1,0:T(8,128)(2,1)S(1)}, u32[]{:S(2)}, u32[]{:S(2)}) collective-permute-start(bf16[128,128]{1,0:T(8,128)(2,1)S(1)} %get-tuple-element.34.refs_7_), channel_id=1, source_target_pairs={{24,8},{25,9},{26,10},{27,11},{28,12},{29,13},{30,14},{31,15}} | collective-permute-start | bytes 98312 | tf_op jit(solution)/shard_map/ppermute | solution.py:816
  38.3 11.0 %collective-permute-start.8 = (bf16[128,128]{1,0:T(8,128)(2,1)S(1)}, bf16[128,128]{1,0:T(8,128)(2,1)S(1)}, u32[]{:S(2)}, u32[]{:S(2)}) collective-permute-start(bf16[128,128]{1,0:T(8,128)(2,1)S(1)} %get-tuple-element.34.refs_7_), channel_id=1, source_target_pairs={{24,16},{25,17},{26,18},{27,19},{28,20},{29,21},{30,22},{31,23}} | collective-permute-start | bytes 98312 | tf_op jit(solution)/shard_map/ppermute | solution.py:816
  43.5 5.8 %collective-permute-start.3 = (bf16[208,256]{1,0:T(8,128)(2,1)S(1)}, bf16[208,256]{1,0:T(8,128)(2,1)S(1)}, u32[]{:S(2)}, u32[]{:S(2)}) collective-permute-start(bf16[208,256]{1,0:T(8,128)(2,1)S(1)} %get-tuple-element.31), channel_id=1, source_target_pairs={{0,1},{1,2},{2,3},{3,4},{4,5},{5,6},{6,7},{7,0},{8,9},{9,10},{10,1... | collective-permute-start | bytes 319496 | tf_op jit(solution)/shard_map/ppermute | solution.py:810
  43.7 8.7 %collective-permute-start.4 = (bf16[208,256]{1,0:T(8,128)(2,1)S(1)}, bf16[208,256]{1,0:T(8,128)(2,1)S(1)}, u32[]{:S(2)}, u32[]{:S(2)}) collective-permute-start(bf16[208,256]{1,0:T(8,128)(2,1)S(1)} %get-tuple-element.32), channel_id=1, source_target_pairs={{0,2},{1,3},{2,4},{3,5},{4,6},{5,7},{6,0},{7,1},{8,10},{9,11},{10,... | collective-permute-start | bytes 319496 | tf_op jit(solution)/shard_map/ppermute | solution.py:810
  45.0 9.5 %collective-permute-start.5 = (bf16[208,256]{1,0:T(8,128)(2,1)S(1)}, bf16[208,256]{1,0:T(8,128)(2,1)S(1)}, u32[]{:S(2)}, u32[]{:S(2)}) collective-permute-start(bf16[208,256]{1,0:T(8,128)(2,1)S(1)} %get-tuple-element.33), channel_id=1, source_target_pairs={{0,3},{1,4},{2,5},{3,6},{4,7},{5,0},{6,1},{7,2},{8,11},{9,12},{10,... | collective-permute-start | bytes 319496 | tf_op jit(solution)/shard_map/ppermute | solution.py:810
  58.6 4.2 %collective-permute-start.9 = (f32[128,128]{1,0:T(8,128)S(1)}, f32[128,128]{1,0:T(8,128)S(1)}, u32[]{:S(2)}, u32[]{:S(2)}) collective-permute-start(f32[128,128]{1,0:T(8,128)S(1)} %get-tuple-element.36.refs_0_), channel_id=1, source_target_pairs={{0,8},{1,9},{2,10},{3,11},{4,12},{5,13},{6,14},{7,15},{8,16},{9,17... | collective-permute-start | bytes 196616 | tf_op jit(solution)/shard_map/ppermute | solution.py:800
  59.4 6.9 %collective-permute-start.13 = (f32[128,128]{1,0:T(8,128)S(1)}, f32[128,128]{1,0:T(8,128)S(1)}, u32[]{:S(2)}, u32[]{:S(2)}) collective-permute-start(f32[128,128]{1,0:T(8,128)S(1)} %get-tuple-element.36.refs_0_), channel_id=1, source_target_pairs={{0,16},{1,17},{2,18},{3,19},{4,20},{5,21},{6,22},{7,23},{8,24},{9,... | collective-permute-start | bytes 196616 | tf_op jit(solution)/shard_map/ppermute | solution.py:800
  60.3 6.0 %collective-permute-start.14 = (f32[128,128]{1,0:T(8,128)S(1)}, f32[128,128]{1,0:T(8,128)S(1)}, u32[]{:S(2)}, u32[]{:S(2)}) collective-permute-start(f32[128,128]{1,0:T(8,128)S(1)} %get-tuple-element.36.refs_0_), channel_id=1, source_target_pairs={{0,24},{1,25},{2,26},{3,27},{4,28},{5,29},{6,30},{7,31},{8,0},{9,1... | collective-permute-start | bytes 196616 | tf_op jit(solution)/shard_map/ppermute | solution.py:800
  62.8 11.8 %collective-permute-start.10 = (f32[2,128,128]{2,1,0:T(8,128)S(1)}, f32[2,128,128]{2,1,0:T(8,128)S(1)}, u32[]{:S(2)}, u32[]{:S(2)}) collective-permute-start(f32[2,128,128]{2,1,0:T(8,128)S(1)} %get-tuple-element.38.refs_3_), channel_id=1, source_target_pairs={{0,24},{1,25},{2,26},{3,27},{4,28},{5,29},{6,30},{7,31}} | collective-permute-start | bytes 393224 | tf_op jit(solution)/shard_map/ppermute | solution.py:822
  64.8 11.7 %collective-permute-start.11 = (f32[2,128,128]{2,1,0:T(8,128)S(1)}, f32[2,128,128]{2,1,0:T(8,128)S(1)}, u32[]{:S(2)}, u32[]{:S(2)}) collective-permute-start(f32[2,128,128]{2,1,0:T(8,128)S(1)} %get-tuple-element.38.refs_3_), channel_id=1, source_target_pairs={{8,24},{9,25},{10,26},{11,27},{12,28},{13,29},{14,30},{15,31}} | collective-permute-start | bytes 393224 | tf_op jit(solution)/shard_map/ppermute | solution.py:822
  65.5 11.1 %collective-permute-start.12 = (f32[2,128,128]{2,1,0:T(8,128)S(1)}, f32[2,128,128]{2,1,0:T(8,128)S(1)}, u32[]{:S(2)}, u32[]{:S(2)}) collective-permute-start(f32[2,128,128]{2,1,0:T(8,128)S(1)} %get-tuple-element.38.refs_3_), channel_id=1, source_target_pairs={{16,24},{17,25},{18,26},{19,27},{20,28},{21,29},{22,30},{23,31}} | collective-permute-start | bytes 393224 | tf_op jit(solution)/shard_map/ppermute | solution.py:822
  66.5 11.0 %collective-permute-start.15 = (f32[64,128]{1,0:T(8,128)S(1)}, f32[64,128]{1,0:T(8,128)S(1)}, u32[]{:S(2)}, u32[]{:S(2)}) collective-permute-start(f32[64,128]{1,0:T(8,128)S(1)} %get-tuple-element.43), channel_id=1, source_target_pairs={{0,7},{1,0},{2,1},{3,2},{4,3},{5,4},{6,5},{7,6},{8,15},{9,8},{10,9... | collective-permute-start | bytes 98312 | tf_op jit(solution)/shard_map/ppermute | solution.py:810
  72.3 5.2 %collective-permute-start.16 = (f32[64,128]{1,0:T(8,128)S(1)}, f32[64,128]{1,0:T(8,128)S(1)}, u32[]{:S(2)}, u32[]{:S(2)}) collective-permute-start(f32[64,128]{1,0:T(8,128)S(1)} %get-tuple-element.44), channel_id=1, source_target_pairs={{0,6},{1,7},{2,0},{3,1},{4,2},{5,3},{6,4},{7,5},{8,14},{9,15},{10,... | collective-permute-start | bytes 98312 | tf_op jit(solution)/shard_map/ppermute | solution.py:810
  74.6 6.1 %collective-permute-start.17 = (f32[64,128]{1,0:T(8,128)S(1)}, f32[64,128]{1,0:T(8,128)S(1)}, u32[]{:S(2)}, u32[]{:S(2)}) collective-permute-start(f32[64,128]{1,0:T(8,128)S(1)} %get-tuple-element.45), channel_id=1, source_target_pairs={{0,5},{1,6},{2,7},{3,0},{4,1},{5,2},{6,3},{7,4},{8,13},{9,14},{10,... | collective-permute-start | bytes 98312 | tf_op jit(solution)/shard_map/ppermute | solution.py:810

commit v13 on v12

--- a/solution.py
+++ b/solution.py
@@ -106,12 +106,12 @@
     (flags, labels, state, up_rows, low_rows, left_in, right_in, own_sides) = refs[:8]
     (mask, mix_atm, mix_ocn, flux_map) = refs[8:12]
     out, surface, sea_copy, packed = refs[12:16]
-    (values, moved, halo_moved, smooth, pairs, mixed, later_smooth, later_pairs, later_mixed) = refs[16:25]
-    (weights, flux_weights, flux_pairs, fluxes, staged, top, in_sems, out_sems) = refs[25:]
+    (values, moved, halo_moved, pairs, mixed, later_pairs, later_mixed) = refs[16:23]
+    (weights, flux_weights, flux_pairs, fluxes, staged, top, in_sems, out_sems) = refs[23:]
     left_cols = left_in.at[left_at : left_at + 2]
     right_cols = right_in.at[right_at : right_at + 2]
-    first = (smooth, pairs, mixed)
-    second = (later_smooth, later_pairs, later_mixed)
+    first = (pairs, mixed)
+    second = (later_pairs, later_mixed)
     rows, cols, levels = state.shape
     chunks = rows // CHUNK
     inner = pl.ds(EDGE, cols)
@@ -172,8 +172,7 @@
 
     def stage(refs, row, total):
         line = SMOOTHING * total
-        refs[0][row] = line
-        refs[1][row * cols : (row + 1) * cols, :] = side_by_side(line)
+        refs[0][row * cols : (row + 1) * cols, :] = side_by_side(line)
 
     def stage_rows(refs, ref, start, count):
         for row in range(count):
@@ -193,11 +192,13 @@
         top[...] = jnp.where(lanes // CHUNK == q, turned, top[...])
 
     def mix_rows(refs, count):
-        refs[2][: count * cols, :] = dot_nn(refs[1][: count * cols, :], weights[...])
+        refs[1][: count * cols, :] = dot_nn(refs[0][: count * cols, :], weights[...])
 
     def finish(refs, row):
-        part = refs[2][row * cols : (row + 1) * cols, :]
-        return refs[0][row] + PHYSICS * jnp.tanh(part[:, :levels] + part[:, levels:])
+        part = refs[1][row * cols : (row + 1) * cols, :]
+        pair = refs[0][row * cols : (row + 1) * cols, :].astype(F32)
+        change = PHYSICS * jnp.tanh(part[:, :levels] + part[:, levels:])
+        return (pair[:, :levels] + pair[:, levels:]) + change
 
     @pl.when(jnp.logical_not(ocean))
     def atmosphere():
@@ -379,10 +380,8 @@
             pltpu.VMEM((rows + 4, cols + 2 * EDGE, levels), F32),
             pltpu.VMEM((rows + 2, cols + 2 * EDGE, levels), F32),
             pltpu.VMEM((2, rows, levels), F32),
-            pltpu.VMEM((CHUNK, cols, levels), F32),
             pltpu.VMEM((CHUNK * cols, 2 * levels), BF16),
             pltpu.VMEM((CHUNK * cols, 2 * levels), F32),
-            pltpu.VMEM((CHUNK, cols, levels), F32),
             pltpu.VMEM((CHUNK * cols, 2 * levels), BF16),
             pltpu.VMEM((CHUNK * cols, 2 * levels), F32),
             pltpu.VMEM((2 * levels, 2 * levels), BF16),

time: 83.6 us -> 84.6 us (1.012)
  Pallas kernels: 26.8 us -> 27.8 us
    pallas_call x1, Pallas kernels: 17.3 us -> 18.3 us  [advance(): pl.pallas_call(functools.partial(advance_kernel, comp_count, left_at, rig...]
where the time goes in v13:
time: 84.6 us; the launch traced here: 84.1 us
  starting transfers between devices  34.6 us (41%)
  Pallas kernels  27.8 us (33%)
  waiting for transfers between devices  19.5 us (23%)
  between operations  1.03 us (1%)
    pallas_call x1, Pallas kernels, advance(): pl.pallas_call(functools.partial(advance_kernel, comp_count, left_at, rig...  18.3 us
    ppermute x6, starting transfers between devices, over_tiles(): return lax.ppermute(value, AXES, pairs)  15.7 us
    ppermute x6, waiting for transfers between devices, over_tiles(): return lax.ppermute(value, AXES, pairs)  8.53 us
    ppermute x3, starting transfers between devices, band_shift(): return lax.ppermute(value, AXES, pairs)  6.35 us
    ppermute x3, waiting for transfers between devices, band_shift(): return lax.ppermute(value, AXES, pairs)  5.26 us
    all_to_all x1, waiting for transfers between devices, over_comp(): lax.all_to_all(value, 'comp', split_axis=0, concat_axis=0, tiled=True)  4.21 us
    pallas_call x1, Pallas kernels, regrid(): pl.pallas_call(functools.partial(regrid_body, count, comp_count), out_sha...  4.1 us
    all_to_all x1, starting transfers between devices, over_comp(): lax.all_to_all(value, 'comp', split_axis=0, concat_axis=0, tiled=True)  4 us
  transfers between devices with their start and end apart: 19, of which 7 were waited for; matrix products, arithmetic and copies ran while one was open for 1% of the time, Pallas kernels for 2%

profile of v13, /device:TPU:1, one launch (start us, length us, event | category | flops | bytes accessed | tf_op | source)
XLA Modules:
  0.0 84.1 jit_solution(818978442074110243)
XLA Ops:
  0.7 1.6 %edges.1 = (bf16[2,128,128]{2,1,0:T(8,128)(2,1)S(1)}, bf16[2,128,128]{2,1,0:T(8,128)(2,1)S(1)}, f32[4,128,128]{2,1,0:T(8,128)S(1)}) custom-call(f32[128,128,128]{2,1,0:T(8,128)} %refs_2_.1), custom_call_target="tpu_custom_call" | custom-call | tf_op jit(solution)/shard_map/edges/pallas_call | solution.py:63
  2.3 4.0 %collective-permute-start = (bf16[2,128,128]{2,1,0:T(8,128)(2,1)S(1)}, bf16[2,128,128]{2,1,0:T(8,128)(2,1)S(1)}, u32[]{:S(2)}, u32[]{:S(2)}) collective-permute-start(bf16[2,128,128]{2,1,0:T(8,128)(2,1)S(1)} %get-tuple-element.25), channel_id=1, source_target_pairs={{0,2},{1,3},{2,4},{3,5},{4,6},{5,7},{6,8},{7,9},{8,10},{9,11},{10,... | collective-permute-start | bytes 196616 | tf_op jit(solution)/shard_map/ppermute | solution.py:755
  6.4 1.3 %collective-permute-start.1 = (bf16[2,128,128]{2,1,0:T(8,128)(2,1)S(1)}, bf16[2,128,128]{2,1,0:T(8,128)(2,1)S(1)}, u32[]{:S(2)}, u32[]{:S(2)}) collective-permute-start(bf16[2,128,128]{2,1,0:T(8,128)(2,1)S(1)} %get-tuple-element.26), channel_id=1, source_target_pairs={{2,0},{3,1},{4,2},{5,3},{6,4},{7,5},{8,6},{9,7},{10,8},{11,9},{12,... | collective-permute-start | bytes 196616 | tf_op jit(solution)/shard_map/ppermute | solution.py:755
  7.7 0.2 copy.18
  7.9 0.3 fusion.4
  8.1 0.2 convert_reduce_fusion
  8.3 0.2 select_reduce_fusion.1
  8.6 4.1 %collective-permute-done.1.low_rows.refs_4_ = bf16[2,128,128]{2,1,0:T(8,128)(2,1)S(1)} collective-permute-done((bf16[2,128,128]{2,1,0:T(8,128)(2,1)S(1)}, bf16[2,128,128]{2,1,0:T(8,128)(2,1)S(1)}, u32[]{:S(2)}, u32[]{:S(2)}) %collective-permute-start.1) | collective-permute-done | bytes 65568 | tf_op jit(solution)/shard_map/ppermute | solution.py:755
  12.8 1.0 %collective-permute-start.2 = (f32[4,144,128]{2,1,0:T(8,128)S(1)}, f32[4,144,128]{2,1,0:T(8,128)S(1)}, u32[]{:S(2)}, u32[]{:S(2)}) collective-permute-start(f32[4,144,128]{2,1,0:T(8,128)S(1)} %frame.1), channel_id=1, source_target_pairs={{0,1},{1,0},{2,3},{3,2},{4,5},{5,4},{6,7},{7,6},{8,9},{9,8},{10,11... | collective-permute-start | bytes 884744 | tf_op jit(solution)/shard_map/ppermute | solution.py:755
  13.8 0.1 pad_add_fusion.refs_0_.flags
  13.9 1.1 %collective-permute-done.2.refs_5_.refs_6_ = f32[4,144,128]{2,1,0:T(8,128)S(1)} collective-permute-done((f32[4,144,128]{2,1,0:T(8,128)S(1)}, f32[4,144,128]{2,1,0:T(8,128)S(1)}, u32[]{:S(2)}, u32[]{:S(2)}) %collective-permute-start.2) | collective-permute-done | bytes 294944 | tf_op jit(solution)/shard_map/ppermute | solution.py:755
  15.0 18.3 %advance.1 = (f32[128,128,128]{2,1,0:T(8,128)}, f32[128,128]{1,0:T(8,128)S(1)}, bf16[128,128]{1,0:T(8,128)(2,1)S(1)}, bf16[4,144,256]{2,1,0:T(8,128)(2,1)}) custom-call(s32[4]{0:T(128)S(1)} %pad_add_fusion.refs_0_.flags, bf16[16,256]{1,0:T(8,128)(2,1)S(1)} %fusion.11.refs_1_, f32[128,128,128]{2,1,0:T(8,128)} %refs_2_.1, ...), custom_call_target="tpu_custom_call" | custom-call | flops 2147483648 | bytes 16777216 | tf_op jit(solution)/shard_map/advance/pallas_call | solution.py:369
  33.3 4.0 %all-to-all-start = ((bf16[4,144,256]{2,1,0:T(8,128)(2,1)}), bf16[4,144,256]{2,1,0:T(8,128)(2,1)S(1)}, u32[]{:S(2)}, u32[]{:S(2)}) async-start(bf16[4,144,256]{2,1,0:T(8,128)(2,1)} %get-tuple-element.29), calls=%async_computation | async-start | bytes 589824 | tf_op jit(solution)/shard_map/all_to_all | solution.py:791
  37.3 1.3 %collective-permute-start.6 = (bf16[128,128]{1,0:T(8,128)(2,1)S(1)}, bf16[128,128]{1,0:T(8,128)(2,1)S(1)}, u32[]{:S(2)}, u32[]{:S(2)}) collective-permute-start(bf16[128,128]{1,0:T(8,128)(2,1)S(1)} %get-tuple-element.34.refs_7_), channel_id=1, source_target_pairs={{24,0},{25,1},{26,2},{27,3},{28,4},{29,5},{30,6},{31,7}} | collective-permute-start | bytes 98312 | tf_op jit(solution)/shard_map/ppermute | solution.py:815
  38.6 0.7 collective-permute-start.7
  39.2 0.7 collective-permute-start.8
  39.9 4.2 %all-to-all-done.slabs = bf16[4,144,256]{2,1,0:T(8,128)(2,1)S(1)} async-done(((bf16[4,144,256]{2,1,0:T(8,128)(2,1)}), bf16[4,144,256]{2,1,0:T(8,128)(2,1)S(1)}, u32[]{:S(2)}, u32[]{:S(2)}) %all-to-all-start) | async-done | bytes 294944 | tf_op jit(solution)/shard_map/all_to_all | solution.py:791
  44.1 0.3 regroup.1
  44.4 0.2 collective-permute-start.3
  44.6 1.3 %collective-permute-start.4 = (bf16[208,256]{1,0:T(8,128)(2,1)S(1)}, bf16[208,256]{1,0:T(8,128)(2,1)S(1)}, u32[]{:S(2)}, u32[]{:S(2)}) collective-permute-start(bf16[208,256]{1,0:T(8,128)(2,1)S(1)} %get-tuple-element.32), channel_id=1, source_target_pairs={{0,2},{1,3},{2,4},{3,5},{4,6},{5,7},{6,0},{7,1},{8,10},{9,11},{10,... | collective-permute-start | bytes 319496 | tf_op jit(solution)/shard_map/ppermute | solution.py:809
  45.9 0.0 collective-permute-done.6.refs_4_
  45.9 4.2 %collective-permute-start.5 = (bf16[208,256]{1,0:T(8,128)(2,1)S(1)}, bf16[208,256]{1,0:T(8,128)(2,1)S(1)}, u32[]{:S(2)}, u32[]{:S(2)}) collective-permute-start(bf16[208,256]{1,0:T(8,128)(2,1)S(1)} %get-tuple-element.33), channel_id=1, source_target_pairs={{0,3},{1,4},{2,5},{3,6},{4,7},{5,0},{6,1},{7,2},{8,11},{9,12},{10,... | collective-permute-start | bytes 319496 | tf_op jit(solution)/shard_map/ppermute | solution.py:809
  50.1 0.1 slice_reduce_fusion.ocean_first
  50.2 0.0 collective-permute-done.7.refs_5_
  50.2 0.0 collective-permute-done.8.refs_6_
  50.2 3.2 %collective-permute-done.4.refs_2_ = bf16[208,256]{1,0:T(8,128)(2,1)S(1)} collective-permute-done((bf16[208,256]{1,0:T(8,128)(2,1)S(1)}, bf16[208,256]{1,0:T(8,128)(2,1)S(1)}, u32[]{:S(2)}, u32[]{:S(2)}) %collective-permute-start.4) | collective-permute-done | bytes 106528 | tf_op jit(solution)/shard_map/ppermute | solution.py:809
  53.4 2.1 %collective-permute-done.5.refs_3_ = bf16[208,256]{1,0:T(8,128)(2,1)S(1)} collective-permute-done((bf16[208,256]{1,0:T(8,128)(2,1)S(1)}, bf16[208,256]{1,0:T(8,128)(2,1)S(1)}, u32[]{:S(2)}, u32[]{:S(2)}) %collective-permute-start.5) | collective-permute-done | bytes 106528 | tf_op jit(solution)/shard_map/ppermute | solution.py:809
  55.4 4.1 %regrid.1 = (f32[2,128,128]{2,1,0:T(8,128)S(1)}, f32[128,128]{1,0:T(8,128)S(1)}, bf16[256,128]{1,0:T(8,128)(2,1)S(1)}) custom-call(s32[4]{0:T(128)S(1)} %pad_add_fusion.refs_0_.flags, f32[8]{0:T(128)S(1)} %slice_reduce_fusion.ocean_first, bf16[208,256]{1,0:T(8,128)(2,1)S(1)} %get-tuple-element.30.refs_0_, ...), custom_call_target="tpu_custom_call" | custom-call | flops 2147483648 | bytes 2097152 | tf_op jit(solution)/shard_map/regrid/pallas_call | solution.py:524
  59.6 0.6 collective-permute-start.9
  60.1 0.1 copy.19
  60.3 0.9 %collective-permute-start.13 = (f32[128,128]{1,0:T(8,128)S(1)}, f32[128,128]{1,0:T(8,128)S(1)}, u32[]{:S(2)}, u32[]{:S(2)}) collective-permute-start(f32[128,128]{1,0:T(8,128)S(1)} %get-tuple-element.36.refs_0_), channel_id=1, source_target_pairs={{0,16},{1,17},{2,18},{3,19},{4,20},{5,21},{6,22},{7,23},{8,24},{9,... | collective-permute-start | bytes 196616 | tf_op jit(solution)/shard_map/ppermute | solution.py:799
  61.2 1.0 %collective-permute-start.14 = (f32[128,128]{1,0:T(8,128)S(1)}, f32[128,128]{1,0:T(8,128)S(1)}, u32[]{:S(2)}, u32[]{:S(2)}) collective-permute-start(f32[128,128]{1,0:T(8,128)S(1)} %get-tuple-element.36.refs_0_), channel_id=1, source_target_pairs={{0,24},{1,25},{2,26},{3,27},{4,28},{5,29},{6,30},{7,31},{8,0},{9,1... | collective-permute-start | bytes 196616 | tf_op jit(solution)/shard_map/ppermute | solution.py:799
  62.3 1.5 %collective-permute-done.9.refs_1_ = f32[128,128]{1,0:T(8,128)S(1)} collective-permute-done((f32[128,128]{1,0:T(8,128)S(1)}, f32[128,128]{1,0:T(8,128)S(1)}, u32[]{:S(2)}, u32[]{:S(2)}) %collective-permute-start.9) | collective-permute-done | bytes 65568 | tf_op jit(solution)/shard_map/ppermute | solution.py:799
  63.7 2.0 %collective-permute-start.10 = (f32[2,128,128]{2,1,0:T(8,128)S(1)}, f32[2,128,128]{2,1,0:T(8,128)S(1)}, u32[]{:S(2)}, u32[]{:S(2)}) collective-permute-start(f32[2,128,128]{2,1,0:T(8,128)S(1)} %get-tuple-element.38.refs_3_), channel_id=1, source_target_pairs={{0,24},{1,25},{2,26},{3,27},{4,28},{5,29},{6,30},{7,31}} | collective-permute-start | bytes 393224 | tf_op jit(solution)/shard_map/ppermute | solution.py:821
  65.8 0.7 collective-permute-start.11
  66.4 0.7 collective-permute-start.12
  67.1 0.1 add_select_fusion.refs_4_
  67.2 0.0 collective-permute-done.14.refs_3_
  67.2 0.2 pick.1
  67.4 5.8 %collective-permute-start.15 = (f32[64,128]{1,0:T(8,128)S(1)}, f32[64,128]{1,0:T(8,128)S(1)}, u32[]{:S(2)}, u32[]{:S(2)}) collective-permute-start(f32[64,128]{1,0:T(8,128)S(1)} %get-tuple-element.43), channel_id=1, source_target_pairs={{0,7},{1,0},{2,1},{3,2},{4,3},{5,4},{6,5},{7,6},{8,15},{9,8},{10,9... | collective-permute-start | bytes 98312 | tf_op jit(solution)/shard_map/ppermute | solution.py:809
  73.2 2.3 %collective-permute-start.16 = (f32[64,128]{1,0:T(8,128)S(1)}, f32[64,128]{1,0:T(8,128)S(1)}, u32[]{:S(2)}, u32[]{:S(2)}) collective-permute-start(f32[64,128]{1,0:T(8,128)S(1)} %get-tuple-element.44), channel_id=1, source_target_pairs={{0,6},{1,7},{2,0},{3,1},{4,2},{5,3},{6,4},{7,5},{8,14},{9,15},{10,... | collective-permute-start | bytes 98312 | tf_op jit(solution)/shard_map/ppermute | solution.py:809
  75.6 0.0 collective-permute-done.10.refs_0_
  75.6 1.9 %collective-permute-start.17 = (f32[64,128]{1,0:T(8,128)S(1)}, f32[64,128]{1,0:T(8,128)S(1)}, u32[]{:S(2)}, u32[]{:S(2)}) collective-permute-start(f32[64,128]{1,0:T(8,128)S(1)} %get-tuple-element.45), channel_id=1, source_target_pairs={{0,5},{1,6},{2,7},{3,0},{4,1},{5,2},{6,3},{7,4},{8,13},{9,14},{10,... | collective-permute-start | bytes 98312 | tf_op jit(solution)/shard_map/ppermute | solution.py:809
  77.5 0.0 collective-permute-done.11.refs_1_
  77.5 0.8 update.1
  78.4 0.0 collective-permute-done.15.refs_1_
  78.4 3.3 %collective-permute-done.17.refs_3_ = f32[64,128]{1,0:T(8,128)S(1)} collective-permute-done((f32[64,128]{1,0:T(8,128)S(1)}, f32[64,128]{1,0:T(8,128)S(1)}, u32[]{:S(2)}, u32[]{:S(2)}) %collective-permute-start.17) | collective-permute-done | bytes 32800 | tf_op jit(solution)/shard_map/ppermute | solution.py:809
  81.7 2.4 %returned.1 = f32[128,128]{1,0:T(8,128)} custom-call(s32[4]{0:T(128)S(1)} %pad_add_fusion.refs_0_.flags, f32[64,128]{1,0:T(8,128)S(1)} %get-tuple-element.42.refs_0_, f32[64,128]{1,0:T(8,128)S(1)} %collective-permute-done.15.refs_1_, f32[64,128]{1,0:T(8,128)S(1)} %collective-permute-done.16.refs_2_, f32[64,128]{1,0:T(8,128)S(1)} %collective-permute-done.17.refs_3_, ...), custom_call_target="tpu_custom_call" | custom-call | tf_op jit(solution)/shard_map/returned/pallas_call | solution.py:709
  (27 shorter events, 0.1 us)
Async XLA Ops:
  0.6 7.0 %copy-start.6 = (s32[128,1,2,3]{0,2,3,1:T(2,128)S(1)}, s32[128,1,2,3]{0,2,3,1:T(2,128)}, u32[]{:S(2)}) copy-start(s32[128,1,2,3]{0,2,3,1:T(2,128)} %param.11) | copy-start | bytes 9220
  0.6 13.2 %copy-start.5 = (s32[128,128]{1,0:T(8,128)S(1)}, s32[128,128]{1,0:T(8,128)}, u32[]{:S(2)}) copy-start(s32[128,128]{1,0:T(8,128)} %param.10) | copy-start | bytes 196612
  0.7 14.3 %copy-start.4 = (f32[128,8]{0,1:T(8,128)S(1)}, f32[128,8]{0,1:T(8,128)}, u32[]{:S(2)}) copy-start(f32[128,8]{0,1:T(8,128)} %param.14) | copy-start | bytes 12292
  0.7 14.3 %copy-start.1 = (f32[128,128]{1,0:T(8,128)S(1)}, f32[128,128]{1,0:T(8,128)}, u32[]{:S(2)}) copy-start(f32[128,128]{1,0:T(8,128)} %refs_9_.1) | copy-start | bytes 196612
  0.7 14.3 %copy-start.2 = (f32[128,128]{1,0:T(8,128)S(1)}, f32[128,128]{1,0:T(8,128)}, u32[]{:S(2)}) copy-start(f32[128,128]{1,0:T(8,128)} %refs_10_.1) | copy-start | bytes 196612
  0.7 49.4 %copy-start.3 = (f32[8,128]{1,0:T(8,128)S(1)}, f32[8,128]{1,0:T(8,128)}, u32[]{:S(2)}) copy-start(f32[8,128]{1,0:T(8,128)} %refs_5_.1) | copy-start | bytes 12292
  0.7 54.8 %copy-start = (bf16[32,128,128]{2,1,0:T(8,128)(2,1)S(1)}, bf16[32,128,128]{2,1,0:T(8,128)(2,1)}, u32[]{:S(2)}) copy-start(bf16[32,128,128]{2,1,0:T(8,128)(2,1)} %refs_6_.1) | copy-start | bytes 3145732
  2.3 6.3 %collective-permute-start = (bf16[2,128,128]{2,1,0:T(8,128)(2,1)S(1)}, bf16[2,128,128]{2,1,0:T(8,128)(2,1)S(1)}, u32[]{:S(2)}, u32[]{:S(2)}) collective-permute-start(bf16[2,128,128]{2,1,0:T(8,128)(2,1)S(1)} %get-tuple-element.25), channel_id=1, source_target_pairs={{0,2},{1,3},{2,4},{3,5},{4,6},{5,7},{6,8},{7,9},{8,10},{9,11},{10,... | collective-permute-start | bytes 196616 | tf_op jit(solution)/shard_map/ppermute | solution.py:755
  6.4 6.4 %collective-permute-start.1 = (bf16[2,128,128]{2,1,0:T(8,128)(2,1)S(1)}, bf16[2,128,128]{2,1,0:T(8,128)(2,1)S(1)}, u32[]{:S(2)}, u32[]{:S(2)}) collective-permute-start(bf16[2,128,128]{2,1,0:T(8,128)(2,1)S(1)} %get-tuple-element.26), channel_id=1, source_target_pairs={{2,0},{3,1},{4,2},{5,3},{6,4},{7,5},{8,6},{9,7},{10,8},{11,9},{12,... | collective-permute-start | bytes 196616 | tf_op jit(solution)/shard_map/ppermute | solution.py:755
  12.8 2.2 %collective-permute-start.2 = (f32[4,144,128]{2,1,0:T(8,128)S(1)}, f32[4,144,128]{2,1,0:T(8,128)S(1)}, u32[]{:S(2)}, u32[]{:S(2)}) collective-permute-start(f32[4,144,128]{2,1,0:T(8,128)S(1)} %frame.1), channel_id=1, source_target_pairs={{0,1},{1,0},{2,3},{3,2},{4,5},{5,4},{6,7},{7,6},{8,9},{9,8},{10,11... | collective-permute-start | bytes 884744 | tf_op jit(solution)/shard_map/ppermute | solution.py:755
  33.3 10.8 %all-to-all-start = ((bf16[4,144,256]{2,1,0:T(8,128)(2,1)}), bf16[4,144,256]{2,1,0:T(8,128)(2,1)S(1)}, u32[]{:S(2)}, u32[]{:S(2)}) async-start(bf16[4,144,256]{2,1,0:T(8,128)(2,1)} %get-tuple-element.29), calls=%async_computation | async-start | bytes 589824 | tf_op jit(solution)/shard_map/all_to_all | solution.py:791
  37.3 8.7 %collective-permute-start.6 = (bf16[128,128]{1,0:T(8,128)(2,1)S(1)}, bf16[128,128]{1,0:T(8,128)(2,1)S(1)}, u32[]{:S(2)}, u32[]{:S(2)}) collective-permute-start(bf16[128,128]{1,0:T(8,128)(2,1)S(1)} %get-tuple-element.34.refs_7_), channel_id=1, source_target_pairs={{24,0},{25,1},{26,2},{27,3},{28,4},{29,5},{30,6},{31,7}} | collective-permute-start | bytes 98312 | tf_op jit(solution)/shard_map/ppermute | solution.py:815
  38.6 11.7 %collective-permute-start.7 = (bf16[128,128]{1,0:T(8,128)(2,1)S(1)}, bf16[128,128]{1,0:T(8,128)(2,1)S(1)}, u32[]{:S(2)}, u32[]{:S(2)}) collective-permute-start(bf16[128,128]{1,0:T(8,128)(2,1)S(1)} %get-tuple-element.34.refs_7_), channel_id=1, source_target_pairs={{24,8},{25,9},{26,10},{27,11},{28,12},{29,13},{30,14},{31,15}} | collective-permute-start | bytes 98312 | tf_op jit(solution)/shard_map/ppermute | solution.py:815
  39.2 11.0 %collective-permute-start.8 = (bf16[128,128]{1,0:T(8,128)(2,1)S(1)}, bf16[128,128]{1,0:T(8,128)(2,1)S(1)}, u32[]{:S(2)}, u32[]{:S(2)}) collective-permute-start(bf16[128,128]{1,0:T(8,128)(2,1)S(1)} %get-tuple-element.34.refs_7_), channel_id=1, source_target_pairs={{24,16},{25,17},{26,18},{27,19},{28,20},{29,21},{30,22},{31,23}} | collective-permute-start | bytes 98312 | tf_op jit(solution)/shard_map/ppermute | solution.py:815
  44.4 5.8 %collective-permute-start.3 = (bf16[208,256]{1,0:T(8,128)(2,1)S(1)}, bf16[208,256]{1,0:T(8,128)(2,1)S(1)}, u32[]{:S(2)}, u32[]{:S(2)}) collective-permute-start(bf16[208,256]{1,0:T(8,128)(2,1)S(1)} %get-tuple-element.31), channel_id=1, source_target_pairs={{0,1},{1,2},{2,3},{3,4},{4,5},{5,6},{6,7},{7,0},{8,9},{9,10},{10,1... | collective-permute-start | bytes 319496 | tf_op jit(solution)/shard_map/ppermute | solution.py:809
  44.6 8.8 %collective-permute-start.4 = (bf16[208,256]{1,0:T(8,128)(2,1)S(1)}, bf16[208,256]{1,0:T(8,128)(2,1)S(1)}, u32[]{:S(2)}, u32[]{:S(2)}) collective-permute-start(bf16[208,256]{1,0:T(8,128)(2,1)S(1)} %get-tuple-element.32), channel_id=1, source_target_pairs={{0,2},{1,3},{2,4},{3,5},{4,6},{5,7},{6,0},{7,1},{8,10},{9,11},{10,... | collective-permute-start | bytes 319496 | tf_op jit(solution)/shard_map/ppermute | solution.py:809
  45.9 9.5 %collective-permute-start.5 = (bf16[208,256]{1,0:T(8,128)(2,1)S(1)}, bf16[208,256]{1,0:T(8,128)(2,1)S(1)}, u32[]{:S(2)}, u32[]{:S(2)}) collective-permute-start(bf16[208,256]{1,0:T(8,128)(2,1)S(1)} %get-tuple-element.33), channel_id=1, source_target_pairs={{0,3},{1,4},{2,5},{3,6},{4,7},{5,0},{6,1},{7,2},{8,11},{9,12},{10,... | collective-permute-start | bytes 319496 | tf_op jit(solution)/shard_map/ppermute | solution.py:809
  59.6 4.2 %collective-permute-start.9 = (f32[128,128]{1,0:T(8,128)S(1)}, f32[128,128]{1,0:T(8,128)S(1)}, u32[]{:S(2)}, u32[]{:S(2)}) collective-permute-start(f32[128,128]{1,0:T(8,128)S(1)} %get-tuple-element.36.refs_0_), channel_id=1, source_target_pairs={{0,8},{1,9},{2,10},{3,11},{4,12},{5,13},{6,14},{7,15},{8,16},{9,17... | collective-permute-start | bytes 196616 | tf_op jit(solution)/shard_map/ppermute | solution.py:799
  60.3 6.9 %collective-permute-start.13 = (f32[128,128]{1,0:T(8,128)S(1)}, f32[128,128]{1,0:T(8,128)S(1)}, u32[]{:S(2)}, u32[]{:S(2)}) collective-permute-start(f32[128,128]{1,0:T(8,128)S(1)} %get-tuple-element.36.refs_0_), channel_id=1, source_target_pairs={{0,16},{1,17},{2,18},{3,19},{4,20},{5,21},{6,22},{7,23},{8,24},{9,... | collective-permute-start | bytes 196616 | tf_op jit(solution)/shard_map/ppermute | solution.py:799
  61.2 6.0 %collective-permute-start.14 = (f32[128,128]{1,0:T(8,128)S(1)}, f32[128,128]{1,0:T(8,128)S(1)}, u32[]{:S(2)}, u32[]{:S(2)}) collective-permute-start(f32[128,128]{1,0:T(8,128)S(1)} %get-tuple-element.36.refs_0_), channel_id=1, source_target_pairs={{0,24},{1,25},{2,26},{3,27},{4,28},{5,29},{6,30},{7,31},{8,0},{9,1... | collective-permute-start | bytes 196616 | tf_op jit(solution)/shard_map/ppermute | solution.py:799
  63.7 11.8 %collective-permute-start.10 = (f32[2,128,128]{2,1,0:T(8,128)S(1)}, f32[2,128,128]{2,1,0:T(8,128)S(1)}, u32[]{:S(2)}, u32[]{:S(2)}) collective-permute-start(f32[2,128,128]{2,1,0:T(8,128)S(1)} %get-tuple-element.38.refs_3_), channel_id=1, source_target_pairs={{0,24},{1,25},{2,26},{3,27},{4,28},{5,29},{6,30},{7,31}} | collective-permute-start | bytes 393224 | tf_op jit(solution)/shard_map/ppermute | solution.py:821
  65.8 11.7 %collective-permute-start.11 = (f32[2,128,128]{2,1,0:T(8,128)S(1)}, f32[2,128,128]{2,1,0:T(8,128)S(1)}, u32[]{:S(2)}, u32[]{:S(2)}) collective-permute-start(f32[2,128,128]{2,1,0:T(8,128)S(1)} %get-tuple-element.38.refs_3_), channel_id=1, source_target_pairs={{8,24},{9,25},{10,26},{11,27},{12,28},{13,29},{14,30},{15,31}} | collective-permute-start | bytes 393224 | tf_op jit(solution)/shard_map/ppermute | solution.py:821
  66.4 11.1 %collective-permute-start.12 = (f32[2,128,128]{2,1,0:T(8,128)S(1)}, f32[2,128,128]{2,1,0:T(8,128)S(1)}, u32[]{:S(2)}, u32[]{:S(2)}) collective-permute-start(f32[2,128,128]{2,1,0:T(8,128)S(1)} %get-tuple-element.38.refs_3_), channel_id=1, source_target_pairs={{16,24},{17,25},{18,26},{19,27},{20,28},{21,29},{22,30},{23,31}} | collective-permute-start | bytes 393224 | tf_op jit(solution)/shard_map/ppermute | solution.py:821
  67.4 11.0 %collective-permute-start.15 = (f32[64,128]{1,0:T(8,128)S(1)}, f32[64,128]{1,0:T(8,128)S(1)}, u32[]{:S(2)}, u32[]{:S(2)}) collective-permute-start(f32[64,128]{1,0:T(8,128)S(1)} %get-tuple-element.43), channel_id=1, source_target_pairs={{0,7},{1,0},{2,1},{3,2},{4,3},{5,4},{6,5},{7,6},{8,15},{9,8},{10,9... | collective-permute-start | bytes 98312 | tf_op jit(solution)/shard_map/ppermute | solution.py:809
  73.2 5.2 %collective-permute-start.16 = (f32[64,128]{1,0:T(8,128)S(1)}, f32[64,128]{1,0:T(8,128)S(1)}, u32[]{:S(2)}, u32[]{:S(2)}) collective-permute-start(f32[64,128]{1,0:T(8,128)S(1)} %get-tuple-element.44), channel_id=1, source_target_pairs={{0,6},{1,7},{2,0},{3,1},{4,2},{5,3},{6,4},{7,5},{8,14},{9,15},{10,... | collective-permute-start | bytes 98312 | tf_op jit(solution)/shard_map/ppermute | solution.py:809
  75.6 6.1 %collective-permute-start.17 = (f32[64,128]{1,0:T(8,128)S(1)}, f32[64,128]{1,0:T(8,128)S(1)}, u32[]{:S(2)}, u32[]{:S(2)}) collective-permute-start(f32[64,128]{1,0:T(8,128)S(1)} %get-tuple-element.45), channel_id=1, source_target_pairs={{0,5},{1,6},{2,7},{3,0},{4,1},{5,2},{6,3},{7,4},{8,13},{9,14},{10,... | collective-permute-start | bytes 98312 | tf_op jit(solution)/shard_map/ppermute | solution.py:809

commit v14 on v12

--- a/solution.py
+++ b/solution.py
@@ -185,12 +185,15 @@
             stage(refs, row, here + near)
 
     def note_top(q, lines):
-        lanes = lax.broadcasted_iota(jnp.int32, (cols, levels), 1)
-        kept = lines[0]
+        shape = (cols // EDGE, EDGE, levels)
+        lanes = lax.broadcasted_iota(jnp.int32, (1, EDGE, levels), 2)
+        kept = lines[0].reshape(shape)
         for row in range(1, CHUNK):
-            kept = jnp.where(lanes == row, pltpu.roll(lines[row], row, 1), kept)
-        turned = pltpu.roll(kept, q * CHUNK, 1)
-        top[...] = jnp.where(lanes // CHUNK == q, turned, top[...])
+            moved_over = pltpu.roll(lines[row], row, 1).reshape(shape)
+            kept = jnp.where(jnp.broadcast_to(lanes == row, shape), moved_over, kept)
+        turned = pltpu.roll(kept.reshape(cols, levels), q * CHUNK, 1)
+        here = lax.broadcasted_iota(jnp.int32, (cols, levels), 1) // CHUNK == q
+        top[...] = jnp.where(here, turned, top[...])
 
     def mix_rows(refs, count):
         refs[2][: count * cols, :] = dot_nn(refs[1][: count * cols, :], weights[...])
@@ -841,7 +844,8 @@
     parts[1], forcing = lax.optimization_barrier((parts[1], forcing))
     picks = pick(parts, hits, neighbours)
     new_surface, picked = picks[0], picks[1:]
-    arrived = [over_tiles(picked[n], -offsets[n], ocean_comp) for n in range(neighbours)]
+    arrived = [over_tiles(picked[n], -offsets[n], ocean_comp) for n in reversed(range(neighbours))]
+    arrived = arrived[::-1]
     fields = [to_ocean(forcing, c) for c in range(ocean_comp)] + [forcing]
     final_state, token = update(flags, moved, fields, mask, ocean_map)
     weight_column = (packed_labels // rows)[:, None]

time: 83.6 us -> 83.6 us (level)
  no operation moved by 1% of the time
where the time goes in v14:
time: 83.6 us; the launch traced here: 83.2 us
  starting transfers between devices  34.6 us (41%)
  Pallas kernels  26.8 us (32%)
  waiting for transfers between devices  19.5 us (23%)
  between operations  1.03 us (1%)
    pallas_call x1, Pallas kernels, advance(): pl.pallas_call(functools.partial(advance_kernel, comp_count, left_at, rig...  17.3 us
    ppermute x6, starting transfers between devices, over_tiles(): return lax.ppermute(value, AXES, pairs)  15.7 us
    ppermute x6, waiting for transfers between devices, over_tiles(): return lax.ppermute(value, AXES, pairs)  8.53 us
    ppermute x3, starting transfers between devices, band_shift(): return lax.ppermute(value, AXES, pairs)  6.35 us
    ppermute x3, waiting for transfers between devices, band_shift(): return lax.ppermute(value, AXES, pairs)  5.26 us
    all_to_all x1, waiting for transfers between devices, over_comp(): lax.all_to_all(value, 'comp', split_axis=0, concat_axis=0, tiled=True)  4.21 us
    pallas_call x1, Pallas kernels, regrid(): pl.pallas_call(functools.partial(regrid_body, count, comp_count), out_sha...  4.1 us
    all_to_all x1, starting transfers between devices, over_comp(): lax.all_to_all(value, 'comp', split_axis=0, concat_axis=0, tiled=True)  4 us
  transfers between devices with their start and end apart: 19, of which 7 were waited for; matrix products, arithmetic and copies ran while one was open for 1% of the time, Pallas kernels for 2%

profile of v14, /device:TPU:1, one launch (start us, length us, event | category | flops | bytes accessed | tf_op | source)
XLA Modules:
  0.0 83.2 jit_solution(13912145880236459373)
XLA Ops:
  0.7 1.6 %edges.1 = (bf16[2,128,128]{2,1,0:T(8,128)(2,1)S(1)}, bf16[2,128,128]{2,1,0:T(8,128)(2,1)S(1)}, f32[4,128,128]{2,1,0:T(8,128)S(1)}) custom-call(f32[128,128,128]{2,1,0:T(8,128)} %refs_2_.1), custom_call_target="tpu_custom_call" | custom-call | tf_op jit(solution)/shard_map/edges/pallas_call | solution.py:63
  2.3 4.0 %collective-permute-start = (bf16[2,128,128]{2,1,0:T(8,128)(2,1)S(1)}, bf16[2,128,128]{2,1,0:T(8,128)(2,1)S(1)}, u32[]{:S(2)}, u32[]{:S(2)}) collective-permute-start(bf16[2,128,128]{2,1,0:T(8,128)(2,1)S(1)} %get-tuple-element.25), channel_id=1, source_target_pairs={{0,2},{1,3},{2,4},{3,5},{4,6},{5,7},{6,8},{7,9},{8,10},{9,11},{10,... | collective-permute-start | bytes 196616 | tf_op jit(solution)/shard_map/ppermute | solution.py:759
  6.4 1.3 %collective-permute-start.1 = (bf16[2,128,128]{2,1,0:T(8,128)(2,1)S(1)}, bf16[2,128,128]{2,1,0:T(8,128)(2,1)S(1)}, u32[]{:S(2)}, u32[]{:S(2)}) collective-permute-start(bf16[2,128,128]{2,1,0:T(8,128)(2,1)S(1)} %get-tuple-element.26), channel_id=1, source_target_pairs={{2,0},{3,1},{4,2},{5,3},{6,4},{7,5},{8,6},{9,7},{10,8},{11,9},{12,... | collective-permute-start | bytes 196616 | tf_op jit(solution)/shard_map/ppermute | solution.py:759
  7.7 0.2 copy.18
  7.9 0.3 fusion.4
  8.1 0.2 convert_reduce_fusion
  8.3 0.2 select_reduce_fusion.1
  8.6 0.0 collective-permute-done.up_rows.refs_3_
  8.6 4.1 %collective-permute-done.1.low_rows.refs_4_ = bf16[2,128,128]{2,1,0:T(8,128)(2,1)S(1)} collective-permute-done((bf16[2,128,128]{2,1,0:T(8,128)(2,1)S(1)}, bf16[2,128,128]{2,1,0:T(8,128)(2,1)S(1)}, u32[]{:S(2)}, u32[]{:S(2)}) %collective-permute-start.1) | collective-permute-done | bytes 65568 | tf_op jit(solution)/shard_map/ppermute | solution.py:759
  12.8 1.0 %collective-permute-start.2 = (f32[4,144,128]{2,1,0:T(8,128)S(1)}, f32[4,144,128]{2,1,0:T(8,128)S(1)}, u32[]{:S(2)}, u32[]{:S(2)}) collective-permute-start(f32[4,144,128]{2,1,0:T(8,128)S(1)} %frame.1), channel_id=1, source_target_pairs={{0,1},{1,0},{2,3},{3,2},{4,5},{5,4},{6,7},{7,6},{8,9},{9,8},{10,11... | collective-permute-start | bytes 884744 | tf_op jit(solution)/shard_map/ppermute | solution.py:759
  13.8 0.1 pad_add_fusion.refs_0_.flags
  13.9 1.1 %collective-permute-done.2.refs_5_.refs_6_ = f32[4,144,128]{2,1,0:T(8,128)S(1)} collective-permute-done((f32[4,144,128]{2,1,0:T(8,128)S(1)}, f32[4,144,128]{2,1,0:T(8,128)S(1)}, u32[]{:S(2)}, u32[]{:S(2)}) %collective-permute-start.2) | collective-permute-done | bytes 294944 | tf_op jit(solution)/shard_map/ppermute | solution.py:759
  15.0 17.3 %advance.1 = (f32[128,128,128]{2,1,0:T(8,128)}, f32[128,128]{1,0:T(8,128)S(1)}, bf16[128,128]{1,0:T(8,128)(2,1)S(1)}, bf16[4,144,256]{2,1,0:T(8,128)(2,1)}) custom-call(s32[4]{0:T(128)S(1)} %pad_add_fusion.refs_0_.flags, bf16[16,256]{1,0:T(8,128)(2,1)S(1)} %fusion.11.refs_1_, f32[128,128,128]{2,1,0:T(8,128)} %refs_2_.1, ...), custom_call_target="tpu_custom_call" | custom-call | flops 2147483648 | bytes 16777216 | tf_op jit(solution)/shard_map/advance/pallas_call | solution.py:371
  32.3 4.0 %all-to-all-start = ((bf16[4,144,256]{2,1,0:T(8,128)(2,1)}), bf16[4,144,256]{2,1,0:T(8,128)(2,1)S(1)}, u32[]{:S(2)}, u32[]{:S(2)}) async-start(bf16[4,144,256]{2,1,0:T(8,128)(2,1)} %get-tuple-element.29), calls=%async_computation | async-start | bytes 589824 | tf_op jit(solution)/shard_map/all_to_all | solution.py:795
  36.3 1.3 %collective-permute-start.6 = (bf16[128,128]{1,0:T(8,128)(2,1)S(1)}, bf16[128,128]{1,0:T(8,128)(2,1)S(1)}, u32[]{:S(2)}, u32[]{:S(2)}) collective-permute-start(bf16[128,128]{1,0:T(8,128)(2,1)S(1)} %get-tuple-element.34.refs_7_), channel_id=1, source_target_pairs={{24,0},{25,1},{26,2},{27,3},{28,4},{29,5},{30,6},{31,7}} | collective-permute-start | bytes 98312 | tf_op jit(solution)/shard_map/ppermute | solution.py:819
  37.6 0.7 collective-permute-start.7
  38.3 0.7 collective-permute-start.8
  39.0 4.2 %all-to-all-done.slabs = bf16[4,144,256]{2,1,0:T(8,128)(2,1)S(1)} async-done(((bf16[4,144,256]{2,1,0:T(8,128)(2,1)}), bf16[4,144,256]{2,1,0:T(8,128)(2,1)S(1)}, u32[]{:S(2)}, u32[]{:S(2)}) %all-to-all-start) | async-done | bytes 294944 | tf_op jit(solution)/shard_map/all_to_all | solution.py:795
  43.2 0.3 regroup.1
  43.5 0.2 collective-permute-start.3
  43.7 1.3 %collective-permute-start.4 = (bf16[208,256]{1,0:T(8,128)(2,1)S(1)}, bf16[208,256]{1,0:T(8,128)(2,1)S(1)}, u32[]{:S(2)}, u32[]{:S(2)}) collective-permute-start(bf16[208,256]{1,0:T(8,128)(2,1)S(1)} %get-tuple-element.32), channel_id=1, source_target_pairs={{0,2},{1,3},{2,4},{3,5},{4,6},{5,7},{6,0},{7,1},{8,10},{9,11},{10,... | collective-permute-start | bytes 319496 | tf_op jit(solution)/shard_map/ppermute | solution.py:813
  45.0 0.0 collective-permute-done.6.refs_4_
  45.0 4.1 %collective-permute-start.5 = (bf16[208,256]{1,0:T(8,128)(2,1)S(1)}, bf16[208,256]{1,0:T(8,128)(2,1)S(1)}, u32[]{:S(2)}, u32[]{:S(2)}) collective-permute-start(bf16[208,256]{1,0:T(8,128)(2,1)S(1)} %get-tuple-element.33), channel_id=1, source_target_pairs={{0,3},{1,4},{2,5},{3,6},{4,7},{5,0},{6,1},{7,2},{8,11},{9,12},{10,... | collective-permute-start | bytes 319496 | tf_op jit(solution)/shard_map/ppermute | solution.py:813
  49.2 0.1 slice_reduce_fusion.ocean_first
  49.3 0.0 collective-permute-done.7.refs_5_
  49.3 3.2 %collective-permute-done.4.refs_2_ = bf16[208,256]{1,0:T(8,128)(2,1)S(1)} collective-permute-done((bf16[208,256]{1,0:T(8,128)(2,1)S(1)}, bf16[208,256]{1,0:T(8,128)(2,1)S(1)}, u32[]{:S(2)}, u32[]{:S(2)}) %collective-permute-start.4) | collective-permute-done | bytes 106528 | tf_op jit(solution)/shard_map/ppermute | solution.py:813
  52.5 2.1 %collective-permute-done.5.refs_3_ = bf16[208,256]{1,0:T(8,128)(2,1)S(1)} collective-permute-done((bf16[208,256]{1,0:T(8,128)(2,1)S(1)}, bf16[208,256]{1,0:T(8,128)(2,1)S(1)}, u32[]{:S(2)}, u32[]{:S(2)}) %collective-permute-start.5) | collective-permute-done | bytes 106528 | tf_op jit(solution)/shard_map/ppermute | solution.py:813
  54.5 4.1 %regrid.1 = (f32[2,128,128]{2,1,0:T(8,128)S(1)}, f32[128,128]{1,0:T(8,128)S(1)}, bf16[256,128]{1,0:T(8,128)(2,1)S(1)}) custom-call(s32[4]{0:T(128)S(1)} %pad_add_fusion.refs_0_.flags, f32[8]{0:T(128)S(1)} %slice_reduce_fusion.ocean_first, bf16[208,256]{1,0:T(8,128)(2,1)S(1)} %get-tuple-element.30.refs_0_, ...), custom_call_target="tpu_custom_call" | custom-call | flops 2147483648 | bytes 2097152 | tf_op jit(solution)/shard_map/regrid/pallas_call | solution.py:528
  58.6 0.6 collective-permute-start.9
  59.2 0.1 copy.19
  59.4 0.9 %collective-permute-start.13 = (f32[128,128]{1,0:T(8,128)S(1)}, f32[128,128]{1,0:T(8,128)S(1)}, u32[]{:S(2)}, u32[]{:S(2)}) collective-permute-start(f32[128,128]{1,0:T(8,128)S(1)} %get-tuple-element.36.refs_0_), channel_id=1, source_target_pairs={{0,16},{1,17},{2,18},{3,19},{4,20},{5,21},{6,22},{7,23},{8,24},{9,... | collective-permute-start | bytes 196616 | tf_op jit(solution)/shard_map/ppermute | solution.py:803
  60.3 1.0 %collective-permute-start.14 = (f32[128,128]{1,0:T(8,128)S(1)}, f32[128,128]{1,0:T(8,128)S(1)}, u32[]{:S(2)}, u32[]{:S(2)}) collective-permute-start(f32[128,128]{1,0:T(8,128)S(1)} %get-tuple-element.36.refs_0_), channel_id=1, source_target_pairs={{0,24},{1,25},{2,26},{3,27},{4,28},{5,29},{6,30},{7,31},{8,0},{9,1... | collective-permute-start | bytes 196616 | tf_op jit(solution)/shard_map/ppermute | solution.py:803
  61.4 1.5 %collective-permute-done.9.refs_1_ = f32[128,128]{1,0:T(8,128)S(1)} collective-permute-done((f32[128,128]{1,0:T(8,128)S(1)}, f32[128,128]{1,0:T(8,128)S(1)}, u32[]{:S(2)}, u32[]{:S(2)}) %collective-permute-start.9) | collective-permute-done | bytes 65568 | tf_op jit(solution)/shard_map/ppermute | solution.py:803
  62.8 2.0 %collective-permute-start.10 = (f32[2,128,128]{2,1,0:T(8,128)S(1)}, f32[2,128,128]{2,1,0:T(8,128)S(1)}, u32[]{:S(2)}, u32[]{:S(2)}) collective-permute-start(f32[2,128,128]{2,1,0:T(8,128)S(1)} %get-tuple-element.38.refs_3_), channel_id=1, source_target_pairs={{0,24},{1,25},{2,26},{3,27},{4,28},{5,29},{6,30},{7,31}} | collective-permute-start | bytes 393224 | tf_op jit(solution)/shard_map/ppermute | solution.py:825
  64.8 0.7 collective-permute-start.11
  65.5 0.7 collective-permute-start.12
  66.2 0.1 add_select_fusion.refs_4_
  66.3 0.0 collective-permute-done.13.refs_2_
  66.3 0.2 pick.1
  66.5 5.8 %collective-permute-start.15 = (f32[64,128]{1,0:T(8,128)S(1)}, f32[64,128]{1,0:T(8,128)S(1)}, u32[]{:S(2)}, u32[]{:S(2)}) collective-permute-start(f32[64,128]{1,0:T(8,128)S(1)} %get-tuple-element.43), channel_id=1, source_target_pairs={{0,7},{1,0},{2,1},{3,2},{4,3},{5,4},{6,5},{7,6},{8,15},{9,8},{10,9... | collective-permute-start | bytes 98312 | tf_op jit(solution)/shard_map/ppermute | solution.py:813
  72.3 2.3 %collective-permute-start.16 = (f32[64,128]{1,0:T(8,128)S(1)}, f32[64,128]{1,0:T(8,128)S(1)}, u32[]{:S(2)}, u32[]{:S(2)}) collective-permute-start(f32[64,128]{1,0:T(8,128)S(1)} %get-tuple-element.44), channel_id=1, source_target_pairs={{0,6},{1,7},{2,0},{3,1},{4,2},{5,3},{6,4},{7,5},{8,14},{9,15},{10,... | collective-permute-start | bytes 98312 | tf_op jit(solution)/shard_map/ppermute | solution.py:813
  74.6 0.0 collective-permute-done.10.refs_0_
  74.6 1.9 %collective-permute-start.17 = (f32[64,128]{1,0:T(8,128)S(1)}, f32[64,128]{1,0:T(8,128)S(1)}, u32[]{:S(2)}, u32[]{:S(2)}) collective-permute-start(f32[64,128]{1,0:T(8,128)S(1)} %get-tuple-element.45), channel_id=1, source_target_pairs={{0,5},{1,6},{2,7},{3,0},{4,1},{5,2},{6,3},{7,4},{8,13},{9,14},{10,... | collective-permute-start | bytes 98312 | tf_op jit(solution)/shard_map/ppermute | solution.py:813
  76.6 0.0 collective-permute-done.12.refs_2_
  76.6 0.8 %update.1 = (f32[128,128,128]{2,1,0:T(8,128)}, f32[8,128]{1,0:T(8,128)S(1)}) custom-call(s32[4]{0:T(128)S(1)} %pad_add_fusion.refs_0_.flags, f32[128,128,128]{2,1,0:T(8,128)} %get-tuple-element.28.state, f32[2,128,128]{2,1,0:T(8,128)S(1)} %collective-permute-done.10.refs_0_, ...), custom_call_target="tpu_custom_call", output_to_operand_aliasing={{0}: (1, {})} | custom-call | flops 805306368 | bytes 16777216 | tf_op jit(solution)/shard_map/update/pallas_call | solution.py:649
  77.4 0.0 collective-permute-done.15.refs_1_
  77.5 3.3 %collective-permute-done.17.refs_3_ = f32[64,128]{1,0:T(8,128)S(1)} collective-permute-done((f32[64,128]{1,0:T(8,128)S(1)}, f32[64,128]{1,0:T(8,128)S(1)}, u32[]{:S(2)}, u32[]{:S(2)}) %collective-permute-start.17) | collective-permute-done | bytes 32800 | tf_op jit(solution)/shard_map/ppermute | solution.py:813
  80.8 2.4 %returned.1 = f32[128,128]{1,0:T(8,128)} custom-call(s32[4]{0:T(128)S(1)} %pad_add_fusion.refs_0_.flags, f32[64,128]{1,0:T(8,128)S(1)} %get-tuple-element.42.refs_0_, f32[64,128]{1,0:T(8,128)S(1)} %collective-permute-done.15.refs_1_, f32[64,128]{1,0:T(8,128)S(1)} %collective-permute-done.16.refs_2_, f32[64,128]{1,0:T(8,128)S(1)} %collective-permute-done.17.refs_3_, ...), custom_call_target="tpu_custom_call" | custom-call | tf_op jit(solution)/shard_map/returned/pallas_call | solution.py:713
  (27 shorter events, 0.1 us)
Async XLA Ops:
  0.6 7.0 %copy-start.6 = (s32[128,1,2,3]{0,2,3,1:T(2,128)S(1)}, s32[128,1,2,3]{0,2,3,1:T(2,128)}, u32[]{:S(2)}) copy-start(s32[128,1,2,3]{0,2,3,1:T(2,128)} %param.11) | copy-start | bytes 9220
  0.6 13.2 %copy-start.5 = (s32[128,128]{1,0:T(8,128)S(1)}, s32[128,128]{1,0:T(8,128)}, u32[]{:S(2)}) copy-start(s32[128,128]{1,0:T(8,128)} %param.10) | copy-start | bytes 196612
  0.7 14.3 %copy-start.4 = (f32[128,8]{0,1:T(8,128)S(1)}, f32[128,8]{0,1:T(8,128)}, u32[]{:S(2)}) copy-start(f32[128,8]{0,1:T(8,128)} %param.14) | copy-start | bytes 12292
  0.7 14.3 %copy-start.1 = (f32[128,128]{1,0:T(8,128)S(1)}, f32[128,128]{1,0:T(8,128)}, u32[]{:S(2)}) copy-start(f32[128,128]{1,0:T(8,128)} %refs_9_.1) | copy-start | bytes 196612
  0.7 14.3 %copy-start.2 = (f32[128,128]{1,0:T(8,128)S(1)}, f32[128,128]{1,0:T(8,128)}, u32[]{:S(2)}) copy-start(f32[128,128]{1,0:T(8,128)} %refs_10_.1) | copy-start | bytes 196612
  0.7 48.5 %copy-start.3 = (f32[8,128]{1,0:T(8,128)S(1)}, f32[8,128]{1,0:T(8,128)}, u32[]{:S(2)}) copy-start(f32[8,128]{1,0:T(8,128)} %refs_5_.1) | copy-start | bytes 12292
  0.7 53.8 %copy-start = (bf16[32,128,128]{2,1,0:T(8,128)(2,1)S(1)}, bf16[32,128,128]{2,1,0:T(8,128)(2,1)}, u32[]{:S(2)}) copy-start(bf16[32,128,128]{2,1,0:T(8,128)(2,1)} %refs_6_.1) | copy-start | bytes 3145732
  2.3 6.3 %collective-permute-start = (bf16[2,128,128]{2,1,0:T(8,128)(2,1)S(1)}, bf16[2,128,128]{2,1,0:T(8,128)(2,1)S(1)}, u32[]{:S(2)}, u32[]{:S(2)}) collective-permute-start(bf16[2,128,128]{2,1,0:T(8,128)(2,1)S(1)} %get-tuple-element.25), channel_id=1, source_target_pairs={{0,2},{1,3},{2,4},{3,5},{4,6},{5,7},{6,8},{7,9},{8,10},{9,11},{10,... | collective-permute-start | bytes 196616 | tf_op jit(solution)/shard_map/ppermute | solution.py:759
  6.4 6.4 %collective-permute-start.1 = (bf16[2,128,128]{2,1,0:T(8,128)(2,1)S(1)}, bf16[2,128,128]{2,1,0:T(8,128)(2,1)S(1)}, u32[]{:S(2)}, u32[]{:S(2)}) collective-permute-start(bf16[2,128,128]{2,1,0:T(8,128)(2,1)S(1)} %get-tuple-element.26), channel_id=1, source_target_pairs={{2,0},{3,1},{4,2},{5,3},{6,4},{7,5},{8,6},{9,7},{10,8},{11,9},{12,... | collective-permute-start | bytes 196616 | tf_op jit(solution)/shard_map/ppermute | solution.py:759
  12.8 2.2 %collective-permute-start.2 = (f32[4,144,128]{2,1,0:T(8,128)S(1)}, f32[4,144,128]{2,1,0:T(8,128)S(1)}, u32[]{:S(2)}, u32[]{:S(2)}) collective-permute-start(f32[4,144,128]{2,1,0:T(8,128)S(1)} %frame.1), channel_id=1, source_target_pairs={{0,1},{1,0},{2,3},{3,2},{4,5},{5,4},{6,7},{7,6},{8,9},{9,8},{10,11... | collective-permute-start | bytes 884744 | tf_op jit(solution)/shard_map/ppermute | solution.py:759
  32.3 10.8 %all-to-all-start = ((bf16[4,144,256]{2,1,0:T(8,128)(2,1)}), bf16[4,144,256]{2,1,0:T(8,128)(2,1)S(1)}, u32[]{:S(2)}, u32[]{:S(2)}) async-start(bf16[4,144,256]{2,1,0:T(8,128)(2,1)} %get-tuple-element.29), calls=%async_computation | async-start | bytes 589824 | tf_op jit(solution)/shard_map/all_to_all | solution.py:795
  36.3 8.7 %collective-permute-start.6 = (bf16[128,128]{1,0:T(8,128)(2,1)S(1)}, bf16[128,128]{1,0:T(8,128)(2,1)S(1)}, u32[]{:S(2)}, u32[]{:S(2)}) collective-permute-start(bf16[128,128]{1,0:T(8,128)(2,1)S(1)} %get-tuple-element.34.refs_7_), channel_id=1, source_target_pairs={{24,0},{25,1},{26,2},{27,3},{28,4},{29,5},{30,6},{31,7}} | collective-permute-start | bytes 98312 | tf_op jit(solution)/shard_map/ppermute | solution.py:819
  37.6 11.7 %collective-permute-start.7 = (bf16[128,128]{1,0:T(8,128)(2,1)S(1)}, bf16[128,128]{1,0:T(8,128)(2,1)S(1)}, u32[]{:S(2)}, u32[]{:S(2)}) collective-permute-start(bf16[128,128]{1,0:T(8,128)(2,1)S(1)} %get-tuple-element.34.refs_7_), channel_id=1, source_target_pairs={{24,8},{25,9},{26,10},{27,11},{28,12},{29,13},{30,14},{31,15}} | collective-permute-start | bytes 98312 | tf_op jit(solution)/shard_map/ppermute | solution.py:819
  38.3 11.0 %collective-permute-start.8 = (bf16[128,128]{1,0:T(8,128)(2,1)S(1)}, bf16[128,128]{1,0:T(8,128)(2,1)S(1)}, u32[]{:S(2)}, u32[]{:S(2)}) collective-permute-start(bf16[128,128]{1,0:T(8,128)(2,1)S(1)} %get-tuple-element.34.refs_7_), channel_id=1, source_target_pairs={{24,16},{25,17},{26,18},{27,19},{28,20},{29,21},{30,22},{31,23}} | collective-permute-start | bytes 98312 | tf_op jit(solution)/shard_map/ppermute | solution.py:819
  43.5 5.8 %collective-permute-start.3 = (bf16[208,256]{1,0:T(8,128)(2,1)S(1)}, bf16[208,256]{1,0:T(8,128)(2,1)S(1)}, u32[]{:S(2)}, u32[]{:S(2)}) collective-permute-start(bf16[208,256]{1,0:T(8,128)(2,1)S(1)} %get-tuple-element.31), channel_id=1, source_target_pairs={{0,1},{1,2},{2,3},{3,4},{4,5},{5,6},{6,7},{7,0},{8,9},{9,10},{10,1... | collective-permute-start | bytes 319496 | tf_op jit(solution)/shard_map/ppermute | solution.py:813
  43.7 8.7 %collective-permute-start.4 = (bf16[208,256]{1,0:T(8,128)(2,1)S(1)}, bf16[208,256]{1,0:T(8,128)(2,1)S(1)}, u32[]{:S(2)}, u32[]{:S(2)}) collective-permute-start(bf16[208,256]{1,0:T(8,128)(2,1)S(1)} %get-tuple-element.32), channel_id=1, source_target_pairs={{0,2},{1,3},{2,4},{3,5},{4,6},{5,7},{6,0},{7,1},{8,10},{9,11},{10,... | collective-permute-start | bytes 319496 | tf_op jit(solution)/shard_map/ppermute | solution.py:813
  45.0 9.5 %collective-permute-start.5 = (bf16[208,256]{1,0:T(8,128)(2,1)S(1)}, bf16[208,256]{1,0:T(8,128)(2,1)S(1)}, u32[]{:S(2)}, u32[]{:S(2)}) collective-permute-start(bf16[208,256]{1,0:T(8,128)(2,1)S(1)} %get-tuple-element.33), channel_id=1, source_target_pairs={{0,3},{1,4},{2,5},{3,6},{4,7},{5,0},{6,1},{7,2},{8,11},{9,12},{10,... | collective-permute-start | bytes 319496 | tf_op jit(solution)/shard_map/ppermute | solution.py:813
  58.6 4.2 %collective-permute-start.9 = (f32[128,128]{1,0:T(8,128)S(1)}, f32[128,128]{1,0:T(8,128)S(1)}, u32[]{:S(2)}, u32[]{:S(2)}) collective-permute-start(f32[128,128]{1,0:T(8,128)S(1)} %get-tuple-element.36.refs_0_), channel_id=1, source_target_pairs={{0,8},{1,9},{2,10},{3,11},{4,12},{5,13},{6,14},{7,15},{8,16},{9,17... | collective-permute-start | bytes 196616 | tf_op jit(solution)/shard_map/ppermute | solution.py:803
  59.4 6.9 %collective-permute-start.13 = (f32[128,128]{1,0:T(8,128)S(1)}, f32[128,128]{1,0:T(8,128)S(1)}, u32[]{:S(2)}, u32[]{:S(2)}) collective-permute-start(f32[128,128]{1,0:T(8,128)S(1)} %get-tuple-element.36.refs_0_), channel_id=1, source_target_pairs={{0,16},{1,17},{2,18},{3,19},{4,20},{5,21},{6,22},{7,23},{8,24},{9,... | collective-permute-start | bytes 196616 | tf_op jit(solution)/shard_map/ppermute | solution.py:803
  60.3 6.0 %collective-permute-start.14 = (f32[128,128]{1,0:T(8,128)S(1)}, f32[128,128]{1,0:T(8,128)S(1)}, u32[]{:S(2)}, u32[]{:S(2)}) collective-permute-start(f32[128,128]{1,0:T(8,128)S(1)} %get-tuple-element.36.refs_0_), channel_id=1, source_target_pairs={{0,24},{1,25},{2,26},{3,27},{4,28},{5,29},{6,30},{7,31},{8,0},{9,1... | collective-permute-start | bytes 196616 | tf_op jit(solution)/shard_map/ppermute | solution.py:803
  62.8 11.8 %collective-permute-start.10 = (f32[2,128,128]{2,1,0:T(8,128)S(1)}, f32[2,128,128]{2,1,0:T(8,128)S(1)}, u32[]{:S(2)}, u32[]{:S(2)}) collective-permute-start(f32[2,128,128]{2,1,0:T(8,128)S(1)} %get-tuple-element.38.refs_3_), channel_id=1, source_target_pairs={{0,24},{1,25},{2,26},{3,27},{4,28},{5,29},{6,30},{7,31}} | collective-permute-start | bytes 393224 | tf_op jit(solution)/shard_map/ppermute | solution.py:825
  64.8 11.7 %collective-permute-start.11 = (f32[2,128,128]{2,1,0:T(8,128)S(1)}, f32[2,128,128]{2,1,0:T(8,128)S(1)}, u32[]{:S(2)}, u32[]{:S(2)}) collective-permute-start(f32[2,128,128]{2,1,0:T(8,128)S(1)} %get-tuple-element.38.refs_3_), channel_id=1, source_target_pairs={{8,24},{9,25},{10,26},{11,27},{12,28},{13,29},{14,30},{15,31}} | collective-permute-start | bytes 393224 | tf_op jit(solution)/shard_map/ppermute | solution.py:825
  65.5 11.1 %collective-permute-start.12 = (f32[2,128,128]{2,1,0:T(8,128)S(1)}, f32[2,128,128]{2,1,0:T(8,128)S(1)}, u32[]{:S(2)}, u32[]{:S(2)}) collective-permute-start(f32[2,128,128]{2,1,0:T(8,128)S(1)} %get-tuple-element.38.refs_3_), channel_id=1, source_target_pairs={{16,24},{17,25},{18,26},{19,27},{20,28},{21,29},{22,30},{23,31}} | collective-permute-start | bytes 393224 | tf_op jit(solution)/shard_map/ppermute | solution.py:825
  66.5 11.0 %collective-permute-start.15 = (f32[64,128]{1,0:T(8,128)S(1)}, f32[64,128]{1,0:T(8,128)S(1)}, u32[]{:S(2)}, u32[]{:S(2)}) collective-permute-start(f32[64,128]{1,0:T(8,128)S(1)} %get-tuple-element.43), channel_id=1, source_target_pairs={{0,7},{1,0},{2,1},{3,2},{4,3},{5,4},{6,5},{7,6},{8,15},{9,8},{10,9... | collective-permute-start | bytes 98312 | tf_op jit(solution)/shard_map/ppermute | solution.py:813
  72.3 5.2 %collective-permute-start.16 = (f32[64,128]{1,0:T(8,128)S(1)}, f32[64,128]{1,0:T(8,128)S(1)}, u32[]{:S(2)}, u32[]{:S(2)}) collective-permute-start(f32[64,128]{1,0:T(8,128)S(1)} %get-tuple-element.44), channel_id=1, source_target_pairs={{0,6},{1,7},{2,0},{3,1},{4,2},{5,3},{6,4},{7,5},{8,14},{9,15},{10,... | collective-permute-start | bytes 98312 | tf_op jit(solution)/shard_map/ppermute | solution.py:813
  74.6 6.1 %collective-permute-start.17 = (f32[64,128]{1,0:T(8,128)S(1)}, f32[64,128]{1,0:T(8,128)S(1)}, u32[]{:S(2)}, u32[]{:S(2)}) collective-permute-start(f32[64,128]{1,0:T(8,128)S(1)} %get-tuple-element.45), channel_id=1, source_target_pairs={{0,5},{1,6},{2,7},{3,0},{4,1},{5,2},{6,3},{7,4},{8,13},{9,14},{10,... | collective-permute-start | bytes 98312 | tf_op jit(solution)/shard_map/ppermute | solution.py:813

commit v15 on v14

--- a/solution.py
+++ b/solution.py
@@ -137,10 +137,9 @@
     ocean = flags[0] == 1
     mix = jnp.where(ocean, mix_ocn[...], mix_atm[...])
     mix_high, mix_low = split_two(mix)
-    weights[:levels, :levels] = mix_high
-    weights[levels:, :levels] = mix_high
-    weights[:levels, levels:] = mix_low
-    weights[levels:, levels:] = mix_low
+    weights[:levels, :] = mix_high
+    weights[levels : 2 * levels, :] = mix_high
+    weights[2 * levels :, :] = mix_low
     sea_copy[...] = mask[...].astype(BF16)
     map_high, map_low = split_two(flux_map[...])
     flux_weights[...] = jnp.concatenate(
@@ -173,7 +172,8 @@
     def stage(refs, row, total):
         line = SMOOTHING * total
         refs[0][row] = line
-        refs[1][row * cols : (row + 1) * cols, :] = side_by_side(line)
+        high, low = split_two(line)
+        refs[1][row * cols : (row + 1) * cols, :] = jnp.concatenate([high, low, high], axis=1)
 
     def stage_rows(refs, ref, start, count):
         for row in range(count):
@@ -199,8 +199,7 @@
         refs[2][: count * cols, :] = dot_nn(refs[1][: count * cols, :], weights[...])
 
     def finish(refs, row):
-        part = refs[2][row * cols : (row + 1) * cols, :]
-        return refs[0][row] + PHYSICS * jnp.tanh(part[:, :levels] + part[:, levels:])
+        return refs[0][row] + PHYSICS * jnp.tanh(refs[2][row * cols : (row + 1) * cols, :])
 
     @pl.when(jnp.logical_not(ocean))
     def atmosphere():
@@ -383,12 +382,12 @@
             pltpu.VMEM((rows + 2, cols + 2 * EDGE, levels), F32),
             pltpu.VMEM((2, rows, levels), F32),
             pltpu.VMEM((CHUNK, cols, levels), F32),
-            pltpu.VMEM((CHUNK * cols, 2 * levels), BF16),
-            pltpu.VMEM((CHUNK * cols, 2 * levels), F32),
+            pltpu.VMEM((CHUNK * cols, 3 * levels), BF16),
+            pltpu.VMEM((CHUNK * cols, levels), F32),
             pltpu.VMEM((CHUNK, cols, levels), F32),
-            pltpu.VMEM((CHUNK * cols, 2 * levels), BF16),
-            pltpu.VMEM((CHUNK * cols, 2 * levels), F32),
-            pltpu.VMEM((2 * levels, 2 * levels), BF16),
+            pltpu.VMEM((CHUNK * cols, 3 * levels), BF16),
+            pltpu.VMEM((CHUNK * cols, levels), F32),
+            pltpu.VMEM((3 * levels, levels), BF16),
             pltpu.VMEM((2 * fluxes, 2 * levels), BF16),
             pltpu.VMEM((CHUNK * cols, 2 * levels), BF16),
             pltpu.VMEM((rows * fluxes, cols), F32),

time: 83.6 us -> 86.9 us (1.039)
  Pallas kernels: 26.8 us -> 30 us
    pallas_call x1, Pallas kernels: 17.3 us -> 20.6 us  [advance(): pl.pallas_call(functools.partial(advance_kernel, comp_count, left_at, rig...]
where the time goes in v15:
time: 86.9 us; the launch traced here: 86.4 us
  starting transfers between devices  34.6 us (40%)
  Pallas kernels  30 us (35%)
  waiting for transfers between devices  19.5 us (22%)
  between operations  1.03 us (1%)
    pallas_call x1, Pallas kernels, advance(): pl.pallas_call(functools.partial(advance_kernel, comp_count, left_at, rig...  20.6 us
    ppermute x6, starting transfers between devices, over_tiles(): return lax.ppermute(value, AXES, pairs)  15.7 us
    ppermute x6, waiting for transfers between devices, over_tiles(): return lax.ppermute(value, AXES, pairs)  8.53 us
    ppermute x3, starting transfers between devices, band_shift(): return lax.ppermute(value, AXES, pairs)  6.35 us
    ppermute x3, waiting for transfers between devices, band_shift(): return lax.ppermute(value, AXES, pairs)  5.26 us
    all_to_all x1, waiting for transfers between devices, over_comp(): lax.all_to_all(value, 'comp', split_axis=0, concat_axis=0, tiled=True)  4.21 us
    pallas_call x1, Pallas kernels, regrid(): pl.pallas_call(functools.partial(regrid_body, count, comp_count), out_sha...  4.1 us
    all_to_all x1, starting transfers between devices, over_comp(): lax.all_to_all(value, 'comp', split_axis=0, concat_axis=0, tiled=True)  4 us
  transfers between devices with their start and end apart: 19, of which 7 were waited for; matrix products, arithmetic and copies ran while one was open for 1% of the time, Pallas kernels for 2%

profile of v15, /device:TPU:1, one launch (start us, length us, event | category | flops | bytes accessed | tf_op | source)
XLA Modules:
  0.0 86.4 jit_solution(16091062057940622212)
XLA Ops:
  0.7 1.6 %edges.1 = (bf16[2,128,128]{2,1,0:T(8,128)(2,1)S(1)}, bf16[2,128,128]{2,1,0:T(8,128)(2,1)S(1)}, f32[4,128,128]{2,1,0:T(8,128)S(1)}) custom-call(f32[128,128,128]{2,1,0:T(8,128)} %refs_2_.1), custom_call_target="tpu_custom_call" | custom-call | tf_op jit(solution)/shard_map/edges/pallas_call | solution.py:63
  2.3 4.0 %collective-permute-start = (bf16[2,128,128]{2,1,0:T(8,128)(2,1)S(1)}, bf16[2,128,128]{2,1,0:T(8,128)(2,1)S(1)}, u32[]{:S(2)}, u32[]{:S(2)}) collective-permute-start(bf16[2,128,128]{2,1,0:T(8,128)(2,1)S(1)} %get-tuple-element.25), channel_id=1, source_target_pairs={{0,2},{1,3},{2,4},{3,5},{4,6},{5,7},{6,8},{7,9},{8,10},{9,11},{10,... | collective-permute-start | bytes 196616 | tf_op jit(solution)/shard_map/ppermute | solution.py:758
  6.4 1.3 %collective-permute-start.1 = (bf16[2,128,128]{2,1,0:T(8,128)(2,1)S(1)}, bf16[2,128,128]{2,1,0:T(8,128)(2,1)S(1)}, u32[]{:S(2)}, u32[]{:S(2)}) collective-permute-start(bf16[2,128,128]{2,1,0:T(8,128)(2,1)S(1)} %get-tuple-element.26), channel_id=1, source_target_pairs={{2,0},{3,1},{4,2},{5,3},{6,4},{7,5},{8,6},{9,7},{10,8},{11,9},{12,... | collective-permute-start | bytes 196616 | tf_op jit(solution)/shard_map/ppermute | solution.py:758
  7.7 0.2 copy.18
  7.9 0.3 fusion.4
  8.1 0.2 convert_reduce_fusion
  8.3 0.2 select_reduce_fusion.1
  8.6 0.0 collective-permute-done.up_rows.refs_3_
  8.6 4.1 %collective-permute-done.1.low_rows.refs_4_ = bf16[2,128,128]{2,1,0:T(8,128)(2,1)S(1)} collective-permute-done((bf16[2,128,128]{2,1,0:T(8,128)(2,1)S(1)}, bf16[2,128,128]{2,1,0:T(8,128)(2,1)S(1)}, u32[]{:S(2)}, u32[]{:S(2)}) %collective-permute-start.1) | collective-permute-done | bytes 65568 | tf_op jit(solution)/shard_map/ppermute | solution.py:758
  12.8 1.0 %collective-permute-start.2 = (f32[4,144,128]{2,1,0:T(8,128)S(1)}, f32[4,144,128]{2,1,0:T(8,128)S(1)}, u32[]{:S(2)}, u32[]{:S(2)}) collective-permute-start(f32[4,144,128]{2,1,0:T(8,128)S(1)} %frame.1), channel_id=1, source_target_pairs={{0,1},{1,0},{2,3},{3,2},{4,5},{5,4},{6,7},{7,6},{8,9},{9,8},{10,11... | collective-permute-start | bytes 884744 | tf_op jit(solution)/shard_map/ppermute | solution.py:758
  13.8 0.1 pad_add_fusion.refs_0_.flags
  13.9 1.1 %collective-permute-done.2.refs_5_.refs_6_ = f32[4,144,128]{2,1,0:T(8,128)S(1)} collective-permute-done((f32[4,144,128]{2,1,0:T(8,128)S(1)}, f32[4,144,128]{2,1,0:T(8,128)S(1)}, u32[]{:S(2)}, u32[]{:S(2)}) %collective-permute-start.2) | collective-permute-done | bytes 294944 | tf_op jit(solution)/shard_map/ppermute | solution.py:758
  15.0 20.6 %advance.1 = (f32[128,128,128]{2,1,0:T(8,128)}, f32[128,128]{1,0:T(8,128)S(1)}, bf16[128,128]{1,0:T(8,128)(2,1)S(1)}, bf16[4,144,256]{2,1,0:T(8,128)(2,1)}) custom-call(s32[4]{0:T(128)S(1)} %pad_add_fusion.refs_0_.flags, bf16[16,256]{1,0:T(8,128)(2,1)S(1)} %fusion.11.refs_1_, f32[128,128,128]{2,1,0:T(8,128)} %refs_2_.1, ...), custom_call_target="tpu_custom_call" | custom-call | flops 2147483648 | bytes 16777216 | tf_op jit(solution)/shard_map/advance/pallas_call | solution.py:370
  35.6 4.0 %all-to-all-start = ((bf16[4,144,256]{2,1,0:T(8,128)(2,1)}), bf16[4,144,256]{2,1,0:T(8,128)(2,1)S(1)}, u32[]{:S(2)}, u32[]{:S(2)}) async-start(bf16[4,144,256]{2,1,0:T(8,128)(2,1)} %get-tuple-element.29), calls=%async_computation | async-start | bytes 589824 | tf_op jit(solution)/shard_map/all_to_all | solution.py:794
  39.6 1.3 %collective-permute-start.6 = (bf16[128,128]{1,0:T(8,128)(2,1)S(1)}, bf16[128,128]{1,0:T(8,128)(2,1)S(1)}, u32[]{:S(2)}, u32[]{:S(2)}) collective-permute-start(bf16[128,128]{1,0:T(8,128)(2,1)S(1)} %get-tuple-element.34.refs_7_), channel_id=1, source_target_pairs={{24,0},{25,1},{26,2},{27,3},{28,4},{29,5},{30,6},{31,7}} | collective-permute-start | bytes 98312 | tf_op jit(solution)/shard_map/ppermute | solution.py:818
  40.9 0.7 collective-permute-start.7
  41.5 0.7 collective-permute-start.8
  42.2 4.2 %all-to-all-done.slabs = bf16[4,144,256]{2,1,0:T(8,128)(2,1)S(1)} async-done(((bf16[4,144,256]{2,1,0:T(8,128)(2,1)}), bf16[4,144,256]{2,1,0:T(8,128)(2,1)S(1)}, u32[]{:S(2)}, u32[]{:S(2)}) %all-to-all-start) | async-done | bytes 294944 | tf_op jit(solution)/shard_map/all_to_all | solution.py:794
  46.4 0.3 regroup.1
  46.7 0.2 collective-permute-start.3
  46.9 1.3 %collective-permute-start.4 = (bf16[208,256]{1,0:T(8,128)(2,1)S(1)}, bf16[208,256]{1,0:T(8,128)(2,1)S(1)}, u32[]{:S(2)}, u32[]{:S(2)}) collective-permute-start(bf16[208,256]{1,0:T(8,128)(2,1)S(1)} %get-tuple-element.32), channel_id=1, source_target_pairs={{0,2},{1,3},{2,4},{3,5},{4,6},{5,7},{6,0},{7,1},{8,10},{9,11},{10,... | collective-permute-start | bytes 319496 | tf_op jit(solution)/shard_map/ppermute | solution.py:812
  48.2 0.0 collective-permute-done.6.refs_4_
  48.2 4.2 %collective-permute-start.5 = (bf16[208,256]{1,0:T(8,128)(2,1)S(1)}, bf16[208,256]{1,0:T(8,128)(2,1)S(1)}, u32[]{:S(2)}, u32[]{:S(2)}) collective-permute-start(bf16[208,256]{1,0:T(8,128)(2,1)S(1)} %get-tuple-element.33), channel_id=1, source_target_pairs={{0,3},{1,4},{2,5},{3,6},{4,7},{5,0},{6,1},{7,2},{8,11},{9,12},{10,... | collective-permute-start | bytes 319496 | tf_op jit(solution)/shard_map/ppermute | solution.py:812
  52.4 0.1 slice_reduce_fusion.ocean_first
  52.5 0.0 collective-permute-done.3.refs_1_
  52.5 3.2 %collective-permute-done.4.refs_2_ = bf16[208,256]{1,0:T(8,128)(2,1)S(1)} collective-permute-done((bf16[208,256]{1,0:T(8,128)(2,1)S(1)}, bf16[208,256]{1,0:T(8,128)(2,1)S(1)}, u32[]{:S(2)}, u32[]{:S(2)}) %collective-permute-start.4) | collective-permute-done | bytes 106528 | tf_op jit(solution)/shard_map/ppermute | solution.py:812
  55.7 2.1 %collective-permute-done.5.refs_3_ = bf16[208,256]{1,0:T(8,128)(2,1)S(1)} collective-permute-done((bf16[208,256]{1,0:T(8,128)(2,1)S(1)}, bf16[208,256]{1,0:T(8,128)(2,1)S(1)}, u32[]{:S(2)}, u32[]{:S(2)}) %collective-permute-start.5) | collective-permute-done | bytes 106528 | tf_op jit(solution)/shard_map/ppermute | solution.py:812
  57.7 4.1 %regrid.1 = (f32[2,128,128]{2,1,0:T(8,128)S(1)}, f32[128,128]{1,0:T(8,128)S(1)}, bf16[256,128]{1,0:T(8,128)(2,1)S(1)}) custom-call(s32[4]{0:T(128)S(1)} %pad_add_fusion.refs_0_.flags, f32[8]{0:T(128)S(1)} %slice_reduce_fusion.ocean_first, bf16[208,256]{1,0:T(8,128)(2,1)S(1)} %get-tuple-element.30.refs_0_, ...), custom_call_target="tpu_custom_call" | custom-call | flops 2147483648 | bytes 2097152 | tf_op jit(solution)/shard_map/regrid/pallas_call | solution.py:527
  61.9 0.6 collective-permute-start.9
  62.4 0.1 copy.19
  62.6 0.9 %collective-permute-start.13 = (f32[128,128]{1,0:T(8,128)S(1)}, f32[128,128]{1,0:T(8,128)S(1)}, u32[]{:S(2)}, u32[]{:S(2)}) collective-permute-start(f32[128,128]{1,0:T(8,128)S(1)} %get-tuple-element.36.refs_0_), channel_id=1, source_target_pairs={{0,16},{1,17},{2,18},{3,19},{4,20},{5,21},{6,22},{7,23},{8,24},{9,... | collective-permute-start | bytes 196616 | tf_op jit(solution)/shard_map/ppermute | solution.py:802
  63.5 1.1 %collective-permute-start.14 = (f32[128,128]{1,0:T(8,128)S(1)}, f32[128,128]{1,0:T(8,128)S(1)}, u32[]{:S(2)}, u32[]{:S(2)}) collective-permute-start(f32[128,128]{1,0:T(8,128)S(1)} %get-tuple-element.36.refs_0_), channel_id=1, source_target_pairs={{0,24},{1,25},{2,26},{3,27},{4,28},{5,29},{6,30},{7,31},{8,0},{9,1... | collective-permute-start | bytes 196616 | tf_op jit(solution)/shard_map/ppermute | solution.py:802
  64.6 1.5 %collective-permute-done.9.refs_1_ = f32[128,128]{1,0:T(8,128)S(1)} collective-permute-done((f32[128,128]{1,0:T(8,128)S(1)}, f32[128,128]{1,0:T(8,128)S(1)}, u32[]{:S(2)}, u32[]{:S(2)}) %collective-permute-start.9) | collective-permute-done | bytes 65568 | tf_op jit(solution)/shard_map/ppermute | solution.py:802
  66.0 2.0 %collective-permute-start.10 = (f32[2,128,128]{2,1,0:T(8,128)S(1)}, f32[2,128,128]{2,1,0:T(8,128)S(1)}, u32[]{:S(2)}, u32[]{:S(2)}) collective-permute-start(f32[2,128,128]{2,1,0:T(8,128)S(1)} %get-tuple-element.38.refs_3_), channel_id=1, source_target_pairs={{0,24},{1,25},{2,26},{3,27},{4,28},{5,29},{6,30},{7,31}} | collective-permute-start | bytes 393224 | tf_op jit(solution)/shard_map/ppermute | solution.py:824
  68.1 0.7 collective-permute-start.11
  68.7 0.7 collective-permute-start.12
  69.4 0.1 add_select_fusion.refs_4_
  69.5 0.0 collective-permute-done.14.refs_3_
  69.5 0.2 pick.1
  69.7 5.8 %collective-permute-start.15 = (f32[64,128]{1,0:T(8,128)S(1)}, f32[64,128]{1,0:T(8,128)S(1)}, u32[]{:S(2)}, u32[]{:S(2)}) collective-permute-start(f32[64,128]{1,0:T(8,128)S(1)} %get-tuple-element.43), channel_id=1, source_target_pairs={{0,7},{1,0},{2,1},{3,2},{4,3},{5,4},{6,5},{7,6},{8,15},{9,8},{10,9... | collective-permute-start | bytes 98312 | tf_op jit(solution)/shard_map/ppermute | solution.py:812
  75.5 2.3 %collective-permute-start.16 = (f32[64,128]{1,0:T(8,128)S(1)}, f32[64,128]{1,0:T(8,128)S(1)}, u32[]{:S(2)}, u32[]{:S(2)}) collective-permute-start(f32[64,128]{1,0:T(8,128)S(1)} %get-tuple-element.44), channel_id=1, source_target_pairs={{0,6},{1,7},{2,0},{3,1},{4,2},{5,3},{6,4},{7,5},{8,14},{9,15},{10,... | collective-permute-start | bytes 98312 | tf_op jit(solution)/shard_map/ppermute | solution.py:812
  77.9 1.9 %collective-permute-start.17 = (f32[64,128]{1,0:T(8,128)S(1)}, f32[64,128]{1,0:T(8,128)S(1)}, u32[]{:S(2)}, u32[]{:S(2)}) collective-permute-start(f32[64,128]{1,0:T(8,128)S(1)} %get-tuple-element.45), channel_id=1, source_target_pairs={{0,5},{1,6},{2,7},{3,0},{4,1},{5,2},{6,3},{7,4},{8,13},{9,14},{10,... | collective-permute-start | bytes 98312 | tf_op jit(solution)/shard_map/ppermute | solution.py:812
  79.8 0.0 collective-permute-done.11.refs_1_
  79.8 0.0 collective-permute-done.12.refs_2_
  79.8 0.8 update.1
  80.7 0.0 collective-permute-done.16.refs_2_
  80.7 3.3 %collective-permute-done.17.refs_3_ = f32[64,128]{1,0:T(8,128)S(1)} collective-permute-done((f32[64,128]{1,0:T(8,128)S(1)}, f32[64,128]{1,0:T(8,128)S(1)}, u32[]{:S(2)}, u32[]{:S(2)}) %collective-permute-start.17) | collective-permute-done | bytes 32800 | tf_op jit(solution)/shard_map/ppermute | solution.py:812
  84.0 2.4 %returned.1 = f32[128,128]{1,0:T(8,128)} custom-call(s32[4]{0:T(128)S(1)} %pad_add_fusion.refs_0_.flags, f32[64,128]{1,0:T(8,128)S(1)} %get-tuple-element.42.refs_0_, f32[64,128]{1,0:T(8,128)S(1)} %collective-permute-done.15.refs_1_, f32[64,128]{1,0:T(8,128)S(1)} %collective-permute-done.16.refs_2_, f32[64,128]{1,0:T(8,128)S(1)} %collective-permute-done.17.refs_3_, ...), custom_call_target="tpu_custom_call" | custom-call | tf_op jit(solution)/shard_map/returned/pallas_call | solution.py:712
  (27 shorter events, 0.1 us)
Async XLA Ops:
  0.6 7.0 %copy-start.6 = (s32[128,1,2,3]{0,2,3,1:T(2,128)S(1)}, s32[128,1,2,3]{0,2,3,1:T(2,128)}, u32[]{:S(2)}) copy-start(s32[128,1,2,3]{0,2,3,1:T(2,128)} %param.11) | copy-start | bytes 9220
  0.6 13.2 %copy-start.5 = (s32[128,128]{1,0:T(8,128)S(1)}, s32[128,128]{1,0:T(8,128)}, u32[]{:S(2)}) copy-start(s32[128,128]{1,0:T(8,128)} %param.10) | copy-start | bytes 196612
  0.7 14.3 %copy-start.4 = (f32[128,8]{0,1:T(8,128)S(1)}, f32[128,8]{0,1:T(8,128)}, u32[]{:S(2)}) copy-start(f32[128,8]{0,1:T(8,128)} %param.14) | copy-start | bytes 12292
  0.7 14.3 %copy-start.1 = (f32[128,128]{1,0:T(8,128)S(1)}, f32[128,128]{1,0:T(8,128)}, u32[]{:S(2)}) copy-start(f32[128,128]{1,0:T(8,128)} %refs_9_.1) | copy-start | bytes 196612
  0.7 14.3 %copy-start.2 = (f32[128,128]{1,0:T(8,128)S(1)}, f32[128,128]{1,0:T(8,128)}, u32[]{:S(2)}) copy-start(f32[128,128]{1,0:T(8,128)} %refs_10_.1) | copy-start | bytes 196612
  0.7 51.7 %copy-start.3 = (f32[8,128]{1,0:T(8,128)S(1)}, f32[8,128]{1,0:T(8,128)}, u32[]{:S(2)}) copy-start(f32[8,128]{1,0:T(8,128)} %refs_5_.1) | copy-start | bytes 12292
  0.7 57.1 %copy-start = (bf16[32,128,128]{2,1,0:T(8,128)(2,1)S(1)}, bf16[32,128,128]{2,1,0:T(8,128)(2,1)}, u32[]{:S(2)}) copy-start(bf16[32,128,128]{2,1,0:T(8,128)(2,1)} %refs_6_.1) | copy-start | bytes 3145732
  2.3 6.3 %collective-permute-start = (bf16[2,128,128]{2,1,0:T(8,128)(2,1)S(1)}, bf16[2,128,128]{2,1,0:T(8,128)(2,1)S(1)}, u32[]{:S(2)}, u32[]{:S(2)}) collective-permute-start(bf16[2,128,128]{2,1,0:T(8,128)(2,1)S(1)} %get-tuple-element.25), channel_id=1, source_target_pairs={{0,2},{1,3},{2,4},{3,5},{4,6},{5,7},{6,8},{7,9},{8,10},{9,11},{10,... | collective-permute-start | bytes 196616 | tf_op jit(solution)/shard_map/ppermute | solution.py:758
  6.4 6.4 %collective-permute-start.1 = (bf16[2,128,128]{2,1,0:T(8,128)(2,1)S(1)}, bf16[2,128,128]{2,1,0:T(8,128)(2,1)S(1)}, u32[]{:S(2)}, u32[]{:S(2)}) collective-permute-start(bf16[2,128,128]{2,1,0:T(8,128)(2,1)S(1)} %get-tuple-element.26), channel_id=1, source_target_pairs={{2,0},{3,1},{4,2},{5,3},{6,4},{7,5},{8,6},{9,7},{10,8},{11,9},{12,... | collective-permute-start | bytes 196616 | tf_op jit(solution)/shard_map/ppermute | solution.py:758
  12.8 2.2 %collective-permute-start.2 = (f32[4,144,128]{2,1,0:T(8,128)S(1)}, f32[4,144,128]{2,1,0:T(8,128)S(1)}, u32[]{:S(2)}, u32[]{:S(2)}) collective-permute-start(f32[4,144,128]{2,1,0:T(8,128)S(1)} %frame.1), channel_id=1, source_target_pairs={{0,1},{1,0},{2,3},{3,2},{4,5},{5,4},{6,7},{7,6},{8,9},{9,8},{10,11... | collective-permute-start | bytes 884744 | tf_op jit(solution)/shard_map/ppermute | solution.py:758
  35.6 10.8 %all-to-all-start = ((bf16[4,144,256]{2,1,0:T(8,128)(2,1)}), bf16[4,144,256]{2,1,0:T(8,128)(2,1)S(1)}, u32[]{:S(2)}, u32[]{:S(2)}) async-start(bf16[4,144,256]{2,1,0:T(8,128)(2,1)} %get-tuple-element.29), calls=%async_computation | async-start | bytes 589824 | tf_op jit(solution)/shard_map/all_to_all | solution.py:794
  39.6 8.7 %collective-permute-start.6 = (bf16[128,128]{1,0:T(8,128)(2,1)S(1)}, bf16[128,128]{1,0:T(8,128)(2,1)S(1)}, u32[]{:S(2)}, u32[]{:S(2)}) collective-permute-start(bf16[128,128]{1,0:T(8,128)(2,1)S(1)} %get-tuple-element.34.refs_7_), channel_id=1, source_target_pairs={{24,0},{25,1},{26,2},{27,3},{28,4},{29,5},{30,6},{31,7}} | collective-permute-start | bytes 98312 | tf_op jit(solution)/shard_map/ppermute | solution.py:818
  40.9 11.7 %collective-permute-start.7 = (bf16[128,128]{1,0:T(8,128)(2,1)S(1)}, bf16[128,128]{1,0:T(8,128)(2,1)S(1)}, u32[]{:S(2)}, u32[]{:S(2)}) collective-permute-start(bf16[128,128]{1,0:T(8,128)(2,1)S(1)} %get-tuple-element.34.refs_7_), channel_id=1, source_target_pairs={{24,8},{25,9},{26,10},{27,11},{28,12},{29,13},{30,14},{31,15}} | collective-permute-start | bytes 98312 | tf_op jit(solution)/shard_map/ppermute | solution.py:818
  41.5 11.0 %collective-permute-start.8 = (bf16[128,128]{1,0:T(8,128)(2,1)S(1)}, bf16[128,128]{1,0:T(8,128)(2,1)S(1)}, u32[]{:S(2)}, u32[]{:S(2)}) collective-permute-start(bf16[128,128]{1,0:T(8,128)(2,1)S(1)} %get-tuple-element.34.refs_7_), channel_id=1, source_target_pairs={{24,16},{25,17},{26,18},{27,19},{28,20},{29,21},{30,22},{31,23}} | collective-permute-start | bytes 98312 | tf_op jit(solution)/shard_map/ppermute | solution.py:818
  46.7 5.8 %collective-permute-start.3 = (bf16[208,256]{1,0:T(8,128)(2,1)S(1)}, bf16[208,256]{1,0:T(8,128)(2,1)S(1)}, u32[]{:S(2)}, u32[]{:S(2)}) collective-permute-start(bf16[208,256]{1,0:T(8,128)(2,1)S(1)} %get-tuple-element.31), channel_id=1, source_target_pairs={{0,1},{1,2},{2,3},{3,4},{4,5},{5,6},{6,7},{7,0},{8,9},{9,10},{10,1... | collective-permute-start | bytes 319496 | tf_op jit(solution)/shard_map/ppermute | solution.py:812
  46.9 8.7 %collective-permute-start.4 = (bf16[208,256]{1,0:T(8,128)(2,1)S(1)}, bf16[208,256]{1,0:T(8,128)(2,1)S(1)}, u32[]{:S(2)}, u32[]{:S(2)}) collective-permute-start(bf16[208,256]{1,0:T(8,128)(2,1)S(1)} %get-tuple-element.32), channel_id=1, source_target_pairs={{0,2},{1,3},{2,4},{3,5},{4,6},{5,7},{6,0},{7,1},{8,10},{9,11},{10,... | collective-permute-start | bytes 319496 | tf_op jit(solution)/shard_map/ppermute | solution.py:812
  48.2 9.5 %collective-permute-start.5 = (bf16[208,256]{1,0:T(8,128)(2,1)S(1)}, bf16[208,256]{1,0:T(8,128)(2,1)S(1)}, u32[]{:S(2)}, u32[]{:S(2)}) collective-permute-start(bf16[208,256]{1,0:T(8,128)(2,1)S(1)} %get-tuple-element.33), channel_id=1, source_target_pairs={{0,3},{1,4},{2,5},{3,6},{4,7},{5,0},{6,1},{7,2},{8,11},{9,12},{10,... | collective-permute-start | bytes 319496 | tf_op jit(solution)/shard_map/ppermute | solution.py:812
  61.9 4.2 %collective-permute-start.9 = (f32[128,128]{1,0:T(8,128)S(1)}, f32[128,128]{1,0:T(8,128)S(1)}, u32[]{:S(2)}, u32[]{:S(2)}) collective-permute-start(f32[128,128]{1,0:T(8,128)S(1)} %get-tuple-element.36.refs_0_), channel_id=1, source_target_pairs={{0,8},{1,9},{2,10},{3,11},{4,12},{5,13},{6,14},{7,15},{8,16},{9,17... | collective-permute-start | bytes 196616 | tf_op jit(solution)/shard_map/ppermute | solution.py:802
  62.6 6.9 %collective-permute-start.13 = (f32[128,128]{1,0:T(8,128)S(1)}, f32[128,128]{1,0:T(8,128)S(1)}, u32[]{:S(2)}, u32[]{:S(2)}) collective-permute-start(f32[128,128]{1,0:T(8,128)S(1)} %get-tuple-element.36.refs_0_), channel_id=1, source_target_pairs={{0,16},{1,17},{2,18},{3,19},{4,20},{5,21},{6,22},{7,23},{8,24},{9,... | collective-permute-start | bytes 196616 | tf_op jit(solution)/shard_map/ppermute | solution.py:802
  63.5 6.0 %collective-permute-start.14 = (f32[128,128]{1,0:T(8,128)S(1)}, f32[128,128]{1,0:T(8,128)S(1)}, u32[]{:S(2)}, u32[]{:S(2)}) collective-permute-start(f32[128,128]{1,0:T(8,128)S(1)} %get-tuple-element.36.refs_0_), channel_id=1, source_target_pairs={{0,24},{1,25},{2,26},{3,27},{4,28},{5,29},{6,30},{7,31},{8,0},{9,1... | collective-permute-start | bytes 196616 | tf_op jit(solution)/shard_map/ppermute | solution.py:802
  66.0 11.8 %collective-permute-start.10 = (f32[2,128,128]{2,1,0:T(8,128)S(1)}, f32[2,128,128]{2,1,0:T(8,128)S(1)}, u32[]{:S(2)}, u32[]{:S(2)}) collective-permute-start(f32[2,128,128]{2,1,0:T(8,128)S(1)} %get-tuple-element.38.refs_3_), channel_id=1, source_target_pairs={{0,24},{1,25},{2,26},{3,27},{4,28},{5,29},{6,30},{7,31}} | collective-permute-start | bytes 393224 | tf_op jit(solution)/shard_map/ppermute | solution.py:824
  68.1 11.7 %collective-permute-start.11 = (f32[2,128,128]{2,1,0:T(8,128)S(1)}, f32[2,128,128]{2,1,0:T(8,128)S(1)}, u32[]{:S(2)}, u32[]{:S(2)}) collective-permute-start(f32[2,128,128]{2,1,0:T(8,128)S(1)} %get-tuple-element.38.refs_3_), channel_id=1, source_target_pairs={{8,24},{9,25},{10,26},{11,27},{12,28},{13,29},{14,30},{15,31}} | collective-permute-start | bytes 393224 | tf_op jit(solution)/shard_map/ppermute | solution.py:824
  68.7 11.1 %collective-permute-start.12 = (f32[2,128,128]{2,1,0:T(8,128)S(1)}, f32[2,128,128]{2,1,0:T(8,128)S(1)}, u32[]{:S(2)}, u32[]{:S(2)}) collective-permute-start(f32[2,128,128]{2,1,0:T(8,128)S(1)} %get-tuple-element.38.refs_3_), channel_id=1, source_target_pairs={{16,24},{17,25},{18,26},{19,27},{20,28},{21,29},{22,30},{23,31}} | collective-permute-start | bytes 393224 | tf_op jit(solution)/shard_map/ppermute | solution.py:824
  69.7 11.0 %collective-permute-start.15 = (f32[64,128]{1,0:T(8,128)S(1)}, f32[64,128]{1,0:T(8,128)S(1)}, u32[]{:S(2)}, u32[]{:S(2)}) collective-permute-start(f32[64,128]{1,0:T(8,128)S(1)} %get-tuple-element.43), channel_id=1, source_target_pairs={{0,7},{1,0},{2,1},{3,2},{4,3},{5,4},{6,5},{7,6},{8,15},{9,8},{10,9... | collective-permute-start | bytes 98312 | tf_op jit(solution)/shard_map/ppermute | solution.py:812
  75.5 5.2 %collective-permute-start.16 = (f32[64,128]{1,0:T(8,128)S(1)}, f32[64,128]{1,0:T(8,128)S(1)}, u32[]{:S(2)}, u32[]{:S(2)}) collective-permute-start(f32[64,128]{1,0:T(8,128)S(1)} %get-tuple-element.44), channel_id=1, source_target_pairs={{0,6},{1,7},{2,0},{3,1},{4,2},{5,3},{6,4},{7,5},{8,14},{9,15},{10,... | collective-permute-start | bytes 98312 | tf_op jit(solution)/shard_map/ppermute | solution.py:812
  77.9 6.1 %collective-permute-start.17 = (f32[64,128]{1,0:T(8,128)S(1)}, f32[64,128]{1,0:T(8,128)S(1)}, u32[]{:S(2)}, u32[]{:S(2)}) collective-permute-start(f32[64,128]{1,0:T(8,128)S(1)} %get-tuple-element.45), channel_id=1, source_target_pairs={{0,5},{1,6},{2,7},{3,0},{4,1},{5,2},{6,3},{7,4},{8,13},{9,14},{10,... | collective-permute-start | bytes 98312 | tf_op jit(solution)/shard_map/ppermute | solution.py:812

commit v16 on v14

--- a/solution.py
+++ b/solution.py
@@ -405,7 +405,7 @@
     )(flags, labels, state, *halos, mask, mix_atm, mix_ocn, flux_map_t)
 
 
-BATCH = 8
+BATCH = 16
 LABEL_ROWS = 16
 
 

time: 83.6 us -> 84.2 us (level)
  no operation moved by 1% of the time
where the time goes in v16:
time: 84.2 us; the launch traced here: 83.8 us
  starting transfers between devices  34.6 us (41%)
  Pallas kernels  27.4 us (33%)
  waiting for transfers between devices  19.5 us (23%)
  between operations  1.03 us (1%)
    pallas_call x1, Pallas kernels, advance(): pl.pallas_call(functools.partial(advance_kernel, comp_count, left_at, rig...  17.3 us
    ppermute x6, starting transfers between devices, over_tiles(): return lax.ppermute(value, AXES, pairs)  15.7 us
    ppermute x6, waiting for transfers between devices, over_tiles(): return lax.ppermute(value, AXES, pairs)  8.53 us
    ppermute x3, starting transfers between devices, band_shift(): return lax.ppermute(value, AXES, pairs)  6.35 us
    ppermute x3, waiting for transfers between devices, band_shift(): return lax.ppermute(value, AXES, pairs)  5.26 us
    pallas_call x1, Pallas kernels, regrid(): pl.pallas_call(functools.partial(regrid_body, count, comp_count), out_sha...  4.65 us
    all_to_all x1, waiting for transfers between devices, over_comp(): lax.all_to_all(value, 'comp', split_axis=0, concat_axis=0, tiled=True)  4.21 us
    all_to_all x1, starting transfers between devices, over_comp(): lax.all_to_all(value, 'comp', split_axis=0, concat_axis=0, tiled=True)  4 us
  transfers between devices with their start and end apart: 19, of which 7 were waited for; matrix products, arithmetic and copies ran while one was open for 1% of the time, Pallas kernels for 2%

profile of v16, /device:TPU:1, one launch (start us, length us, event | category | flops | bytes accessed | tf_op | source)
XLA Modules:
  0.0 83.8 jit_solution(9033043628009683670)
XLA Ops:
  0.7 1.6 %edges.1 = (bf16[2,128,128]{2,1,0:T(8,128)(2,1)S(1)}, bf16[2,128,128]{2,1,0:T(8,128)(2,1)S(1)}, f32[4,128,128]{2,1,0:T(8,128)S(1)}) custom-call(f32[128,128,128]{2,1,0:T(8,128)} %refs_2_.1), custom_call_target="tpu_custom_call" | custom-call | tf_op jit(solution)/shard_map/edges/pallas_call | solution.py:63
  2.3 4.0 %collective-permute-start = (bf16[2,128,128]{2,1,0:T(8,128)(2,1)S(1)}, bf16[2,128,128]{2,1,0:T(8,128)(2,1)S(1)}, u32[]{:S(2)}, u32[]{:S(2)}) collective-permute-start(bf16[2,128,128]{2,1,0:T(8,128)(2,1)S(1)} %get-tuple-element.25), channel_id=1, source_target_pairs={{0,2},{1,3},{2,4},{3,5},{4,6},{5,7},{6,8},{7,9},{8,10},{9,11},{10,... | collective-permute-start | bytes 196616 | tf_op jit(solution)/shard_map/ppermute | solution.py:759
  6.4 1.3 %collective-permute-start.1 = (bf16[2,128,128]{2,1,0:T(8,128)(2,1)S(1)}, bf16[2,128,128]{2,1,0:T(8,128)(2,1)S(1)}, u32[]{:S(2)}, u32[]{:S(2)}) collective-permute-start(bf16[2,128,128]{2,1,0:T(8,128)(2,1)S(1)} %get-tuple-element.26), channel_id=1, source_target_pairs={{2,0},{3,1},{4,2},{5,3},{6,4},{7,5},{8,6},{9,7},{10,8},{11,9},{12,... | collective-permute-start | bytes 196616 | tf_op jit(solution)/shard_map/ppermute | solution.py:759
  7.7 0.2 copy.18
  7.9 0.3 fusion.4
  8.1 0.2 convert_reduce_fusion
  8.3 0.2 select_reduce_fusion.1
  8.6 0.0 collective-permute-done.up_rows.refs_3_
  8.6 4.1 %collective-permute-done.1.low_rows.refs_4_ = bf16[2,128,128]{2,1,0:T(8,128)(2,1)S(1)} collective-permute-done((bf16[2,128,128]{2,1,0:T(8,128)(2,1)S(1)}, bf16[2,128,128]{2,1,0:T(8,128)(2,1)S(1)}, u32[]{:S(2)}, u32[]{:S(2)}) %collective-permute-start.1) | collective-permute-done | bytes 65568 | tf_op jit(solution)/shard_map/ppermute | solution.py:759
  12.8 1.0 %collective-permute-start.2 = (f32[4,144,128]{2,1,0:T(8,128)S(1)}, f32[4,144,128]{2,1,0:T(8,128)S(1)}, u32[]{:S(2)}, u32[]{:S(2)}) collective-permute-start(f32[4,144,128]{2,1,0:T(8,128)S(1)} %frame.1), channel_id=1, source_target_pairs={{0,1},{1,0},{2,3},{3,2},{4,5},{5,4},{6,7},{7,6},{8,9},{9,8},{10,11... | collective-permute-start | bytes 884744 | tf_op jit(solution)/shard_map/ppermute | solution.py:759
  13.8 0.1 pad_add_fusion.refs_0_.flags
  13.9 1.1 %collective-permute-done.2.refs_5_.refs_6_ = f32[4,144,128]{2,1,0:T(8,128)S(1)} collective-permute-done((f32[4,144,128]{2,1,0:T(8,128)S(1)}, f32[4,144,128]{2,1,0:T(8,128)S(1)}, u32[]{:S(2)}, u32[]{:S(2)}) %collective-permute-start.2) | collective-permute-done | bytes 294944 | tf_op jit(solution)/shard_map/ppermute | solution.py:759
  15.0 17.3 %advance.1 = (f32[128,128,128]{2,1,0:T(8,128)}, f32[128,128]{1,0:T(8,128)S(1)}, bf16[128,128]{1,0:T(8,128)(2,1)S(1)}, bf16[4,144,256]{2,1,0:T(8,128)(2,1)}) custom-call(s32[4]{0:T(128)S(1)} %pad_add_fusion.refs_0_.flags, bf16[16,256]{1,0:T(8,128)(2,1)S(1)} %fusion.11.refs_1_, f32[128,128,128]{2,1,0:T(8,128)} %refs_2_.1, ...), custom_call_target="tpu_custom_call" | custom-call | flops 2147483648 | bytes 16777216 | tf_op jit(solution)/shard_map/advance/pallas_call | solution.py:371
  32.3 4.0 %all-to-all-start = ((bf16[4,144,256]{2,1,0:T(8,128)(2,1)}), bf16[4,144,256]{2,1,0:T(8,128)(2,1)S(1)}, u32[]{:S(2)}, u32[]{:S(2)}) async-start(bf16[4,144,256]{2,1,0:T(8,128)(2,1)} %get-tuple-element.29), calls=%async_computation | async-start | bytes 589824 | tf_op jit(solution)/shard_map/all_to_all | solution.py:795
  36.3 1.3 %collective-permute-start.6 = (bf16[128,128]{1,0:T(8,128)(2,1)S(1)}, bf16[128,128]{1,0:T(8,128)(2,1)S(1)}, u32[]{:S(2)}, u32[]{:S(2)}) collective-permute-start(bf16[128,128]{1,0:T(8,128)(2,1)S(1)} %get-tuple-element.34.refs_7_), channel_id=1, source_target_pairs={{24,0},{25,1},{26,2},{27,3},{28,4},{29,5},{30,6},{31,7}} | collective-permute-start | bytes 98312 | tf_op jit(solution)/shard_map/ppermute | solution.py:819
  37.6 0.7 collective-permute-start.7
  38.3 0.7 collective-permute-start.8
  39.0 4.2 %all-to-all-done.slabs = bf16[4,144,256]{2,1,0:T(8,128)(2,1)S(1)} async-done(((bf16[4,144,256]{2,1,0:T(8,128)(2,1)}), bf16[4,144,256]{2,1,0:T(8,128)(2,1)S(1)}, u32[]{:S(2)}, u32[]{:S(2)}) %all-to-all-start) | async-done | bytes 294944 | tf_op jit(solution)/shard_map/all_to_all | solution.py:795
  43.2 0.3 regroup.1
  43.5 0.2 collective-permute-start.3
  43.7 1.3 %collective-permute-start.4 = (bf16[208,256]{1,0:T(8,128)(2,1)S(1)}, bf16[208,256]{1,0:T(8,128)(2,1)S(1)}, u32[]{:S(2)}, u32[]{:S(2)}) collective-permute-start(bf16[208,256]{1,0:T(8,128)(2,1)S(1)} %get-tuple-element.32), channel_id=1, source_target_pairs={{0,2},{1,3},{2,4},{3,5},{4,6},{5,7},{6,0},{7,1},{8,10},{9,11},{10,... | collective-permute-start | bytes 319496 | tf_op jit(solution)/shard_map/ppermute | solution.py:813
  45.0 0.0 collective-permute-done.6.refs_4_
  45.0 4.1 %collective-permute-start.5 = (bf16[208,256]{1,0:T(8,128)(2,1)S(1)}, bf16[208,256]{1,0:T(8,128)(2,1)S(1)}, u32[]{:S(2)}, u32[]{:S(2)}) collective-permute-start(bf16[208,256]{1,0:T(8,128)(2,1)S(1)} %get-tuple-element.33), channel_id=1, source_target_pairs={{0,3},{1,4},{2,5},{3,6},{4,7},{5,0},{6,1},{7,2},{8,11},{9,12},{10,... | collective-permute-start | bytes 319496 | tf_op jit(solution)/shard_map/ppermute | solution.py:813
  49.2 0.1 slice_reduce_fusion.ocean_first
  49.3 0.0 collective-permute-done.8.refs_6_
  49.3 3.2 %collective-permute-done.4.refs_2_ = bf16[208,256]{1,0:T(8,128)(2,1)S(1)} collective-permute-done((bf16[208,256]{1,0:T(8,128)(2,1)S(1)}, bf16[208,256]{1,0:T(8,128)(2,1)S(1)}, u32[]{:S(2)}, u32[]{:S(2)}) %collective-permute-start.4) | collective-permute-done | bytes 106528 | tf_op jit(solution)/shard_map/ppermute | solution.py:813
  52.5 2.1 %collective-permute-done.5.refs_3_ = bf16[208,256]{1,0:T(8,128)(2,1)S(1)} collective-permute-done((bf16[208,256]{1,0:T(8,128)(2,1)S(1)}, bf16[208,256]{1,0:T(8,128)(2,1)S(1)}, u32[]{:S(2)}, u32[]{:S(2)}) %collective-permute-start.5) | collective-permute-done | bytes 106528 | tf_op jit(solution)/shard_map/ppermute | solution.py:813
  54.5 4.6 %regrid.1 = (f32[2,128,128]{2,1,0:T(8,128)S(1)}, f32[128,128]{1,0:T(8,128)S(1)}, bf16[256,128]{1,0:T(8,128)(2,1)S(1)}) custom-call(s32[4]{0:T(128)S(1)} %pad_add_fusion.refs_0_.flags, f32[8]{0:T(128)S(1)} %slice_reduce_fusion.ocean_first, bf16[208,256]{1,0:T(8,128)(2,1)S(1)} %get-tuple-element.30.refs_0_, ...), custom_call_target="tpu_custom_call" | custom-call | flops 2147483648 | bytes 2097152 | tf_op jit(solution)/shard_map/regrid/pallas_call | solution.py:528
  59.2 0.6 collective-permute-start.9
  59.8 0.1 copy.19
  59.9 0.9 %collective-permute-start.13 = (f32[128,128]{1,0:T(8,128)S(1)}, f32[128,128]{1,0:T(8,128)S(1)}, u32[]{:S(2)}, u32[]{:S(2)}) collective-permute-start(f32[128,128]{1,0:T(8,128)S(1)} %get-tuple-element.36.refs_0_), channel_id=1, source_target_pairs={{0,16},{1,17},{2,18},{3,19},{4,20},{5,21},{6,22},{7,23},{8,24},{9,... | collective-permute-start | bytes 196616 | tf_op jit(solution)/shard_map/ppermute | solution.py:803
  60.9 1.0 %collective-permute-start.14 = (f32[128,128]{1,0:T(8,128)S(1)}, f32[128,128]{1,0:T(8,128)S(1)}, u32[]{:S(2)}, u32[]{:S(2)}) collective-permute-start(f32[128,128]{1,0:T(8,128)S(1)} %get-tuple-element.36.refs_0_), channel_id=1, source_target_pairs={{0,24},{1,25},{2,26},{3,27},{4,28},{5,29},{6,30},{7,31},{8,0},{9,1... | collective-permute-start | bytes 196616 | tf_op jit(solution)/shard_map/ppermute | solution.py:803
  61.9 1.5 %collective-permute-done.9.refs_1_ = f32[128,128]{1,0:T(8,128)S(1)} collective-permute-done((f32[128,128]{1,0:T(8,128)S(1)}, f32[128,128]{1,0:T(8,128)S(1)}, u32[]{:S(2)}, u32[]{:S(2)}) %collective-permute-start.9) | collective-permute-done | bytes 65568 | tf_op jit(solution)/shard_map/ppermute | solution.py:803
  63.4 2.0 %collective-permute-start.10 = (f32[2,128,128]{2,1,0:T(8,128)S(1)}, f32[2,128,128]{2,1,0:T(8,128)S(1)}, u32[]{:S(2)}, u32[]{:S(2)}) collective-permute-start(f32[2,128,128]{2,1,0:T(8,128)S(1)} %get-tuple-element.38.refs_3_), channel_id=1, source_target_pairs={{0,24},{1,25},{2,26},{3,27},{4,28},{5,29},{6,30},{7,31}} | collective-permute-start | bytes 393224 | tf_op jit(solution)/shard_map/ppermute | solution.py:825
  65.4 0.7 collective-permute-start.11
  66.1 0.7 collective-permute-start.12
  66.7 0.1 add_select_fusion.refs_4_
  66.8 0.0 collective-permute-done.14.refs_3_
  66.8 0.2 pick.1
  67.0 5.8 %collective-permute-start.15 = (f32[64,128]{1,0:T(8,128)S(1)}, f32[64,128]{1,0:T(8,128)S(1)}, u32[]{:S(2)}, u32[]{:S(2)}) collective-permute-start(f32[64,128]{1,0:T(8,128)S(1)} %get-tuple-element.43), channel_id=1, source_target_pairs={{0,7},{1,0},{2,1},{3,2},{4,3},{5,4},{6,5},{7,6},{8,15},{9,8},{10,9... | collective-permute-start | bytes 98312 | tf_op jit(solution)/shard_map/ppermute | solution.py:813
  72.8 2.3 %collective-permute-start.16 = (f32[64,128]{1,0:T(8,128)S(1)}, f32[64,128]{1,0:T(8,128)S(1)}, u32[]{:S(2)}, u32[]{:S(2)}) collective-permute-start(f32[64,128]{1,0:T(8,128)S(1)} %get-tuple-element.44), channel_id=1, source_target_pairs={{0,6},{1,7},{2,0},{3,1},{4,2},{5,3},{6,4},{7,5},{8,14},{9,15},{10,... | collective-permute-start | bytes 98312 | tf_op jit(solution)/shard_map/ppermute | solution.py:813
  75.2 0.0 collective-permute-done.10.refs_0_
  75.2 1.9 %collective-permute-start.17 = (f32[64,128]{1,0:T(8,128)S(1)}, f32[64,128]{1,0:T(8,128)S(1)}, u32[]{:S(2)}, u32[]{:S(2)}) collective-permute-start(f32[64,128]{1,0:T(8,128)S(1)} %get-tuple-element.45), channel_id=1, source_target_pairs={{0,5},{1,6},{2,7},{3,0},{4,1},{5,2},{6,3},{7,4},{8,13},{9,14},{10,... | collective-permute-start | bytes 98312 | tf_op jit(solution)/shard_map/ppermute | solution.py:813
  77.1 0.0 collective-permute-done.12.refs_2_
  77.1 0.8 %update.1 = (f32[128,128,128]{2,1,0:T(8,128)}, f32[8,128]{1,0:T(8,128)S(1)}) custom-call(s32[4]{0:T(128)S(1)} %pad_add_fusion.refs_0_.flags, f32[128,128,128]{2,1,0:T(8,128)} %get-tuple-element.28.state, f32[2,128,128]{2,1,0:T(8,128)S(1)} %collective-permute-done.10.refs_0_, ...), custom_call_target="tpu_custom_call", output_to_operand_aliasing={{0}: (1, {})} | custom-call | flops 805306368 | bytes 16777216 | tf_op jit(solution)/shard_map/update/pallas_call | solution.py:649
  78.0 0.0 collective-permute-done.15.refs_1_
  78.0 3.3 %collective-permute-done.17.refs_3_ = f32[64,128]{1,0:T(8,128)S(1)} collective-permute-done((f32[64,128]{1,0:T(8,128)S(1)}, f32[64,128]{1,0:T(8,128)S(1)}, u32[]{:S(2)}, u32[]{:S(2)}) %collective-permute-start.17) | collective-permute-done | bytes 32800 | tf_op jit(solution)/shard_map/ppermute | solution.py:813
  81.3 2.4 %returned.1 = f32[128,128]{1,0:T(8,128)} custom-call(s32[4]{0:T(128)S(1)} %pad_add_fusion.refs_0_.flags, f32[64,128]{1,0:T(8,128)S(1)} %get-tuple-element.42.refs_0_, f32[64,128]{1,0:T(8,128)S(1)} %collective-permute-done.15.refs_1_, f32[64,128]{1,0:T(8,128)S(1)} %collective-permute-done.16.refs_2_, f32[64,128]{1,0:T(8,128)S(1)} %collective-permute-done.17.refs_3_, ...), custom_call_target="tpu_custom_call" | custom-call | tf_op jit(solution)/shard_map/returned/pallas_call | solution.py:713
  (27 shorter events, 0.1 us)
Async XLA Ops:
  0.6 7.0 %copy-start.6 = (s32[128,1,2,3]{0,2,3,1:T(2,128)S(1)}, s32[128,1,2,3]{0,2,3,1:T(2,128)}, u32[]{:S(2)}) copy-start(s32[128,1,2,3]{0,2,3,1:T(2,128)} %param.11) | copy-start | bytes 9220
  0.6 13.2 %copy-start.5 = (s32[128,128]{1,0:T(8,128)S(1)}, s32[128,128]{1,0:T(8,128)}, u32[]{:S(2)}) copy-start(s32[128,128]{1,0:T(8,128)} %param.10) | copy-start | bytes 196612
  0.7 14.3 %copy-start.4 = (f32[128,8]{0,1:T(8,128)S(1)}, f32[128,8]{0,1:T(8,128)}, u32[]{:S(2)}) copy-start(f32[128,8]{0,1:T(8,128)} %param.14) | copy-start | bytes 12292
  0.7 14.3 %copy-start.1 = (f32[128,128]{1,0:T(8,128)S(1)}, f32[128,128]{1,0:T(8,128)}, u32[]{:S(2)}) copy-start(f32[128,128]{1,0:T(8,128)} %refs_9_.1) | copy-start | bytes 196612
  0.7 14.3 %copy-start.2 = (f32[128,128]{1,0:T(8,128)S(1)}, f32[128,128]{1,0:T(8,128)}, u32[]{:S(2)}) copy-start(f32[128,128]{1,0:T(8,128)} %refs_10_.1) | copy-start | bytes 196612
  0.7 48.5 %copy-start.3 = (f32[8,128]{1,0:T(8,128)S(1)}, f32[8,128]{1,0:T(8,128)}, u32[]{:S(2)}) copy-start(f32[8,128]{1,0:T(8,128)} %refs_5_.1) | copy-start | bytes 12292
  0.7 53.8 %copy-start = (bf16[32,128,128]{2,1,0:T(8,128)(2,1)S(1)}, bf16[32,128,128]{2,1,0:T(8,128)(2,1)}, u32[]{:S(2)}) copy-start(bf16[32,128,128]{2,1,0:T(8,128)(2,1)} %refs_6_.1) | copy-start | bytes 3145732
  2.3 6.3 %collective-permute-start = (bf16[2,128,128]{2,1,0:T(8,128)(2,1)S(1)}, bf16[2,128,128]{2,1,0:T(8,128)(2,1)S(1)}, u32[]{:S(2)}, u32[]{:S(2)}) collective-permute-start(bf16[2,128,128]{2,1,0:T(8,128)(2,1)S(1)} %get-tuple-element.25), channel_id=1, source_target_pairs={{0,2},{1,3},{2,4},{3,5},{4,6},{5,7},{6,8},{7,9},{8,10},{9,11},{10,... | collective-permute-start | bytes 196616 | tf_op jit(solution)/shard_map/ppermute | solution.py:759
  6.4 6.4 %collective-permute-start.1 = (bf16[2,128,128]{2,1,0:T(8,128)(2,1)S(1)}, bf16[2,128,128]{2,1,0:T(8,128)(2,1)S(1)}, u32[]{:S(2)}, u32[]{:S(2)}) collective-permute-start(bf16[2,128,128]{2,1,0:T(8,128)(2,1)S(1)} %get-tuple-element.26), channel_id=1, source_target_pairs={{2,0},{3,1},{4,2},{5,3},{6,4},{7,5},{8,6},{9,7},{10,8},{11,9},{12,... | collective-permute-start | bytes 196616 | tf_op jit(solution)/shard_map/ppermute | solution.py:759
  12.8 2.2 %collective-permute-start.2 = (f32[4,144,128]{2,1,0:T(8,128)S(1)}, f32[4,144,128]{2,1,0:T(8,128)S(1)}, u32[]{:S(2)}, u32[]{:S(2)}) collective-permute-start(f32[4,144,128]{2,1,0:T(8,128)S(1)} %frame.1), channel_id=1, source_target_pairs={{0,1},{1,0},{2,3},{3,2},{4,5},{5,4},{6,7},{7,6},{8,9},{9,8},{10,11... | collective-permute-start | bytes 884744 | tf_op jit(solution)/shard_map/ppermute | solution.py:759
  32.3 10.8 %all-to-all-start = ((bf16[4,144,256]{2,1,0:T(8,128)(2,1)}), bf16[4,144,256]{2,1,0:T(8,128)(2,1)S(1)}, u32[]{:S(2)}, u32[]{:S(2)}) async-start(bf16[4,144,256]{2,1,0:T(8,128)(2,1)} %get-tuple-element.29), calls=%async_computation | async-start | bytes 589824 | tf_op jit(solution)/shard_map/all_to_all | solution.py:795
  36.3 8.7 %collective-permute-start.6 = (bf16[128,128]{1,0:T(8,128)(2,1)S(1)}, bf16[128,128]{1,0:T(8,128)(2,1)S(1)}, u32[]{:S(2)}, u32[]{:S(2)}) collective-permute-start(bf16[128,128]{1,0:T(8,128)(2,1)S(1)} %get-tuple-element.34.refs_7_), channel_id=1, source_target_pairs={{24,0},{25,1},{26,2},{27,3},{28,4},{29,5},{30,6},{31,7}} | collective-permute-start | bytes 98312 | tf_op jit(solution)/shard_map/ppermute | solution.py:819
  37.6 11.7 %collective-permute-start.7 = (bf16[128,128]{1,0:T(8,128)(2,1)S(1)}, bf16[128,128]{1,0:T(8,128)(2,1)S(1)}, u32[]{:S(2)}, u32[]{:S(2)}) collective-permute-start(bf16[128,128]{1,0:T(8,128)(2,1)S(1)} %get-tuple-element.34.refs_7_), channel_id=1, source_target_pairs={{24,8},{25,9},{26,10},{27,11},{28,12},{29,13},{30,14},{31,15}} | collective-permute-start | bytes 98312 | tf_op jit(solution)/shard_map/ppermute | solution.py:819
  38.3 11.0 %collective-permute-start.8 = (bf16[128,128]{1,0:T(8,128)(2,1)S(1)}, bf16[128,128]{1,0:T(8,128)(2,1)S(1)}, u32[]{:S(2)}, u32[]{:S(2)}) collective-permute-start(bf16[128,128]{1,0:T(8,128)(2,1)S(1)} %get-tuple-element.34.refs_7_), channel_id=1, source_target_pairs={{24,16},{25,17},{26,18},{27,19},{28,20},{29,21},{30,22},{31,23}} | collective-permute-start | bytes 98312 | tf_op jit(solution)/shard_map/ppermute | solution.py:819
  43.5 5.8 %collective-permute-start.3 = (bf16[208,256]{1,0:T(8,128)(2,1)S(1)}, bf16[208,256]{1,0:T(8,128)(2,1)S(1)}, u32[]{:S(2)}, u32[]{:S(2)}) collective-permute-start(bf16[208,256]{1,0:T(8,128)(2,1)S(1)} %get-tuple-element.31), channel_id=1, source_target_pairs={{0,1},{1,2},{2,3},{3,4},{4,5},{5,6},{6,7},{7,0},{8,9},{9,10},{10,1... | collective-permute-start | bytes 319496 | tf_op jit(solution)/shard_map/ppermute | solution.py:813
  43.7 8.7 %collective-permute-start.4 = (bf16[208,256]{1,0:T(8,128)(2,1)S(1)}, bf16[208,256]{1,0:T(8,128)(2,1)S(1)}, u32[]{:S(2)}, u32[]{:S(2)}) collective-permute-start(bf16[208,256]{1,0:T(8,128)(2,1)S(1)} %get-tuple-element.32), channel_id=1, source_target_pairs={{0,2},{1,3},{2,4},{3,5},{4,6},{5,7},{6,0},{7,1},{8,10},{9,11},{10,... | collective-permute-start | bytes 319496 | tf_op jit(solution)/shard_map/ppermute | solution.py:813
  45.0 9.5 %collective-permute-start.5 = (bf16[208,256]{1,0:T(8,128)(2,1)S(1)}, bf16[208,256]{1,0:T(8,128)(2,1)S(1)}, u32[]{:S(2)}, u32[]{:S(2)}) collective-permute-start(bf16[208,256]{1,0:T(8,128)(2,1)S(1)} %get-tuple-element.33), channel_id=1, source_target_pairs={{0,3},{1,4},{2,5},{3,6},{4,7},{5,0},{6,1},{7,2},{8,11},{9,12},{10,... | collective-permute-start | bytes 319496 | tf_op jit(solution)/shard_map/ppermute | solution.py:813
  59.2 4.2 %collective-permute-start.9 = (f32[128,128]{1,0:T(8,128)S(1)}, f32[128,128]{1,0:T(8,128)S(1)}, u32[]{:S(2)}, u32[]{:S(2)}) collective-permute-start(f32[128,128]{1,0:T(8,128)S(1)} %get-tuple-element.36.refs_0_), channel_id=1, source_target_pairs={{0,8},{1,9},{2,10},{3,11},{4,12},{5,13},{6,14},{7,15},{8,16},{9,17... | collective-permute-start | bytes 196616 | tf_op jit(solution)/shard_map/ppermute | solution.py:803
  59.9 6.9 %collective-permute-start.13 = (f32[128,128]{1,0:T(8,128)S(1)}, f32[128,128]{1,0:T(8,128)S(1)}, u32[]{:S(2)}, u32[]{:S(2)}) collective-permute-start(f32[128,128]{1,0:T(8,128)S(1)} %get-tuple-element.36.refs_0_), channel_id=1, source_target_pairs={{0,16},{1,17},{2,18},{3,19},{4,20},{5,21},{6,22},{7,23},{8,24},{9,... | collective-permute-start | bytes 196616 | tf_op jit(solution)/shard_map/ppermute | solution.py:803
  60.9 6.0 %collective-permute-start.14 = (f32[128,128]{1,0:T(8,128)S(1)}, f32[128,128]{1,0:T(8,128)S(1)}, u32[]{:S(2)}, u32[]{:S(2)}) collective-permute-start(f32[128,128]{1,0:T(8,128)S(1)} %get-tuple-element.36.refs_0_), channel_id=1, source_target_pairs={{0,24},{1,25},{2,26},{3,27},{4,28},{5,29},{6,30},{7,31},{8,0},{9,1... | collective-permute-start | bytes 196616 | tf_op jit(solution)/shard_map/ppermute | solution.py:803
  63.4 11.8 %collective-permute-start.10 = (f32[2,128,128]{2,1,0:T(8,128)S(1)}, f32[2,128,128]{2,1,0:T(8,128)S(1)}, u32[]{:S(2)}, u32[]{:S(2)}) collective-permute-start(f32[2,128,128]{2,1,0:T(8,128)S(1)} %get-tuple-element.38.refs_3_), channel_id=1, source_target_pairs={{0,24},{1,25},{2,26},{3,27},{4,28},{5,29},{6,30},{7,31}} | collective-permute-start | bytes 393224 | tf_op jit(solution)/shard_map/ppermute | solution.py:825
  65.4 11.7 %collective-permute-start.11 = (f32[2,128,128]{2,1,0:T(8,128)S(1)}, f32[2,128,128]{2,1,0:T(8,128)S(1)}, u32[]{:S(2)}, u32[]{:S(2)}) collective-permute-start(f32[2,128,128]{2,1,0:T(8,128)S(1)} %get-tuple-element.38.refs_3_), channel_id=1, source_target_pairs={{8,24},{9,25},{10,26},{11,27},{12,28},{13,29},{14,30},{15,31}} | collective-permute-start | bytes 393224 | tf_op jit(solution)/shard_map/ppermute | solution.py:825
  66.1 11.1 %collective-permute-start.12 = (f32[2,128,128]{2,1,0:T(8,128)S(1)}, f32[2,128,128]{2,1,0:T(8,128)S(1)}, u32[]{:S(2)}, u32[]{:S(2)}) collective-permute-start(f32[2,128,128]{2,1,0:T(8,128)S(1)} %get-tuple-element.38.refs_3_), channel_id=1, source_target_pairs={{16,24},{17,25},{18,26},{19,27},{20,28},{21,29},{22,30},{23,31}} | collective-permute-start | bytes 393224 | tf_op jit(solution)/shard_map/ppermute | solution.py:825
  67.0 11.0 %collective-permute-start.15 = (f32[64,128]{1,0:T(8,128)S(1)}, f32[64,128]{1,0:T(8,128)S(1)}, u32[]{:S(2)}, u32[]{:S(2)}) collective-permute-start(f32[64,128]{1,0:T(8,128)S(1)} %get-tuple-element.43), channel_id=1, source_target_pairs={{0,7},{1,0},{2,1},{3,2},{4,3},{5,4},{6,5},{7,6},{8,15},{9,8},{10,9... | collective-permute-start | bytes 98312 | tf_op jit(solution)/shard_map/ppermute | solution.py:813
  72.8 5.2 %collective-permute-start.16 = (f32[64,128]{1,0:T(8,128)S(1)}, f32[64,128]{1,0:T(8,128)S(1)}, u32[]{:S(2)}, u32[]{:S(2)}) collective-permute-start(f32[64,128]{1,0:T(8,128)S(1)} %get-tuple-element.44), channel_id=1, source_target_pairs={{0,6},{1,7},{2,0},{3,1},{4,2},{5,3},{6,4},{7,5},{8,14},{9,15},{10,... | collective-permute-start | bytes 98312 | tf_op jit(solution)/shard_map/ppermute | solution.py:813
  75.2 6.1 %collective-permute-start.17 = (f32[64,128]{1,0:T(8,128)S(1)}, f32[64,128]{1,0:T(8,128)S(1)}, u32[]{:S(2)}, u32[]{:S(2)}) collective-permute-start(f32[64,128]{1,0:T(8,128)S(1)} %get-tuple-element.45), channel_id=1, source_target_pairs={{0,5},{1,6},{2,7},{3,0},{4,1},{5,2},{6,3},{7,4},{8,13},{9,14},{10,... | collective-permute-start | bytes 98312 | tf_op jit(solution)/shard_map/ppermute | solution.py:813
